TPU v7x, 32 devices: a whole 2x2x4 slice. The times are simulated.
32 devices in a mesh: fsdp: 8 (over y, x, core), dp: 4 (over z).
Axes of the slice: x: 2, y: 2, z: 4, core: 2. Of those that a mesh axis runs over, the one named last changes fastest.
Arguments:
- inputs: bfloat16 [32768, 768], P(('fsdp', 'dp')), may hold values from -6 to 6
- time_of_row: float32 [32768], P(('fsdp', 'dp')), may hold values from 0 to 1
- coords: float32 [3, 32768], P(None, ('fsdp', 'dp')), may hold values from -8 to 8
- segment_ids: int32 [32768], P(('fsdp', 'dp')), may hold values from 0 to 2047, never falling along the last dimension, each value on 1 to 48 neighbouring positions
- cotangent: bfloat16 [32768, 768], P(('fsdp', 'dp')), may hold values from -6 to 6
- time_weight: bfloat16 [768], P('fsdp'), may hold values from -5 to 5
- ln1_gain: bfloat16 [768], P('fsdp'), may hold values from 0.5 to 1.5
- ln1_bias: bfloat16 [768], P('fsdp'), may hold values from -1.5 to 1.5
- w_qkv: bfloat16 [768, 2304], P('fsdp'), may hold values from -0.21875 to 0.21875
- q_bias: bfloat16 [768], P('fsdp'), may hold values from -2.5 to 2.5
- v_bias: bfloat16 [768], P('fsdp'), may hold values from -1.5 to 1.5
- w_out: bfloat16 [768, 768], P('fsdp'), may hold values from -0.875 to 0.875
- out_bias: bfloat16 [768], P('fsdp'), may hold values from -1.5 to 1.5
- kernel_mean: bfloat16 [128], P('fsdp'), may hold values from 0 to 8
- kernel_width: bfloat16 [128], P('fsdp'), may hold values from 0.5 to 3
- kernel_map: bfloat16 [128, 32], P('fsdp'), may hold values from -2 to 2
- ln2_gain: bfloat16 [768], P('fsdp'), may hold values from 0.5 to 1.5
- ln2_bias: bfloat16 [768], P('fsdp'), may hold values from -1.5 to 1.5
- w_up: bfloat16 [768, 3072], P('fsdp'), may hold values from -0.21875 to 0.21875
- up_bias: bfloat16 [3072], P('fsdp'), may hold values from -1.5 to 1.5
- w_down: bfloat16 [3072, 768], P('fsdp'), may hold values from -0.109375 to 0.109375
- down_bias: bfloat16 [768], P('fsdp'), may hold values from -1.5 to 1.5
Outputs:
- output: bfloat16 [32768, 768], P(('fsdp', 'dp'))
- grad_inputs: bfloat16 [32768, 768], P(('fsdp', 'dp'))
- grad_time_weight: float32 [768], P('fsdp')
- grad_ln1_gain: float32 [768], P('fsdp')
- grad_ln1_bias: float32 [768], P('fsdp')
- grad_w_qkv: float32 [768, 2304], P('fsdp')
- grad_q_bias: float32 [768], P('fsdp')
- grad_v_bias: float32 [768], P('fsdp')
- grad_w_out: float32 [768, 768], P('fsdp')
- grad_out_bias: float32 [768], P('fsdp')
- grad_kernel_mean: float32 [128], P('fsdp')
- grad_kernel_width: float32 [128], P('fsdp')
- grad_kernel_map: float32 [128, 32], P('fsdp')
- grad_ln2_gain: float32 [768], P('fsdp')
- grad_ln2_bias: float32 [768], P('fsdp')
- grad_w_up: float32 [768, 3072], P('fsdp')
- grad_up_bias: float32 [3072], P('fsdp')
- grad_w_down: float32 [3072, 768], P('fsdp')
- grad_down_bias: float32 [768], P('fsdp')
Inputs may be any that keep to these rules, and one draw needn't show every extreme that they name: segment_ids never falls along the rows; each id covers 1 to 48 consecutive rows and some id exactly 48.
All inputs are finite; a program needn't handle non-finite values.
Results may differ from a plain program's by a relative error of at most 0.017.
Values may be sent and summed in bfloat16 or wider, within the bound.
No kernel may reach another device: no remote copies, remote signals or barrier semaphores. Data moves between devices by JAX's collectives and lax.ppermute only.
A program may use at most 192 MiB of HBM per device.

v0:
```python
from functools import partial
import math

import jax
import jax.numpy as jnp
from jax import lax
from jax.sharding import PartitionSpec as P

SET = 256


epsilon = 1e-05
root_tau = math.sqrt(2.0 * math.pi)
masked_fill = -1e30


def layer_norm(values_in, gain_vec, shift_vec):
    average = jnp.mean(values_in, axis=-1, keepdims=True)
    centred = values_in - average
    variance = jnp.mean(centred * centred, axis=-1, keepdims=True)
    return centred * lax.rsqrt(variance + epsilon) * gain_vec + shift_vec


def contract_rows(left, right):
    return lax.dot_general(
        left, right, (((0,), (0,)), ((), ())), preferred_element_type=jnp.float32
    )


def times_transpose(left, right):
    return lax.dot_general(
        left, right, (((1,), (1,)), ((), ())), preferred_element_type=jnp.float32
    )


def block_scores(queries_b, keys_b, coords_b, segs_b, kernel_mean, kernel_width, kernel_map):
    offsets = coords_b[:, :, :, None] - coords_b[:, :, None, :]
    radius = jnp.sqrt(jnp.sum(offsets * offsets, axis=1))
    standard = (radius[..., None] - kernel_mean) / kernel_width
    features = jnp.exp(-0.5 * standard * standard) / (root_tau * kernel_width)
    features_low = features.astype(jnp.bfloat16)
    pair_bias = jnp.einsum(
        "bijk,kh->bhij", features_low, kernel_map, preferred_element_type=jnp.float32
    )
    scores = (
        jnp.einsum("bihe,bjhe->bhij", queries_b, keys_b, preferred_element_type=jnp.float32)
        + pair_bias
    )
    joined = segs_b[:, :, None] == segs_b[:, None, :]
    scores = jnp.where(joined[:, None], scores, masked_fill)
    return (scores, features, features_low, standard)


def attend_forward(pieces, kernel_mean, kernel_width, kernel_map):
    queries_b, keys_b, values_b, coords_b, segs_b = pieces
    scores = block_scores(
        queries_b, keys_b, coords_b, segs_b, kernel_mean, kernel_width, kernel_map
    )[0]
    row_max = jnp.max(scores, axis=-1, keepdims=True)
    exponent = jnp.exp(scores - row_max)
    row_total = jnp.sum(exponent, axis=-1, keepdims=True)
    probs = exponent / row_total
    attended_b = jnp.einsum(
        "bhij,bjhe->bihe", probs.astype(jnp.bfloat16), values_b, preferred_element_type=jnp.float32
    )
    return (attended_b, row_max + jnp.log(row_total))


def attend_backward(pieces, kernel_mean, kernel_width, kernel_map):
    queries_b, keys_b, values_b, coords_b, segs_b, grad_b, log_total = pieces
    scores, features, features_low, standard = block_scores(
        queries_b, keys_b, coords_b, segs_b, kernel_mean, kernel_width, kernel_map
    )
    probs = jnp.exp(scores - log_total)
    grad_probs = jnp.einsum("bihe,bjhe->bhij", grad_b, values_b, preferred_element_type=jnp.float32)
    delta_row = jnp.sum(probs * grad_probs, axis=-1, keepdims=True)
    grad_scores = (probs * (grad_probs - delta_row)).astype(jnp.bfloat16)
    grad_queries = jnp.einsum(
        "bhij,bjhe->bihe", grad_scores, keys_b, preferred_element_type=jnp.float32
    )
    grad_keys = jnp.einsum(
        "bhij,bihe->bjhe", grad_scores, queries_b, preferred_element_type=jnp.float32
    )
    grad_values = jnp.einsum(
        "bhij,bihe->bjhe", probs.astype(jnp.bfloat16), grad_b, preferred_element_type=jnp.float32
    )
    grad_map = jnp.einsum(
        "bijk,bhij->kh", features_low, grad_scores, preferred_element_type=jnp.float32
    )
    scores_wide = grad_scores.astype(jnp.float32)
    scaled = features * standard / kernel_width
    mean_terms = jnp.einsum(
        "bijk,bhij->kh", scaled, scores_wide, preferred_element_type=jnp.float32
    )
    width_terms = jnp.einsum(
        "bijk,bhij->kh",
        scaled * standard - features / kernel_width,
        scores_wide,
        preferred_element_type=jnp.float32,
    )
    map_wide = kernel_map.astype(jnp.float32)
    grad_mean = jnp.sum(mean_terms * map_wide, axis=1)
    grad_width = jnp.sum(width_terms * map_wide, axis=1)
    return ((grad_queries, grad_keys, grad_values), (grad_map, grad_mean, grad_width))


def on_device(
    inputs,
    time_of_row,
    coords,
    segment_ids,
    cotangent,
    time_weight,
    ln1_gain,
    ln1_bias,
    w_qkv,
    q_bias,
    v_bias,
    w_out,
    out_bias,
    kernel_mean,
    kernel_width,
    kernel_map,
    ln2_gain,
    ln2_bias,
    w_up,
    up_bias,
    w_down,
    down_bias,
):
    attn_full = (
        lax.all_gather(time_weight, "fsdp", axis=0, tiled=True),
        lax.all_gather(ln1_gain, "fsdp", axis=0, tiled=True),
        lax.all_gather(ln1_bias, "fsdp", axis=0, tiled=True),
        lax.all_gather(w_qkv, "fsdp", axis=0, tiled=True),
        lax.all_gather(q_bias, "fsdp", axis=0, tiled=True),
        lax.all_gather(v_bias, "fsdp", axis=0, tiled=True),
        lax.all_gather(w_out, "fsdp", axis=0, tiled=True),
        lax.all_gather(out_bias, "fsdp", axis=0, tiled=True),
        lax.all_gather(kernel_mean, "fsdp", axis=0, tiled=True),
        lax.all_gather(kernel_width, "fsdp", axis=0, tiled=True),
        lax.all_gather(kernel_map, "fsdp", axis=0, tiled=True),
    )
    (
        time_full,
        gain_first,
        shift_first,
        qkv_full,
        qbias_full,
        vbias_full,
        wout_full,
        obias_full,
        mean_full,
        width_full,
        map_full,
    ) = attn_full
    rows_here = inputs.shape[0]
    width_model = inputs.shape[1]
    head_count = map_full.shape[1]
    head_width = width_model // head_count
    sets_here = rows_here // SET
    per_block = math.gcd(sets_here, max(1, 512 // SET))
    block_count = sets_here // per_block
    query_scale = head_width ** (-0.5)

    def to_blocks(array):
        return array.reshape(block_count, per_block, SET, head_count, head_width)

    start = inputs.astype(jnp.float32) + time_of_row[:, None] * time_full.astype(jnp.float32)
    normed_low = layer_norm(
        start, gain_first.astype(jnp.float32), shift_first.astype(jnp.float32)
    ).astype(jnp.bfloat16)
    projected = jnp.dot(normed_low, qkv_full, preferred_element_type=jnp.float32)
    queries = ((projected[:, :width_model] + qbias_full.astype(jnp.float32)) * query_scale).astype(
        jnp.bfloat16
    )
    keys_low = projected[:, width_model : 2 * width_model].astype(jnp.bfloat16)
    values_low = (projected[:, 2 * width_model :] + vbias_full.astype(jnp.float32)).astype(
        jnp.bfloat16
    )
    coords_blocks = jnp.transpose(coords.reshape(3, block_count, per_block, SET), (1, 2, 0, 3))
    segs_blocks = segment_ids.reshape(block_count, per_block, SET)
    query_blocks = to_blocks(queries)
    key_blocks = to_blocks(keys_low)
    value_blocks = to_blocks(values_low)
    attended_blocks, log_totals = lax.map(
        partial(
            attend_forward,
            kernel_mean=mean_full.astype(jnp.float32),
            kernel_width=width_full.astype(jnp.float32),
            kernel_map=map_full,
        ),
        (query_blocks, key_blocks, value_blocks, coords_blocks, segs_blocks),
    )
    attended = attended_blocks.reshape(rows_here, width_model).astype(jnp.bfloat16)
    middle = (
        start
        + jnp.dot(attended, wout_full, preferred_element_type=jnp.float32)
        + obias_full.astype(jnp.float32)
    )
    ffn_full = (
        lax.all_gather(ln2_gain, "fsdp", axis=0, tiled=True),
        lax.all_gather(ln2_bias, "fsdp", axis=0, tiled=True),
        lax.all_gather(w_up, "fsdp", axis=0, tiled=True),
        lax.all_gather(up_bias, "fsdp", axis=0, tiled=True),
        lax.all_gather(w_down, "fsdp", axis=0, tiled=True),
        lax.all_gather(down_bias, "fsdp", axis=0, tiled=True),
    )
    gain_second, shift_second, up_full, upbias_full, down_full, dbias_full = ffn_full
    normed2_low = layer_norm(
        middle, gain_second.astype(jnp.float32), shift_second.astype(jnp.float32)
    ).astype(jnp.bfloat16)
    pre_hidden = jnp.dot(
        normed2_low, up_full, preferred_element_type=jnp.float32
    ) + upbias_full.astype(jnp.float32)
    hidden_low = jax.nn.gelu(pre_hidden, approximate=False).astype(jnp.bfloat16)
    result = (
        middle
        + jnp.dot(hidden_low, down_full, preferred_element_type=jnp.float32)
        + dbias_full.astype(jnp.float32)
    )
    output = result.astype(jnp.bfloat16)
    ffn_back = (
        lax.all_gather(ln2_gain, "fsdp", axis=0, tiled=True),
        lax.all_gather(ln2_bias, "fsdp", axis=0, tiled=True),
        lax.all_gather(w_up, "fsdp", axis=0, tiled=True),
        lax.all_gather(up_bias, "fsdp", axis=0, tiled=True),
        lax.all_gather(w_down, "fsdp", axis=0, tiled=True),
        lax.all_gather(down_bias, "fsdp", axis=0, tiled=True),
    )
    grad_output = cotangent.astype(jnp.float32)
    grad_w_down = contract_rows(hidden_low, cotangent)
    grad_down_bias = jnp.sum(grad_output, axis=0)
    grad_hidden = times_transpose(cotangent, ffn_back[4])
    unused_gelu, gelu_pull = jax.vjp(partial(jax.nn.gelu, approximate=False), pre_hidden)
    grad_pre = gelu_pull(grad_hidden)[0].astype(jnp.bfloat16)
    grad_w_up = contract_rows(normed2_low, grad_pre)
    grad_up_bias = jnp.sum(grad_pre.astype(jnp.float32), axis=0)
    grad_normed2 = times_transpose(grad_pre, ffn_back[2])
    unused_second, second_pull = jax.vjp(
        layer_norm, middle, ffn_back[0].astype(jnp.float32), ffn_back[1].astype(jnp.float32)
    )
    grad_middle_part, grad_ln2_gain, grad_ln2_bias = second_pull(grad_normed2)
    grad_middle = grad_output + grad_middle_part
    attn_back = (
        lax.all_gather(time_weight, "fsdp", axis=0, tiled=True),
        lax.all_gather(ln1_gain, "fsdp", axis=0, tiled=True),
        lax.all_gather(ln1_bias, "fsdp", axis=0, tiled=True),
        lax.all_gather(w_qkv, "fsdp", axis=0, tiled=True),
        lax.all_gather(q_bias, "fsdp", axis=0, tiled=True),
        lax.all_gather(v_bias, "fsdp", axis=0, tiled=True),
        lax.all_gather(w_out, "fsdp", axis=0, tiled=True),
        lax.all_gather(out_bias, "fsdp", axis=0, tiled=True),
        lax.all_gather(kernel_mean, "fsdp", axis=0, tiled=True),
        lax.all_gather(kernel_width, "fsdp", axis=0, tiled=True),
        lax.all_gather(kernel_map, "fsdp", axis=0, tiled=True),
    )
    grad_attn = grad_middle.astype(jnp.bfloat16)
    grad_w_out = contract_rows(attended, grad_attn)
    grad_out_bias = jnp.sum(grad_attn.astype(jnp.float32), axis=0)
    grad_attended = times_transpose(grad_attn, attn_back[6]).astype(jnp.bfloat16)
    mean_back = attn_back[8].astype(jnp.float32)
    width_back = attn_back[9].astype(jnp.float32)
    map_back = attn_back[10]

    def back_step(carried, pieces):
        row_grads, kernel_grads = attend_backward(pieces, mean_back, width_back, map_back)
        summed = (
            carried[0] + kernel_grads[0],
            carried[1] + kernel_grads[1],
            carried[2] + kernel_grads[2],
        )
        return (summed, row_grads)

    start_carry = (
        jnp.zeros(map_back.shape, jnp.float32),
        jnp.zeros(mean_back.shape, jnp.float32),
        jnp.zeros(mean_back.shape, jnp.float32),
    )
    kernel_sums, row_blocks = lax.scan(
        back_step,
        start_carry,
        (
            query_blocks,
            key_blocks,
            value_blocks,
            coords_blocks,
            segs_blocks,
            to_blocks(grad_attended),
            log_totals,
        ),
    )
    grad_kernel_map, grad_kernel_mean, grad_kernel_width = kernel_sums
    grad_pre_query = (row_blocks[0].reshape(rows_here, width_model) * query_scale).astype(
        jnp.bfloat16
    )
    grad_keys = row_blocks[1].reshape(rows_here, width_model).astype(jnp.bfloat16)
    grad_values = row_blocks[2].reshape(rows_here, width_model).astype(jnp.bfloat16)
    grad_projected = jnp.concatenate((grad_pre_query, grad_keys, grad_values), axis=1)
    grad_w_qkv = contract_rows(normed_low, grad_projected)
    grad_q_bias = jnp.sum(grad_pre_query.astype(jnp.float32), axis=0)
    grad_v_bias = jnp.sum(grad_values.astype(jnp.float32), axis=0)
    grad_normed = times_transpose(grad_projected, attn_back[3])
    unused_first, first_pull = jax.vjp(
        layer_norm, start, attn_back[1].astype(jnp.float32), attn_back[2].astype(jnp.float32)
    )
    grad_start_part, grad_ln1_gain, grad_ln1_bias = first_pull(grad_normed)
    grad_start = grad_middle + grad_start_part
    grad_time_weight = jnp.sum(time_of_row[:, None] * grad_start, axis=0)
    grad_inputs = grad_start.astype(jnp.bfloat16)
    owned = (
        lax.psum_scatter(grad_time_weight, "fsdp", scatter_dimension=0, tiled=True),
        lax.psum_scatter(grad_ln1_gain, "fsdp", scatter_dimension=0, tiled=True),
        lax.psum_scatter(grad_ln1_bias, "fsdp", scatter_dimension=0, tiled=True),
        lax.psum_scatter(grad_w_qkv, "fsdp", scatter_dimension=0, tiled=True),
        lax.psum_scatter(grad_q_bias, "fsdp", scatter_dimension=0, tiled=True),
        lax.psum_scatter(grad_v_bias, "fsdp", scatter_dimension=0, tiled=True),
        lax.psum_scatter(grad_w_out, "fsdp", scatter_dimension=0, tiled=True),
        lax.psum_scatter(grad_out_bias, "fsdp", scatter_dimension=0, tiled=True),
        lax.psum_scatter(grad_kernel_mean, "fsdp", scatter_dimension=0, tiled=True),
        lax.psum_scatter(grad_kernel_width, "fsdp", scatter_dimension=0, tiled=True),
        lax.psum_scatter(grad_kernel_map, "fsdp", scatter_dimension=0, tiled=True),
        lax.psum_scatter(grad_ln2_gain, "fsdp", scatter_dimension=0, tiled=True),
        lax.psum_scatter(grad_ln2_bias, "fsdp", scatter_dimension=0, tiled=True),
        lax.psum_scatter(grad_w_up, "fsdp", scatter_dimension=0, tiled=True),
        lax.psum_scatter(grad_up_bias, "fsdp", scatter_dimension=0, tiled=True),
        lax.psum_scatter(grad_w_down, "fsdp", scatter_dimension=0, tiled=True),
        lax.psum_scatter(grad_down_bias, "fsdp", scatter_dimension=0, tiled=True),
    )
    owned = (
        lax.psum(owned[0].astype(jnp.bfloat16), "dp").astype(jnp.float32),
        lax.psum(owned[1].astype(jnp.bfloat16), "dp").astype(jnp.float32),
        lax.psum(owned[2].astype(jnp.bfloat16), "dp").astype(jnp.float32),
        lax.psum(owned[3].astype(jnp.bfloat16), "dp").astype(jnp.float32),
        lax.psum(owned[4].astype(jnp.bfloat16), "dp").astype(jnp.float32),
        lax.psum(owned[5].astype(jnp.bfloat16), "dp").astype(jnp.float32),
        lax.psum(owned[6].astype(jnp.bfloat16), "dp").astype(jnp.float32),
        lax.psum(owned[7].astype(jnp.bfloat16), "dp").astype(jnp.float32),
        lax.psum(owned[8].astype(jnp.bfloat16), "dp").astype(jnp.float32),
        lax.psum(owned[9].astype(jnp.bfloat16), "dp").astype(jnp.float32),
        lax.psum(owned[10].astype(jnp.bfloat16), "dp").astype(jnp.float32),
        lax.psum(owned[11].astype(jnp.bfloat16), "dp").astype(jnp.float32),
        lax.psum(owned[12].astype(jnp.bfloat16), "dp").astype(jnp.float32),
        lax.psum(owned[13].astype(jnp.bfloat16), "dp").astype(jnp.float32),
        lax.psum(owned[14].astype(jnp.bfloat16), "dp").astype(jnp.float32),
        lax.psum(owned[15].astype(jnp.bfloat16), "dp").astype(jnp.float32),
        lax.psum(owned[16].astype(jnp.bfloat16), "dp").astype(jnp.float32),
    )
    return (
        output,
        grad_inputs,
        owned[0],
        owned[1],
        owned[2],
        owned[3],
        owned[4],
        owned[5],
        owned[6],
        owned[7],
        owned[8],
        owned[9],
        owned[10],
        owned[11],
        owned[12],
        owned[13],
        owned[14],
        owned[15],
        owned[16],
    )


def solution(mesh):
    placed = (
        P(("fsdp", "dp"), None),
        P(("fsdp", "dp")),
        P(None, ("fsdp", "dp")),
        P(("fsdp", "dp")),
        P(("fsdp", "dp"), None),
        P("fsdp"),
        P("fsdp"),
        P("fsdp"),
        P("fsdp", None),
        P("fsdp"),
        P("fsdp"),
        P("fsdp", None),
        P("fsdp"),
        P("fsdp"),
        P("fsdp"),
        P("fsdp", None),
        P("fsdp"),
        P("fsdp"),
        P("fsdp", None),
        P("fsdp"),
        P("fsdp", None),
        P("fsdp"),
    )
    return jax.shard_map(
        on_device,
        mesh=mesh,
        in_specs=placed,
        out_specs=(
            P(("fsdp", "dp"), None),
            P(("fsdp", "dp"), None),
            P("fsdp"),
            P("fsdp"),
            P("fsdp"),
            P("fsdp", None),
            P("fsdp"),
            P("fsdp"),
            P("fsdp", None),
            P("fsdp"),
            P("fsdp"),
            P("fsdp"),
            P("fsdp", None),
            P("fsdp"),
            P("fsdp"),
            P("fsdp", None),
            P("fsdp"),
            P("fsdp", None),
            P("fsdp"),
        ),
        check_vma=False,
    )
```

profile of v0, /device:TPU:0, one launch (start us, length us, event | category | flops | bytes accessed | tf_op | source)
XLA Modules:
  0.0 1174.8 jit_solution(6479069952369899799)
XLA Ops:
  17.6 26.7 %all-reduce.24 = (bf16[768]{0:T(1024)(128)(2,1)S(1)}, bf16[768]{0:T(1024)(128)(2,1)S(1)}, bf16[768]{0:T(1024)(128)(2,1)S(1)}, bf16[768]{0:T(1024)(128)(2,1)S(1)}...) all-reduce(bf16[768]{0:T(1024)(128)(2,1)S(1)} %dynamic-update-slice, ...), channel_id=1, replica_groups=mesh['fsdp'=8,'dp'=4] {'fsdp'}, use_global_device_ids=true, to_apply=%add.2 | all-reduce | flops 7168 | bytes 28672
  46.8 7.3 all-gather
  54.7 9.8 all_gather.68
  69.1 6.4 fusion.104
  92.1 171.5 %while.35 = (s32[]{:T(128)}, bf16[2,2,256,32,24]{2,4,3,1,0:T(8,128)(2,1)}, f32[2,2,32,256,1]{3,2,1,4,0:T(8,128)}, bf16[2,2,256,32,24]{2,4,3,1,0:T(8,128)(2,1)}, ...) while((s32[]{:T(128)}, ...), condition=%wide.region_6.7_spmd.clone, body=%wide.region_2.6_spmd.sunk.clone | while | flops 1611776128 | bytes 157324144 | solution.py:186
  94.9 33.7 %fusion.209 = f32[2,256,256,32]{2,3,1,0:T(8,128)} fusion(f32[128]{0:T(128)S(1)} %broadcast_multiply_fusion.6, f32[128]{0:T(128)S(1)} %get-tuple-element.840, f32[128]{0:T(128)S(1)} %get-tuple-element.839, f32[2,256,256]{2,1,0:T(8,128)S(1)} %sqrt.19, bf16[128,32]{0,1:T(8,128)(2,1)S(1)} %get-tuple-element.841), kind=kOutput, calls=%fused_computation.4.clone.2.clone | convolution fusion | flops 1174405120 | bytes 17311232 | tf_op jit(solution)/shard_map/while/body/eval_jaxpr/bijk,kh->bhij/dot_general | solution.py:42
  128.6 19.5 %copy.199 = f32[2,256,256,32]{1,2,3,0:T(8,128)} copy(f32[2,256,256,32]{2,3,1,0:T(8,128)} %fusion.209) | data formatting | bytes 33554432 | tf_op jit(solution)/shard_map/while/body/eval_jaxpr/bijk,kh->bhij/dot_general | solution.py:42
  148.1 10.7 fusion.210
  158.8 10.0 fusion.211
  168.8 7.4 bitcast_dynamic-update-slice_fusion.15
  180.6 33.7 %fusion.209 = f32[2,256,256,32]{2,3,1,0:T(8,128)} fusion(f32[128]{0:T(128)S(1)} %broadcast_multiply_fusion.6, f32[128]{0:T(128)S(1)} %get-tuple-element.840, f32[128]{0:T(128)S(1)} %get-tuple-element.839, f32[2,256,256]{2,1,0:T(8,128)S(1)} %sqrt.19, bf16[128,32]{0,1:T(8,128)(2,1)S(1)} %get-tuple-element.841), kind=kOutput, calls=%fused_computation.4.clone.2.clone | convolution fusion | flops 1174405120 | bytes 17311232 | tf_op jit(solution)/shard_map/while/body/eval_jaxpr/bijk,kh->bhij/dot_general | solution.py:42
  214.3 19.4 %copy.199 = f32[2,256,256,32]{1,2,3,0:T(8,128)} copy(f32[2,256,256,32]{2,3,1,0:T(8,128)} %fusion.209) | data formatting | bytes 33554432 | tf_op jit(solution)/shard_map/while/body/eval_jaxpr/bijk,kh->bhij/dot_general | solution.py:42
  233.7 10.6 fusion.210
  244.3 10.0 fusion.211
  254.3 7.4 bitcast_dynamic-update-slice_fusion.15
  263.6 3.1 copy.156
  269.6 3.6 fusion.112
  275.3 37.8 %multiply_convert_fusion.1 = (bf16[1024,3072]{1,0:T(8,128)(2,1)}, f32[1024,3072]{1,0:T(8,128)}, f32[1024,3072]{1,0:T(8,128)}) fusion(f32[3072]{0:T(1024)S(1)} %bitcast.251, bf16[768,3072]{1,0:T(8,128)(2,1)} %all-gather.10.cloned.1.call-done, f32[1024,768]{0,1:T(8,128)} %copy-done.15, f32[768]{0:T(1024)S(1)} %copy-done.85, f32[768]{0:T(1024)S(1)} %copy-done.61, ...), kind=kOutput, calls=%fused_computation.103 | convolution fusion | flops 5043388416 | bytes 39348224 | tf_op jit(solution)/shard_map/dot_general | solution.py:213
  313.1 17.6 %convert_reduce_fusion = (f32[3072]{0:T(1024)}, bf16[1024,3072]{1,0:T(8,128)(2,1)}) fusion(f32[1024,3072]{1,0:T(8,128)} %get-tuple-element.527, bf16[1024,768]{1,0:T(8,128)(2,1)S(1)} %copy-done.36, bf16[3072,768]{1,0:T(8,128)(2,1)} %all-gather.12.cloned.1.call-done, f32[1024,3072]{1,0:T(8,128)} %get-tuple-element.546, f32[3072]{0:T(1024)S(1)} %bitcast.252), kind=kOutput, calls=%fused_computation.101 | convolution fusion | flops 4885312512 | bytes 37773312 | tf_op jit(solution)/shard_map/dot_general | solution.py:31
  330.6 10.3 fusion.114
  341.0 3.6 copy.159
  344.6 3.5 multiply_reduce_fusion.3
  359.2 426.8 %while.36 = (s32[]{:T(128)}, f32[128,32]{0,1:T(8,128)}, f32[128]{0:T(128)}, f32[128]{0:T(128)}, f32[2,2,256,32,24]{2,4,3,1,0:T(8,128)}, /*index=5*/bf16[2,2,256,...) while((s32[]{:T(128)}, f32[128,32]{0,1:T(8,128)}, ...), condition=%wide.region_16.17_spmd.clone.clone, body=%wide.region_11.16_spmd.clone.sunk.clone | while | flops 5827084800 | bytes 428160960 | solution.py:280
  364.8 9.8 fusion.225
  374.7 33.7 %fusion.227 = f32[2,256,256,32]{2,3,1,0:T(8,128)} fusion(f32[128]{0:T(128)S(1)} %get-tuple-element.784, f32[128]{0:T(128)S(1)} %get-tuple-element.885, f32[128]{0:T(128)S(1)} %get-tuple-element.884, f32[2,256,256]{2,1,0:T(8,128)S(1)} %sqrt.20, bf16[128,32]{0,1:T(8,128)(2,1)S(1)} %get-tuple-element.889), kind=kOutput, calls=%fused_computation.45.clone.1.clone | convolution fusion | flops 1174405120 | bytes 17311232 | tf_op jit(solution)/shard_map/while/body/eval_jaxpr/bijk,kh->bhij/dot_general | solution.py:42
  408.4 19.4 %copy.202 = f32[2,256,256,32]{1,2,3,0:T(8,128)} copy(f32[2,256,256,32]{2,3,1,0:T(8,128)} %fusion.227) | data formatting | bytes 33554432 | tf_op jit(solution)/shard_map/while/body/eval_jaxpr/bijk,kh->bhij/dot_general | solution.py:42
  427.8 18.7 %multiply_reduce_fusion.18 = (f32[2,32,256]{2,1,0:T(8,128)S(1)}, f32[2,32,256,256]{2,3,1,0:T(8,128)}) fusion(f32[2,32,256,256]{2,3,1,0:T(8,128)} %fusion.225, f32[2,32,256]{2,1,0:T(8,128)S(1)} %copy-done.29, f32[2,256,256,32]{1,2,3,0:T(8,128)} %copy.202, bf16[2,2,256,32,24]{2,4,3,1,0:T(8,128)(2,1)S(1)} %copy-done.8, s32[]{:T(128)S(6)} %copy.236, ...), kind=kOutput, calls=%fused_computation.51.clone.1.clone | convolution fusion | flops 222281728 | bytes 52167680 | tf_op jit(solution)/shard_map/while/body/eval_jaxpr/bihe,bjhe->bhij/dot_general | solution.py:46
  446.5 15.6 %multiply_convert_fusion.6 = bf16[2,32,256,256]{2,3,1,0:T(8,128)(2,1)} fusion(f32[2,32,256,256]{2,3,1,0:T(8,128)} %get-tuple-element.785, f32[2,32,256,256]{2,3,1,0:T(8,128)} %fusion.225, f32[2,32,256]{2,1,0:T(8,128)S(1)} %get-tuple-element.786), kind=kLoop, calls=%fused_computation.50.clone.1.clone | loop fusion | flops 12582912 | bytes 42008576 | tf_op jit(solution)/shard_map/while/body/eval_jaxpr/convert_element_type | solution.py:77
  462.1 2.8 copy-done
  465.1 3.3 bitcast_dynamic-update-slice_fusion.19
  468.3 7.0 bitcast_dynamic-update-slice_fusion.18
  477.8 14.7 %copy.203 = bf16[2,32,256,256]{3,1,2,0:T(8,128)(2,1)} copy(bf16[2,32,256,256]{2,3,1,0:T(8,128)(2,1)} %multiply_convert_fusion.6) | data formatting | bytes 16777216 | tf_op jit(solution)/shard_map/while/body/eval_jaxpr/convert_element_type | solution.py:77
  492.5 36.5 %fusion.231 = f32[128]{0:T(128)} fusion(bf16[2,32,256,256]{3,1,2,0:T(8,128)(2,1)} %copy.203, f32[128]{0:T(128)S(1)} %copy-done.108, f32[128]{0:T(128)S(1)} %get-tuple-element.885, f32[128]{0:T(128)S(1)} %get-tuple-element.884, f32[2,256,256]{2,1,0:T(8,128)S(1)} %copy-done.28, f32[128]{0:T(128)S(1)} %get-tuple-element.784, ...), kind=kOutput, calls=%fused_computation.65.clone.2.clone | convolution fusion | flops 1241526144 | bytes 8923648 | tf_op jit(solution)/shard_map/while/body/eval_jaxpr/bijk,bhij->kh/dot_general | solution.py:95
  529.0 23.8 %fusion.230 = f32[128]{0:T(128)} fusion(bf16[2,32,256,256]{3,1,2,0:T(8,128)(2,1)S(1)} %copy-done.2, f32[128]{0:T(128)S(1)} %get-tuple-element.784, f32[128]{0:T(128)S(1)} %get-tuple-element.885, f32[128]{0:T(128)S(1)} %get-tuple-element.884, f32[2,256,256]{2,1,0:T(8,128)S(1)} %copy-done.28, bf16[128,32]{0,1:T(8,128)(2,1)S(1)} %get-tuple-element.889), kind=kOutput, calls=%fused_computation.64.clone.2.clone | convolution fusion | flops 1191194496 | bytes 8923136 | tf_op jit(solution)/shard_map/while/body/eval_jaxpr/bijk,bhij->kh/dot_general | solution.py:92
  552.9 19.3 %fusion.229 = f32[128,32]{0,1:T(8,128)S(1)} fusion(bf16[2,32,256,256]{3,1,2,0:T(8,128)(2,1)S(1)} %copy-done.2, f32[128]{0:T(128)S(1)} %get-tuple-element.784, f32[128]{0:T(128)S(1)} %get-tuple-element.885, f32[128]{0:T(128)S(1)} %get-tuple-element.884, f32[2,256,256]{2,1,0:T(8,128)S(1)} %copy-done.28, f32[128,32]{0,1:T(8,128)S(1)} %copy-done.72, ...), kind=kOutput, calls=%fused_computation.63.clone.2.clone | convolution fusion | flops 1174413312 | bytes 8947201 | tf_op jit(solution)/shard_map/while/body/eval_jaxpr/bijk,bhij->kh/dot_general | solution.py:87
  578.0 9.6 fusion.225
  587.6 33.7 %fusion.227 = f32[2,256,256,32]{2,3,1,0:T(8,128)} fusion(f32[128]{0:T(128)S(1)} %get-tuple-element.784, f32[128]{0:T(128)S(1)} %get-tuple-element.885, f32[128]{0:T(128)S(1)} %get-tuple-element.884, f32[2,256,256]{2,1,0:T(8,128)S(1)} %sqrt.20, bf16[128,32]{0,1:T(8,128)(2,1)S(1)} %get-tuple-element.889), kind=kOutput, calls=%fused_computation.45.clone.1.clone | convolution fusion | flops 1174405120 | bytes 17311232 | tf_op jit(solution)/shard_map/while/body/eval_jaxpr/bijk,kh->bhij/dot_general | solution.py:42
  621.3 19.4 %copy.202 = f32[2,256,256,32]{1,2,3,0:T(8,128)} copy(f32[2,256,256,32]{2,3,1,0:T(8,128)} %fusion.227) | data formatting | bytes 33554432 | tf_op jit(solution)/shard_map/while/body/eval_jaxpr/bijk,kh->bhij/dot_general | solution.py:42
  640.8 18.7 %multiply_reduce_fusion.18 = (f32[2,32,256]{2,1,0:T(8,128)S(1)}, f32[2,32,256,256]{2,3,1,0:T(8,128)}) fusion(f32[2,32,256,256]{2,3,1,0:T(8,128)} %fusion.225, f32[2,32,256]{2,1,0:T(8,128)S(1)} %copy-done.29, f32[2,256,256,32]{1,2,3,0:T(8,128)} %copy.202, bf16[2,2,256,32,24]{2,4,3,1,0:T(8,128)(2,1)S(1)} %copy-done.8, s32[]{:T(128)S(6)} %copy.236, ...), kind=kOutput, calls=%fused_computation.51.clone.1.clone | convolution fusion | flops 222281728 | bytes 52167680 | tf_op jit(solution)/shard_map/while/body/eval_jaxpr/bihe,bjhe->bhij/dot_general | solution.py:46
  659.5 15.6 %multiply_convert_fusion.6 = bf16[2,32,256,256]{2,3,1,0:T(8,128)(2,1)} fusion(f32[2,32,256,256]{2,3,1,0:T(8,128)} %get-tuple-element.785, f32[2,32,256,256]{2,3,1,0:T(8,128)} %fusion.225, f32[2,32,256]{2,1,0:T(8,128)S(1)} %get-tuple-element.786), kind=kLoop, calls=%fused_computation.50.clone.1.clone | loop fusion | flops 12582912 | bytes 42008576 | tf_op jit(solution)/shard_map/while/body/eval_jaxpr/convert_element_type | solution.py:77
  675.1 2.8 copy-done
  678.0 3.3 bitcast_dynamic-update-slice_fusion.19
  681.3 7.0 bitcast_dynamic-update-slice_fusion.18
  690.7 14.7 %copy.203 = bf16[2,32,256,256]{3,1,2,0:T(8,128)(2,1)} copy(bf16[2,32,256,256]{2,3,1,0:T(8,128)(2,1)} %multiply_convert_fusion.6) | data formatting | bytes 16777216 | tf_op jit(solution)/shard_map/while/body/eval_jaxpr/convert_element_type | solution.py:77
  705.4 36.5 %fusion.231 = f32[128]{0:T(128)} fusion(bf16[2,32,256,256]{3,1,2,0:T(8,128)(2,1)} %copy.203, f32[128]{0:T(128)S(1)} %copy-done.108, f32[128]{0:T(128)S(1)} %get-tuple-element.885, f32[128]{0:T(128)S(1)} %get-tuple-element.884, f32[2,256,256]{2,1,0:T(8,128)S(1)} %copy-done.28, f32[128]{0:T(128)S(1)} %get-tuple-element.784, ...), kind=kOutput, calls=%fused_computation.65.clone.2.clone | convolution fusion | flops 1241526144 | bytes 8923648 | tf_op jit(solution)/shard_map/while/body/eval_jaxpr/bijk,bhij->kh/dot_general | solution.py:95
  741.9 23.8 %fusion.230 = f32[128]{0:T(128)} fusion(bf16[2,32,256,256]{3,1,2,0:T(8,128)(2,1)S(1)} %copy-done.2, f32[128]{0:T(128)S(1)} %get-tuple-element.784, f32[128]{0:T(128)S(1)} %get-tuple-element.885, f32[128]{0:T(128)S(1)} %get-tuple-element.884, f32[2,256,256]{2,1,0:T(8,128)S(1)} %copy-done.28, bf16[128,32]{0,1:T(8,128)(2,1)S(1)} %get-tuple-element.889), kind=kOutput, calls=%fused_computation.64.clone.2.clone | convolution fusion | flops 1191194496 | bytes 8923136 | tf_op jit(solution)/shard_map/while/body/eval_jaxpr/bijk,bhij->kh/dot_general | solution.py:92
  765.8 19.3 %fusion.229 = f32[128,32]{0,1:T(8,128)S(1)} fusion(bf16[2,32,256,256]{3,1,2,0:T(8,128)(2,1)S(1)} %copy-done.2, f32[128]{0:T(128)S(1)} %get-tuple-element.784, f32[128]{0:T(128)S(1)} %get-tuple-element.885, f32[128]{0:T(128)S(1)} %get-tuple-element.884, f32[2,256,256]{2,1,0:T(8,128)S(1)} %copy-done.28, f32[128,32]{0,1:T(8,128)S(1)} %copy-done.72, ...), kind=kOutput, calls=%fused_computation.63.clone.2.clone | convolution fusion | flops 1174413312 | bytes 8947201 | tf_op jit(solution)/shard_map/while/body/eval_jaxpr/bijk,bhij->kh/dot_general | solution.py:87
  786.0 4.3 copy.167
  790.3 2.8 convert_element_type.266
  795.9 3.8 convert_element_type.268
  810.4 6.6 fusion.103
  817.7 10.8 fusion.101
  830.1 10.8 fusion.116
  843.8 9.5 add_convert_fusion.1
  853.3 8.0 fusion.113
  861.3 3.6 copy.169
  866.6 16.2 %reduce-scatter.6.cloned.1.call-done = f32[96,2304]{1,0:T(8,128)} async-done(((f32[768,2304]{1,0:T(8,128)}), f32[96,2304]{1,0:T(8,128)}) %reduce-scatter.6.cloned.1.call-update) | async-done | bytes 884752 | tf_op jit(solution)/shard_map/reduce_scatter | solution.py:315
  884.8 78.0 %reduce-scatter.12.cloned.1.call-done = f32[96,3072]{1,0:T(8,128)} async-done(((f32[768,3072]{1,0:T(8,128)}), f32[96,3072]{1,0:T(8,128)}) %reduce-scatter.12.cloned.1.call-update) | async-done | bytes 1179664 | tf_op jit(solution)/shard_map/reduce_scatter | solution.py:325
  965.0 77.9 %reduce-scatter.14.cloned.1.call-done = f32[384,768]{1,0:T(8,128)} async-done(((f32[3072,768]{1,0:T(8,128)}), f32[384,768]{1,0:T(8,128)}) %reduce-scatter.14.cloned.1.call-update) | async-done | bytes 1179664 | tf_op jit(solution)/shard_map/reduce_scatter | solution.py:327
  1049.5 3.2 fusion.105
  1052.8 5.5 multiply_reduce_fusion.4
  1058.3 23.6 %all-reduce.23 = (bf16[768]{0:T(1024)(128)(2,1)S(1)}, bf16[768]{0:T(1024)(128)(2,1)S(1)}, bf16[768]{0:T(1024)(128)(2,1)S(1)}, bf16[768]{0:T(1024)(128)(2,1)S(1)}...) all-reduce(f32[768]{0:T(1024)S(1)} %get-tuple-element.422, ...), channel_id=2, replica_groups=mesh['fsdp'=8,'dp'=4] {'fsdp'}, use_global_device_ids=true, to_apply=%region_20.21.clone | all-reduce | flops 10240 | bytes 61440
  1086.1 19.7 %all-reduce.25 = (bf16[96]{0:T(256)(128)(2,1)S(1)}, bf16[96]{0:T(256)(128)(2,1)S(1)}, bf16[96]{0:T(256)(128)(2,1)S(1)}, bf16[96]{0:T(256)(128)(2,1)S(1)}, bf16[9...) all-reduce(bf16[96]{0:T(256)(128)(2,1)S(1)} %dynamic-slice.58, ...), channel_id=1, replica_groups=mesh['fsdp'=8,'dp'=4] {'dp'}, use_global_device_ids=true, to_apply=%region_21.22 | all-reduce | flops 1792 | bytes 7168 | tf_op jit(solution)/shard_map/psum | solution.py:331
  1112.6 48.1 %all-reduce.29.cloned.1.call-done = (bf16[96,2304]{1,0:T(8,128)(2,1)}, bf16[96,768]{1,0:T(8,128)(2,1)}, bf16[96,3072]{1,0:T(8,128)(2,1)}, bf16[384,768]{1,0:T(8,128)(2,1)}) async-done(((bf16[96,2304]{1,0:T(8,128)(2,1)}, bf16[96,768]{1,0:T(8,128)(2,1)}, bf16[96,3072]{1,0:T(8,128)(2,1)}, bf16[384,768]{1,0:T(8,128)(2,1)}), (bf16[96,2304]{1,0:T(8,128)(2,1)}, bf16[96,768]{1,0:T(8,128)(2,1)}, ...) | async-done | bytes 1769488 | tf_op jit(solution)/shard_map/psum | solution.py:334
  (468 shorter events, 120.9 us)
Async XLA Ops:
  7.2 61.8 %all-gather.6.cloned.1.call-start = ((), (), s32[]{:S(2)}) async-start(), calls=%async_computation.5 | async-start | bytes 3981312 | tf_op jit(solution)/shard_map/all_gather | solution.py:135
  7.9 261.6 %all-gather.8.cloned.1.call-start = ((), (), s32[]{:S(2)}) async-start(), calls=%async_computation.6 | async-start | bytes 1327104 | tf_op jit(solution)/shard_map/all_gather | solution.py:138
  8.7 266.6 %all-gather.10.cloned.1.call-start = ((), (), s32[]{:S(2)}) async-start(), calls=%async_computation.7 | async-start | bytes 5308416 | tf_op jit(solution)/shard_map/all_gather | solution.py:204
  9.4 303.7 %all-gather.12.cloned.1.call-start = ((), (), s32[]{:S(2)}) async-start(), calls=%async_computation.8 | async-start | bytes 5308416 | tf_op jit(solution)/shard_map/all_gather | solution.py:206
  10.0 854.9 %reduce-scatter.8.cloned.1.call-start = ((), (), s32[]{:S(2)}) async-start(), calls=%async_computation.10 | async-start | bytes 2654208 | tf_op jit(solution)/shard_map/reduce_scatter | solution.py:318
  10.4 35.2 %copy-start.90 = (s32[1024]{0:T(1024)S(1)}, s32[1024]{0:T(1024)}, u32[]{:S(2)}) copy-start(s32[1024]{0:T(1024)} %param.29) | copy-start | bytes 12292
  10.4 44.4 %copy-start.83 = (bf16[16,32]{1,0:T(8,128)(2,1)S(1)}, bf16[16,32]{1,0:T(8,128)(2,1)}, u32[]{:S(2)}) copy-start(bf16[16,32]{1,0:T(8,128)(2,1)} %param.41) | copy-start | bytes 3076
  10.4 54.2 %copy-start.34 = (bf16[1024,768]{1,0:T(8,128)(2,1)S(1)}, bf16[1024,768]{1,0:T(8,128)(2,1)}, u32[]{:S(2)}) copy-start(bf16[1024,768]{1,0:T(8,128)(2,1)} %param.26) | copy-start | bytes 4718596
  11.9 53.5 %copy-start.46 = (f32[1024]{0:T(1024)S(1)}, f32[1024]{0:T(1024)}, u32[]{:S(2)}) copy-start(f32[1024]{0:T(1024)} %param.27) | copy-start | bytes 12292
  44.4 24.7 %copy-start.87 = (f32[768]{0:T(1024)}, f32[768]{0:T(1024)S(1)}, u32[]{:S(2)}) copy-start(f32[768]{0:T(1024)S(1)} %convert_element_type.241) | copy-start | bytes 9220
  44.4 24.7 %copy-start.43 = (f32[768]{0:T(1024)}, f32[768]{0:T(1024)S(1)}, u32[]{:S(2)}) copy-start(f32[768]{0:T(1024)S(1)} %convert_element_type.239) | copy-start | bytes 9220
  44.4 24.6 %copy-start.53 = (f32[768]{0:T(1024)}, f32[768]{0:T(1024)S(1)}, u32[]{:S(2)}) copy-start(f32[768]{0:T(1024)S(1)} %convert_element_type.240) | copy-start | bytes 9220
  128.6 19.5 %copy-start.5 = (bf16[2,2,256,32,24]{2,4,3,1,0:T(8,128)(2,1)S(1)}, bf16[2,2,256,32,24]{2,4,3,1,0:T(8,128)(2,1)}, u32[]{:S(2)}) copy-start(bf16[2,2,256,32,24]{2,4,3,1,0:T(8,128)(2,1)} %get-tuple-element.836) | copy-start | bytes 4718596 | tf_op jit(solution)/shard_map/while
  128.6 19.5 %copy-start.7 = (bf16[2,2,256,32,24]{2,4,3,1,0:T(8,128)(2,1)S(1)}, bf16[2,2,256,32,24]{2,4,3,1,0:T(8,128)(2,1)}, u32[]{:S(2)}) copy-start(bf16[2,2,256,32,24]{2,4,3,1,0:T(8,128)(2,1)} %get-tuple-element.837) | copy-start | bytes 4718596 | tf_op jit(solution)/shard_map/while
  128.6 19.5 %copy-start.26 = (pred[2,256,256]{1,2,0:T(8,128)(4,1)S(1)}, pred[2,256,256]{1,2,0:T(8,128)(4,1)}, u32[]{:S(2)}) copy-start(pred[2,256,256]{1,2,0:T(8,128)(4,1)} %broadcast_compare_fusion.6) | copy-start | bytes 393220 | tf_op jit(solution)/shard_map/while
  158.8 10.0 copy-start.30
  214.3 19.4 %copy-start.5 = (bf16[2,2,256,32,24]{2,4,3,1,0:T(8,128)(2,1)S(1)}, bf16[2,2,256,32,24]{2,4,3,1,0:T(8,128)(2,1)}, u32[]{:S(2)}) copy-start(bf16[2,2,256,32,24]{2,4,3,1,0:T(8,128)(2,1)} %get-tuple-element.836) | copy-start | bytes 4718596 | tf_op jit(solution)/shard_map/while
  214.3 19.4 %copy-start.7 = (bf16[2,2,256,32,24]{2,4,3,1,0:T(8,128)(2,1)S(1)}, bf16[2,2,256,32,24]{2,4,3,1,0:T(8,128)(2,1)}, u32[]{:S(2)}) copy-start(bf16[2,2,256,32,24]{2,4,3,1,0:T(8,128)(2,1)} %get-tuple-element.837) | copy-start | bytes 4718596 | tf_op jit(solution)/shard_map/while
  214.3 19.4 %copy-start.26 = (pred[2,256,256]{1,2,0:T(8,128)(4,1)S(1)}, pred[2,256,256]{1,2,0:T(8,128)(4,1)}, u32[]{:S(2)}) copy-start(pred[2,256,256]{1,2,0:T(8,128)(4,1)} %broadcast_compare_fusion.6) | copy-start | bytes 393220 | tf_op jit(solution)/shard_map/while
  244.3 10.0 copy-start.30
  273.2 75.0 %copy-start.51 = (f32[1024]{0:T(1024)}, f32[1024]{0:T(1024)S(1)}, u32[]{:S(2)}) copy-start(f32[1024]{0:T(1024)S(1)} %broadcast_multiply_fusion.2) | copy-start | bytes 12292
  275.2 72.9 %copy-start.63 = (f32[1024]{0:T(1024)}, f32[1024]{0:T(1024)S(1)}, u32[]{:S(2)}) copy-start(f32[1024]{0:T(1024)S(1)} %fusion.100) | copy-start | bytes 12292
  275.3 37.8 %copy-start.36 = (bf16[1024,768]{1,0:T(8,128)(2,1)S(1)}, bf16[1024,768]{1,0:T(8,128)(2,1)}, u32[]{:S(2)}) copy-start(bf16[1024,768]{1,0:T(8,128)(2,1)} %param.30) | copy-start | bytes 4718596
  359.1 523.7 %reduce-scatter.6.cloned.1.call-start = ((), (), s32[]{:S(2)}) async-start(), calls=%async_computation.9 | async-start | bytes 7962624 | tf_op jit(solution)/shard_map/reduce_scatter | solution.py:315
  359.6 15.0 %copy-start.19 = (bf16[2,2,256,32,24]{2,1,0,4,3:T(2,128)(2,1)}, bf16[2,2,256,32,24]{2,1,0,4,3:T(2,128)(2,1)S(1)}, u32[]{:S(2)}) copy-start(bf16[2,2,256,32,24]{2,1,0,4,3:T(2,128)(2,1)S(1)} %get-tuple-element.891) | copy-start | bytes 4718596 | tf_op jit(solution)/shard_map/while
  364.2 10.4 copy-start.27
  408.3 19.4 %copy-start.6 = (bf16[2,2,256,32,24]{2,4,3,1,0:T(8,128)(2,1)S(1)}, bf16[2,2,256,32,24]{2,4,3,1,0:T(8,128)(2,1)}, u32[]{:S(2)}) copy-start(bf16[2,2,256,32,24]{2,4,3,1,0:T(8,128)(2,1)} %get-tuple-element.887) | copy-start | bytes 4718596 | tf_op jit(solution)/shard_map/while
  408.3 19.4 %copy-start.8 = (bf16[2,2,256,32,24]{2,4,3,1,0:T(8,128)(2,1)S(1)}, bf16[2,2,256,32,24]{2,4,3,1,0:T(8,128)(2,1)}, u32[]{:S(2)}) copy-start(bf16[2,2,256,32,24]{2,4,3,1,0:T(8,128)(2,1)} %get-tuple-element.888) | copy-start | bytes 4718596 | tf_op jit(solution)/shard_map/while
  408.4 19.4 %copy-start.25 = (pred[2,256,256]{1,2,0:T(8,128)(4,1)S(1)}, pred[2,256,256]{1,2,0:T(8,128)(4,1)}, u32[]{:S(2)}) copy-start(pred[2,256,256]{1,2,0:T(8,128)(4,1)} %broadcast_compare_fusion.7) | copy-start | bytes 393220 | tf_op jit(solution)/shard_map/while
  408.4 19.4 %copy-start.29 = (f32[2,32,256]{2,1,0:T(8,128)S(1)}, f32[2,32,256]{2,1,0:T(8,128)}, u32[]{:S(2)}) copy-start(f32[2,32,256]{2,1,0:T(8,128)} %dynamic-slice_bitcast_fusion.14) | copy-start | bytes 196612 | tf_op jit(solution)/shard_map/while
  446.5 18.4 %copy-start = (f32[2,32,256,256]{2,3,1,0:T(8,128)S(1)}, f32[2,32,256,256]{2,3,1,0:T(8,128)}, u32[]{:S(2)}) copy-start(f32[2,32,256,256]{2,3,1,0:T(8,128)} %get-tuple-element.785) | copy-start | bytes 50331652 | tf_op jit(solution)/shard_map/while
  446.5 18.5 %copy-start.4 = (bf16[1,2,256,32,24]{2,1,0,4,3:T(2,128)(2,1)S(1)}, bf16[1,2,256,32,24]{2,1,0,4,3:T(2,128)(2,1)}, u32[]{:S(2)}) copy-start(bf16[1,2,256,32,24]{2,1,0,4,3:T(2,128)(2,1)} %copy-done.3) | copy-start | bytes 2359300 | tf_op jit(solution)/shard_map/while
  477.8 14.7 %copy-start.28 = (f32[2,256,256]{2,1,0:T(8,128)S(1)}, f32[2,256,256]{2,1,0:T(8,128)}, u32[]{:S(2)}) copy-start(f32[2,256,256]{2,1,0:T(8,128)} %copy-done.27) | copy-start | bytes 1572868 | tf_op jit(solution)/shard_map/while
  477.8 14.7 %copy-start.108 = (f32[128]{0:T(128)S(1)}, f32[128]{0:T(128)}, u32[]{:S(2)}) copy-start(f32[128]{0:T(128)} %get-tuple-element.787) | copy-start | bytes 1540 | tf_op jit(solution)/shard_map/while
  492.5 36.5 %copy-start.2 = (bf16[2,32,256,256]{3,1,2,0:T(8,128)(2,1)S(1)}, bf16[2,32,256,256]{3,1,2,0:T(8,128)(2,1)}, u32[]{:S(2)}) copy-start(bf16[2,32,256,256]{3,1,2,0:T(8,128)(2,1)} %copy.203) | copy-start | bytes 25165828 | tf_op jit(solution)/shard_map/while
  529.0 23.9 %copy-start.72 = (f32[128,32]{0,1:T(8,128)S(1)}, f32[128,32]{0,1:T(8,128)}, u32[]{:S(2)}) copy-start(f32[128,32]{0,1:T(8,128)} %get-tuple-element.860) | copy-start | bytes 49156 | tf_op jit(solution)/shard_map/while
  552.8 19.4 %copy-start.65 = (f32[128]{0:T(128)S(1)}, f32[128]{0:T(128)}, u32[]{:S(2)}) copy-start(f32[128]{0:T(128)} %get-tuple-element.862) | copy-start | bytes 1540 | tf_op jit(solution)/shard_map/while
  552.8 19.4 %copy-start.68 = (f32[128]{0:T(128)S(1)}, f32[128]{0:T(128)}, u32[]{:S(2)}) copy-start(f32[128]{0:T(128)} %get-tuple-element.861) | copy-start | bytes 1540 | tf_op jit(solution)/shard_map/while
  552.8 19.4 %copy-start.76 = (f32[128]{0:T(128)S(1)}, f32[128]{0:T(128)}, u32[]{:S(2)}) copy-start(f32[128]{0:T(128)} %fusion.231) | copy-start | bytes 1540 | tf_op jit(solution)/shard_map/while
  552.8 19.4 %copy-start.77 = (f32[128]{0:T(128)S(1)}, f32[128]{0:T(128)}, u32[]{:S(2)}) copy-start(f32[128]{0:T(128)} %fusion.230) | copy-start | bytes 1540 | tf_op jit(solution)/shard_map/while
  552.8 20.0 %copy-start.20 = (bf16[2,2,256,32,24]{2,1,0,4,3:T(2,128)(2,1)S(1)}, bf16[2,2,256,32,24]{2,1,0,4,3:T(2,128)(2,1)}, u32[]{:S(2)}) copy-start(bf16[2,2,256,32,24]{2,1,0,4,3:T(2,128)(2,1)} %copy-done.19) | copy-start | bytes 4718596 | tf_op jit(solution)/shard_map/while
  552.9 20.0 %copy-start.82 = (bf16[128,32]{0,1:T(8,128)(2,1)S(1)}, bf16[128,32]{0,1:T(8,128)(2,1)}, u32[]{:S(2)}) copy-start(bf16[128,32]{0,1:T(8,128)(2,1)} %get-tuple-element.963) | copy-start | bytes 24580 | tf_op jit(solution)/shard_map/while
  572.9 14.8 %copy-start.19 = (bf16[2,2,256,32,24]{2,1,0,4,3:T(2,128)(2,1)}, bf16[2,2,256,32,24]{2,1,0,4,3:T(2,128)(2,1)S(1)}, u32[]{:S(2)}) copy-start(bf16[2,2,256,32,24]{2,1,0,4,3:T(2,128)(2,1)S(1)} %get-tuple-element.891) | copy-start | bytes 4718596 | tf_op jit(solution)/shard_map/while
  577.4 10.2 copy-start.27
  621.3 19.4 %copy-start.6 = (bf16[2,2,256,32,24]{2,4,3,1,0:T(8,128)(2,1)S(1)}, bf16[2,2,256,32,24]{2,4,3,1,0:T(8,128)(2,1)}, u32[]{:S(2)}) copy-start(bf16[2,2,256,32,24]{2,4,3,1,0:T(8,128)(2,1)} %get-tuple-element.887) | copy-start | bytes 4718596 | tf_op jit(solution)/shard_map/while
  621.3 19.4 %copy-start.8 = (bf16[2,2,256,32,24]{2,4,3,1,0:T(8,128)(2,1)S(1)}, bf16[2,2,256,32,24]{2,4,3,1,0:T(8,128)(2,1)}, u32[]{:S(2)}) copy-start(bf16[2,2,256,32,24]{2,4,3,1,0:T(8,128)(2,1)} %get-tuple-element.888) | copy-start | bytes 4718596 | tf_op jit(solution)/shard_map/while
  621.3 19.4 %copy-start.25 = (pred[2,256,256]{1,2,0:T(8,128)(4,1)S(1)}, pred[2,256,256]{1,2,0:T(8,128)(4,1)}, u32[]{:S(2)}) copy-start(pred[2,256,256]{1,2,0:T(8,128)(4,1)} %broadcast_compare_fusion.7) | copy-start | bytes 393220 | tf_op jit(solution)/shard_map/while
  621.3 19.4 %copy-start.29 = (f32[2,32,256]{2,1,0:T(8,128)S(1)}, f32[2,32,256]{2,1,0:T(8,128)}, u32[]{:S(2)}) copy-start(f32[2,32,256]{2,1,0:T(8,128)} %dynamic-slice_bitcast_fusion.14) | copy-start | bytes 196612 | tf_op jit(solution)/shard_map/while
  659.5 18.4 %copy-start = (f32[2,32,256,256]{2,3,1,0:T(8,128)S(1)}, f32[2,32,256,256]{2,3,1,0:T(8,128)}, u32[]{:S(2)}) copy-start(f32[2,32,256,256]{2,3,1,0:T(8,128)} %get-tuple-element.785) | copy-start | bytes 50331652 | tf_op jit(solution)/shard_map/while
  659.5 18.5 %copy-start.4 = (bf16[1,2,256,32,24]{2,1,0,4,3:T(2,128)(2,1)S(1)}, bf16[1,2,256,32,24]{2,1,0,4,3:T(2,128)(2,1)}, u32[]{:S(2)}) copy-start(bf16[1,2,256,32,24]{2,1,0,4,3:T(2,128)(2,1)} %copy-done.3) | copy-start | bytes 2359300 | tf_op jit(solution)/shard_map/while
  690.7 14.7 %copy-start.28 = (f32[2,256,256]{2,1,0:T(8,128)S(1)}, f32[2,256,256]{2,1,0:T(8,128)}, u32[]{:S(2)}) copy-start(f32[2,256,256]{2,1,0:T(8,128)} %copy-done.27) | copy-start | bytes 1572868 | tf_op jit(solution)/shard_map/while
  690.7 14.7 %copy-start.108 = (f32[128]{0:T(128)S(1)}, f32[128]{0:T(128)}, u32[]{:S(2)}) copy-start(f32[128]{0:T(128)} %get-tuple-element.787) | copy-start | bytes 1540 | tf_op jit(solution)/shard_map/while
  705.4 36.5 %copy-start.2 = (bf16[2,32,256,256]{3,1,2,0:T(8,128)(2,1)S(1)}, bf16[2,32,256,256]{3,1,2,0:T(8,128)(2,1)}, u32[]{:S(2)}) copy-start(bf16[2,32,256,256]{3,1,2,0:T(8,128)(2,1)} %copy.203) | copy-start | bytes 25165828 | tf_op jit(solution)/shard_map/while
  741.9 23.9 %copy-start.72 = (f32[128,32]{0,1:T(8,128)S(1)}, f32[128,32]{0,1:T(8,128)}, u32[]{:S(2)}) copy-start(f32[128,32]{0,1:T(8,128)} %get-tuple-element.860) | copy-start | bytes 49156 | tf_op jit(solution)/shard_map/while
  765.8 19.4 %copy-start.65 = (f32[128]{0:T(128)S(1)}, f32[128]{0:T(128)}, u32[]{:S(2)}) copy-start(f32[128]{0:T(128)} %get-tuple-element.862) | copy-start | bytes 1540 | tf_op jit(solution)/shard_map/while
  765.8 19.4 %copy-start.68 = (f32[128]{0:T(128)S(1)}, f32[128]{0:T(128)}, u32[]{:S(2)}) copy-start(f32[128]{0:T(128)} %get-tuple-element.861) | copy-start | bytes 1540 | tf_op jit(solution)/shard_map/while
  765.8 19.4 %copy-start.76 = (f32[128]{0:T(128)S(1)}, f32[128]{0:T(128)}, u32[]{:S(2)}) copy-start(f32[128]{0:T(128)} %fusion.231) | copy-start | bytes 1540 | tf_op jit(solution)/shard_map/while
  765.8 19.4 %copy-start.77 = (f32[128]{0:T(128)S(1)}, f32[128]{0:T(128)}, u32[]{:S(2)}) copy-start(f32[128]{0:T(128)} %fusion.230) | copy-start | bytes 1540 | tf_op jit(solution)/shard_map/while
  765.8 20.0 %copy-start.20 = (bf16[2,2,256,32,24]{2,1,0,4,3:T(2,128)(2,1)S(1)}, bf16[2,2,256,32,24]{2,1,0,4,3:T(2,128)(2,1)}, u32[]{:S(2)}) copy-start(bf16[2,2,256,32,24]{2,1,0,4,3:T(2,128)(2,1)} %copy-done.19) | copy-start | bytes 4718596 | tf_op jit(solution)/shard_map/while
  765.8 20.0 %copy-start.82 = (bf16[128,32]{0,1:T(8,128)(2,1)S(1)}, bf16[128,32]{0,1:T(8,128)(2,1)}, u32[]{:S(2)}) copy-start(bf16[128,32]{0,1:T(8,128)(2,1)} %get-tuple-element.963) | copy-start | bytes 24580 | tf_op jit(solution)/shard_map/while
  817.0 145.8 %reduce-scatter.12.cloned.1.call-start = ((), (), s32[]{:S(2)}) async-start(), calls=%async_computation.12 | async-start | bytes 10616832 | tf_op jit(solution)/shard_map/reduce_scatter | solution.py:325
  828.4 214.4 %reduce-scatter.14.cloned.1.call-start = ((), (), s32[]{:S(2)}) async-start(), calls=%async_computation.13 | async-start | bytes 10616832 | tf_op jit(solution)/shard_map/reduce_scatter | solution.py:327
  840.9 244.5 %reduce-scatter.10.cloned.1.call-start = ((), (), s32[]{:S(2)}) async-start(), calls=%async_computation.11 | async-start | bytes 73728 | tf_op jit(solution)/shard_map/reduce_scatter | solution.py:322
  843.7 317.0 %all-reduce.29.cloned.1.call-start = ((), (), s32[]{:S(2)}) async-start(), calls=%async_computation.14 | async-start | bytes 3538944 | tf_op jit(solution)/shard_map/psum | solution.py:334
  (89 other events, 358.0 us)
Sparse Core Ops, SparseCore 0:
  9.9 36.8 all-gather.5
  48.7 24.0 all-gather.7
  74.8 38.9 all-gather.9
  115.5 38.8 all-gather.11
  359.3 42.3 reduce-scatter.7
  817.1 65.6 reduce-scatter.5
  886.3 76.4 reduce-scatter.11
  966.3 76.4 reduce-scatter.13
  1045.8 33.1 reduce-scatter.9
  1083.4 77.2 all-reduce.28
where the time goes:
time: 1180 us; the launch traced here: 1170 us
  matrix products  539 us (46%)
  waiting for transfers between devices  223 us (19%)
  local copies, waits for them, and re-layouts  200 us (17%)
  other arithmetic  105 us (9%)
  blocking collectives  87.1 us (7%)
  between operations  18.9 us (2%)
    dot_general x4, matrix products, block_scores(): jnp.einsum('bijk,kh->bhij', features_low, kernel_map, preferred_element_t...  135 us
    reduce_scatter x1, waiting for transfers between devices, on_device(): lax.psum_scatter(grad_w_up, 'fsdp', scatter_dimension=0, tiled=True)  78 us
    reduce_scatter x1, waiting for transfers between devices, on_device(): lax.psum_scatter(grad_w_down, 'fsdp', scatter_dimension=0, tiled=True)  77.9 us
    dot_general x4, local copies, waits for them, and re-layouts, block_scores(): jnp.einsum('bijk,kh->bhij', features_low, kernel_map, preferred_element_t...  77.8 us
    dot_general x2, matrix products, attend_backward(): jnp.einsum('bijk,bhij->kh', scaled * standard - features / kernel_width,...  73 us
    dot_general x4, matrix products, block_scores(): jnp.einsum('bihe,bjhe->bhij', queries_b, keys_b, preferred_element_type=j...  58.8 us
    unnamed x2, blocking collectives  50.3 us
    psum x1, waiting for transfers between devices, on_device(): lax.psum(owned[3].astype(jnp.bfloat16), 'dp').astype(jnp.float32)  48.1 us
  transfers between devices with their start and end apart: 10, of which 4 were waited for; matrix products, arithmetic and copies ran while one was open for 66% of the time, Pallas kernels for 0%

commit v1 on v0

--- a/solution.py
+++ b/solution.py
@@ -1,17 +1,17 @@
-from functools import partial
+import functools
 import math
 
 import jax
 import jax.numpy as jnp
 from jax import lax
+from jax.experimental import pallas as pl
+from jax.experimental.pallas import tpu as pltpu
 from jax.sharding import PartitionSpec as P
 
 SET = 256
 
 
 epsilon = 1e-05
-root_tau = math.sqrt(2.0 * math.pi)
-masked_fill = -1e30
 
 
 def layer_norm(values_in, gain_vec, shift_vec):
@@ -33,75 +33,272 @@
     )
 
 
-def block_scores(queries_b, keys_b, coords_b, segs_b, kernel_mean, kernel_width, kernel_map):
-    offsets = coords_b[:, :, :, None] - coords_b[:, :, None, :]
-    radius = jnp.sqrt(jnp.sum(offsets * offsets, axis=1))
-    standard = (radius[..., None] - kernel_mean) / kernel_width
-    features = jnp.exp(-0.5 * standard * standard) / (root_tau * kernel_width)
-    features_low = features.astype(jnp.bfloat16)
-    pair_bias = jnp.einsum(
-        "bijk,kh->bhij", features_low, kernel_map, preferred_element_type=jnp.float32
-    )
-    scores = (
-        jnp.einsum("bihe,bjhe->bhij", queries_b, keys_b, preferred_element_type=jnp.float32)
-        + pair_bias
-    )
-    joined = segs_b[:, :, None] == segs_b[:, None, :]
-    scores = jnp.where(joined[:, None], scores, masked_fill)
-    return (scores, features, features_low, standard)
-
-
-def attend_forward(pieces, kernel_mean, kernel_width, kernel_map):
-    queries_b, keys_b, values_b, coords_b, segs_b = pieces
-    scores = block_scores(
-        queries_b, keys_b, coords_b, segs_b, kernel_mean, kernel_width, kernel_map
-    )[0]
-    row_max = jnp.max(scores, axis=-1, keepdims=True)
-    exponent = jnp.exp(scores - row_max)
-    row_total = jnp.sum(exponent, axis=-1, keepdims=True)
-    probs = exponent / row_total
-    attended_b = jnp.einsum(
-        "bhij,bjhe->bihe", probs.astype(jnp.bfloat16), values_b, preferred_element_type=jnp.float32
-    )
-    return (attended_b, row_max + jnp.log(row_total))
-
-
-def attend_backward(pieces, kernel_mean, kernel_width, kernel_map):
-    queries_b, keys_b, values_b, coords_b, segs_b, grad_b, log_total = pieces
-    scores, features, features_low, standard = block_scores(
-        queries_b, keys_b, coords_b, segs_b, kernel_mean, kernel_width, kernel_map
-    )
-    probs = jnp.exp(scores - log_total)
-    grad_probs = jnp.einsum("bihe,bjhe->bhij", grad_b, values_b, preferred_element_type=jnp.float32)
-    delta_row = jnp.sum(probs * grad_probs, axis=-1, keepdims=True)
-    grad_scores = (probs * (grad_probs - delta_row)).astype(jnp.bfloat16)
-    grad_queries = jnp.einsum(
-        "bhij,bjhe->bihe", grad_scores, keys_b, preferred_element_type=jnp.float32
-    )
-    grad_keys = jnp.einsum(
-        "bhij,bihe->bjhe", grad_scores, queries_b, preferred_element_type=jnp.float32
-    )
-    grad_values = jnp.einsum(
-        "bhij,bihe->bjhe", probs.astype(jnp.bfloat16), grad_b, preferred_element_type=jnp.float32
-    )
-    grad_map = jnp.einsum(
-        "bijk,bhij->kh", features_low, grad_scores, preferred_element_type=jnp.float32
-    )
-    scores_wide = grad_scores.astype(jnp.float32)
-    scaled = features * standard / kernel_width
-    mean_terms = jnp.einsum(
-        "bijk,bhij->kh", scaled, scores_wide, preferred_element_type=jnp.float32
-    )
-    width_terms = jnp.einsum(
-        "bijk,bhij->kh",
-        scaled * standard - features / kernel_width,
-        scores_wide,
-        preferred_element_type=jnp.float32,
-    )
-    map_wide = kernel_map.astype(jnp.float32)
-    grad_mean = jnp.sum(mean_terms * map_wide, axis=1)
-    grad_width = jnp.sum(width_terms * map_wide, axis=1)
-    return ((grad_queries, grad_keys, grad_values), (grad_map, grad_mean, grad_width))
+CH = 32
+WIN = 128
+GROUPS = ((0, 0, 10), (128, 10, 16), (384, 16, 26), (512, 26, 32))
+HW = 24
+VM = 60 * 1024 * 1024
+root_half_log2e = math.sqrt(0.5 * math.log2(math.e))
+f32, bf16 = jnp.float32, jnp.bfloat16
+NT = (((1,), (1,)), ((), ()))
+TN = (((0,), (0,)), ((), ()))
+
+
+def dot(a, b, dims=(((1,), (0,)), ((), ()))):
+    return lax.dot_general(a, b, dims, preferred_element_type=f32)
+
+
+def lane_mask(lane0, head, rows):
+    lanes = lax.broadcasted_iota(jnp.int32, (rows, 256), 1) + lane0
+    return (lanes >= head * HW) & (lanes < (head + 1) * HW)
+
+
+def spread_heads(block, lane0, h0, h1):
+    wide = block.astype(f32)
+    zero = jnp.zeros_like(wide)
+    return jnp.concatenate(
+        [jnp.where(lane_mask(lane0, h, wide.shape[0]), wide, zero).astype(bf16) for h in range(h0, h1)], axis=0
+    )
+
+
+def pick_heads(full, lane0, h0, h1):
+    n = h1 - h0
+    full = full.reshape(n, CH, 256)
+    out = jnp.zeros((CH, 256), f32)
+    for j in range(n):
+        out = jnp.where(lane_mask(lane0, h0 + j, CH), full[j], out)
+    return out
+
+
+def window_start(i, rows):
+    return pl.multiple_of(jnp.clip(i * CH - 48, 0, rows - WIN), 16)
+
+
+def radius_of(ac, aw):
+    d = ac[:, 0:1] - aw[0:1, :]
+    s = d * d
+    for j in (1, 2):
+        d = ac[:, j : j + 1] - aw[j : j + 1, :]
+        s = s + d * d
+    return jnp.sqrt(s)
+
+
+def fwd_kernel(q_ref, k_ref, v_ref, aw_ref, ac_ref, kp_ref, bmat_ref, o_ref, p_ref, rho_scr, f_scr, b_scr):
+    rows = k_ref.shape[0]
+    w = window_start(pl.program_id(0), rows)
+    ac, aw = ac_ref[...], aw_ref[0]
+    rho_scr[...] = radius_of(ac, aw)
+    joined = ac[:, 3:4] == aw[3:4, :]
+    for p in range(2):
+        for kt in range(8):
+            ks = slice(16 * kt, 16 * kt + 16)
+            A, B, C = kp_ref[0, ks, :], kp_ref[1, ks, :], kp_ref[2, ks, :]
+            for r in range(8):
+                for gg in range(2):
+                    rr = rho_scr[pl.ds(16 * p + 8 * gg + r, 1), :]
+                    y = rr * A - B
+                    f = jnp.exp2(C - y * y)
+                    f_scr[p, r * 128 + 16 * kt : r * 128 + 16 * kt + 16, gg * 128 : gg * 128 + 128] = f.astype(bf16)
+        bias = dot(bmat_ref[...], f_scr[p])
+        for gg in range(2):
+            b_scr[:, 2 * p + gg] = bias[:, gg * 128 : gg * 128 + 128].reshape(32, 8, 128)
+    kwin = k_ref[pl.ds(w, WIN), :]
+    vwin = v_ref[pl.ds(w, WIN), :]
+    acc = []
+    for lane0, h0, h1 in GROUPS:
+        n = h1 - h0
+        sl = slice(lane0, lane0 + 256)
+        qm = spread_heads(q_ref[:, sl], lane0, h0, h1)
+        s = dot(qm, kwin[:, sl], NT).reshape(n, CH, WIN) + b_scr[h0:h1].reshape(n, CH, WIN)
+        s = jnp.where(joined[None], s, -1e30)
+        e = jnp.exp(s - jnp.max(s, axis=-1, keepdims=True))
+        pr = (e * (1.0 / jnp.sum(e, axis=-1, keepdims=True))).reshape(n * CH, WIN).astype(bf16)
+        p_ref[0, h0 * CH : h1 * CH, :] = pr
+        acc.append(pick_heads(dot(pr, vwin[:, sl]), lane0, h0, h1))
+    for half in range(2):
+        a, b = acc[2 * half], acc[2 * half + 1]
+        full = jnp.concatenate([a[:, :128], a[:, 128:] + b[:, :128], b[:, 128:]], axis=1)
+        o_ref[:, 384 * half : 384 * half + 384] = full.astype(bf16)
+
+
+def bwd_kernel(q_ref, do_ref, k_ref, v_ref, p_ref, gp_ref, ds_ref, dk_scr, dv_scr, *, scale):
+    rows = k_ref.shape[0]
+    i = pl.program_id(0)
+    w = window_start(i, rows)
+    width = 32 * HW
+
+    @pl.when(i == 0)
+    def _():
+        dk_scr[...] = jnp.zeros_like(dk_scr)
+        dv_scr[...] = jnp.zeros_like(dv_scr)
+
+    kwin = k_ref[pl.ds(w, WIN), :]
+    vwin = v_ref[pl.ds(w, WIN), :]
+    acc = []
+    for lane0, h0, h1 in GROUPS:
+        n = h1 - h0
+        sl = slice(lane0, lane0 + 256)
+        qm = spread_heads(q_ref[:, sl], lane0, h0, h1)
+        dom = spread_heads(do_ref[:, sl], lane0, h0, h1)
+        p_low = p_ref[0, h0 * CH : h1 * CH, :]
+        dp = dot(dom, vwin[:, sl], NT)
+        pf = p_low.astype(f32)
+        pd = pf * dp
+        ds = pd - pf * jnp.sum(pd, axis=-1, keepdims=True)
+        ds4 = ds.reshape(n, 4, 8, WIN)
+        for g in range(4):
+            ds_ref[0, g // 2, h0 * 8 : h1 * 8, (g % 2) * 128 : (g % 2) * 128 + 128] = (
+                ds4[:, g].reshape(n * 8, WIN).astype(bf16)
+            )
+        ds_low = ds.astype(bf16)
+        acc.append(pick_heads(dot(ds_low, kwin[:, sl]), lane0, h0, h1))
+        dk_scr[pl.ds(w, WIN), sl] += dot(ds_low, qm, TN)
+        dv_scr[pl.ds(w, WIN), sl] += dot(p_low, dom, TN)
+    r0 = pl.multiple_of(i * CH, CH)
+    for half in range(2):
+        a, b = acc[2 * half], acc[2 * half + 1]
+        full = jnp.concatenate([a[:, :128], a[:, 128:] + b[:, :128], b[:, 128:]], axis=1)
+        gp_ref[pl.ds(r0, CH), 384 * half : 384 * half + 384] = (full * scale).astype(bf16)
+
+    @pl.when(i == pl.num_programs(0) - 1)
+    def _():
+        gp_ref[:, width : 2 * width] = dk_scr[...].astype(bf16)
+        gp_ref[:, 2 * width :] = dv_scr[...].astype(bf16)
+
+
+def feat_kernel(ds_ref, aw_ref, ac_ref, kp_ref, amat_ref, m0_ref, acc_ref, rho_scr, f_scr, gf_scr):
+    i = pl.program_id(0)
+
+    @pl.when(i == 0)
+    def _():
+        m0_ref[...] = jnp.zeros_like(m0_ref)
+        acc_ref[...] = jnp.zeros_like(acc_ref)
+
+    rho_scr[...] = radius_of(ac_ref[...], aw_ref[0])
+    for p in range(2):
+        gf_scr[p] = dot(amat_ref[...], ds_ref[0, p])
+    for p in range(2):
+        for kt in range(8):
+            ks = slice(16 * kt, 16 * kt + 16)
+            A, B, C = kp_ref[0, ks, :], kp_ref[1, ks, :], kp_ref[2, ks, :]
+            a1 = acc_ref[0, ks, :]
+            a2 = acc_ref[1, ks, :]
+            for r in range(8):
+                for gg in range(2):
+                    rr = rho_scr[pl.ds(16 * p + 8 * gg + r, 1), :]
+                    at = (p, slice(r * 128 + 16 * kt, r * 128 + 16 * kt + 16), slice(gg * 128, gg * 128 + 128))
+                    y = rr * A - B
+                    f = jnp.exp2(C - y * y)
+                    f_scr[at] = f.astype(bf16)
+                    ty = gf_scr[at] * f * y
+                    a1 = a1 + ty
+                    a2 = a2 + ty * y
+            acc_ref[0, ks, :] = a1
+            acc_ref[1, ks, :] = a2
+        m0_ref[...] += dot(f_scr[p], ds_ref[0, p], NT)
+
+
+def full_spec(shape):
+    return pl.BlockSpec(shape, lambda i: (0,) * len(shape))
+
+
+def params(limit=VM):
+    return pltpu.CompilerParams(vmem_limit_bytes=limit, dimension_semantics=("arbitrary",))
+
+
+def attn_fwd(q, k, v, aw, ac, kp, bmat):
+    rows, width = q.shape
+    c = rows // CH
+    return pl.pallas_call(
+        fwd_kernel,
+        grid=(c,),
+        in_specs=[
+            pl.BlockSpec((CH, width), lambda i: (i, 0)),
+            full_spec(k.shape), full_spec(v.shape),
+            pl.BlockSpec((1, 8, WIN), lambda i: (i, 0, 0)),
+            pl.BlockSpec((CH, 4), lambda i: (i, 0)),
+            full_spec(kp.shape), full_spec(bmat.shape),
+        ],
+        out_specs=[pl.BlockSpec((CH, width), lambda i: (i, 0)), pl.BlockSpec((1, 32 * CH, WIN), lambda i: (i, 0, 0))],
+        out_shape=[jax.ShapeDtypeStruct((rows, width), bf16), jax.ShapeDtypeStruct((c, 32 * CH, WIN), bf16)],
+        scratch_shapes=[pltpu.VMEM((CH, WIN), f32), pltpu.VMEM((2, 1024, 256), bf16), pltpu.VMEM((32, 4, 8, 128), f32)],
+        compiler_params=params(),
+        name="attn_fwd",
+    )(q, k, v, aw, ac, kp, bmat)
+
+
+def attn_bwd(q, do, k, v, p, scale):
+    rows, width = q.shape
+    c = rows // CH
+    return pl.pallas_call(
+        functools.partial(bwd_kernel, scale=scale),
+        grid=(c,),
+        in_specs=[
+            pl.BlockSpec((CH, width), lambda i: (i, 0)),
+            pl.BlockSpec((CH, width), lambda i: (i, 0)),
+            full_spec(k.shape), full_spec(v.shape),
+            pl.BlockSpec((1, 32 * CH, WIN), lambda i: (i, 0, 0)),
+        ],
+        out_specs=[full_spec((rows, 3 * width)), pl.BlockSpec((1, 2, 256, 256), lambda i: (i, 0, 0, 0))],
+        out_shape=[jax.ShapeDtypeStruct((rows, 3 * width), bf16), jax.ShapeDtypeStruct((c, 2, 256, 256), bf16)],
+        scratch_shapes=[pltpu.VMEM((rows, width), f32)] * 2,
+        compiler_params=params(),
+        name="attn_bwd",
+    )(q, do, k, v, p)
+
+
+def attn_feat(ds, aw, ac, kp, amat):
+    c = ds.shape[0]
+    return pl.pallas_call(
+        feat_kernel,
+        grid=(c,),
+        in_specs=[
+            pl.BlockSpec((1, 2, 256, 256), lambda i: (i, 0, 0, 0)),
+            pl.BlockSpec((1, 8, WIN), lambda i: (i, 0, 0)),
+            pl.BlockSpec((CH, 4), lambda i: (i, 0)),
+            full_spec(kp.shape), full_spec(amat.shape),
+        ],
+        out_specs=[full_spec((1024, 256)), full_spec((2, 128, 128))],
+        out_shape=[jax.ShapeDtypeStruct((1024, 256), f32), jax.ShapeDtypeStruct((2, 128, 128), f32)],
+        scratch_shapes=[pltpu.VMEM((CH, WIN), f32), pltpu.VMEM((2, 1024, 256), bf16), pltpu.VMEM((2, 1024, 256), f32)],
+        compiler_params=params(),
+        name="attn_feat",
+    )(ds, aw, ac, kp, amat)
+
+
+def aux_of(coords, segment_ids):
+    rows = coords.shape[1]
+    place = jnp.arange(rows, dtype=jnp.int32) // SET
+    key = (segment_ids * (rows // SET) + place).astype(f32)
+    packed = jnp.concatenate([coords, key[None], jnp.zeros((4, rows), f32)], axis=0)
+    starts = [min(max(CH * i - 48, 0), rows - WIN) for i in range(rows // CH)]
+    aw = jnp.stack([packed[:, s : s + WIN] for s in starts])
+    ac = packed[:4].T
+    return aw, ac
+
+
+def kernel_consts(mean, width, kmap):
+    mean, width = mean.astype(f32), width.astype(f32)
+    a = root_half_log2e / width
+    b = mean * a
+    c = -jnp.log2(math.sqrt(2 * math.pi) * width)
+    kp = jnp.broadcast_to(jnp.stack([a, b, c])[:, :, None], (3, mean.shape[0], 128))
+    eye = jnp.eye(8, dtype=bf16)
+    heads = kmap.shape[1]
+    amat = (eye[:, None, None, :] * kmap[None, :, :, None]).reshape(8 * kmap.shape[0], heads * 8)
+    return kp, amat
+
+
+def feat_finish(m0, acc, width, kmap):
+    n, heads = kmap.shape
+    m = m0.reshape(8, n, heads, 8)
+    g_map = jnp.sum(m * jnp.eye(8, dtype=f32)[:, None, None, :], axis=(0, 3))
+    width = width.astype(f32)
+    s = jnp.sum(acc, axis=-1)
+    a0 = jnp.sum(g_map * kmap.astype(f32), axis=1)
+    g_mean = s[0] / (root_half_log2e * width)
+    g_width = (s[1] / (root_half_log2e * root_half_log2e) - a0) / width
+    return g_map, g_mean, g_width
 
 
 def on_device(
@@ -158,13 +355,7 @@
     width_model = inputs.shape[1]
     head_count = map_full.shape[1]
     head_width = width_model // head_count
-    sets_here = rows_here // SET
-    per_block = math.gcd(sets_here, max(1, 512 // SET))
-    block_count = sets_here // per_block
     query_scale = head_width ** (-0.5)
-
-    def to_blocks(array):
-        return array.reshape(block_count, per_block, SET, head_count, head_width)
 
     start = inputs.astype(jnp.float32) + time_of_row[:, None] * time_full.astype(jnp.float32)
     normed_low = layer_norm(
@@ -178,21 +369,11 @@
     values_low = (projected[:, 2 * width_model :] + vbias_full.astype(jnp.float32)).astype(
         jnp.bfloat16
     )
-    coords_blocks = jnp.transpose(coords.reshape(3, block_count, per_block, SET), (1, 2, 0, 3))
-    segs_blocks = segment_ids.reshape(block_count, per_block, SET)
-    query_blocks = to_blocks(queries)
-    key_blocks = to_blocks(keys_low)
-    value_blocks = to_blocks(values_low)
-    attended_blocks, log_totals = lax.map(
-        partial(
-            attend_forward,
-            kernel_mean=mean_full.astype(jnp.float32),
-            kernel_width=width_full.astype(jnp.float32),
-            kernel_map=map_full,
-        ),
-        (query_blocks, key_blocks, value_blocks, coords_blocks, segs_blocks),
-    )
-    attended = attended_blocks.reshape(rows_here, width_model).astype(jnp.bfloat16)
+    aux_win, aux_col = aux_of(coords, segment_ids)
+    consts, spread_map = kernel_consts(mean_full, width_full, map_full)
+    attended, probs = attn_fwd(
+        queries, keys_low, values_low, aux_win, aux_col, consts, spread_map.T
+    )
     middle = (
         start
         + jnp.dot(attended, wout_full, preferred_element_type=jnp.float32)
@@ -232,7 +413,7 @@
     grad_w_down = contract_rows(hidden_low, cotangent)
     grad_down_bias = jnp.sum(grad_output, axis=0)
     grad_hidden = times_transpose(cotangent, ffn_back[4])
-    unused_gelu, gelu_pull = jax.vjp(partial(jax.nn.gelu, approximate=False), pre_hidden)
+    unused_gelu, gelu_pull = jax.vjp(functools.partial(jax.nn.gelu, approximate=False), pre_hidden)
     grad_pre = gelu_pull(grad_hidden)[0].astype(jnp.bfloat16)
     grad_w_up = contract_rows(normed2_low, grad_pre)
     grad_up_bias = jnp.sum(grad_pre.astype(jnp.float32), axis=0)
@@ -259,44 +440,15 @@
     grad_w_out = contract_rows(attended, grad_attn)
     grad_out_bias = jnp.sum(grad_attn.astype(jnp.float32), axis=0)
     grad_attended = times_transpose(grad_attn, attn_back[6]).astype(jnp.bfloat16)
-    mean_back = attn_back[8].astype(jnp.float32)
-    width_back = attn_back[9].astype(jnp.float32)
-    map_back = attn_back[10]
-
-    def back_step(carried, pieces):
-        row_grads, kernel_grads = attend_backward(pieces, mean_back, width_back, map_back)
-        summed = (
-            carried[0] + kernel_grads[0],
-            carried[1] + kernel_grads[1],
-            carried[2] + kernel_grads[2],
-        )
-        return (summed, row_grads)
-
-    start_carry = (
-        jnp.zeros(map_back.shape, jnp.float32),
-        jnp.zeros(mean_back.shape, jnp.float32),
-        jnp.zeros(mean_back.shape, jnp.float32),
-    )
-    kernel_sums, row_blocks = lax.scan(
-        back_step,
-        start_carry,
-        (
-            query_blocks,
-            key_blocks,
-            value_blocks,
-            coords_blocks,
-            segs_blocks,
-            to_blocks(grad_attended),
-            log_totals,
-        ),
-    )
-    grad_kernel_map, grad_kernel_mean, grad_kernel_width = kernel_sums
-    grad_pre_query = (row_blocks[0].reshape(rows_here, width_model) * query_scale).astype(
-        jnp.bfloat16
-    )
-    grad_keys = row_blocks[1].reshape(rows_here, width_model).astype(jnp.bfloat16)
-    grad_values = row_blocks[2].reshape(rows_here, width_model).astype(jnp.bfloat16)
-    grad_projected = jnp.concatenate((grad_pre_query, grad_keys, grad_values), axis=1)
+    grad_projected, grad_scores = attn_bwd(
+        queries, grad_attended, keys_low, values_low, probs, query_scale
+    )
+    map_parts, feature_parts = attn_feat(grad_scores, aux_win, aux_col, consts, spread_map)
+    grad_kernel_map, grad_kernel_mean, grad_kernel_width = feat_finish(
+        map_parts, feature_parts, width_full, map_full
+    )
+    grad_pre_query = grad_projected[:, :width_model]
+    grad_values = grad_projected[:, 2 * width_model :]
     grad_w_qkv = contract_rows(normed_low, grad_projected)
     grad_q_bias = jnp.sum(grad_pre_query.astype(jnp.float32), axis=0)
     grad_v_bias = jnp.sum(grad_values.astype(jnp.float32), axis=0)

time: 1180 us -> 660 us (0.56)
  matrix products: 539 us -> 131 us
  local copies, waits for them, and re-layouts: 200 us -> 45.6 us
  Pallas kernels: 0 us -> 154 us
  other arithmetic: 105 us -> 43.2 us
  waiting for transfers between devices: 223 us -> 173 us
    dot_general x24 -> x0, matrix products: 412 us -> none  [the longest x4 135 us: block_scores(): jnp.einsum('bijk,kh->bhij', features_low, kernel_map, preferred_element_t...]
    pallas_call x0 -> x3, Pallas kernels: none -> 154 us  [the longest x1 56.4 us: attn_bwd(): pl.pallas_call(functools.partial(bwd_kernel, scale=scale), grid=(c,), in_...]
    dot_general x4 -> x0, local copies, waits for them, and re-layouts: 77.8 us -> none  [block_scores(): jnp.einsum('bijk,kh->bhij', features_low, kernel_map, preferred_element_t...]
    reduce_scatter x1, waiting for transfers between devices: 78 us -> 16 us  [on_device(): lax.psum_scatter(grad_w_up, 'fsdp', scatter_dimension=0, tiled=True)]
    convert_element_type x13 -> x0, local copies, waits for them, and re-layouts: 56 us -> none  [the longest x2 29.4 us: attend_backward(): grad_scores = (probs * (grad_probs - delta_row)).astype(jnp.bfloat16)]
    convert_element_type x7 -> x4, other arithmetic: 34.8 us -> 2.3 us  [the longest x1 2.28 us: on_device(): (projected[:, 2 * width_model:] + vbias_full.astype(jnp.float32)).astype(...]
    unnamed x10 -> x11, waiting for transfers between devices: 2.68 us -> 24.5 us
    reduce_sum x7 -> x4, other arithmetic: 23.4 us -> 5.16 us  [the longest x1 2.38 us: on_device(): grad_v_bias = jnp.sum(grad_values.astype(jnp.float32), axis=0)]
  transfers between devices with their start and end apart: 10 -> 10, of which waited for: 4 -> 4; matrix products, arithmetic and copies ran while one was open for 66% -> 26% of each run, Pallas kernels for 0% -> 24%
where the time goes in v1:
time: 660 us; the launch traced here: 654 us
  waiting for transfers between devices  173 us (26%)
  Pallas kernels  154 us (23%)
  matrix products  131 us (20%)
  blocking collectives  88.8 us (13%)
  local copies, waits for them, and re-layouts  45.6 us (7%)
  other arithmetic  43.2 us (7%)
  between operations  18.5 us (3%)
    reduce_scatter x1, waiting for transfers between devices, on_device(): lax.psum_scatter(grad_w_down, 'fsdp', scatter_dimension=0, tiled=True)  77.9 us
    pallas_call x1, Pallas kernels, attn_bwd(): pl.pallas_call(functools.partial(bwd_kernel, scale=scale), grid=(c,), in_...  56.4 us
    pallas_call x1, Pallas kernels, attn_fwd(): pl.pallas_call(fwd_kernel, grid=(c,), in_specs=[pl.BlockSpec((CH, width),...  56.2 us
    psum x1, waiting for transfers between devices, on_device(): lax.psum(owned[3].astype(jnp.bfloat16), 'dp').astype(jnp.float32)  54.2 us
    unnamed x2, blocking collectives  52.4 us
    pallas_call x1, Pallas kernels, attn_feat(): pl.pallas_call(feat_kernel, grid=(c,), in_specs=[pl.BlockSpec((1, 2, 256,...  41.7 us
    dot_general x4, matrix products, times_transpose(): lax.dot_general(left, right, (((1,), (1,)), ((), ())), preferred_element_...  40.2 us
    dot_general x1, matrix products, on_device(): jnp.dot(normed2_low, up_full, preferred_element_type=jnp.float32)  38.1 us
  transfers between devices with their start and end apart: 10, of which 4 were waited for; matrix products, arithmetic and copies ran while one was open for 26% of the time, Pallas kernels for 24%

profile of v1, /device:TPU:0, one launch (start us, length us, event | category | flops | bytes accessed | tf_op | source)
XLA Modules:
  0.0 654.5 jit_solution(4557534700850204418)
XLA Ops:
  10.1 1.3 fusion.34
  12.7 0.8 dynamic-update-slice
  13.6 0.8 dynamic-update-slice.1
  14.4 0.8 dynamic-update-slice.10
  15.2 0.8 dynamic-update-slice.2
  16.1 0.8 dynamic-update-slice.3
  16.9 0.8 dynamic-update-slice.4
  17.7 0.8 dynamic-update-slice.7
  18.6 0.8 dynamic-update-slice.8
  19.4 0.8 dynamic-update-slice.9
  20.3 0.8 dynamic-update-slice.5
  21.1 0.8 dynamic-update-slice.6
  21.9 26.4 %all-reduce.24 = (bf16[768]{0:T(1024)(128)(2,1)S(1)}, bf16[768]{0:T(1024)(128)(2,1)S(1)}, bf16[768]{0:T(1024)(128)(2,1)S(1)}, bf16[768]{0:T(1024)(128)(2,1)S(1)}...) all-reduce(bf16[768]{0:T(1024)(128)(2,1)S(1)} %dynamic-update-slice, ...), channel_id=1, replica_groups=mesh['fsdp'=8,'dp'=4] {'fsdp'}, use_global_device_ids=true, to_apply=%add.2 | all-reduce | flops 7168 | bytes 28672
  48.4 1.7 copy.81
  53.7 7.6 %all_gather.65 = bf16[128,32]{1,0:T(8,128)(2,1)S(1)} all-gather(bf16[16,32]{1,0:T(8,128)(2,1)S(1)} %copy-done.25), channel_id=1, replica_groups=mesh['fsdp'=8,'dp'=4] {'fsdp'}, dimensions={0}, use_global_device_ids=true | all-gather | bytes 9216 | tf_op jit(solution)/shard_map/all_gather | solution.py:339
  61.5 0.9 copy.105
  62.4 1.0 copy.82
  63.5 9.6 %all-gather = bf16[8,1,384]{2,1,0:T(2,128)(2,1)S(1)} all-gather(bf16[1,1,384]{2,1,0:T(2,128)(2,1)S(1)} %reshape.167), channel_id=1, replica_groups=mesh['fsdp'=8,'dp'=4] {'fsdp'}, dimensions={0}, use_global_device_ids=true | all-gather | bytes 6912 | tf_op jit(solution)/shard_map/all_gather | solution.py:386
  73.1 1.6 copy.85
  74.8 6.4 fusion.29
  81.3 1.3 slice.293.k_ref
  82.6 2.3 fusion.6
  85.7 56.2 %attn_fwd.1 = (bf16[1024,768]{1,0:T(8,128)(2,1)}, bf16[32,1024,128]{2,1,0:T(8,128)(2,1)}) custom-call(bf16[1024,768]{1,0:T(8,128)(2,1)} %get-tuple-element.164.q_ref, bf16[1024,768]{1,0:T(8,128)(2,1)} %slice.293.k_ref, bf16[1024,768]{1,0:T(8,128)(2,1)} %get-tuple-element.163.v_ref, f32[32,8,128]{2,1,0:T(8,128)} %copy-done.10, f32[1024,4]{1,0:T(8,128)} %bitcast.182, ...), custom_call_target="tpu_custom_call" | custom-call | tf_op jit(solution)/shard_map/attn_fwd/pallas_call | solution.py:212
  141.9 3.6 fusion.35
  145.5 1.7 copy-done.1
  147.7 38.1 %multiply_convert_fusion = (bf16[1024,3072]{1,0:T(8,128)(2,1)}, f32[1024,3072]{1,0:T(8,128)}, f32[1024,3072]{1,0:T(8,128)}) fusion(f32[3072]{0:T(1024)S(1)} %bitcast.189, bf16[768,3072]{1,0:T(8,128)(2,1)} %all-gather.10.cloned.1.call-done, f32[1024,768]{0,1:T(8,128)} %copy-done.1, f32[768]{0:T(1024)S(1)} %convert_element_type.225, ...), kind=kOutput, calls=%fused_computation.4 | convolution fusion | flops 5043388416 | bytes 39348224 | tf_op jit(solution)/shard_map/dot_general | solution.py:394
  185.8 16.8 %convert_reduce_fusion = (f32[3072]{0:T(1024)S(1)}, bf16[1024,3072]{1,0:T(8,128)(2,1)}) fusion(f32[1024,3072]{1,0:T(8,128)} %get-tuple-element.159, bf16[1024,768]{1,0:T(8,128)(2,1)S(1)} %copy-done.8, bf16[3072,768]{1,0:T(8,128)(2,1)} %all-gather.12.cloned.1.call-done, f32[1024,3072]{1,0:T(8,128)} %get-tuple-element.174, f32[3072]{0:T(1024)S(1)} %bitcast.190), kind=kOutput, calls=%fused_computation.2 | convolution fusion | flops 4885312512 | bytes 37773312 | tf_op jit(solution)/shard_map/dot_general | solution.py:31
  202.6 9.9 %fusion.37 = (f32[768]{0:T(1024)S(1)}, f32[1024,768]{1,0:T(8,128)}) fusion(bf16[1024,3072]{1,0:T(8,128)(2,1)} %get-tuple-element.180, bf16[768,3072]{1,0:T(8,128)(2,1)} %all-gather.10.cloned.1.call-done), kind=kOutput, calls=%fused_computation.170 | convolution fusion | flops 4832623616 | bytes 14158848 | tf_op jit(solution)/shard_map/dot_general | solution.py:31
  212.5 3.6 copy.86
  216.0 3.9 multiply_reduce_fusion
  223.2 1.2 copy-done.9
  224.4 2.9 fusion.38
  227.3 4.4 convolution_convert_fusion.do_ref
  231.7 56.4 %attn_bwd.1 = (bf16[1024,2304]{1,0:T(8,128)(2,1)}, bf16[32,2,256,256]{3,2,1,0:T(8,128)(2,1)}) custom-call(bf16[1024,768]{1,0:T(8,128)(2,1)} %get-tuple-element.164.q_ref, bf16[1024,768]{1,0:T(8,128)(2,1)} %convolution_convert_fusion.do_ref, bf16[1024,768]{1,0:T(8,128)(2,1)} %slice.293.k_ref, bf16[1024,768]{1,0:T(8,128)(2,1)} %get-tuple-element.163.v_ref, ...), custom_call_target="tpu_custom_call" | custom-call | tf_op jit(solution)/shard_map/attn_bwd/pallas_call | solution.py:233
  288.2 8.7 %fusion.28 = f32[768,2304]{1,0:T(8,128)} fusion(bf16[1024,2304]{1,0:T(8,128)(2,1)} %get-tuple-element.27, bf16[1024,768]{0,1:T(8,128)(2,1)S(1)} %copy.81, f32[768]{0:T(1024)S(1)} %copy-done.27, f32[768]{0:T(1024)S(1)} %copy-done.20, f32[1024]{0:T(1024)S(1)} %copy-done.24, f32[1024]{0:T(1024)S(1)} %copy-done.15, f32[768]{0:T(1024)S(1)} %convert_element_type.211, ...), kind=kOutput, calls=%fused_computation.163 | convolution fusion | flops 3630170112 | bytes 13390848 | tf_op jit(solution)/shard_map/dot_general | solution.py:25
  297.0 11.0 %fusion.26 = f32[768,3072]{1,0:T(8,128)} fusion(bf16[1024,3072]{1,0:T(8,128)(2,1)} %get-tuple-element.180, f32[1024,768]{0,1:T(8,128)} %copy-done.1, f32[768]{0:T(1024)S(1)} %convert_element_type.225, f32[768]{0:T(1024)S(1)} %convert_element_type.224, f32[1024]{0:T(1024)S(1)} %fusion.23, f32[1024]{0:T(1024)S(1)} %broadcast_multiply_fusion), kind=kOutput, calls=%fused_computation.161 | convolution fusion | flops 4835770368 | bytes 18888704 | tf_op jit(solution)/shard_map/dot_general | solution.py:25
  308.0 10.6 %fusion.39 = f32[3072,768]{1,0:T(8,128)} fusion(bf16[1024,3072]{1,0:T(8,128)(2,1)} %get-tuple-element.158, bf16[1024,768]{1,0:T(8,128)(2,1)} %param.26), kind=kOutput, calls=%fused_computation.172 | convolution fusion | flops 4831838208 | bytes 17301504 | tf_op jit(solution)/shard_map/dot_general | solution.py:25
  318.7 2.0 copy.89.amat_ref
  322.7 41.7 %attn_feat.1 = (f32[1024,256]{1,0:T(8,128)}, f32[2,128,128]{2,1,0:T(8,128)}) custom-call(bf16[32,2,256,256]{3,2,1,0:T(8,128)(2,1)} %get-tuple-element.28.ds_ref, f32[32,8,128]{2,1,0:T(8,128)} %copy-done.10, f32[1024,4]{1,0:T(8,128)} %bitcast.183, f32[3,128,128]{2,1,0:T(8,128)} %broadcast_in_dim.16.kp_ref, bf16[1024,256]{1,0:T(8,128)(2,1)} %copy.89.amat_ref), custom_call_target="tpu_custom_call" | custom-call | tf_op jit(solution)/shard_map/attn_feat/pallas_call | solution.py:252
  364.4 2.5 copy.90
  366.9 1.0 reduce_sum.209
  367.9 9.1 %fusion.36 = (f32[768]{0:T(1024)S(1)}, f32[1024,768]{1,0:T(8,128)}) fusion(bf16[1024,2304]{1,0:T(8,128)(2,1)} %get-tuple-element.27, bf16[768,2304]{1,0:T(8,128)(2,1)} %all-gather.6.cloned.1.call-done), kind=kOutput, calls=%fused_computation.169 | convolution fusion | flops 3624664320 | bytes 11406336 | tf_op jit(solution)/shard_map/dot_general | solution.py:31
  377.0 4.2 copy.87
  381.2 1.7 fusion.13
  383.7 2.9 multiply_reduce_fusion.3
  386.7 1.2 fusion.30
  387.9 2.4 convert_reduce_fusion.3
  390.3 4.2 multiply_reduce_fusion.1
  394.5 25.9 %all-reduce.23 = (bf16[768]{0:T(1024)(128)(2,1)S(1)}, bf16[768]{0:T(1024)(128)(2,1)S(1)}, bf16[768]{0:T(1024)(128)(2,1)S(1)}, bf16[768]{0:T(1024)(128)(2,1)S(1)}...) all-reduce(f32[768]{0:T(1024)S(1)} %get-tuple-element.110, ...), channel_id=2, replica_groups=mesh['fsdp'=8,'dp'=4] {'fsdp'}, use_global_device_ids=true, to_apply=%region_9.10.clone | all-reduce | flops 10240 | bytes 61440
  421.3 2.6 copy.94
  423.9 1.6 convert_element_type.250
  425.5 2.1 convert_element_type.242
  427.7 16.0 %reduce-scatter.12.cloned.1.call-done = f32[96,3072]{1,0:T(8,128)} async-done(((f32[768,3072]{1,0:T(8,128)}), f32[96,3072]{1,0:T(8,128)}) %reduce-scatter.12.cloned.1.call-update) | async-done | bytes 1179664 | tf_op jit(solution)/shard_map/reduce_scatter | solution.py:477
  443.7 2.2 convert_element_type.267
  445.8 77.9 %reduce-scatter.14.cloned.1.call-done = f32[384,768]{1,0:T(8,128)} async-done(((f32[3072,768]{1,0:T(8,128)}), f32[384,768]{1,0:T(8,128)}) %reduce-scatter.14.cloned.1.call-update) | async-done | bytes 1179664 | tf_op jit(solution)/shard_map/reduce_scatter | solution.py:479
  523.7 2.1 convert_element_type.272
  525.9 9.5 %add_convert_fusion.1 = bf16[1024,768]{0,1:T(8,128)(2,1)} fusion(f32[1024,768]{0,1:T(8,128)S(1)} %copy-done.3, bf16[1024,3072]{1,0:T(8,128)(2,1)} %get-tuple-element.158, bf16[3072,768]{1,0:T(8,128)(2,1)} %all-gather.12.cloned.1.call-done, f32[768]{0:T(1024)S(1)} %convert_element_type.229), kind=kOutput, calls=%fused_computation.37 | convolution fusion | flops 4834197504 | bytes 15731712 | tf_op jit(solution)/shard_map/dot_general | solution.py:400
  535.4 2.6 copy.93
  538.1 21.9 %reduce-scatter.16.cloned.1.call-done = f32[16,32]{1,0:T(8,128)} async-done(((f32[128,32]{1,0:T(8,128)}), f32[16,32]{1,0:T(8,128)}) %reduce-scatter.16.cloned.1.call-update) | async-done | bytes 2064
  560.7 19.3 %all-reduce.25 = (bf16[16,32]{0,1:T(8,128)(2,1)S(1)}, bf16[96]{0:T(256)(128)(2,1)S(1)}, bf16[96]{0:T(256)(128)(2,1)S(1)}, bf16[96]{0:T(256)(128)(2,1)S(1)}, bf16...) all-reduce(bf16[16,32]{0,1:T(8,128)(2,1)S(1)} %copy.98, ...), channel_id=1, replica_groups=mesh['fsdp'=8,'dp'=4] {'dp'}, use_global_device_ids=true, to_apply=%region_38.39 | all-reduce | flops 1792 | bytes 7168 | tf_op jit(solution)/shard_map/psum | solution.py:493
  586.9 54.2 %all-reduce.29.cloned.1.call-done = (bf16[96,2304]{1,0:T(8,128)(2,1)}, bf16[96,768]{1,0:T(8,128)(2,1)}, bf16[96,3072]{1,0:T(8,128)(2,1)}, bf16[384,768]{1,0:T(8,128)(2,1)}) async-done(((bf16[96,2304]{1,0:T(8,128)(2,1)}, bf16[96,768]{1,0:T(8,128)(2,1)}, bf16[96,3072]{1,0:T(8,128)(2,1)}, bf16[384,768]{1,0:T(8,128)(2,1)}), (bf16[96,2304]{1,0:T(8,128)(2,1)}, bf16[96,768]{1,0:T(8,128)(2,1)}, ...) | async-done | bytes 1769488 | tf_op jit(solution)/shard_map/psum | solution.py:486
  641.1 2.2 convert_element_type.268
  643.3 2.2 convert_element_type.273
  645.5 1.0 convert_element_type.243
  (201 shorter events, 21.4 us)
Async XLA Ops:
  7.2 43.0 %copy-start.13 = (f32[1024]{0:T(1024)S(1)}, f32[1024]{0:T(1024)}, u32[]{:S(2)}) copy-start(f32[1024]{0:T(1024)} %param.23) | copy-start | bytes 12292
  7.2 67.6 %all-gather.6.cloned.1.call-start = ((), (), s32[]{:S(2)}) async-start(), calls=%async_computation.5 | async-start | bytes 3981312 | tf_op jit(solution)/shard_map/all_gather | solution.py:332
  7.9 133.9 %all-gather.8.cloned.1.call-start = ((), (), s32[]{:S(2)}) async-start(), calls=%async_computation.6 | async-start | bytes 1327104 | tf_op jit(solution)/shard_map/all_gather | solution.py:335
  8.7 139.0 %all-gather.10.cloned.1.call-start = ((), (), s32[]{:S(2)}) async-start(), calls=%async_computation.7 | async-start | bytes 5308416 | tf_op jit(solution)/shard_map/all_gather | solution.py:385
  9.4 176.4 %all-gather.12.cloned.1.call-start = ((), (), s32[]{:S(2)}) async-start(), calls=%async_computation.8 | async-start | bytes 5308416 | tf_op jit(solution)/shard_map/all_gather | solution.py:387
  10.0 413.9 %reduce-scatter.10.cloned.1.call-start = ((), (), s32[]{:S(2)}) async-start(), calls=%async_computation.10 | async-start | bytes 2654208 | tf_op jit(solution)/shard_map/reduce_scatter | solution.py:470
  48.4 26.4 %copy-start.30 = (bf16[128]{0:T(256)(128)(2,1)}, bf16[128]{0:T(256)(128)(2,1)S(1)}, u32[]{:S(2)}) copy-start(bf16[128]{0:T(256)(128)(2,1)S(1)} %get-tuple-element.131) | copy-start | bytes 772
  48.4 3.1 copy-start.28
  48.4 3.2 copy-start.18
  48.4 5.3 copy-start.25
  50.2 13.3 %copy-start.32 = (bf16[384]{0:T(512)(128)(2,1)S(1)}, bf16[384]{0:T(512)(128)(2,1)}, u32[]{:S(2)}) copy-start(bf16[384]{0:T(512)(128)(2,1)} %param.41) | copy-start | bytes 2308
  50.2 22.9 %copy-start.8 = (bf16[1024,768]{1,0:T(8,128)(2,1)S(1)}, bf16[1024,768]{1,0:T(8,128)(2,1)}, u32[]{:S(2)}) copy-start(bf16[1024,768]{1,0:T(8,128)(2,1)} %param.26) | copy-start | bytes 4718596
  50.7 24.1 %copy-start.14 = (f32[1024]{0:T(1024)}, f32[1024]{0:T(1024)S(1)}, u32[]{:S(2)}) copy-start(f32[1024]{0:T(1024)S(1)} %broadcast_multiply_fusion.1) | copy-start | bytes 12292
  51.4 2.3 copy-start.21
  51.4 29.8 %copy-start.23 = (f32[1024]{0:T(1024)}, f32[1024]{0:T(1024)S(1)}, u32[]{:S(2)}) copy-start(f32[1024]{0:T(1024)S(1)} %fusion.22) | copy-start | bytes 12292
  51.4 29.8 %copy-start.19 = (f32[768]{0:T(1024)}, f32[768]{0:T(1024)S(1)}, u32[]{:S(2)}) copy-start(f32[768]{0:T(1024)S(1)} %convert_element_type.212) | copy-start | bytes 9220
  51.5 29.8 %copy-start.26 = (f32[768]{0:T(1024)}, f32[768]{0:T(1024)S(1)}, u32[]{:S(2)}) copy-start(f32[768]{0:T(1024)S(1)} %convert_element_type.213) | copy-start | bytes 9220
  53.7 27.5 %copy-start.10 = (f32[32,8,128]{2,1,0:T(8,128)}, f32[32,8,128]{2,1,0:T(8,128)S(1)}, u32[]{:S(2)}) copy-start(f32[32,8,128]{2,1,0:T(8,128)S(1)} %constant_dynamic-update-slice_fusion.aw_ref) | copy-start | bytes 393220
  61.4 19.9 %copy-start.16 = (bf16[128,32]{0,1:T(8,128)(2,1)}, bf16[128,32]{0,1:T(8,128)(2,1)S(1)}, u32[]{:S(2)}) copy-start(bf16[128,32]{0,1:T(8,128)(2,1)S(1)} %copy.83) | copy-start | bytes 24580
  145.5 1.8 copy-start.1
  216.0 3.9 copy-start.2
  216.0 4.7 copy-start.6
  220.7 1.4 copy-start.7
  221.5 1.6 copy-start.4
  222.2 2.2 copy-start.33
  223.2 1.2 copy-start.9
  227.3 198.3 %reduce-scatter.8.cloned.1.call-start = ((), (), s32[]{:S(2)}) async-start(), calls=%async_computation.9 | async-start | bytes 7962624 | tf_op jit(solution)/shard_map/reduce_scatter | solution.py:467
  231.7 56.5 %copy-start.15 = (f32[1024]{0:T(1024)S(1)}, f32[1024]{0:T(1024)}, u32[]{:S(2)}) copy-start(f32[1024]{0:T(1024)} %copy-done.14) | copy-start | bytes 12292
  231.7 56.5 %copy-start.20 = (f32[768]{0:T(1024)S(1)}, f32[768]{0:T(1024)}, u32[]{:S(2)}) copy-start(f32[768]{0:T(1024)} %copy-done.19) | copy-start | bytes 9220
  231.7 56.5 %copy-start.24 = (f32[1024]{0:T(1024)S(1)}, f32[1024]{0:T(1024)}, u32[]{:S(2)}) copy-start(f32[1024]{0:T(1024)} %copy-done.23) | copy-start | bytes 12292
  231.7 56.5 %copy-start.27 = (f32[768]{0:T(1024)S(1)}, f32[768]{0:T(1024)}, u32[]{:S(2)}) copy-start(f32[768]{0:T(1024)} %copy-done.26) | copy-start | bytes 9220
  296.9 146.8 %reduce-scatter.12.cloned.1.call-start = ((), (), s32[]{:S(2)}) async-start(), calls=%async_computation.11 | async-start | bytes 10616832 | tf_op jit(solution)/shard_map/reduce_scatter | solution.py:477
  308.0 215.7 %reduce-scatter.14.cloned.1.call-start = ((), (), s32[]{:S(2)}) async-start(), calls=%async_computation.12 | async-start | bytes 10616832 | tf_op jit(solution)/shard_map/reduce_scatter | solution.py:479
  318.6 4.1 copy-start.29
  318.6 241.3 %reduce-scatter.16.cloned.1.call-start = ((), (), s32[]{:S(2)}) async-start(), calls=%async_computation.13 | async-start | bytes 73728
  377.0 6.7 %copy-start.17 = (bf16[128,32]{0,1:T(8,128)(2,1)S(1)}, bf16[128,32]{0,1:T(8,128)(2,1)}, u32[]{:S(2)}) copy-start(bf16[128,32]{0,1:T(8,128)(2,1)} %copy-done.16) | copy-start | bytes 24580
  381.2 5.4 copy-start.22
  383.7 2.9 copy-start
  386.7 3.6 copy-start.5
  390.3 4.2 copy-start.31
  394.4 246.6 %all-reduce.29.cloned.1.call-start = ((), (), s32[]{:S(2)}) async-start(), calls=%async_computation.14 | async-start | bytes 3538944 | tf_op jit(solution)/shard_map/psum | solution.py:486
  425.5 100.3 %copy-start.3 = (f32[1024,768]{0,1:T(8,128)S(1)}, f32[1024,768]{0,1:T(8,128)}, u32[]{:S(2)}) copy-start(f32[1024,768]{0,1:T(8,128)} %copy-done.1) | copy-start | bytes 9437188
  641.1 4.4 copy-start.11
  641.1 5.4 copy-start.12
Sparse Core Ops, SparseCore 0:
  9.9 36.8 all-gather.5
  48.7 24.1 all-gather.7
  74.8 38.9 all-gather.9
  115.5 38.9 all-gather.11
  227.4 42.7 reduce-scatter.9
  297.0 65.5 reduce-scatter.7
  366.1 77.5 reduce-scatter.11
  447.2 76.4 reduce-scatter.13
  526.7 33.1 reduce-scatter.15
  564.3 76.7 all-reduce.28

commit v2 on v1

v2 whole, which is shorter than its diff:
```python
import functools, math
import jax, jax.numpy as jnp
from jax import lax
from jax.experimental import pallas as pl
from jax.experimental.pallas import tpu as pltpu
from jax.sharding import PartitionSpec as P

SET = 256
CH = 32
WIN = 128
GROUPS = ((0, 0, 10), (128, 10, 16), (384, 16, 26), (512, 26, 32))
HW = 24
VM = 60 * 1024 * 1024
root_half_log2e = math.sqrt(0.5 * math.log2(math.e))
f32, bf16 = jnp.float32, jnp.bfloat16
NT = (((1,), (1,)), ((), ()))
TN = (((0,), (0,)), ((), ()))


def dot(a, b, dims=(((1,), (0,)), ((), ()))):
    return lax.dot_general(a, b, dims, preferred_element_type=f32)


def lane_mask(lane0, head, rows):
    lanes = lax.broadcasted_iota(jnp.int32, (rows, 256), 1) + lane0
    return (lanes >= head * HW) & (lanes < (head + 1) * HW)


def spread_heads(block, lane0, h0, h1):
    wide = block.astype(f32)
    zero = jnp.zeros_like(wide)
    return jnp.concatenate(
        [jnp.where(lane_mask(lane0, h, wide.shape[0]), wide, zero).astype(bf16) for h in range(h0, h1)], axis=0
    )


def pick_heads(full, lane0, h0, h1):
    n = h1 - h0
    full = full.reshape(n, CH, 256)
    out = jnp.zeros((CH, 256), f32)
    for j in range(n):
        out = jnp.where(lane_mask(lane0, h0 + j, CH), full[j], out)
    return out


def window_start(i, rows):
    return pl.multiple_of(jnp.clip(i * CH - 48, 0, rows - WIN), 16)


def radius_of(ac, aw):
    d = ac[:, 0:1] - aw[0:1, :]
    s = d * d
    for j in (1, 2):
        d = ac[:, j : j + 1] - aw[j : j + 1, :]
        s = s + d * d
    return jnp.sqrt(s)


def bias_kernel(aw_ref, ac_ref, kp_ref, bmat_ref, b_ref, rho_scr, f_scr):
    ac, aw = ac_ref[...], aw_ref[0]
    rho_scr[...] = radius_of(ac, aw)
    joined = ac[:, 3:4] == aw[3:4, :]
    for p in range(2):
        for kt in range(8):
            ks = slice(16 * kt, 16 * kt + 16)
            A, B, C = kp_ref[0, ks, :], kp_ref[1, ks, :], kp_ref[2, ks, :]
            for r in range(8):
                for gg in range(2):
                    rr = rho_scr[pl.ds(16 * p + 8 * gg + r, 1), :]
                    y = rr * A - B
                    f = jnp.exp2(C - y * y)
                    f_scr[p, r * 128 + 16 * kt : r * 128 + 16 * kt + 16, gg * 128 : gg * 128 + 128] = f.astype(bf16)
    for p in range(2):
        bias = dot(bmat_ref[...], f_scr[p])
        for gg in range(2):
            g = 2 * p + gg
            part = bias[:, gg * 128 : gg * 128 + 128].reshape(32, 8, WIN)
            b_ref[0, :, 8 * g : 8 * g + 8, :] = jnp.where(joined[8 * g : 8 * g + 8][None], part, -1e30)


def fwd_kernel(q_ref, k_ref, v_ref, b_ref, o_ref, p_ref):
    rows = k_ref.shape[0]
    w = window_start(pl.program_id(0), rows)
    kwin = k_ref[pl.ds(w, WIN), :]
    vwin = v_ref[pl.ds(w, WIN), :]
    acc = []
    for lane0, h0, h1 in GROUPS:
        n = h1 - h0
        sl = slice(lane0, lane0 + 256)
        qm = spread_heads(q_ref[:, sl], lane0, h0, h1)
        s = dot(qm, kwin[:, sl], NT).reshape(n, CH, WIN) + b_ref[0, h0:h1]
        e = jnp.exp(s - jnp.max(s, axis=-1, keepdims=True))
        pr = (e * (1.0 / jnp.sum(e, axis=-1, keepdims=True))).reshape(n * CH, WIN).astype(bf16)
        p_ref[0, h0 * CH : h1 * CH, :] = pr
        acc.append(pick_heads(dot(pr, vwin[:, sl]), lane0, h0, h1))
    store_lanes(o_ref, slice(None), acc, 1.0)


def store_lanes(ref, rows, acc, scale):
    for half in range(2):
        a, b = acc[2 * half], acc[2 * half + 1]
        full = jnp.concatenate([a[:, :128], a[:, 128:] + b[:, :128], b[:, 128:]], axis=1)
        if scale != 1.0:
            full = full * scale
        ref[rows, 384 * half : 384 * half + 384] = full.astype(bf16)


def bwd_kernel(q_ref, do_ref, k_ref, v_ref, p_ref, gp_ref, ds_ref, dk_scr, dv_scr, *, scale):
    rows = k_ref.shape[0]
    i = pl.program_id(0)
    w = window_start(i, rows)
    width = 32 * HW

    @pl.when(i == 0)
    def _():
        dk_scr[...] = jnp.zeros_like(dk_scr)
        dv_scr[...] = jnp.zeros_like(dv_scr)

    kwin = k_ref[pl.ds(w, WIN), :]
    vwin = v_ref[pl.ds(w, WIN), :]
    acc = []
    for lane0, h0, h1 in GROUPS:
        n = h1 - h0
        sl = slice(lane0, lane0 + 256)
        qm = spread_heads(q_ref[:, sl], lane0, h0, h1)
        dom = spread_heads(do_ref[:, sl], lane0, h0, h1)
        p_low = p_ref[0, h0 * CH : h1 * CH, :]
        dp = dot(dom, vwin[:, sl], NT)
        pf = p_low.astype(f32)
        pd = pf * dp
        ds = pd - pf * jnp.sum(pd, axis=-1, keepdims=True)
        ds4 = ds.reshape(n, 4, 8, WIN)
        for g in range(4):
            ds_ref[0, g // 2, h0 * 8 : h1 * 8, (g % 2) * 128 : (g % 2) * 128 + 128] = (
                ds4[:, g].reshape(n * 8, WIN).astype(bf16)
            )
        ds_low = ds.astype(bf16)
        acc.append(pick_heads(dot(ds_low, kwin[:, sl]), lane0, h0, h1))
        dk_scr[pl.ds(w, WIN), sl] += dot(ds_low, qm, TN)
        dv_scr[pl.ds(w, WIN), sl] += dot(p_low, dom, TN)
    store_lanes(gp_ref, pl.ds(pl.multiple_of(i * CH, CH), CH), acc, scale)

    @pl.when(i == pl.num_programs(0) - 1)
    def _():
        gp_ref[:, width : 2 * width] = dk_scr[...].astype(bf16)
        gp_ref[:, 2 * width :] = dv_scr[...].astype(bf16)


def feat_kernel(n_before, ds_ref, aw_ref, ac_ref, kp_ref, amat_ref, *rest):
    before, (m0_ref, acc_ref, rho_scr, f_scr, gf_scr) = rest[:n_before], rest[n_before:]
    i = pl.program_id(0)

    @pl.when(i == 0)
    def _():
        m0_ref[...] = before[0][...] if before else jnp.zeros_like(m0_ref)
        acc_ref[...] = before[1][...] if before else jnp.zeros_like(acc_ref)

    rho_scr[...] = radius_of(ac_ref[...], aw_ref[0])
    for p in range(2):
        gf_scr[p] = dot(amat_ref[...], ds_ref[0, p])
    for p in range(2):
        for kt in range(8):
            ks = slice(16 * kt, 16 * kt + 16)
            A, B, C = kp_ref[0, ks, :], kp_ref[1, ks, :], kp_ref[2, ks, :]
            a1 = acc_ref[0, ks, :]
            a2 = acc_ref[1, ks, :]
            for r in range(8):
                for gg in range(2):
                    rr = rho_scr[pl.ds(16 * p + 8 * gg + r, 1), :]
                    at = (p, slice(r * 128 + 16 * kt, r * 128 + 16 * kt + 16), slice(gg * 128, gg * 128 + 128))
                    y = rr * A - B
                    f = jnp.exp2(C - y * y)
                    f_scr[at] = f.astype(bf16)
                    ty = gf_scr[at] * f * y
                    a1 = a1 + ty
                    a2 = a2 + ty * y
            acc_ref[0, ks, :] = a1
            acc_ref[1, ks, :] = a2
        m0_ref[...] += dot(f_scr[p], ds_ref[0, p], NT)


def cost(micros):
    return pl.CostEstimate(flops=int(micros * 1.1535e9), bytes_accessed=0, transcendentals=0)


def full_spec(shape):
    return pl.BlockSpec(shape, lambda i: (0,) * len(shape))


def params(limit=VM):
    return pltpu.CompilerParams(vmem_limit_bytes=limit, dimension_semantics=("arbitrary",))


PARTS = 4


def shifted(spec_shape, base):
    return pl.BlockSpec(spec_shape, lambda i: (i + base,) + (0,) * (len(spec_shape) - 1))


def half_spec(shape, part):
    return pl.BlockSpec(shape, lambda i: (part,) + (0,) * (len(shape) - 1))


def attn_bias(aw, ac, kp, bmat):
    c = aw.shape[0]
    return pl.pallas_call(
        bias_kernel,
        grid=(c,),
        in_specs=[shifted((1, 8, WIN), 0), shifted((CH, 4), 0), full_spec(kp.shape), full_spec(bmat.shape)],
        out_specs=shifted((1, 32, CH, WIN), 0),
        out_shape=jax.ShapeDtypeStruct((c, 32, CH, WIN), f32),
        scratch_shapes=[pltpu.VMEM((CH, WIN), f32), pltpu.VMEM((2, 1024, 256), bf16)],
        compiler_params=params(),
        cost_estimate=cost(30),
        name="attn_bias",
    )(aw, ac, kp, bmat)


def attn_fwd(part, q, k, v, bias, before):
    rows, width = q.shape
    c = rows // CH
    per = c // PARTS
    base = part * per
    kv = half_spec((rows // PARTS, width), part)
    n_in = 4
    return pl.pallas_call(
        functools.partial(skip_refs, fwd_kernel, n_in, len(before)),
        grid=(per,),
        in_specs=[shifted((CH, width), base), kv, kv, shifted((1, 32, CH, WIN), base)]
        + [pl.BlockSpec(memory_space=pl.ANY)] * len(before),
        out_specs=[shifted((CH, width), base), shifted((1, 32 * CH, WIN), base)],
        out_shape=[jax.ShapeDtypeStruct((rows, width), bf16), jax.ShapeDtypeStruct((c, 32 * CH, WIN), bf16)],
        input_output_aliases={n_in + t: t for t in range(len(before))},
        compiler_params=params(),
        cost_estimate=cost(28 // PARTS),
        name="attn_fwd",
    )(q, k, v, bias, *before)


def skip_refs(kernel, n_in, n_before, *refs):
    kernel(*refs[:n_in], *refs[n_in + n_before :])


def attn_bwd(part, q, do, k, v, p, scale, before):
    rows, width = q.shape
    c = rows // CH
    per = c // PARTS
    base = part * per
    kv = half_spec((rows // PARTS, width), part)
    n_in = 5
    return pl.pallas_call(
        functools.partial(skip_refs, functools.partial(bwd_kernel, scale=scale), n_in, len(before)),
        grid=(per,),
        in_specs=[
            shifted((CH, width), base), shifted((CH, width), base), kv, kv,
            shifted((1, 32 * CH, WIN), base),
        ] + [pl.BlockSpec(memory_space=pl.ANY)] * len(before),
        out_specs=[half_spec((rows // PARTS, 3 * width), part), shifted((1, 2, 256, 256), base)],
        out_shape=[jax.ShapeDtypeStruct((rows, 3 * width), bf16), jax.ShapeDtypeStruct((c, 2, 256, 256), bf16)],
        scratch_shapes=[pltpu.VMEM((rows // PARTS, width), f32)] * 2,
        input_output_aliases={n_in + t: t for t in range(len(before))},
        compiler_params=params(),
        cost_estimate=cost(56 // PARTS),
        name="attn_bwd",
    )(q, do, k, v, p, *before)


def attn_feat(part, ds, aw, ac, kp, amat, before):
    per = ds.shape[0] // PARTS
    base = part * per
    n_in = 5
    return pl.pallas_call(
        functools.partial(feat_kernel, len(before)),
        grid=(per,),
        in_specs=[
            shifted((1, 2, 256, 256), base), shifted((1, 8, WIN), base), shifted((CH, 4), base),
            full_spec(kp.shape), full_spec(amat.shape),
        ] + [full_spec(b.shape) for b in before],
        out_specs=[full_spec((1024, 256)), full_spec((2, 128, 128))],
        out_shape=[jax.ShapeDtypeStruct((1024, 256), f32), jax.ShapeDtypeStruct((2, 128, 128), f32)],
        scratch_shapes=[pltpu.VMEM((CH, WIN), f32), pltpu.VMEM((2, 1024, 256), bf16), pltpu.VMEM((2, 1024, 256), f32)],
        compiler_params=params(),
        cost_estimate=cost(42 // PARTS),
        name="attn_feat",
    )(ds, aw, ac, kp, amat, *before)


def aux_of(coords, segment_ids):
    rows = coords.shape[1]
    place = jnp.arange(rows, dtype=jnp.int32) // SET
    key = (segment_ids * (rows // SET) + place).astype(f32)
    packed = jnp.concatenate([coords, key[None], jnp.zeros((4, rows), f32)], axis=0)
    half = rows // PARTS
    starts = [b + min(max(i - 48, 0), half - WIN) for b in range(0, rows, half) for i in range(0, half, CH)]
    aw = jnp.stack([packed[:, s : s + WIN] for s in starts])
    ac = packed[:4].T
    return aw, ac


def kernel_consts(mean, width, kmap):
    mean, width = mean.astype(f32), width.astype(f32)
    a = root_half_log2e / width
    b = mean * a
    c = -jnp.log2(math.sqrt(2 * math.pi) * width)
    kp = jnp.broadcast_to(jnp.stack([a, b, c])[:, :, None], (3, mean.shape[0], 128))
    eye = jnp.eye(8, dtype=bf16)
    heads = kmap.shape[1]
    amat = (eye[:, None, None, :] * kmap[None, :, :, None]).reshape(8 * kmap.shape[0], heads * 8)
    return kp, amat


def feat_finish(m0, acc, width, kmap):
    n, heads = kmap.shape
    m = m0.reshape(8, n, heads, 8)
    g_map = jnp.sum(m * jnp.eye(8, dtype=f32)[:, None, None, :], axis=(0, 3))
    width = width.astype(f32)
    s = jnp.sum(acc, axis=-1)
    a0 = jnp.sum(g_map * kmap.astype(f32), axis=1)
    g_mean = s[0] / (root_half_log2e * width)
    g_width = (s[1] / (root_half_log2e * root_half_log2e) - a0) / width
    return g_map, g_mean, g_width


TILE = 256
epsilon = 1e-05


def ln_parts(v):
    mean = jnp.mean(v, axis=-1, keepdims=True)
    centred = v - mean
    rstd = lax.rsqrt(jnp.mean(centred * centred, axis=-1, keepdims=True) + epsilon)
    return centred * rstd, rstd


def ln_back(xhat, rstd, dn, gain):
    dg = dn * gain
    m1 = jnp.mean(dg, axis=-1, keepdims=True)
    m2 = jnp.mean(dg * xhat, axis=-1, keepdims=True)
    return rstd * (dg - m1 - xhat * m2)


def rows_sum(v):
    return jnp.sum(v, axis=0, keepdims=True)


def fetch(idx_ref, pieces, moves, sem, base=0):
    copies = []
    for m, piece in enumerate(pieces):
        for dest, first, column, rows, columns in moves:
            at = pl.multiple_of(idx_ref[m] * rows, 16)
            copies.append(
                pltpu.make_async_copy(
                    piece.at[pl.ds(first, rows), :],
                    dest.at[pl.ds(at, rows), pl.ds(column, columns)],
                    sem.at[base + len(copies)],
                )
            )
    return copies


def fetch_whole(arrays, dests, sem):
    return [pltpu.make_async_copy(a, d, sem.at[i]) for i, (a, d) in enumerate(zip(arrays, dests))]


def qkv_copies(idx_ref, pieces, w_scr, sem):
    if len(pieces) == 1:
        return fetch_whole(pieces, [w_scr], sem)
    r, columns = pieces[0].shape
    return fetch(idx_ref, pieces, [(w_scr, 0, 0, r, columns)], sem)


def ffn_copies(idx_ref, pieces, wo, up, down, sem):
    if len(pieces) == 3:
        return fetch_whole(pieces, [wo, up, down], sem)
    width = wo.shape[0]
    n = len(pieces) // 2
    r = width // n
    wide = up.shape[1] // width
    moves = [(wo, 0, 0, r, width)] + [(up, r + b * r, b * width, r, width) for b in range(wide)]
    copies = fetch(idx_ref, pieces[:n], moves, sem)
    return copies + fetch(idx_ref, pieces[n:], [(down, 0, 0, wide * r, width)], sem, len(copies))


def any_spec():
    return pl.BlockSpec(memory_space=pl.ANY)


def row_spec(width, tile=TILE):
    return pl.BlockSpec((tile, width), lambda i, *_: (i, 0))


def whole_spec(shape):
    return pl.BlockSpec(shape, lambda i, *_: (0,) * len(shape))


def qkv_kernel(n, scale, idx_ref, x_ref, t_ref, vec_ref, *rest):
    pieces, (normed_ref, q_ref, k_ref, v_ref, w_scr, sem) = rest[:n], rest[n:]
    width = x_ref.shape[1]

    @pl.when(pl.program_id(0) == 0)
    def _():
        for c in qkv_copies(idx_ref, pieces, w_scr, sem):
            c.start()

    start = x_ref[...].astype(f32) + t_ref[...] * vec_ref[0:1, :]
    normed = (ln_parts(start)[0] * vec_ref[1:2, :] + vec_ref[2:3, :]).astype(bf16)
    normed_ref[...] = normed

    @pl.when(pl.program_id(0) == 0)
    def _():
        for c in qkv_copies(idx_ref, pieces, w_scr, sem):
            c.wait()

    q_ref[...] = ((dot(normed, w_scr[:, :width]) + vec_ref[3:4, :]) * scale).astype(bf16)
    k_ref[...] = dot(normed, w_scr[:, width : 2 * width]).astype(bf16)
    v_ref[...] = (dot(normed, w_scr[:, 2 * width :]) + vec_ref[4:5, :]).astype(bf16)


def qkv_forward(idx, x, t, vecs, pieces, scale):
    rows, width = x.shape
    n = len(pieces)
    out = jax.ShapeDtypeStruct((rows, width), bf16)
    return pl.pallas_call(
        functools.partial(qkv_kernel, n, scale),
        grid_spec=pltpu.PrefetchScalarGridSpec(
            num_scalar_prefetch=1,
            grid=(rows // TILE,),
            in_specs=[row_spec(width), row_spec(1), whole_spec(vecs.shape)] + [any_spec()] * n,
            out_specs=[row_spec(width)] * 4,
            scratch_shapes=[pltpu.VMEM((width, 3 * width), bf16), pltpu.SemaphoreType.DMA((n,))],
        ),
        out_shape=[out] * 4,
        compiler_params=params(),
        cost_estimate=cost(10),
        name="qkv_forward",
    )(idx, x, t, vecs, *pieces)


def gelu_parts(x):
    a = jnp.abs(x)
    t = 1.0 / (1.0 + (0.3275911 * math.sqrt(0.5)) * a)
    e = jnp.exp(-0.5 * x * x)
    poly = t * (0.254829592 + t * (-0.284496736 + t * (1.421413741 + t * (-1.453152027 + t * 1.061405429))))
    tail = 0.5 * poly * e
    cdf = jnp.where(x >= 0, 1.0 - tail, tail)
    return x * cdf, cdf + x * e * (1.0 / math.sqrt(2.0 * math.pi))


def split_cores(value, core, owners):
    rows, c = value.shape
    pairs = value.reshape(owners // 2, 2, rows // owners, c)
    even, odd = pairs[:, 0], pairs[:, 1]
    return jnp.where(core == 0, even, odd), jnp.where(core == 0, odd, even)


def ffn_kernel(n, split, steps, idx_ref, x_ref, t_ref, att_ref, cot_ref, vec_ref, upb_ref, *rest):
    pieces = rest[:n]
    (out_ref, ga_ref, gvec_ref, gupb_ref, gm_hbm, keep_hbm, send_hbm,
     wo, up, down, mid, n2, n2t, acc, gn2, hid, gp, stage_up, stage_down, stage_out, sem, out_sem) = rest[n:]
    j = pl.program_id(0)
    rows, width = x_ref.shape
    fc = hid.shape[1]
    tiles = rows // TILE
    core = lax.rem(idx_ref[0], 2)
    r = width // split if split else 0

    def up_copies(step):
        if not split:
            return [pltpu.make_async_copy(stage_up, keep_hbm.at[step], out_sem.at[0])]
        at = pl.ds(pl.multiple_of(step * r, r), r)
        return [
            pltpu.make_async_copy(stage_up.at[s], dest.at[:, at, :], out_sem.at[s])
            for s, dest in enumerate((keep_hbm, send_hbm))
        ]

    def down_copies(step):
        if not split:
            return [pltpu.make_async_copy(stage_down, send_hbm.at[pl.ds(step * fc, fc), :], out_sem.at[2])]
        pairs = fc // (2 * steps * r)
        at = pl.ds(steps * r, steps * r)
        return [
            pltpu.make_async_copy(stage_down.at[s], dest.at[pl.ds(step * pairs, pairs), at, :], out_sem.at[2 + s])
            for s, dest in enumerate((keep_hbm, send_hbm))
        ]

    def out_copies():
        if not split:
            return [pltpu.make_async_copy(stage_out, keep_hbm.at[steps], out_sem.at[4])]
        at = pl.ds(2 * steps * r, r)
        return [
            pltpu.make_async_copy(stage_out.at[s], dest.at[:, at, :], out_sem.at[4 + s])
            for s, dest in enumerate((keep_hbm, send_hbm))
        ]

    def put(stage, value, owners):
        if not split:
            stage[...] = value.astype(bf16)
            return
        keep, send = split_cores(value, core, owners)
        stage[0] = keep.astype(bf16)
        stage[1] = send.astype(bf16)

    @pl.when(j == 0)
    def _():
        copies = ffn_copies(idx_ref, pieces, wo, up, down, sem)
        for c in copies:
            c.start()
        for c in copies:
            c.wait()
        for i in range(tiles):
            rs = pl.ds(i * TILE, TILE)
            start = x_ref[rs, :].astype(f32) + t_ref[rs, :] * vec_ref[0:1, :]
            middle = start + dot(att_ref[rs, :], wo[...]) + vec_ref[1:2, :]
            mid[rs, :] = middle
            normed = (ln_parts(middle)[0] * vec_ref[2:3, :] + vec_ref[3:4, :]).astype(bf16)
            n2[rs, :] = normed
            n2t[:, i * TILE : (i + 1) * TILE] = normed.T

    f0 = pl.multiple_of(j * fc, fc)
    up_c = up[:, pl.ds(f0, fc)]
    down_c = down[pl.ds(f0, fc), :]
    upb = upb_ref[...]
    gb = jnp.zeros((1, fc), f32)
    for i in range(tiles):
        rs = pl.ds(i * TILE, TILE)
        pre = dot(n2[rs, :], up_c) + upb
        gh = dot(cot_ref[rs, :], down_c, NT)
        h, slope = gelu_parts(pre)
        h = h.astype(bf16)
        g = (gh * slope).astype(bf16)
        hid[rs, :] = h
        gp[rs, :] = g
        gb = gb + rows_sum(g.astype(f32))
        o = dot(h, down_c)
        b = dot(g, up_c, NT)

        @pl.when(j == 0)
        def _():
            acc[rs, :] = o
            gn2[rs, :] = b

        @pl.when(j > 0)
        def _():
            acc[rs, :] += o
            gn2[rs, :] += b

    gupb_ref[...] = gb

    @pl.when(j > 0)
    def _():
        for c in up_copies(j - 1) + down_copies(j - 1):
            c.wait()

    put(stage_down, dot(hid[...], cot_ref[...], TN), 2 * (fc // (2 * steps * r)) if split else 0)
    for c in down_copies(j):
        c.start()
    put(stage_up, dot(n2t[...], gp[...]), split)
    for c in up_copies(j):
        c.start()

    @pl.when(j == steps - 1)
    def _():
        sums = [jnp.zeros((1, width), f32)] * 4
        for i in range(tiles):
            rs = pl.ds(i * TILE, TILE)
            middle = mid[rs, :]
            out_ref[rs, :] = (middle + acc[rs, :] + vec_ref[4:5, :]).astype(bf16)
            xhat, rstd = ln_parts(middle)
            dn = gn2[rs, :]
            cot = cot_ref[rs, :].astype(f32)
            gm = cot + ln_back(xhat, rstd, dn, vec_ref[2:3, :])
            mid[rs, :] = gm
            ga = gm.astype(bf16)
            hid[rs, :] = ga
            ga_ref[rs, :] = dot(ga, wo[...], NT).astype(bf16)
            sums = [s + rows_sum(v) for s, v in zip(sums, (dn * xhat, dn, cot, ga.astype(f32)))]
        gvec_ref[...] = jnp.concatenate(sums + [jnp.zeros((4, width), f32)], axis=0)
        mid_copy = pltpu.make_async_copy(mid, gm_hbm, out_sem.at[6])
        mid_copy.start()
        put(stage_out, dot(att_ref[...], hid[...], TN), split)
        last = out_copies()
        for c in last:
            c.start()
        for c in last + up_copies(j) + down_copies(j):
            c.wait()
        mid_copy.wait()


def ffn_both(idx, x, t, att, cot, vecs, upb, pieces, ff, split):
    rows, width = x.shape
    n = len(pieces)
    fc = width
    steps = ff // fc
    sd = jax.ShapeDtypeStruct
    V = pltpu.VMEM
    if split:
        half = split // 2
        r = width // split
        grads = [sd((half, (2 * steps + 1) * r, width), bf16)] * 2
        stages = [V((2, half, r, width), bf16), V((2, fc // (2 * steps * r), steps * r, width), bf16), V((2, half, r, width), bf16)]
    else:
        grads = [sd((steps + 1, width, width), bf16), sd((ff, width), bf16)]
        stages = [V((width, width), bf16)] * 3
    return pl.pallas_call(
        functools.partial(ffn_kernel, n, split, steps),
        grid_spec=pltpu.PrefetchScalarGridSpec(
            num_scalar_prefetch=1,
            grid=(steps,),
            in_specs=[whole_spec((rows, width)), whole_spec((rows, 1)), whole_spec((rows, width)), whole_spec((rows, width)),
                      whole_spec(vecs.shape), pl.BlockSpec((1, fc), lambda j, *_: (0, j))] + [any_spec()] * n,
            out_specs=[whole_spec((rows, width)), whole_spec((rows, width)), whole_spec((8, width)),
                       pl.BlockSpec((1, fc), lambda j, *_: (0, j)), any_spec(), any_spec(), any_spec()],
            scratch_shapes=[V((width, width), bf16), V((width, ff), bf16), V((ff, width), bf16),
                            V((rows, width), f32), V((rows, width), bf16), V((width, rows), bf16),
                            V((rows, width), f32), V((rows, width), f32),
                            V((rows, fc), bf16), V((rows, fc), bf16), *stages,
                            pltpu.SemaphoreType.DMA((6 * n,)), pltpu.SemaphoreType.DMA((7,))],
        ),
        out_shape=[sd((rows, width), bf16), sd((rows, width), bf16), sd((8, width), f32), sd((1, ff), f32),
                   sd((rows, width), f32), *grads],
        compiler_params=params(),
        cost_estimate=cost(60),
        name="ffn_both",
    )(idx, x, t, att, cot, vecs, upb, *pieces)


def gqkv_kernel(split, idx_ref, normed_ref, gp_ref, *rest):
    outs, nt = rest[:-1], rest[-1]

    @pl.when(pl.program_id(0) == 0)
    def _():
        nt[...] = normed_ref[...].T

    grad = dot(nt[...], gp_ref[...])
    if split:
        keep, send = split_cores(grad, lax.rem(idx_ref[0], 2), split)
        outs[0][...] = keep.astype(bf16)
        outs[1][...] = send.astype(bf16)
    else:
        outs[0][0] = grad.astype(bf16)


def qkv_weight_grad(idx, normed, gp, split):
    rows, width = normed.shape
    sd = jax.ShapeDtypeStruct
    if split:
        half, r = split // 2, width // split
        out_specs = [pl.BlockSpec((half, r, width), lambda j, *_: (0, j, 0))] * 2
        out_shape = [sd((half, 3 * r, width), bf16)] * 2
    else:
        out_specs = [pl.BlockSpec((1, width, width), lambda j, *_: (j, 0, 0))]
        out_shape = [sd((3, width, width), bf16)]
    return pl.pallas_call(
        functools.partial(gqkv_kernel, split),
        grid_spec=pltpu.PrefetchScalarGridSpec(
            num_scalar_prefetch=1,
            grid=(3,),
            in_specs=[whole_spec((rows, width)), pl.BlockSpec((rows, width), lambda j, *_: (0, j))],
            out_specs=out_specs,
            scratch_shapes=[pltpu.VMEM((width, rows), bf16)],
        ),
        out_shape=out_shape,
        compiler_params=params(),
        cost_estimate=cost(8),
        name="qkv_weight_grad",
    )(idx, normed, gp)


def first_kernel(n, idx_ref, x_ref, t_ref, gm_ref, gp_ref, vec_ref, *rest):
    pieces, (gi_ref, gvec_ref, w_scr, sem) = rest[:n], rest[n:]
    i = pl.program_id(0)
    width = x_ref.shape[1]

    @pl.when(i == 0)
    def _():
        for c in qkv_copies(idx_ref, pieces, w_scr, sem):
            c.start()
        gvec_ref[...] = jnp.zeros_like(gvec_ref)
        for c in qkv_copies(idx_ref, pieces, w_scr, sem):
            c.wait()

    t = t_ref[...]
    dn = dot(gp_ref[...], w_scr[...], NT)
    start = x_ref[...].astype(f32) + t * vec_ref[0:1, :]
    xhat, rstd = ln_parts(start)
    gs = gm_ref[...] + ln_back(xhat, rstd, dn, vec_ref[1:2, :])
    gi_ref[...] = gs.astype(bf16)
    parts = [t * gs, dn * xhat, dn, gp_ref[:, :width].astype(f32), gp_ref[:, 2 * width :].astype(f32)]
    gvec_ref[...] += jnp.concatenate([rows_sum(v) for v in parts] + [jnp.zeros((3, width), f32)], axis=0)


def first_backward(idx, x, t, gm, gp, vecs, pieces):
    rows, width = x.shape
    n = len(pieces)
    sd = jax.ShapeDtypeStruct
    return pl.pallas_call(
        functools.partial(first_kernel, n),
        grid_spec=pltpu.PrefetchScalarGridSpec(
            num_scalar_prefetch=1,
            grid=(rows // TILE,),
            in_specs=[row_spec(width), row_spec(1), row_spec(width), row_spec(3 * width), whole_spec(vecs.shape)] + [any_spec()] * n,
            out_specs=[row_spec(width), whole_spec((8, width))],
            scratch_shapes=[pltpu.VMEM((width, 3 * width), bf16), pltpu.SemaphoreType.DMA((n,))],
        ),
        out_shape=[sd((rows, width), bf16), sd((8, width), f32)],
        compiler_params=params(),
        cost_estimate=cost(11),
        name="first_backward",
    )(idx, x, t, gm, gp, vecs, *pieces)


SHARDS = 8


def swap(value, axis, size, bit_mask):
    return lax.ppermute(value, axis, [(i, i ^ bit_mask) for i in range(size)])


def near(value):
    return swap(value, "fsdp", SHARDS, 1)


def along_x(value):
    return swap(value, "fsdp", SHARDS, 2)


def along_y(value):
    return swap(value, "fsdp", SHARDS, 4)


def with_near(far):
    pieces = []
    for piece in far:
        pieces += [piece, near(piece)]
    return pieces


def in_order(pieces, order):
    stacked = jnp.stack(pieces).astype(f32)
    hit = (jnp.arange(len(pieces))[:, None] == order[None, :]).astype(f32)
    return jnp.sum(hit.reshape(hit.shape + (1,) * (stacked.ndim - 1)) * stacked[None], axis=1)


def blocks_of(weight, width):
    r = weight.shape[0]
    return jnp.transpose(weight.reshape(r, -1, width), (1, 0, 2)).reshape(-1, width)


def far_first(kept, came, spot):
    place = spot // 2
    cut = kept.shape[1] // 32 * 16

    def total(mask, rows):
        pick = lambda v: lax.dynamic_index_in_dim(v, place ^ mask, 0, keepdims=False)[rows].astype(f32)
        return (pick(kept) + pick(came)).astype(kept.dtype)

    top, low = slice(None, cut), slice(cut, None)
    stay = (total(0, top), total(2, top), total(0, low), total(1, low))
    go_x = jnp.stack([total(1, top), total(3, top)])
    go_y = jnp.stack([total(2, low), total(3, low)])
    return stay, go_x, go_y


def add_low(a, b):
    return (a.astype(f32) + b.astype(f32)).astype(a.dtype)


def far_second(stay, from_x, from_y):
    own_top, y_top, own_low, x_low = stay
    return (add_low(own_top, from_x[0]), add_low(own_low, from_y[0])), add_low(y_top, from_x[1]), add_low(x_low, from_y[1])


def far_third(own, from_y, from_x):
    return jnp.concatenate([add_low(own[0], from_y), add_low(own[1], from_x)])


def halves(owned, spot):
    parts = owned.reshape(2, owned.shape[0] // 2, owned.shape[1])
    side = spot % 2
    return (
        lax.dynamic_index_in_dim(parts, side, 0, keepdims=False),
        lax.dynamic_index_in_dim(parts, 1 - side, 0, keepdims=False),
    )


def rows_first(kept, sent, size):
    return add_low(kept, swap(sent, "dp", size, 1))


def rows_middle(half, size):
    step = 2
    while step < size:
        half = add_low(half, swap(half, "dp", size, step))
        step *= 2
    return half


def rows_last(half, size, spot):
    other = swap(half, "dp", size, 1)
    even = spot % 2 == 0
    return jnp.concatenate([jnp.where(even, half, other), jnp.where(even, other, half)]).astype(f32)


def on_device(
    sizes,
    inputs,
    time_of_row,
    coords,
    segment_ids,
    cotangent,
    time_weight,
    ln1_gain,
    ln1_bias,
    w_qkv,
    q_bias,
    v_bias,
    w_out,
    out_bias,
    kernel_mean,
    kernel_width,
    kernel_map,
    ln2_gain,
    ln2_bias,
    w_up,
    up_bias,
    w_down,
    down_bias,
):
    n, planes = sizes
    direct = n == SHARDS
    split = n if direct else 0
    barrier = lax.optimization_barrier
    spot = lax.axis_index("fsdp")
    level = lax.axis_index("dp")
    order = (spot ^ jnp.arange(n)).astype(jnp.int32)
    width = inputs.shape[1]
    r = w_qkv.shape[0]
    heads = kernel_map.shape[1]
    own_kernels = kernel_map.shape[0]
    kernels = own_kernels * n
    wide = up_bias.shape[0] // r
    ff = n * wide * r
    scale = (width // heads) ** (-0.5)
    times = time_of_row[:, None]

    flat = jnp.concatenate([kernel_map.reshape(-1), kernel_mean, kernel_width])
    kernel_rows = -(-flat.shape[0] // r)
    flat = jnp.pad(flat, (0, kernel_rows * r - flat.shape[0])).reshape(kernel_rows, r)
    vectors = (time_weight, ln1_gain, ln1_bias, q_bias, v_bias, out_bias, ln2_gain, ln2_bias, down_bias)
    small = jnp.concatenate([jnp.stack(vectors), up_bias.reshape(wide, r), flat])
    if direct:
        small_all = [small] + [swap(small, "fsdp", n, m) for m in range(1, n)]
        qkv_far = [w_qkv] + [swap(w_qkv, "fsdp", n, 2 * m) for m in range(1, n // 2)]
        top = jnp.concatenate([w_out, blocks_of(w_up, width)])
        small_all = in_order(small_all, order)
    else:
        small_all = lax.all_gather(small, "fsdp", axis=0).astype(f32)
        qkv_p = (lax.all_gather(w_qkv, "fsdp", axis=0, tiled=True),)
        ffn_p = tuple(lax.all_gather(w, "fsdp", axis=0, tiled=True) for w in (w_out, w_up, w_down))
    vecs = jnp.transpose(small_all[:, :9], (1, 0, 2)).reshape(9, width)
    up_bias_all = small_all[:, 9 : 9 + wide].reshape(1, ff)
    tail = small_all[:, 9 + wide :].reshape(n, kernel_rows * r)
    map_size = own_kernels * heads
    map_all = tail[:, :map_size].reshape(kernels, heads).astype(bf16)
    mean_all = tail[:, map_size : map_size + own_kernels].reshape(kernels)
    width_all = tail[:, map_size + own_kernels : map_size + 2 * own_kernels].reshape(kernels)

    def rows_of(*picked):
        return jnp.concatenate([vecs[p : p + 1] for p in picked] + [jnp.zeros((8 - len(picked), width), f32)])

    aux_win, aux_col = aux_of(coords, segment_ids)
    consts, spread_map = kernel_consts(mean_all, width_all, map_all)
    bias = attn_bias(aux_win, aux_col, consts, spread_map.T)

    if direct:
        bias, qkv_far, top, bottom = barrier((bias, qkv_far, top, w_down))
        top_x, top_y, low_x, low_y = along_x(top), along_y(top), along_x(bottom), along_y(bottom)
        qkv_p = tuple(with_near(qkv_far))
    normed, queries, keys, values = qkv_forward(order, inputs, times, rows_of(0, 1, 2, 3, 4), qkv_p, scale)
    done = attn_fwd(0, queries, keys, values, bias, ())
    done = attn_fwd(1, queries, keys, values, bias, done)
    if direct:
        done, top_x, top_y, low_x, low_y = barrier((done, top_x, top_y, low_x, low_y))
        top_d, low_d = along_y(top_x), along_x(low_y)
    done = attn_fwd(2, queries, keys, values, bias, done)
    if direct:
        done, top_d, low_d = barrier((done, top_d, low_d))
        ffn_p = tuple(with_near((top, top_x, top_y, top_d)) + with_near((bottom, low_x, low_y, low_d)))
    attended, probs = attn_fwd(3, queries, keys, values, bias, done)

    output, grad_attended, ffn_vecs, grad_up_bias, grad_middle, ffn_keep, ffn_send = ffn_both(
        order, inputs, times, attended, cotangent, rows_of(0, 5, 6, 7, 8), up_bias_all, ffn_p, ff, split
    )

    def backward(part, before):
        return attn_bwd(part, queries, grad_attended, keys, values, probs, scale, before)

    def feat(part, before):
        return attn_feat(part, grad_scores, aux_win, aux_col, consts, spread_map, before)

    def by_owner(array, blocks):
        return array.reshape(blocks, n, -1, width)

    def scattered(array, blocks):
        owned = lax.psum_scatter(by_owner(array, blocks), "fsdp", scatter_dimension=1)
        return owned.reshape(-1, width)

    if direct:
        ffn_came = near(ffn_send)
        done = backward(0, ())
        stay, go_x, go_y = far_first(ffn_keep, ffn_came, spot)
        done, stay, go_x, go_y = barrier((done, stay, go_x, go_y))
        from_x, from_y = along_x(go_x), along_y(go_y)
        done = backward(2, backward(1, done))
        own, go_y, go_x = far_second(stay, from_x, from_y)
        done, own, go_y, go_x = barrier((done, own, go_y, go_x))
        from_y, from_x = along_y(go_y), along_x(go_x)
        grad_projected, grad_scores = backward(3, done)
        ffn_z = halves(far_third(own, from_y, from_x), level)
        grad_projected, ffn_z = barrier((grad_projected, ffn_z))
        ffn_z = rows_first(*ffn_z, planes)
        qkv_keep, qkv_send = qkv_weight_grad(order, normed, grad_projected, split)
        stay, go_x, go_y = far_first(qkv_keep, near(qkv_send), spot)
        grad_projected, stay, go_x, go_y = barrier((grad_projected, stay, go_x, go_y))
        from_x, from_y = along_x(go_x), along_y(go_y)
    else:
        done = backward(2, backward(1, backward(0, ())))
        grad_projected, grad_scores = backward(3, done)
        ffn_owned = jnp.concatenate([scattered(ffn_keep[:wide], wide), scattered(ffn_send, 1), scattered(ffn_keep[wide:], 1)])
        ffn_z = rows_first(*halves(ffn_owned, level), planes)
        qkv_owned = scattered(qkv_weight_grad(order, normed, grad_projected, split)[0], 3)
    grad_inputs, first_vecs = first_backward(
        order, inputs, times, grad_middle, grad_projected, rows_of(0, 1), qkv_p
    )
    if direct:
        own, go_y, go_x = far_second(stay, from_x, from_y)
        grad_scores, first_vecs, ffn_z, own, go_y, go_x = barrier((grad_scores, first_vecs, ffn_z, own, go_y, go_x))
        from_y, from_x = along_y(go_y), along_x(go_x)
    ffn_z = rows_middle(ffn_z, planes)
    sums = feat(0, ())
    if direct:
        qkv_owned = far_third(own, from_y, from_x)
    sums, qkv_z = barrier((sums, halves(qkv_owned, level)))
    qkv_z = rows_first(*qkv_z, planes)
    sums = feat(1, sums)
    sums, ffn_z, qkv_z = barrier((sums, ffn_z, qkv_z))
    ffn_owned = rows_last(ffn_z, planes, level)
    qkv_z = rows_middle(qkv_z, planes)
    sums = feat(2, sums)
    sums, qkv_z, ffn_owned = barrier((sums, qkv_z, ffn_owned))
    qkv_owned = rows_last(qkv_z, planes, level)
    grad_map, grad_mean, grad_width = feat_finish(*feat(3, sums), width_all, map_all)

    grad_rows = [first_vecs[:5], ffn_vecs[3:4], ffn_vecs[:3]]
    flat = jnp.concatenate(
        [grad_map.reshape(n, map_size), grad_mean.reshape(n, own_kernels), grad_width.reshape(n, own_kernels)], axis=1
    )
    flat = jnp.pad(flat, ((0, 0), (0, kernel_rows * r - flat.shape[1]))).reshape(n, kernel_rows, r)
    vector_rows = jnp.transpose(jnp.concatenate(grad_rows).reshape(9, n, r), (1, 0, 2))
    packed = jnp.concatenate([vector_rows, grad_up_bias.reshape(n, wide, r), flat], axis=1)
    if direct:
        total = lax.dynamic_index_in_dim(packed, spot, 0, keepdims=False)
        for m in range(1, n):
            total = total + swap(lax.dynamic_index_in_dim(packed, spot ^ m, 0, keepdims=False), "fsdp", n, m)
    else:
        total = lax.psum_scatter(packed, "fsdp", scatter_dimension=0)
    step = 1
    while step < planes:
        total = total + swap(total, "dp", planes, step)
        step *= 2
    tail = total[9 + wide :].reshape(-1)
    up_rows = wide * r
    grad_up, grad_down, grad_out = ffn_owned[:up_rows], ffn_owned[up_rows : 2 * up_rows], ffn_owned[2 * up_rows :]

    def columns(array):
        return jnp.transpose(array.reshape(-1, r, width), (1, 0, 2)).reshape(r, -1)

    return (
        output,
        grad_inputs,
        total[0],
        total[1],
        total[2],
        columns(qkv_owned),
        total[3],
        total[4],
        grad_out,
        total[5],
        tail[map_size : map_size + own_kernels],
        tail[map_size + own_kernels : map_size + 2 * own_kernels],
        tail[:map_size].reshape(own_kernels, heads),
        total[6],
        total[7],
        columns(grad_up),
        total[9 : 9 + wide].reshape(up_rows),
        grad_down,
        total[8],
    )


def solution(mesh):
    rows, split, whole = P(("fsdp", "dp"), None), P("fsdp"), P("fsdp", None)
    placed = (
        rows,
        P(("fsdp", "dp")),
        P(None, ("fsdp", "dp")),
        P(("fsdp", "dp")),
        rows,
        split,
        split,
        split,
        whole,
        split,
        split,
        whole,
        split,
        split,
        split,
        whole,
        split,
        split,
        whole,
        split,
        whole,
        split,
    )
    out_placed = (
        rows,
        rows,
        split,
        split,
        split,
        whole,
        split,
        split,
        whole,
        split,
        split,
        split,
        whole,
        split,
        split,
        whole,
        split,
        whole,
        split,
    )
    return jax.shard_map(
        functools.partial(on_device, (mesh.shape["fsdp"], mesh.shape["dp"])),
        mesh=mesh,
        in_specs=placed,
        out_specs=out_placed,
        check_vma=False,
    )
```

time: 660 us -> 424 us (0.64)
  waiting for transfers between devices: 173 us -> 35.6 us
  Pallas kernels: 154 us -> 288 us
  matrix products: 131 us -> 0 us
  blocking collectives: 88.8 us -> 0 us
  starting transfers between devices: 0.4 us -> 47.6 us
  other arithmetic: 43.2 us -> 21.6 us
  local copies, waits for them, and re-layouts: 45.6 us -> 26.5 us
  between operations: 18.5 us -> 1.68 us
    pallas_call x3 -> x17, Pallas kernels: 154 us -> 288 us  [the longest x1 71 us: ffn_both(): pl.pallas_call(functools.partial(ffn_kernel, n, split, steps), grid_spec=...]
    dot_general x12 -> x0, matrix products: 131 us -> none  [the longest x4 40.2 us: times_transpose(): lax.dot_general(left, right, (((1,), (1,)), ((), ())), preferred_element_...]
    reduce_scatter x4 -> x0, waiting for transfers between devices: 93.9 us -> none  [the longest x1 77.9 us: on_device(): lax.psum_scatter(grad_w_down, 'fsdp', scatter_dimension=0, tiled=True)]
    psum x1 -> x0, waiting for transfers between devices: 54.2 us -> none  [on_device(): lax.psum(owned[3].astype(jnp.bfloat16), 'dp').astype(jnp.float32)]
    unnamed x2 -> x0, blocking collectives: 52.4 us -> none
    ppermute x0 -> x53, starting transfers between devices: none -> 47.6 us  [swap(): return lax.ppermute(value, axis, [(i, i ^ bit_mask) for i in range(size)])]
    ppermute x0 -> x53, waiting for transfers between devices: none -> 35.6 us  [swap(): return lax.ppermute(value, axis, [(i, i ^ bit_mask) for i in range(size)])]
    unnamed x143 -> x93, local copies, waits for them, and re-layouts: 30 us -> 3.28 us
  transfers between devices with their start and end apart: 10 -> 53, of which waited for: 4 -> 13; matrix products, arithmetic and copies ran while one was open for 26% -> 6% of each run, Pallas kernels for 24% -> 47%
where the time goes in v2:
time: 424 us; the launch traced here: 421 us
  Pallas kernels  288 us (68%)
  starting transfers between devices  47.6 us (11%)
  waiting for transfers between devices  35.6 us (8%)
  local copies, waits for them, and re-layouts  26.5 us (6%)
  other arithmetic  21.6 us (5%)
    pallas_call x1, Pallas kernels, ffn_both(): pl.pallas_call(functools.partial(ffn_kernel, n, split, steps), grid_spec=...  71 us
    pallas_call x4, Pallas kernels, attn_bwd(): pl.pallas_call(functools.partial(skip_refs, functools.partial(bwd_kernel,...  61.4 us
    pallas_call x4, Pallas kernels, attn_feat(): pl.pallas_call(functools.partial(feat_kernel, len(before)), grid=(per,),...  49.5 us
    ppermute x53, starting transfers between devices, swap(): return lax.ppermute(value, axis, [(i, i ^ bit_mask) for i in range(size)])  47.6 us
    pallas_call x4, Pallas kernels, attn_fwd(): pl.pallas_call(functools.partial(skip_refs, fwd_kernel, n_in, len(before)...  44.6 us
    ppermute x53, waiting for transfers between devices, swap(): return lax.ppermute(value, axis, [(i, i ^ bit_mask) for i in range(size)])  35.6 us
    pallas_call x1, Pallas kernels, attn_bias(): pl.pallas_call(bias_kernel, grid=(c,), in_specs=[shifted((1, 8, WIN), 0),...  31.1 us
    pallas_call x1, Pallas kernels, first_backward(): pl.pallas_call(functools.partial(first_kernel, n), grid_spec=pltpu.Prefet...  11.8 us
  transfers between devices with their start and end apart: 53, of which 13 were waited for; matrix products, arithmetic and copies ran while one was open for 6% of the time, Pallas kernels for 47%

profile of v2, /device:TPU:0, one launch (start us, length us, event | category | flops | bytes accessed | tf_op | source)
XLA Modules:
  0.0 421.4 jit_solution(16433546427075240868)
XLA Ops:
  3.1 1.6 concatenate.50
  5.2 2.6 collective-permute-start.1
  7.8 1.8 collective-permute-start.3
  12.4 1.1 copy.355
  13.6 2.7 collective-permute-start.5
  16.5 1.0 copy.312
  17.6 1.7 collective-permute-start.7
  19.3 1.6 collective-permute-start.8
  24.3 31.1 %attn_bias.1.refs_3_ = f32[32,32,32,128]{3,2,1,0:T(8,128)} custom-call(f32[32,8,128]{2,1,0:T(8,128)} %copy-done.18, f32[1024,4]{1,0:T(8,128)} %bitcast.304, f32[3,128,128]{2,1,0:T(8,128)} %broadcast_in_dim.13.kp_ref, bf16[256,1024]{1,0:T(8,128)(2,1)} %bitcast.297), custom_call_target="tpu_custom_call" | custom-call | flops 34604998656 | tf_op jit(solution)/shard_map/attn_bias/pallas_call | solution.py:207
  56.5 1.0 copy.316.t_ref
  60.4 1.6 collective-permute-start.14
  62.0 1.5 collective-permute-start.15
  64.5 10.2 %qkv_forward.1 = (bf16[1024,768]{1,0:T(8,128)(2,1)}, bf16[1024,768]{1,0:T(8,128)(2,1)}, bf16[1024,768]{1,0:T(8,128)(2,1)}, bf16[1024,768]{1,0:T(8,128)(2,1)}) custom-call(s32[8]{0:T(128)} %copy-done.17, bf16[1024,768]{1,0:T(8,128)(2,1)} %x_ref.5, f32[1024,1]{1,0:T(8,128)} %copy.316.t_ref, f32[8,768]{1,0:T(8,128)} %concatenate.51.vec_ref, ...), custom_call_target="tpu_custom_call" | custom-call | flops 11534999552 | tf_op jit(solution)/shard_map/qkv_forward/pallas_call | solution.py:424
  74.7 11.2 %attn_fwd.4 = (bf16[1024,768]{1,0:T(8,128)(2,1)}, bf16[32,1024,128]{2,1,0:T(8,128)(2,1)}) custom-call(bf16[1024,768]{1,0:T(8,128)(2,1)} %get-tuple-element.122.refs_0_, bf16[1024,768]{1,0:T(8,128)(2,1)} %get-tuple-element.123.refs_1_.refs_2_, bf16[1024,768]{1,0:T(8,128)(2,1)} %get-tuple-element.124.refs_2_.refs_3_, f32[32,32,32,128]{3,2,1,0:T(8,128)} %attn_bias.1.refs_3_), custom_call_target="tpu_custom_call" | custom-call | flops 8074500096 | tf_op jit(solution)/shard_map/attn_fwd/pallas_call | solution.py:227
  85.9 11.1 %attn_fwd.5 = (bf16[1024,768]{1,0:T(8,128)(2,1)}, bf16[32,1024,128]{2,1,0:T(8,128)(2,1)}) custom-call(bf16[1024,768]{1,0:T(8,128)(2,1)} %get-tuple-element.122.refs_0_, bf16[1024,768]{1,0:T(8,128)(2,1)} %get-tuple-element.123.refs_1_.refs_2_, bf16[1024,768]{1,0:T(8,128)(2,1)} %get-tuple-element.124.refs_2_.refs_3_, ...), custom_call_target="tpu_custom_call", output_to_operand_aliasing={{0}: (4, {}), {1}: (5, {})} | custom-call | flops 8074500096 | tf_op jit(solution)/shard_map/attn_fwd/pallas_call | solution.py:227
  97.6 1.7 collective-permute-start.18
  99.3 1.5 collective-permute-start.19
  100.8 11.2 %attn_fwd.6 = (bf16[1024,768]{1,0:T(8,128)(2,1)}, bf16[32,1024,128]{2,1,0:T(8,128)(2,1)}) custom-call(bf16[1024,768]{1,0:T(8,128)(2,1)} %get-tuple-element.122.refs_0_, bf16[1024,768]{1,0:T(8,128)(2,1)} %get-tuple-element.123.refs_1_.refs_2_, bf16[1024,768]{1,0:T(8,128)(2,1)} %get-tuple-element.124.refs_2_.refs_3_, ...), custom_call_target="tpu_custom_call", output_to_operand_aliasing={{0}: (4, {}), {1}: (5, {})} | custom-call | flops 8074500096 | tf_op jit(solution)/shard_map/attn_fwd/pallas_call | solution.py:227
  112.0 2.7 collective-permute-done.19.rest_14_
  114.7 1.6 collective-permute-done.18.rest_6_
  117.3 11.1 %attn_fwd.7 = (bf16[1024,768]{1,0:T(8,128)(2,1)}, bf16[32,1024,128]{2,1,0:T(8,128)(2,1)}) custom-call(bf16[1024,768]{1,0:T(8,128)(2,1)} %get-tuple-element.122.refs_0_, bf16[1024,768]{1,0:T(8,128)(2,1)} %get-tuple-element.123.refs_1_.refs_2_, bf16[1024,768]{1,0:T(8,128)(2,1)} %get-tuple-element.124.refs_2_.refs_3_, ...), custom_call_target="tpu_custom_call", output_to_operand_aliasing={{0}: (4, {}), {1}: (5, {})} | custom-call | flops 8074500096 | tf_op jit(solution)/shard_map/attn_fwd/pallas_call | solution.py:227
  129.5 71.0 %ffn_both.1 = (bf16[1024,768]{1,0:T(8,128)(2,1)}, bf16[1024,768]{1,0:T(8,128)(2,1)}, f32[8,768]{1,0:T(8,128)}, f32[1,3072]{1,0:T(1,128)}, f32[1024,768]{1,0:T(8,...) custom-call(s32[8]{0:T(128)} %copy-done.17, bf16[1024,768]{1,0:T(8,128)(2,1)} %x_ref.5, ...), custom_call_target="tpu_custom_call" | custom-call | flops 69209997312 | tf_op jit(solution)/shard_map/ffn_both/pallas_call | solution.py:605
  200.7 15.3 %attn_bwd.4 = (bf16[1024,2304]{1,0:T(8,128)(2,1)}, bf16[32,2,256,256]{3,2,1,0:T(8,128)(2,1)}) custom-call(bf16[1024,768]{1,0:T(8,128)(2,1)} %get-tuple-element.122.refs_0_, bf16[1024,768]{1,0:T(8,128)(2,1)} %get-tuple-element.147.refs_1_, bf16[1024,768]{1,0:T(8,128)(2,1)} %get-tuple-element.123.refs_1_.refs_2_, ...), custom_call_target="tpu_custom_call" | custom-call | flops 16149000192 | tf_op jit(solution)/shard_map/attn_bwd/pallas_call | solution.py:252
  216.1 5.2 %add_convert_fusion.5 = (bf16[1,432,768]{2,1,0:T(8,128)(2,1)S(1)}, bf16[1,432,768]{2,1,0:T(8,128)(2,1)S(1)}, bf16[432,768]{1,0:T(8,128)(2,1)S(1)}, bf16[432,768]...) fusion(bf16[4,864,768]{2,1,0:T(8,128)(2,1)} %collective-permute, ...), kind=kLoop, calls=%fused_computation.17 | loop fusion | flops 10616832 | bytes 15925268 | tf_op jit(solution)/shard_map/convert_element_type | solution.py:756
  221.3 1.3 pad_maximum_fusion
  222.6 1.7 collective-permute-start.30
  224.3 1.5 collective-permute-start.29
  225.8 15.3 %attn_bwd.5 = (bf16[1024,2304]{1,0:T(8,128)(2,1)}, bf16[32,2,256,256]{3,2,1,0:T(8,128)(2,1)}) custom-call(bf16[1024,768]{1,0:T(8,128)(2,1)} %get-tuple-element.122.refs_0_, bf16[1024,768]{1,0:T(8,128)(2,1)} %get-tuple-element.147.refs_1_, bf16[1024,768]{1,0:T(8,128)(2,1)} %get-tuple-element.123.refs_1_.refs_2_, ...), custom_call_target="tpu_custom_call", output_to_operand_aliasing={{0}: (5, {}), {1}: (6, {})} | custom-call | flops 16149000192 | tf_op jit(solution)/shard_map/attn_bwd/pallas_call | solution.py:252
  241.1 15.3 %attn_bwd.6 = (bf16[1024,2304]{1,0:T(8,128)(2,1)}, bf16[32,2,256,256]{3,2,1,0:T(8,128)(2,1)}) custom-call(bf16[1024,768]{1,0:T(8,128)(2,1)} %get-tuple-element.122.refs_0_, bf16[1024,768]{1,0:T(8,128)(2,1)} %get-tuple-element.147.refs_1_, bf16[1024,768]{1,0:T(8,128)(2,1)} %get-tuple-element.123.refs_1_.refs_2_, ...), custom_call_target="tpu_custom_call", output_to_operand_aliasing={{0}: (5, {}), {1}: (6, {})} | custom-call | flops 16149000192 | tf_op jit(solution)/shard_map/attn_bwd/pallas_call | solution.py:252
  256.4 1.6 fusion
  258.1 1.6 fusion.1
  260.8 15.3 %attn_bwd.7 = (bf16[1024,2304]{1,0:T(8,128)(2,1)}, bf16[32,2,256,256]{3,2,1,0:T(8,128)(2,1)}) custom-call(bf16[1024,768]{1,0:T(8,128)(2,1)} %get-tuple-element.122.refs_0_, bf16[1024,768]{1,0:T(8,128)(2,1)} %get-tuple-element.147.refs_1_, bf16[1024,768]{1,0:T(8,128)(2,1)} %get-tuple-element.123.refs_1_.refs_2_, ...), custom_call_target="tpu_custom_call", output_to_operand_aliasing={{0}: (5, {}), {1}: (6, {})} | custom-call | flops 16149000192 | tf_op jit(solution)/shard_map/attn_bwd/pallas_call | solution.py:252
  277.9 8.9 %qkv_weight_grad.1 = (bf16[4,288,768]{2,1,0:T(8,128)(2,1)}, bf16[4,288,768]{2,1,0:T(8,128)(2,1)}) custom-call(s32[8]{0:T(128)} %copy-done.17, bf16[1024,768]{1,0:T(8,128)(2,1)} %get-tuple-element.173.normed_ref, bf16[1024,2304]{1,0:T(8,128)(2,1)} %get-tuple-element.176.gp_ref), custom_call_target="tpu_custom_call" | custom-call | flops 9228000256 | tf_op jit(solution)/shard_map/qkv_weight_grad/pallas_call | solution.py:654
  286.8 1.6 collective-permute-start.34
  288.5 1.0 copy.321.amat_ref
  291.5 12.9 %collective-permute-done.34 = bf16[432,768]{1,0:T(8,128)(2,1)} collective-permute-done((bf16[432,768]{1,0:T(8,128)(2,1)}, bf16[432,768]{1,0:T(8,128)(2,1)}, u32[]{:S(2)}, u32[]{:S(2)}) %collective-permute-start.34) | collective-permute-done | bytes 663584 | tf_op jit(solution)/shard_map/ppermute | solution.py:717
  304.4 1.3 add_convert_fusion.1
  305.7 2.1 add_convert_fusion.17
  307.9 1.6 collective-permute-start.36
  309.5 1.2 collective-permute-start.35
  310.6 11.8 %first_backward.1 = (bf16[1024,768]{1,0:T(8,128)(2,1)}, f32[8,768]{1,0:T(8,128)}) custom-call(s32[8]{0:T(128)} %copy-done.17, bf16[1024,768]{1,0:T(8,128)(2,1)} %x_ref.5, f32[1024,1]{1,0:T(8,128)} %copy.316.t_ref, f32[1024,768]{1,0:T(8,128)} %get-tuple-element.146.gm_ref, bf16[1024,2304]{1,0:T(8,128)(2,1)} %get-tuple-element.176.gp_ref, ...), custom_call_target="tpu_custom_call" | custom-call | flops 12688499712 | tf_op jit(solution)/shard_map/first_backward/pallas_call | solution.py:697
  324.2 2.6 collective-permute-start.39
  326.8 12.1 %attn_feat.4 = (f32[1024,256]{1,0:T(8,128)}, f32[2,128,128]{2,1,0:T(8,128)}) custom-call(bf16[32,2,256,256]{3,2,1,0:T(8,128)(2,1)} %get-tuple-element.191.ds_ref, f32[32,8,128]{2,1,0:T(8,128)} %copy-done.18, f32[1024,4]{1,0:T(8,128)} %bitcast.305, f32[3,128,128]{2,1,0:T(8,128)} %broadcast_in_dim.13.kp_ref, bf16[1024,256]{1,0:T(8,128)(2,1)} %copy.321.amat_ref), custom_call_target="tpu_custom_call" | custom-call | flops 11534999552 | tf_op jit(solution)/shard_map/attn_feat/pallas_call | solution.py:273
  339.2 1.6 collective-permute-start.40
  340.8 12.5 %attn_feat.5 = (f32[1024,256]{1,0:T(8,128)}, f32[2,128,128]{2,1,0:T(8,128)}) custom-call(bf16[32,2,256,256]{3,2,1,0:T(8,128)(2,1)} %get-tuple-element.191.ds_ref, f32[32,8,128]{2,1,0:T(8,128)} %copy-done.18, f32[1024,4]{1,0:T(8,128)} %bitcast.306, f32[3,128,128]{2,1,0:T(8,128)} %broadcast_in_dim.13.kp_ref, bf16[1024,256]{1,0:T(8,128)(2,1)} %copy.321.amat_ref, ...), custom_call_target="tpu_custom_call" | custom-call | flops 11534999552 | tf_op jit(solution)/shard_map/attn_feat/pallas_call | solution.py:273
  353.3 4.7 %collective-permute-done.40 = bf16[144,768]{1,0:T(8,128)(2,1)S(1)} collective-permute-done((bf16[144,768]{1,0:T(8,128)(2,1)S(1)}, bf16[144,768]{1,0:T(8,128)(2,1)S(1)}, u32[]{:S(2)}, u32[]{:S(2)}) %collective-permute-start.40) | collective-permute-done | bytes 221216 | tf_op jit(solution)/shard_map/ppermute | solution.py:717
  358.3 3.0 collective-permute-start.41
  361.3 12.5 %attn_feat.6 = (f32[1024,256]{1,0:T(8,128)}, f32[2,128,128]{2,1,0:T(8,128)}) custom-call(bf16[32,2,256,256]{3,2,1,0:T(8,128)(2,1)} %get-tuple-element.191.ds_ref, f32[32,8,128]{2,1,0:T(8,128)} %copy-done.18, f32[1024,4]{1,0:T(8,128)} %bitcast.307, f32[3,128,128]{2,1,0:T(8,128)} %broadcast_in_dim.13.kp_ref, bf16[1024,256]{1,0:T(8,128)(2,1)} %copy.321.amat_ref, ...), custom_call_target="tpu_custom_call" | custom-call | flops 11534999552 | tf_op jit(solution)/shard_map/attn_feat/pallas_call | solution.py:273
  373.8 2.6 collective-permute-done.41
  376.4 2.1 collective-permute-done.42
  378.9 12.5 %attn_feat.7 = (f32[1024,256]{1,0:T(8,128)}, f32[2,128,128]{2,1,0:T(8,128)}) custom-call(bf16[32,2,256,256]{3,2,1,0:T(8,128)(2,1)} %get-tuple-element.191.ds_ref, f32[32,8,128]{2,1,0:T(8,128)} %copy-done.18, f32[1024,4]{1,0:T(8,128)} %bitcast.308, f32[3,128,128]{2,1,0:T(8,128)} %broadcast_in_dim.13.kp_ref, bf16[1024,256]{1,0:T(8,128)(2,1)} %copy.321.amat_ref, ...), custom_call_target="tpu_custom_call" | custom-call | flops 11534999552 | tf_op jit(solution)/shard_map/attn_feat/pallas_call | solution.py:273
  391.4 2.6 copy.322
  394.0 1.6 fusion.4
  397.3 1.2 collective-permute-start.44
  399.1 1.5 collective-permute-start.46
  400.9 2.2 collective-permute-start.48
  403.7 1.8 collective-permute-done.48
  405.5 1.5 collective-permute-done.49
  407.5 3.3 collective-permute-done.50
  410.8 1.3 collective-permute-start.51
  412.1 1.2 fusion.37
  414.8 1.1 copy.339
  418.4 1.7 collective-permute-done.52
  420.3 1.0 copy.338
  (280 shorter events, 32.6 us)
Async XLA Ops:
  4.6 9.0 %collective-permute-start = (bf16[19,96]{1,0:T(8,128)(2,1)S(1)}, bf16[19,96]{1,0:T(8,128)(2,1)S(1)}, u32[]{:S(2)}, u32[]{:S(2)}) collective-permute-start(bf16[19,96]{1,0:T(8,128)(2,1)S(1)} %concatenate.50), channel_id=1, source_target_pairs={{0,4},{4,0},{8,12},{12,8},{16,20},{20,16},{24,28},{28,24},{1,5},{5... | collective-permute-start | bytes 10952 | tf_op jit(solution)/shard_map/ppermute | solution.py:717
  5.2 11.2 %collective-permute-start.1 = (bf16[19,96]{1,0:T(8,128)(2,1)S(1)}, bf16[19,96]{1,0:T(8,128)(2,1)S(1)}, u32[]{:S(2)}, u32[]{:S(2)}) collective-permute-start(bf16[19,96]{1,0:T(8,128)(2,1)S(1)} %concatenate.50), channel_id=1, source_target_pairs={{0,8},{4,12},{8,0},{12,4},{16,24},{20,28},{24,16},{28,20},{1,9},{5... | collective-permute-start | bytes 10952 | tf_op jit(solution)/shard_map/ppermute | solution.py:717
  7.7 9.8 %collective-permute-start.2 = (bf16[19,96]{1,0:T(8,128)(2,1)S(1)}, bf16[19,96]{1,0:T(8,128)(2,1)S(1)}, u32[]{:S(2)}, u32[]{:S(2)}) collective-permute-start(bf16[19,96]{1,0:T(8,128)(2,1)S(1)} %concatenate.50), channel_id=1, source_target_pairs={{0,12},{4,8},{8,4},{12,0},{16,28},{20,24},{24,20},{28,16},{1,13},{... | collective-permute-start | bytes 10952 | tf_op jit(solution)/shard_map/ppermute | solution.py:717
  7.8 11.5 %collective-permute-start.3 = (bf16[19,96]{1,0:T(8,128)(2,1)S(1)}, bf16[19,96]{1,0:T(8,128)(2,1)S(1)}, u32[]{:S(2)}, u32[]{:S(2)}) collective-permute-start(bf16[19,96]{1,0:T(8,128)(2,1)S(1)} %concatenate.50), channel_id=1, source_target_pairs={{0,16},{4,20},{8,24},{12,28},{16,0},{20,4},{24,8},{28,12},{1,17},{... | collective-permute-start | bytes 10952 | tf_op jit(solution)/shard_map/ppermute | solution.py:717
  9.6 11.3 %collective-permute-start.4 = (bf16[19,96]{1,0:T(8,128)(2,1)S(1)}, bf16[19,96]{1,0:T(8,128)(2,1)S(1)}, u32[]{:S(2)}, u32[]{:S(2)}) collective-permute-start(bf16[19,96]{1,0:T(8,128)(2,1)S(1)} %concatenate.50), channel_id=1, source_target_pairs={{0,20},{4,16},{8,28},{12,24},{16,4},{20,0},{24,12},{28,8},{1,21},{... | collective-permute-start | bytes 10952 | tf_op jit(solution)/shard_map/ppermute | solution.py:717
  13.6 50.8 %copy-start.2 = (bf16[480,768]{1,0:T(8,128)(2,1)}, bf16[480,768]{1,0:T(8,128)(2,1)S(1)}, u32[]{:S(2)}) copy-start(bf16[480,768]{1,0:T(8,128)(2,1)S(1)} %pad_maximum_fusion.3.rest_0_) | copy-start | bytes 2211844
  13.6 7.7 %collective-permute-start.5 = (bf16[19,96]{1,0:T(8,128)(2,1)S(1)}, bf16[19,96]{1,0:T(8,128)(2,1)S(1)}, u32[]{:S(2)}, u32[]{:S(2)}) collective-permute-start(bf16[19,96]{1,0:T(8,128)(2,1)S(1)} %concatenate.50), channel_id=1, source_target_pairs={{0,24},{4,28},{8,16},{12,20},{16,8},{20,12},{24,0},{28,4},{1,25},{... | collective-permute-start | bytes 10952 | tf_op jit(solution)/shard_map/ppermute | solution.py:717
  16.3 5.0 %collective-permute-start.6 = (bf16[19,96]{1,0:T(8,128)(2,1)S(1)}, bf16[19,96]{1,0:T(8,128)(2,1)S(1)}, u32[]{:S(2)}, u32[]{:S(2)}) collective-permute-start(bf16[19,96]{1,0:T(8,128)(2,1)S(1)} %concatenate.50), channel_id=1, source_target_pairs={{0,28},{4,24},{8,20},{12,16},{16,12},{20,8},{24,4},{28,0},{1,29},{... | collective-permute-start | bytes 10952 | tf_op jit(solution)/shard_map/ppermute | solution.py:717
  17.6 37.8 %collective-permute-start.7 = (bf16[96,2304]{1,0:T(8,128)(2,1)S(1)}, bf16[96,2304]{1,0:T(8,128)(2,1)S(1)}, u32[]{:S(2)}, u32[]{:S(2)}) collective-permute-start(bf16[96,2304]{1,0:T(8,128)(2,1)S(1)} %copy-done.25), channel_id=1, source_target_pairs={{0,8},{4,12},{8,0},{12,4},{16,24},{20,28},{24,16},{28,20},{1,9},{5... | collective-permute-start | bytes 1327112 | tf_op jit(solution)/shard_map/ppermute | solution.py:717
  19.3 36.1 %collective-permute-start.8 = (bf16[96,2304]{1,0:T(8,128)(2,1)S(1)}, bf16[96,2304]{1,0:T(8,128)(2,1)}, u32[]{:S(2)}, u32[]{:S(2)}) collective-permute-start(bf16[96,2304]{1,0:T(8,128)(2,1)S(1)} %copy-done.25), channel_id=1, source_target_pairs={{0,16},{4,20},{8,24},{12,28},{16,0},{20,4},{24,8},{28,12},{1,17},{... | collective-permute-start | bytes 1327112 | tf_op jit(solution)/shard_map/ppermute | solution.py:717
  20.9 34.5 %collective-permute-start.9 = (bf16[96,2304]{1,0:T(8,128)(2,1)S(1)}, bf16[96,2304]{1,0:T(8,128)(2,1)}, u32[]{:S(2)}, u32[]{:S(2)}) collective-permute-start(bf16[96,2304]{1,0:T(8,128)(2,1)S(1)} %copy-done.25), channel_id=1, source_target_pairs={{0,24},{4,28},{8,16},{12,20},{16,8},{20,12},{24,0},{28,4},{1,25},{... | collective-permute-start | bytes 1327112 | tf_op jit(solution)/shard_map/ppermute | solution.py:717
  21.9 33.5 %copy-start.5 = (f32[8,576]{1,0:T(8,128)}, f32[8,576]{1,0:T(8,128)S(1)}, u32[]{:S(2)}) copy-start(f32[8,576]{1,0:T(8,128)S(1)} %reshape.375) | copy-start | bytes 55300
  22.4 33.0 %copy-start.6 = (bf16[128,32]{0,1:T(8,128)(2,1)}, bf16[128,32]{0,1:T(8,128)(2,1)S(1)}, u32[]{:S(2)}) copy-start(bf16[128,32]{0,1:T(8,128)(2,1)S(1)} %copy.313) | copy-start | bytes 24580
  24.2 32.2 %copy-start.16 = (f32[1024]{0:T(1024)S(1)}, f32[1024]{0:T(1024)}, u32[]{:S(2)}) copy-start(f32[1024]{0:T(1024)} %param.23) | copy-start | bytes 12292
  24.2 39.2 %copy-start.23 = (bf16[384,768]{1,0:T(8,128)(2,1)S(1)}, bf16[384,768]{1,0:T(8,128)(2,1)}, u32[]{:S(2)}) copy-start(bf16[384,768]{1,0:T(8,128)(2,1)} %rest_8_) | copy-start | bytes 1769476
  55.4 6.6 %collective-permute-start.10 = (bf16[96,2304]{1,0:T(8,128)(2,1)S(1)}, bf16[96,2304]{1,0:T(8,128)(2,1)}, u32[]{:S(2)}, u32[]{:S(2)}) collective-permute-start(bf16[96,2304]{1,0:T(8,128)(2,1)S(1)} %copy-done.25), channel_id=1, source_target_pairs={{0,4},{4,0},{8,12},{12,8},{16,20},{20,16},{24,28},{28,24},{1,5},{5... | collective-permute-start | bytes 1327112 | tf_op jit(solution)/shard_map/ppermute | solution.py:717
  55.5 8.0 %collective-permute-start.11 = (bf16[96,2304]{1,0:T(8,128)(2,1)S(1)}, bf16[96,2304]{1,0:T(8,128)(2,1)}, u32[]{:S(2)}, u32[]{:S(2)}) collective-permute-start(bf16[96,2304]{1,0:T(8,128)(2,1)S(1)} %collective-permute-done.7.rest_2_), channel_id=1, source_target_pairs={{0,4},{4,0},{8,12},{12,8},{16,20},{20,16},{24,28},{28,24},{1,5},{5... | collective-permute-start | bytes 1327112 | tf_op jit(solution)/shard_map/ppermute | solution.py:717
  56.0 8.1 %collective-permute-start.12 = (bf16[96,2304]{1,0:T(8,128)(2,1)}, bf16[96,2304]{1,0:T(8,128)(2,1)}, u32[]{:S(2)}, u32[]{:S(2)}) collective-permute-start(bf16[96,2304]{1,0:T(8,128)(2,1)} %collective-permute-done.8.rest_4_), channel_id=1, source_target_pairs={{0,4},{4,0},{8,12},{12,8},{16,20},{20,16},{24,28},{28,24},{1,5},{5... | collective-permute-start | bytes 1327112 | tf_op jit(solution)/shard_map/ppermute | solution.py:717
  56.1 8.4 %collective-permute-start.13 = (bf16[96,2304]{1,0:T(8,128)(2,1)}, bf16[96,2304]{1,0:T(8,128)(2,1)}, u32[]{:S(2)}, u32[]{:S(2)}) collective-permute-start(bf16[96,2304]{1,0:T(8,128)(2,1)} %collective-permute-done.9.rest_6_), channel_id=1, source_target_pairs={{0,4},{4,0},{8,12},{12,8},{16,20},{20,16},{24,28},{28,24},{1,5},{5... | collective-permute-start | bytes 1327112 | tf_op jit(solution)/shard_map/ppermute | solution.py:717
  57.7 17.0 %copy-start.9 = (f32[1,768]{1,0:T(1,128)}, f32[1,768]{1,0:T(1,128)S(1)}, u32[]{:S(2)}) copy-start(f32[1,768]{1,0:T(1,128)S(1)} %slice.381) | copy-start | bytes 9220
  57.8 16.9 %copy-start.11 = (f32[1,768]{1,0:T(1,128)}, f32[1,768]{1,0:T(1,128)S(1)}, u32[]{:S(2)}) copy-start(f32[1,768]{1,0:T(1,128)S(1)} %slice.383) | copy-start | bytes 9220
  60.4 37.2 %collective-permute-start.14 = (bf16[480,768]{1,0:T(8,128)(2,1)S(1)}, bf16[480,768]{1,0:T(8,128)(2,1)S(1)}, u32[]{:S(2)}, u32[]{:S(2)}) collective-permute-start(bf16[480,768]{1,0:T(8,128)(2,1)S(1)} %pad_maximum_fusion.3.rest_0_), channel_id=1, source_target_pairs={{0,8},{4,12},{8,0},{12,4},{16,24},{20,28},{24,16},{28,20},{1,9},{5... | collective-permute-start | bytes 2211848 | tf_op jit(solution)/shard_map/ppermute | solution.py:717
  62.0 35.6 %collective-permute-start.15 = (bf16[480,768]{1,0:T(8,128)(2,1)S(1)}, bf16[480,768]{1,0:T(8,128)(2,1)S(1)}, u32[]{:S(2)}, u32[]{:S(2)}) collective-permute-start(bf16[480,768]{1,0:T(8,128)(2,1)S(1)} %pad_maximum_fusion.3.rest_0_), channel_id=1, source_target_pairs={{0,16},{4,20},{8,24},{12,28},{16,0},{20,4},{24,8},{28,12},{1,17},{... | collective-permute-start | bytes 2211848 | tf_op jit(solution)/shard_map/ppermute | solution.py:717
  63.5 33.5 %collective-permute-start.16 = (bf16[384,768]{1,0:T(8,128)(2,1)S(1)}, bf16[384,768]{1,0:T(8,128)(2,1)}, u32[]{:S(2)}, u32[]{:S(2)}) collective-permute-start(bf16[384,768]{1,0:T(8,128)(2,1)S(1)} %copy-done.23), channel_id=1, source_target_pairs={{0,8},{4,12},{8,0},{12,4},{16,24},{20,28},{24,16},{28,20},{1,9},{5... | collective-permute-start | bytes 1769480 | tf_op jit(solution)/shard_map/ppermute | solution.py:717
  64.1 33.5 %collective-permute-start.17 = (bf16[384,768]{1,0:T(8,128)(2,1)S(1)}, bf16[384,768]{1,0:T(8,128)(2,1)}, u32[]{:S(2)}, u32[]{:S(2)}) collective-permute-start(bf16[384,768]{1,0:T(8,128)(2,1)S(1)} %copy-done.23), channel_id=1, source_target_pairs={{0,16},{4,20},{8,24},{12,28},{16,0},{20,4},{24,8},{28,12},{1,17},{... | collective-permute-start | bytes 1769480 | tf_op jit(solution)/shard_map/ppermute | solution.py:717
  64.4 52.3 %collective-permute-start.20 = (bf16[480,768]{1,0:T(8,128)(2,1)S(1)}, bf16[480,768]{1,0:T(8,128)(2,1)S(1)}, u32[]{:S(2)}, u32[]{:S(2)}) collective-permute-start(bf16[480,768]{1,0:T(8,128)(2,1)S(1)} %pad_maximum_fusion.3.rest_0_), channel_id=1, source_target_pairs={{0,4},{4,0},{8,12},{12,8},{16,20},{20,16},{24,28},{28,24},{1,5},{5... | collective-permute-start | bytes 2211848 | tf_op jit(solution)/shard_map/ppermute | solution.py:717
  97.0 19.2 %collective-permute-start.24 = (bf16[384,768]{1,0:T(8,128)(2,1)S(1)}, bf16[384,768]{1,0:T(8,128)(2,1)}, u32[]{:S(2)}, u32[]{:S(2)}) collective-permute-start(bf16[384,768]{1,0:T(8,128)(2,1)S(1)} %copy-done.23), channel_id=1, source_target_pairs={{0,4},{4,0},{8,12},{12,8},{16,20},{20,16},{24,28},{28,24},{1,5},{5... | collective-permute-start | bytes 1769480 | tf_op jit(solution)/shard_map/ppermute | solution.py:717
  97.6 17.1 %copy-start.19 = (bf16[480,768]{1,0:T(8,128)(2,1)}, bf16[480,768]{1,0:T(8,128)(2,1)S(1)}, u32[]{:S(2)}) copy-start(bf16[480,768]{1,0:T(8,128)(2,1)S(1)} %collective-permute-done.14.rest_2_) | copy-start | bytes 2211844
  97.6 18.6 %copy-start.20 = (bf16[480,768]{1,0:T(8,128)(2,1)}, bf16[480,768]{1,0:T(8,128)(2,1)S(1)}, u32[]{:S(2)}) copy-start(bf16[480,768]{1,0:T(8,128)(2,1)S(1)} %collective-permute-done.15.rest_4_) | copy-start | bytes 2211844
  97.6 18.6 %collective-permute-start.18 = (bf16[480,768]{1,0:T(8,128)(2,1)S(1)}, bf16[480,768]{1,0:T(8,128)(2,1)}, u32[]{:S(2)}, u32[]{:S(2)}) collective-permute-start(bf16[480,768]{1,0:T(8,128)(2,1)S(1)} %collective-permute-done.14.rest_2_), channel_id=1, source_target_pairs={{0,16},{4,20},{8,24},{12,28},{16,0},{20,4},{24,8},{28,12},{1,17},{... | collective-permute-start | bytes 2211848 | tf_op jit(solution)/shard_map/ppermute | solution.py:717
  99.3 15.3 %collective-permute-start.19 = (bf16[384,768]{1,0:T(8,128)(2,1)}, bf16[384,768]{1,0:T(8,128)(2,1)}, u32[]{:S(2)}, u32[]{:S(2)}) collective-permute-start(bf16[384,768]{1,0:T(8,128)(2,1)} %collective-permute-done.17.rest_12_), channel_id=1, source_target_pairs={{0,8},{4,12},{8,0},{12,4},{16,24},{20,28},{24,16},{28,20},{1,9},{5... | collective-permute-start | bytes 1769480 | tf_op jit(solution)/shard_map/ppermute | solution.py:717
  100.8 16.0 %collective-permute-start.25 = (bf16[384,768]{1,0:T(8,128)(2,1)}, bf16[384,768]{1,0:T(8,128)(2,1)}, u32[]{:S(2)}, u32[]{:S(2)}) collective-permute-start(bf16[384,768]{1,0:T(8,128)(2,1)} %collective-permute-done.16.rest_10_), channel_id=1, source_target_pairs={{0,4},{4,0},{8,12},{12,8},{16,20},{20,16},{24,28},{28,24},{1,5},{5... | collective-permute-start | bytes 1769480 | tf_op jit(solution)/shard_map/ppermute | solution.py:717
  114.7 13.8 %collective-permute-start.21 = (bf16[480,768]{1,0:T(8,128)(2,1)S(1)}, bf16[480,768]{1,0:T(8,128)(2,1)}, u32[]{:S(2)}, u32[]{:S(2)}) collective-permute-start(bf16[480,768]{1,0:T(8,128)(2,1)S(1)} %collective-permute-done.14.rest_2_), channel_id=1, source_target_pairs={{0,4},{4,0},{8,12},{12,8},{16,20},{20,16},{24,28},{28,24},{1,5},{5... | collective-permute-start | bytes 2211848 | tf_op jit(solution)/shard_map/ppermute | solution.py:717
  116.2 12.2 %collective-permute-start.26 = (bf16[384,768]{1,0:T(8,128)(2,1)}, bf16[384,768]{1,0:T(8,128)(2,1)}, u32[]{:S(2)}, u32[]{:S(2)}) collective-permute-start(bf16[384,768]{1,0:T(8,128)(2,1)} %collective-permute-done.17.rest_12_), channel_id=1, source_target_pairs={{0,4},{4,0},{8,12},{12,8},{16,20},{20,16},{24,28},{28,24},{1,5},{5... | collective-permute-start | bytes 1769480 | tf_op jit(solution)/shard_map/ppermute | solution.py:717
  116.2 12.2 %collective-permute-start.22 = (bf16[480,768]{1,0:T(8,128)(2,1)S(1)}, bf16[480,768]{1,0:T(8,128)(2,1)}, u32[]{:S(2)}, u32[]{:S(2)}) collective-permute-start(bf16[480,768]{1,0:T(8,128)(2,1)S(1)} %collective-permute-done.15.rest_4_), channel_id=1, source_target_pairs={{0,4},{4,0},{8,12},{12,8},{16,20},{20,16},{24,28},{28,24},{1,5},{5... | collective-permute-start | bytes 2211848 | tf_op jit(solution)/shard_map/ppermute | solution.py:717
  116.7 11.7 %collective-permute-start.23 = (bf16[480,768]{1,0:T(8,128)(2,1)}, bf16[480,768]{1,0:T(8,128)(2,1)S(1)}, u32[]{:S(2)}, u32[]{:S(2)}) collective-permute-start(bf16[480,768]{1,0:T(8,128)(2,1)} %collective-permute-done.18.rest_6_), channel_id=1, source_target_pairs={{0,4},{4,0},{8,12},{12,8},{16,20},{20,16},{24,28},{28,24},{1,5},{5... | collective-permute-start | bytes 2211848 | tf_op jit(solution)/shard_map/ppermute | solution.py:717
  116.8 11.6 %collective-permute-start.27 = (bf16[384,768]{1,0:T(8,128)(2,1)}, bf16[384,768]{1,0:T(8,128)(2,1)S(1)}, u32[]{:S(2)}, u32[]{:S(2)}) collective-permute-start(bf16[384,768]{1,0:T(8,128)(2,1)} %collective-permute-done.19.rest_14_), channel_id=1, source_target_pairs={{0,4},{4,0},{8,12},{12,8},{16,20},{20,16},{24,28},{28,24},{1,5},{5... | collective-permute-start | bytes 1769480 | tf_op jit(solution)/shard_map/ppermute | solution.py:717
  200.6 15.5 %collective-permute-start.28 = (bf16[4,864,768]{2,1,0:T(8,128)(2,1)}, bf16[4,864,768]{2,1,0:T(8,128)(2,1)}, u32[]{:S(2)}, u32[]{:S(2)}) collective-permute-start(bf16[4,864,768]{2,1,0:T(8,128)(2,1)} %get-tuple-element.152), channel_id=1, source_target_pairs={{0,4},{4,0},{8,12},{12,8},{16,20},{20,16},{24,28},{28,24},{1,5},{5... | collective-permute-start | bytes 15925256 | tf_op jit(solution)/shard_map/ppermute | solution.py:717
  222.6 33.8 %collective-permute-start.30 = (bf16[2,432,768]{2,1,0:T(8,128)(2,1)S(1)}, bf16[2,432,768]{2,1,0:T(8,128)(2,1)}, u32[]{:S(2)}, u32[]{:S(2)}) collective-permute-start(bf16[2,432,768]{2,1,0:T(8,128)(2,1)S(1)} %get-tuple-element.162), channel_id=1, source_target_pairs={{0,16},{4,20},{8,24},{12,28},{16,0},{20,4},{24,8},{28,12},{1,17},{... | collective-permute-start | bytes 3981320 | tf_op jit(solution)/shard_map/ppermute | solution.py:717
  224.3 33.8 %collective-permute-start.29 = (bf16[2,432,768]{2,1,0:T(8,128)(2,1)}, bf16[2,432,768]{2,1,0:T(8,128)(2,1)}, u32[]{:S(2)}, u32[]{:S(2)}) collective-permute-start(bf16[2,432,768]{2,1,0:T(8,128)(2,1)} %get-tuple-element.160), channel_id=1, source_target_pairs={{0,8},{4,12},{8,0},{12,4},{16,24},{20,28},{24,16},{28,20},{1,9},{5... | collective-permute-start | bytes 3981320 | tf_op jit(solution)/shard_map/ppermute | solution.py:717
  259.8 16.7 %collective-permute-start.31 = (bf16[432,768]{1,0:T(8,128)(2,1)S(1)}, bf16[432,768]{1,0:T(8,128)(2,1)S(1)}, u32[]{:S(2)}, u32[]{:S(2)}) collective-permute-start(bf16[432,768]{1,0:T(8,128)(2,1)S(1)} %get-tuple-element.169), channel_id=1, source_target_pairs={{0,16},{4,20},{8,24},{12,28},{16,0},{20,4},{24,8},{28,12},{1,17},{... | collective-permute-start | bytes 1990664 | tf_op jit(solution)/shard_map/ppermute | solution.py:717
  260.3 16.4 %collective-permute-start.32 = (bf16[432,768]{1,0:T(8,128)(2,1)S(1)}, bf16[432,768]{1,0:T(8,128)(2,1)S(1)}, u32[]{:S(2)}, u32[]{:S(2)}) collective-permute-start(bf16[432,768]{1,0:T(8,128)(2,1)S(1)} %get-tuple-element.171), channel_id=1, source_target_pairs={{0,8},{4,12},{8,0},{12,4},{16,24},{20,28},{24,16},{28,20},{1,9},{5... | collective-permute-start | bytes 1990664 | tf_op jit(solution)/shard_map/ppermute | solution.py:717
  286.8 18.9 %collective-permute-start.33 = (bf16[4,288,768]{2,1,0:T(8,128)(2,1)}, bf16[4,288,768]{2,1,0:T(8,128)(2,1)}, u32[]{:S(2)}, u32[]{:S(2)}) collective-permute-start(bf16[4,288,768]{2,1,0:T(8,128)(2,1)} %get-tuple-element.175), channel_id=1, source_target_pairs={{0,4},{4,0},{8,12},{12,8},{16,20},{20,16},{24,28},{28,24},{1,5},{5... | collective-permute-start | bytes 5308424 | tf_op jit(solution)/shard_map/ppermute | solution.py:717
  286.8 17.6 %collective-permute-start.34 = (bf16[432,768]{1,0:T(8,128)(2,1)}, bf16[432,768]{1,0:T(8,128)(2,1)}, u32[]{:S(2)}, u32[]{:S(2)}) collective-permute-start(bf16[432,768]{1,0:T(8,128)(2,1)} %get-tuple-element.181), channel_id=1, source_target_pairs={{0,1},{1,0},{2,3},{3,2},{4,5},{5,4},{6,7},{7,6},{8,9},{9,8},{10,11... | collective-permute-start | bytes 1990664 | tf_op jit(solution)/shard_map/ppermute | solution.py:717
  289.5 16.2 %copy-start.1 = (bf16[4,288,768]{2,1,0:T(8,128)(2,1)S(1)}, bf16[4,288,768]{2,1,0:T(8,128)(2,1)}, u32[]{:S(2)}) copy-start(bf16[4,288,768]{2,1,0:T(8,128)(2,1)} %get-tuple-element.174) | copy-start | bytes 5308420
  307.9 14.6 %collective-permute-start.36 = (bf16[2,144,768]{2,1,0:T(8,128)(2,1)S(1)}, bf16[2,144,768]{2,1,0:T(8,128)(2,1)S(1)}, u32[]{:S(2)}, u32[]{:S(2)}) collective-permute-start(bf16[2,144,768]{2,1,0:T(8,128)(2,1)S(1)} %pad_maximum_fusion.5), channel_id=1, source_target_pairs={{0,16},{4,20},{8,24},{12,28},{16,0},{20,4},{24,8},{28,12},{1,17},{... | collective-permute-start | bytes 1327112 | tf_op jit(solution)/shard_map/ppermute | solution.py:717
  309.5 13.1 %collective-permute-start.35 = (bf16[2,144,768]{2,1,0:T(8,128)(2,1)S(1)}, bf16[2,144,768]{2,1,0:T(8,128)(2,1)S(1)}, u32[]{:S(2)}, u32[]{:S(2)}) collective-permute-start(bf16[2,144,768]{2,1,0:T(8,128)(2,1)S(1)} %pad_maximum_fusion.4), channel_id=1, source_target_pairs={{0,8},{4,12},{8,0},{12,4},{16,24},{20,28},{24,16},{28,20},{1,9},{5... | collective-permute-start | bytes 1327112 | tf_op jit(solution)/shard_map/ppermute | solution.py:717
  322.7 16.1 %copy-start.13 = (f32[8,768]{1,0:T(8,128)S(1)}, f32[8,768]{1,0:T(8,128)}, u32[]{:S(2)}) copy-start(f32[8,768]{1,0:T(8,128)} %get-tuple-element.188) | copy-start | bytes 73732
  322.7 16.2 %collective-permute-start.37 = (bf16[144,768]{1,0:T(8,128)(2,1)S(1)}, bf16[144,768]{1,0:T(8,128)(2,1)S(1)}, u32[]{:S(2)}, u32[]{:S(2)}) collective-permute-start(bf16[144,768]{1,0:T(8,128)(2,1)S(1)} %get-tuple-element.195), channel_id=1, source_target_pairs={{0,16},{4,20},{8,24},{12,28},{16,0},{20,4},{24,8},{28,12},{1,17},{... | collective-permute-start | bytes 663560 | tf_op jit(solution)/shard_map/ppermute | solution.py:717
  323.3 15.7 %collective-permute-start.38 = (bf16[144,768]{1,0:T(8,128)(2,1)S(1)}, bf16[144,768]{1,0:T(8,128)(2,1)S(1)}, u32[]{:S(2)}, u32[]{:S(2)}) collective-permute-start(bf16[144,768]{1,0:T(8,128)(2,1)S(1)} %get-tuple-element.197), channel_id=1, source_target_pairs={{0,8},{4,12},{8,0},{12,4},{16,24},{20,28},{24,16},{28,20},{1,9},{5... | collective-permute-start | bytes 663560 | tf_op jit(solution)/shard_map/ppermute | solution.py:717
  324.2 33.9 %collective-permute-start.39 = (bf16[432,768]{1,0:T(8,128)(2,1)S(1)}, bf16[432,768]{1,0:T(8,128)(2,1)S(1)}, u32[]{:S(2)}, u32[]{:S(2)}) collective-permute-start(bf16[432,768]{1,0:T(8,128)(2,1)S(1)} %add_convert_fusion.1), channel_id=1, source_target_pairs={{0,2},{1,3},{2,0},{3,1},{4,6},{5,7},{6,4},{7,5},{8,10},{9,11},{10,... | collective-permute-start | bytes 1990664 | tf_op jit(solution)/shard_map/ppermute | solution.py:717
  339.2 18.8 %collective-permute-start.40 = (bf16[144,768]{1,0:T(8,128)(2,1)S(1)}, bf16[144,768]{1,0:T(8,128)(2,1)S(1)}, u32[]{:S(2)}, u32[]{:S(2)}) collective-permute-start(bf16[144,768]{1,0:T(8,128)(2,1)S(1)} %get-tuple-element.204), channel_id=1, source_target_pairs={{0,1},{1,0},{2,3},{3,2},{4,5},{5,4},{6,7},{7,6},{8,9},{9,8},{10,11... | collective-permute-start | bytes 663560 | tf_op jit(solution)/shard_map/ppermute | solution.py:717
  358.2 20.3 %collective-permute-start.42 = (bf16[432,768]{1,0:T(8,128)(2,1)S(1)}, bf16[432,768]{1,0:T(8,128)(2,1)S(1)}, u32[]{:S(2)}, u32[]{:S(2)}) collective-permute-start(bf16[432,768]{1,0:T(8,128)(2,1)S(1)} %add_convert_fusion), channel_id=1, source_target_pairs={{0,1},{1,0},{2,3},{3,2},{4,5},{5,4},{6,7},{7,6},{8,9},{9,8},{10,11... | collective-permute-start | bytes 1990664 | tf_op jit(solution)/shard_map/ppermute | solution.py:717
  358.3 18.1 %collective-permute-start.41 = (bf16[144,768]{1,0:T(8,128)(2,1)S(1)}, bf16[144,768]{1,0:T(8,128)(2,1)S(1)}, u32[]{:S(2)}, u32[]{:S(2)}) collective-permute-start(bf16[144,768]{1,0:T(8,128)(2,1)S(1)} %add_convert_fusion.13), channel_id=1, source_target_pairs={{0,2},{1,3},{2,0},{3,1},{4,6},{5,7},{6,4},{7,5},{8,10},{9,11},{10,... | collective-permute-start | bytes 663560 | tf_op jit(solution)/shard_map/ppermute | solution.py:717
  397.2 3.7 collective-permute-start.43
  397.3 5.7 %collective-permute-start.44 = (f32[19,96]{1,0:T(8,128)S(1)}, f32[19,96]{1,0:T(8,128)S(1)}, u32[]{:S(2)}, u32[]{:S(2)}) collective-permute-start(f32[19,96]{1,0:T(8,128)S(1)} %bitcast.315), channel_id=1, source_target_pairs={{0,8},{4,12},{8,0},{12,4},{16,24},{20,28},{24,16},{28,20},{1,9},{5... | collective-permute-start | bytes 21896 | tf_op jit(solution)/shard_map/ppermute | solution.py:717
  398.5 5.1 %collective-permute-start.45 = (f32[19,96]{1,0:T(8,128)S(1)}, f32[19,96]{1,0:T(8,128)S(1)}, u32[]{:S(2)}, u32[]{:S(2)}) collective-permute-start(f32[19,96]{1,0:T(8,128)S(1)} %bitcast.314), channel_id=1, source_target_pairs={{0,12},{4,8},{8,4},{12,0},{16,28},{20,24},{24,20},{28,16},{1,13},{... | collective-permute-start | bytes 21896 | tf_op jit(solution)/shard_map/ppermute | solution.py:717
  399.1 4.5 %collective-permute-start.46 = (f32[19,96]{1,0:T(8,128)S(1)}, f32[19,96]{1,0:T(8,128)S(1)}, u32[]{:S(2)}, u32[]{:S(2)}) collective-permute-start(f32[19,96]{1,0:T(8,128)S(1)} %bitcast.316), channel_id=1, source_target_pairs={{0,16},{4,20},{8,24},{12,28},{16,0},{20,4},{24,8},{28,12},{1,17},{... | collective-permute-start | bytes 21896 | tf_op jit(solution)/shard_map/ppermute | solution.py:717
  400.6 3.1 collective-permute-start.47
  400.9 4.7 %collective-permute-start.48 = (f32[19,96]{1,0:T(8,128)S(1)}, f32[19,96]{1,0:T(8,128)S(1)}, u32[]{:S(2)}, u32[]{:S(2)}) collective-permute-start(f32[19,96]{1,0:T(8,128)S(1)} %bitcast.320), channel_id=1, source_target_pairs={{0,24},{4,28},{8,16},{12,20},{16,8},{20,12},{24,0},{28,4},{1,25},{... | collective-permute-start | bytes 21896 | tf_op jit(solution)/shard_map/ppermute | solution.py:717
  403.0 4.0 collective-permute-start.49
  407.0 3.8 collective-permute-start.50
  410.8 5.1 %collective-permute-start.51 = (f32[19,96]{1,0:T(8,128)S(1)}, f32[19,96]{1,0:T(8,128)S(1)}, u32[]{:S(2)}, u32[]{:S(2)}) collective-permute-start(f32[19,96]{1,0:T(8,128)S(1)} %add.288), channel_id=1, source_target_pairs={{0,2},{1,3},{2,0},{3,1},{4,6},{5,7},{6,4},{7,5},{8,10},{9,11},{10,... | collective-permute-start | bytes 21896 | tf_op jit(solution)/shard_map/ppermute | solution.py:717
  414.0 6.2 %collective-permute-start.52 = (bf16[144,768]{1,0:T(8,128)(2,1)S(1)}, bf16[144,768]{1,0:T(8,128)(2,1)S(1)}, u32[]{:S(2)}, u32[]{:S(2)}) collective-permute-start(bf16[144,768]{1,0:T(8,128)(2,1)S(1)} %add_convert_fusion.12), channel_id=1, source_target_pairs={{0,1},{1,0},{2,3},{3,2},{4,5},{5,4},{6,7},{7,6},{8,9},{9,8},{10,11... | collective-permute-start | bytes 663560 | tf_op jit(solution)/shard_map/ppermute | solution.py:717
  (16 other events, 110.9 us)

commit v3 on v2

v3 whole, which is shorter than its diff:
```python
import functools, math
import jax, jax.numpy as jnp
from jax import lax
from jax.experimental import pallas as pl
from jax.experimental.pallas import tpu as pltpu
from jax.sharding import PartitionSpec as P

SET = 256
CH = 32
STEP = 4
UNROLL = 4
PAIR = 4
FEAT_STEP = 2
WIN = 128
GROUPS = ((0, 0), (128, 8), (384, 16), (512, 24))
HW = 24
VM = 60 * 1024 * 1024
f32, bf16 = jnp.float32, jnp.bfloat16
NT = (((1,), (1,)), ((), ()))
TN = (((0,), (0,)), ((), ()))


def dot(a, b, dims=(((1,), (0,)), ((), ()))):
    return lax.dot_general(a, b, dims, preferred_element_type=f32)


def spread_heads(block, lane0, h0):
    wide = block.astype(f32)
    lanes = lax.broadcasted_iota(jnp.int32, (8, 256), 1) + lane0
    masks = [(lanes >= h * HW) & (lanes < (h + 1) * HW) for h in range(h0, h0 + 8)]
    zero = jnp.zeros((8, 256), f32)
    parts = [jnp.where(m, wide[8 * g : 8 * g + 8], zero) for g in range(4) for m in masks]
    return jnp.concatenate(parts, axis=0).astype(bf16)


def own_rows(full, lane0, h0):
    lanes = lax.broadcasted_iota(jnp.int32, (8, 256), 1) + lane0
    groups = []
    for g in range(4):
        out = jnp.zeros((8, 256), f32)
        for h in range(8):
            m = (lanes >= (h0 + h) * HW) & (lanes < (h0 + h + 1) * HW)
            out = jnp.where(m, full[64 * g + 8 * h : 64 * g + 8 * h + 8], out)
        groups.append(out)
    return jnp.concatenate(groups, axis=0)


def window_start(i):
    per = SET // CH
    base = i // per * SET
    return pl.multiple_of(jnp.clip(i * CH - 48, base, base + SET - WIN), 16)


def radius_of(ac, aw):
    d = ac[:, 0:1] - aw[0:1, :]
    s = d * d
    for j in (1, 2):
        d = ac[:, j : j + 1] - aw[j : j + 1, :]
        s = s + d * d
    return jnp.sqrt(s)


def per_chunk(body, unroll):
    if STEP == unroll:
        for t in range(STEP):
            body(t)
        return

    @pl.loop(0, STEP // unroll)
    def _(s):
        for t in range(unroll):
            body(s * unroll + t)


def chunk_rows(t):
    return pl.ds(pl.multiple_of(t * CH, CH), CH)


def parts3(v):
    high = v.astype(bf16).astype(f32)
    rest = v - high
    middle = rest.astype(bf16).astype(f32)
    return high, middle, (rest - middle).astype(bf16).astype(f32)


def distance_rows(ac, aw):
    rho = radius_of(ac, aw)
    rho = jnp.concatenate([rho[8 * g : 8 * g + 8] for g in range(4)], axis=1)
    (sh, sm, sl), (h, m, l) = parts3(rho * rho), parts3(rho)
    one = jnp.ones_like(rho)
    slots = [sh, sh, sm, sm, sh, sl, h, h, m, m, h, l, one, one, one, jnp.zeros_like(rho)]
    return jnp.concatenate(slots, axis=0).astype(bf16)


def bias_kernel(aw_ref, ac_ref, gmat_ref, bmat_ref, b_ref, f_ref, t_scr):
    @pl.loop(0, STEP // PAIR)
    def _(s):
        chunks = [s * PAIR + u for u in range(PAIR)]
        ac = [ac_ref[chunk_rows(t), :] for t in chunks]
        aw = [aw_ref[t] for t in chunks]
        dist = [distance_rows(a, w) for a, w in zip(ac, aw)]
        e = [dot(gmat_ref[...], d) for d in dist]
        f = [jnp.exp2(v).astype(bf16) for v in e]
        bias = [dot(bmat_ref[...], v) for v in f]
        for u, t in enumerate(chunks):
            f_ref[t] = f[u]
            joined = ac[u][:, 3:4] == aw[u][3:4, :]
            for g in range(4):
                part = bias[u][:, 128 * g : 128 * g + 128].reshape(32, 8, WIN)
                part = jnp.where(joined[8 * g : 8 * g + 8][None], part, -1e30)
                for q in range(4):
                    t_scr[u, 256 * q + 64 * g : 256 * q + 64 * g + 64, :] = part[8 * q : 8 * q + 8].reshape(64, WIN)
        for u, t in enumerate(chunks):
            for n in range(8):
                b_ref[t, :, 128 * n : 128 * n + 128] = t_scr[u, 128 * n : 128 * n + 128, :].T


def fwd_kernel(q_ref, k_ref, v_ref, b_ref, o_ref, p_ref):
    def chunk(t):
        w = window_start(pl.program_id(0) * STEP + t)
        rt = chunk_rows(t)
        kwin = k_ref[pl.ds(w, WIN), :]
        vwin = v_ref[pl.ds(w, WIN), :]
        spans = [slice(lane0, lane0 + 256) for lane0, _ in GROUPS]
        wide = [spread_heads(q_ref[rt, sl], lane0, h0) for sl, (lane0, h0) in zip(spans, GROUPS)]
        s = [dot(kwin[:, sl], qm, NT) + b_ref[t, :, 256 * j : 256 * j + 256] for j, (sl, qm) in enumerate(zip(spans, wide))]
        e = [jnp.exp(v - jnp.max(v, axis=0, keepdims=True)) for v in s]
        pr = [(v * (1.0 / jnp.sum(v, axis=0, keepdims=True))).astype(bf16) for v in e]
        full = [dot(v, vwin[:, sl], TN) for sl, v in zip(spans, pr)]
        acc = [own_rows(v, *GROUPS[j]) for j, v in enumerate(full)]
        for j, v in enumerate(pr):
            p_ref[t, :, 256 * j : 256 * j + 256] = v
        store_lanes(o_ref, rt, acc)

    per_chunk(chunk, UNROLL)


def store_lanes(ref, rows, acc):
    for half in range(2):
        a, b = acc[2 * half], acc[2 * half + 1]
        full = jnp.concatenate([a[:, :128], a[:, 128:] + b[:, :128], b[:, 128:]], axis=1)
        ref[rows, 384 * half : 384 * half + 384] = full.astype(bf16)


def bwd_kernel(q_ref, do_ref, k_ref, v_ref, p_ref, gp_ref, ds_ref, dk_scr, dv_scr, *, scale):
    i = pl.program_id(0)
    width = 32 * HW

    @pl.when(i == 0)
    def _():
        dk_scr[...] = jnp.zeros_like(dk_scr)
        dv_scr[...] = jnp.zeros_like(dv_scr)

    def chunk(t):
        w = window_start(i * STEP + t)
        rt = chunk_rows(t)
        kwin = k_ref[pl.ds(w, WIN), :]
        vwin = v_ref[pl.ds(w, WIN), :]
        left = lax.broadcasted_iota(jnp.int32, (WIN, 128), 1) < 64
        spans = [slice(lane0, lane0 + 256) for lane0, _ in GROUPS]
        qm = [spread_heads(q_ref[rt, sl], lane0, h0) for sl, (lane0, h0) in zip(spans, GROUPS)]
        dom = [spread_heads(do_ref[rt, sl], lane0, h0) for sl, (lane0, h0) in zip(spans, GROUPS)]
        p_low = [p_ref[t, :, 256 * j : 256 * j + 256] for j in range(4)]
        dp = [dot(vwin[:, sl], v, NT) for sl, v in zip(spans, dom)]
        dv = [dot(a, b) for a, b in zip(p_low, dom)]
        pf = [v.astype(f32) for v in p_low]
        pd = [a * b for a, b in zip(pf, dp)]
        ds = [a - b * jnp.sum(a, axis=0, keepdims=True) for a, b in zip(pd, pf)]
        ds_low = [v.astype(bf16) for v in ds]
        full = [dot(v, kwin[:, sl], TN) for sl, v in zip(spans, ds_low)]
        dk = [dot(a, b) for a, b in zip(ds_low, qm)]
        acc = [own_rows(v, *GROUPS[j]) * scale for j, v in enumerate(full)]
        for j in (0, 2):
            for p in range(2):
                a, b = (ds[j + t][:, 128 * p : 128 * p + 128] for t in range(2))
                at = slice(64 * j, 64 * j + 128)
                ds_ref[t, 256 * p : 256 * p + WIN, at] = jnp.where(left, a, pltpu.roll(b, 64, 1)).astype(bf16)
                ds_ref[t, 256 * p + WIN : 256 * p + 256, at] = jnp.where(left, pltpu.roll(a, 64, 1), b).astype(bf16)
        for scr, parts in ((dk_scr, dk), (dv_scr, dv)):
            for half in range(2):
                a, b = parts[2 * half : 2 * half + 2]
                both = jnp.concatenate([a[:, :128], a[:, 128:] + b[:, :128], b[:, 128:]], axis=1)
                scr[pl.ds(w, WIN), 384 * half : 384 * half + 384] += both
        store_lanes(gp_ref, pl.ds(pl.multiple_of((i * STEP + t) * CH, CH), CH), acc)

    per_chunk(chunk, UNROLL)

    @pl.when(i == pl.num_programs(0) - 1)
    def _():
        gp_ref[:, width : 2 * width] = dk_scr[...].astype(bf16)
        gp_ref[:, 2 * width :] = dv_scr[...].astype(bf16)


def feat_kernel(n_before, last, ds_ref, f_ref, aw_ref, ac_ref, amat_ref, kcol_ref, *rest):
    before, (m0_ref, s_ref, *out_ref, rho_scr, gf_scr) = rest[:n_before], rest[n_before:]

    @pl.when(pl.program_id(0) == 0)
    def _():
        m0_ref[...] = before[0][...] if before else jnp.zeros_like(m0_ref)
        s_ref[...] = before[1][...] if before else jnp.zeros_like(s_ref)

    for u in range(FEAT_STEP):
        t = u
        rho = radius_of(ac_ref[chunk_rows(t), :], aw_ref[t])
        rho_scr[u] = jnp.concatenate([rho[8 * g : 8 * g + 8] for g in range(4)], axis=1)
    for u in range(FEAT_STEP):
        t = u
        for rb in range(4):
            span = slice(256 * rb, 256 * rb + 256)
            gf_scr[u, span, :] = dot(amat_ref[span, :], ds_ref[t], NT)
            m0_ref[span, :] += dot(f_ref[t, span, :], ds_ref[t])
            for kt in range(8):
                ks = slice(16 * kt, 16 * kt + 16)
                s1, s2 = s_ref[0, ks, :], s_ref[1, ks, :]
                for r in (2 * rb, 2 * rb + 1):
                    for g in range(4):
                        at = (u, slice(128 * r + 16 * kt, 128 * r + 16 * kt + 16), slice(128 * g, 128 * g + 128))
                        rr = rho_scr[u, r : r + 1, 128 * g : 128 * g + 128]
                        w = gf_scr[at] * f_ref[t, at[1], at[2]].astype(f32) * rr
                        s1 = s1 + w
                        s2 = s2 + w * rr
                s_ref[0, ks, :] = s1
                s_ref[1, ks, :] = s2

    if last:

        @pl.when(pl.program_id(0) == pl.num_programs(0) - 1)
        def _():
            out_ref[0][...] = kernel_grads(m0_ref, s_ref, kcol_ref[...])


def kernel_grads(m0_ref, s_ref, kcol):
    n = kcol.shape[0]
    lanes = lax.broadcasted_iota(jnp.int32, (n, 256), 1)
    m = jnp.zeros((n, 256), f32)
    for r in range(8):
        m = jnp.where(lanes % 8 == r, m0_ref[n * r : n * r + n, :], m)
    heads = lax.broadcasted_iota(jnp.int32, (256, 128), 0) // 8 == lax.broadcasted_iota(jnp.int32, (256, 128), 1)
    heads = heads.astype(f32).astype(bf16)
    g_map = sum(dot(v.astype(bf16), heads) for v in parts3(m))
    lanes = lanes[:, :128]
    s0 = jnp.sum(jnp.where(lanes < 32, g_map * kcol, 0.0), axis=-1, keepdims=True)
    s1 = jnp.sum(s_ref[0], axis=-1, keepdims=True)
    s2 = jnp.sum(s_ref[1], axis=-1, keepdims=True)
    mean, width = kcol[:, 32:33], kcol[:, 33:34]
    square = width * width
    g_mean = (s1 - mean * s0) / square
    g_width = ((s2 - 2.0 * mean * s1 + mean * mean * s0) / square - s0) / width
    return jnp.where(lanes == 32, g_mean, jnp.where(lanes == 33, g_width, g_map))


def cost(micros):
    return pl.CostEstimate(flops=int(micros * 1.1535e9), bytes_accessed=0, transcendentals=0)


def full_spec(shape):
    return pl.BlockSpec(shape, lambda i: (0,) * len(shape))


def params(limit=VM):
    return pltpu.CompilerParams(vmem_limit_bytes=limit, dimension_semantics=("arbitrary",))


BIAS_PARTS = 2
FWD_PARTS = 2
BWD_PARTS = 4
FEAT_PARTS = 4


def shifted(spec_shape, base):
    return pl.BlockSpec(spec_shape, lambda i: (i + base,) + (0,) * (len(spec_shape) - 1))


def half_spec(shape, part):
    return pl.BlockSpec(shape, lambda i: (part,) + (0,) * (len(shape) - 1))


def attn_bias(part, aw, ac, gmat, bmat, before):
    c = aw.shape[0]
    per = c // BIAS_PARTS // STEP
    base = part * per
    n_in = 4
    return pl.pallas_call(
        functools.partial(skip_refs, bias_kernel, n_in, len(before)),
        grid=(per,),
        in_specs=[
            shifted((STEP, 8, WIN), base), shifted((STEP * CH, 4), base), full_spec(gmat.shape), full_spec(bmat.shape),
        ] + [pl.BlockSpec(memory_space=pl.ANY)] * len(before),
        out_specs=[shifted((STEP, WIN, 1024), base), shifted((STEP, 1024, 4 * WIN), base)],
        out_shape=[jax.ShapeDtypeStruct((c, WIN, 1024), f32), jax.ShapeDtypeStruct((c, 1024, 4 * WIN), bf16)],
        scratch_shapes=[pltpu.VMEM((PAIR, 1024, WIN), f32)],
        input_output_aliases={n_in + t: t for t in range(len(before))},
        compiler_params=params(),
        cost_estimate=cost(24 // BIAS_PARTS),
        name="attn_bias",
    )(aw, ac, gmat, bmat, *before)


def attn_fwd(part, q, k, v, bias, before):
    rows, width = q.shape
    c = rows // CH
    per = c // FWD_PARTS // STEP
    base = part * per
    kv = half_spec((rows // FWD_PARTS, width), part)
    n_in = 4
    return pl.pallas_call(
        functools.partial(skip_refs, fwd_kernel, n_in, len(before)),
        grid=(per,),
        in_specs=[shifted((STEP * CH, width), base), kv, kv, shifted((STEP, WIN, 1024), base)]
        + [pl.BlockSpec(memory_space=pl.ANY)] * len(before),
        out_specs=[shifted((STEP * CH, width), base), shifted((STEP, WIN, 1024), base)],
        out_shape=[jax.ShapeDtypeStruct((rows, width), bf16), jax.ShapeDtypeStruct((c, WIN, 1024), bf16)],
        input_output_aliases={n_in + t: t for t in range(len(before))},
        compiler_params=params(),
        cost_estimate=cost(16 // FWD_PARTS),
        name="attn_fwd",
    )(q, k, v, bias, *before)


def skip_refs(kernel, n_in, n_before, *refs):
    kernel(*refs[:n_in], *refs[n_in + n_before :])


def attn_bwd(part, q, do, k, v, p, scale, before):
    rows, width = q.shape
    c = rows // CH
    per = c // BWD_PARTS // STEP
    base = part * per
    kv = half_spec((rows // BWD_PARTS, width), part)
    n_in = 5
    return pl.pallas_call(
        functools.partial(skip_refs, functools.partial(bwd_kernel, scale=scale), n_in, len(before)),
        grid=(per,),
        in_specs=[
            shifted((STEP * CH, width), base), shifted((STEP * CH, width), base), kv, kv,
            shifted((STEP, WIN, 1024), base),
        ] + [pl.BlockSpec(memory_space=pl.ANY)] * len(before),
        out_specs=[half_spec((rows // BWD_PARTS, 3 * width), part), shifted((STEP, 4 * WIN, 256), base)],
        out_shape=[jax.ShapeDtypeStruct((rows, 3 * width), bf16), jax.ShapeDtypeStruct((c, 4 * WIN, 256), bf16)],
        scratch_shapes=[pltpu.VMEM((rows // BWD_PARTS, width), f32)] * 2,
        input_output_aliases={n_in + t: t for t in range(len(before))},
        compiler_params=params(),
        cost_estimate=cost(24 // BWD_PARTS),
        name="attn_bwd",
    )(q, do, k, v, p, *before)


def attn_feat(part, ds, feats, aw, ac, amat, kcol, before):
    per = ds.shape[0] // FEAT_PARTS // FEAT_STEP
    base = part * per
    last = part == FEAT_PARTS - 1
    n = kcol.shape[0]
    shapes = [(1024, 256), (2, n, WIN)] + [(n, 128)] * last
    return pl.pallas_call(
        functools.partial(feat_kernel, len(before), last),
        grid=(per,),
        in_specs=[
            shifted((FEAT_STEP, 4 * WIN, 256), base), shifted((FEAT_STEP, 1024, 4 * WIN), base),
            shifted((FEAT_STEP, 8, WIN), base), shifted((FEAT_STEP * CH, 4), base),
            full_spec(amat.shape), full_spec(kcol.shape),
        ] + [full_spec(b.shape) for b in before],
        out_specs=[full_spec(s) for s in shapes],
        out_shape=[jax.ShapeDtypeStruct(s, f32) for s in shapes],
        scratch_shapes=[pltpu.VMEM((FEAT_STEP, 8, 4 * WIN), f32), pltpu.VMEM((FEAT_STEP, 1024, 4 * WIN), f32)],
        compiler_params=params(),
        cost_estimate=cost(32 // FEAT_PARTS),
        name="attn_feat",
    )(ds, feats, aw, ac, amat, kcol, *before)


def aux_of(coords, segment_ids):
    rows = coords.shape[1]
    place = jnp.arange(rows, dtype=jnp.int32) // SET
    key = (segment_ids * (rows // SET) + place).astype(f32)
    packed = jnp.concatenate([coords, key[None], jnp.zeros((4, rows), f32)], axis=0)
    half = SET
    starts = [b + min(max(i - 48, 0), half - WIN) for b in range(0, rows, half) for i in range(0, half, CH)]
    aw = jnp.stack([packed[:, s : s + WIN] for s in starts])
    ac = packed[:4].T
    return aw, ac


def split3(v):
    high = lax.reduce_precision(v, 8, 7)
    middle = lax.reduce_precision(v - high, 8, 7)
    return high, middle, lax.reduce_precision(v - high - middle, 8, 7)


def kernel_consts(mean, width, kmap):
    mean, width = mean.astype(f32), width.astype(f32)
    half = 0.5 * math.log2(math.e) / (width * width)
    ah, am, al = split3(-half)
    bh, bm, bl = split3(2.0 * half * mean)
    ch, cm, cl = split3(-half * mean * mean - jnp.log2(math.sqrt(2.0 * math.pi) * width))
    slots = jnp.stack([ah, am, ah, am, al, ah, bh, bm, bh, bm, bl, bh, ch, cm, cl, jnp.zeros_like(ah)], axis=1)
    eye = jnp.eye(8, dtype=f32)
    n, heads = kmap.shape
    gmat = (eye[:, None, None, :] * slots[None, :, :, None]).reshape(8 * n, 128).astype(bf16)
    amat = (eye[:, None, None, :] * kmap.astype(f32)[None, :, :, None]).reshape(8 * n, heads * 8).astype(bf16)
    kcol = jnp.concatenate([kmap.astype(f32), mean[:, None], width[:, None], jnp.zeros((n, 94), f32)], axis=1)
    return gmat, amat, kcol


TILE = 256
epsilon = 1e-05


def ln_parts(v):
    mean = jnp.mean(v, axis=-1, keepdims=True)
    centred = v - mean
    rstd = lax.rsqrt(jnp.mean(centred * centred, axis=-1, keepdims=True) + epsilon)
    return centred * rstd, rstd


def ln_back(xhat, rstd, dn, gain):
    dg = dn * gain
    m1 = jnp.mean(dg, axis=-1, keepdims=True)
    m2 = jnp.mean(dg * xhat, axis=-1, keepdims=True)
    return rstd * (dg - m1 - xhat * m2)


def rows_sum(v):
    return jnp.sum(v, axis=0, keepdims=True)


def fetch(idx_ref, pieces, moves, sem, base=0):
    copies = []
    for m, (piece, top) in enumerate(pieces):
        for dest, first, column, rows, columns in moves:
            at = pl.multiple_of(idx_ref[m] * rows, 16)
            copies.append(
                pltpu.make_async_copy(
                    piece.at[pl.ds(top + first, rows), :],
                    dest.at[pl.ds(at, rows), pl.ds(column, columns)],
                    sem.at[base + len(copies)],
                )
            )
    return copies


def fetch_whole(arrays, dests, sem):
    return [pltpu.make_async_copy(a, d, sem.at[i]) for i, (a, d) in enumerate(zip(arrays, dests))]


def qkv_copies(idx_ref, pieces, w_scr, sem):
    if len(pieces) == 1:
        return fetch_whole(pieces, [w_scr], sem)
    r, columns = pieces[0].shape
    return fetch(idx_ref, [(p, 0) for p in pieces], [(w_scr, 0, 0, r, columns)], sem)


def ffn_copies(idx_ref, pieces, wo, up, down, sem):
    if len(pieces) == 3:
        copies = fetch_whole(pieces, [wo, up, down], sem)
        return copies[:1], copies[1:]
    width = wo.shape[0]
    n = len(pieces) - 2
    r = width // n
    wide = up.shape[1] // width
    cut = (1 + wide) * r
    tops = [(p, 0) for p in pieces[:n]]
    lows = [(p, cut) for p in pieces[: n - 2]] + [(p, 0) for p in pieces[n:]]
    first = fetch(idx_ref, tops, [(wo, 0, 0, r, width)], sem)
    moves = [(up, r + b * r, b * width, r, width) for b in range(wide)]
    later = fetch(idx_ref, tops, moves, sem, len(first))
    return first, later + fetch(idx_ref, lows, [(down, 0, 0, wide * r, width)], sem, len(first) + len(later))


def any_spec():
    return pl.BlockSpec(memory_space=pl.ANY)


def row_spec(width, tile=TILE):
    return pl.BlockSpec((tile, width), lambda i, *_: (i, 0))


def whole_spec(shape):
    return pl.BlockSpec(shape, lambda i, *_: (0,) * len(shape))


def qkv_kernel(n, scale, idx_ref, x_ref, t_ref, vec_ref, *rest):
    pieces, (normed_ref, q_ref, k_ref, v_ref, w_scr, sem) = rest[:n], rest[n:]
    width = x_ref.shape[1]

    @pl.when(pl.program_id(0) == 0)
    def _():
        for c in qkv_copies(idx_ref, pieces, w_scr, sem):
            c.start()

    start = x_ref[...].astype(f32) + t_ref[...] * vec_ref[0:1, :]
    normed = (ln_parts(start)[0] * vec_ref[1:2, :] + vec_ref[2:3, :]).astype(bf16)
    normed_ref[...] = normed

    @pl.when(pl.program_id(0) == 0)
    def _():
        for c in qkv_copies(idx_ref, pieces, w_scr, sem):
            c.wait()

    q_ref[...] = ((dot(normed, w_scr[:, :width]) + vec_ref[3:4, :]) * scale).astype(bf16)
    k_ref[...] = dot(normed, w_scr[:, width : 2 * width]).astype(bf16)
    v_ref[...] = (dot(normed, w_scr[:, 2 * width :]) + vec_ref[4:5, :]).astype(bf16)


def qkv_forward(idx, x, t, vecs, pieces, scale):
    rows, width = x.shape
    n = len(pieces)
    out = jax.ShapeDtypeStruct((rows, width), bf16)
    return pl.pallas_call(
        functools.partial(qkv_kernel, n, scale),
        grid_spec=pltpu.PrefetchScalarGridSpec(
            num_scalar_prefetch=1,
            grid=(rows // TILE,),
            in_specs=[row_spec(width), row_spec(1), whole_spec(vecs.shape)] + [any_spec()] * n,
            out_specs=[row_spec(width)] * 4,
            scratch_shapes=[pltpu.VMEM((width, 3 * width), bf16), pltpu.SemaphoreType.DMA((n,))],
        ),
        out_shape=[out] * 4,
        compiler_params=params(),
        cost_estimate=cost(10),
        name="qkv_forward",
    )(idx, x, t, vecs, *pieces)


def gelu_parts(x):
    a = jnp.abs(x)
    t = 1.0 / (1.0 + (0.3275911 * math.sqrt(0.5)) * a)
    e = jnp.exp(-0.5 * x * x)
    poly = t * (0.254829592 + t * (-0.284496736 + t * (1.421413741 + t * (-1.453152027 + t * 1.061405429))))
    tail = 0.5 * poly * e
    cdf = jnp.where(x >= 0, 1.0 - tail, tail)
    return x * cdf, cdf + x * e * (1.0 / math.sqrt(2.0 * math.pi))


def split_cores(value, core, owners):
    rows, c = value.shape
    pairs = value.reshape(owners // 2, 2, rows // owners, c)
    even, odd = pairs[:, 0], pairs[:, 1]
    return jnp.where(core == 0, even, odd), jnp.where(core == 0, odd, even)


def ffn_kernel(n, split, steps, idx_ref, x_ref, t_ref, att_ref, cot_ref, vec_ref, upb_ref, *rest):
    pieces = rest[:n]
    (out_ref, ga_ref, gvec_ref, gupb_ref, gm_hbm, keep_hbm, send_hbm,
     wo, up, down, mid, n2, acc, gn2, hid, gp, stage_up, stage_down, sem, out_sem, gm_sem) = rest[n:]
    j = pl.program_id(0)
    rows, width = x_ref.shape
    fc = hid.shape[1]
    tiles = rows // TILE
    core = lax.rem(idx_ref[0], 2)
    r = width // split if split else 0

    def moves(step):
        slot = lax.rem(step, 2)
        if not split:
            return [
                pltpu.make_async_copy(stage_up.at[slot], keep_hbm.at[step], out_sem.at[slot, 0]),
                pltpu.make_async_copy(stage_down.at[slot], send_hbm.at[pl.ds(step * fc, fc), :], out_sem.at[slot, 2]),
            ]
        pairs = fc // (2 * steps * r)
        up_at = pl.ds(pl.multiple_of(step * r, r), r)
        down_at = pl.ds(steps * r, steps * r)
        copies = []
        for s, dest in enumerate((keep_hbm, send_hbm)):
            copies.append(pltpu.make_async_copy(stage_up.at[slot, s], dest.at[:, up_at, :], out_sem.at[slot, s]))
            copies.append(
                pltpu.make_async_copy(
                    stage_down.at[slot, s], dest.at[pl.ds(step * pairs, pairs), down_at, :], out_sem.at[slot, 2 + s]
                )
            )
        return copies

    def out_copies():
        if not split:
            return [pltpu.make_async_copy(stage_up.at[0], keep_hbm.at[steps], out_sem.at[0, 0])]
        at = pl.ds(2 * steps * r, r)
        return [
            pltpu.make_async_copy(stage_up.at[0, s], dest.at[:, at, :], out_sem.at[0, s])
            for s, dest in enumerate((keep_hbm, send_hbm))
        ]

    def put(stage, slot, value, owners):
        if not split:
            stage[slot] = value.astype(bf16)
            return
        keep, send = split_cores(value, core, owners)
        stage[slot, 0] = keep.astype(bf16)
        stage[slot, 1] = send.astype(bf16)

    @pl.when(j == 0)
    def _():
        first, later = ffn_copies(idx_ref, pieces, wo, up, down, sem)
        for c in first + later:
            c.start()
        for c in first:
            c.wait()
        for i in range(tiles):
            rs = pl.ds(i * TILE, TILE)
            start = x_ref[rs, :].astype(f32) + t_ref[rs, :] * vec_ref[0:1, :]
            middle = start + dot(att_ref[rs, :], wo[...]) + vec_ref[1:2, :]
            mid[rs, :] = middle
            acc[rs, :] = middle + vec_ref[4:5, :]
            gn2[rs, :] = jnp.zeros((TILE, width), f32)
            normed = (ln_parts(middle)[0] * vec_ref[2:3, :] + vec_ref[3:4, :]).astype(bf16)
            n2[rs, :] = normed
        for c in later:
            c.wait()

    @pl.when(j > 1)
    def _():
        for c in moves(j - 2):
            c.wait()

    f0 = pl.multiple_of(j * fc, fc)
    up_c = up[:, pl.ds(f0, fc)]
    down_c = down[pl.ds(f0, fc), :]
    upb = upb_ref[...]
    gb = jnp.zeros((1, fc), f32)
    ahead = []

    def enter(i):
        rs = pl.ds(i * TILE, TILE)
        ahead.append((dot(n2[rs, :], up_c), dot(cot_ref[rs, :], down_c, NT)))

    enter(0)
    for i in range(tiles):
        rs = pl.ds(i * TILE, TILE)
        if i + 1 < tiles:
            enter(i + 1)
        pre, gh = ahead[i]
        h, slope = gelu_parts(pre + upb)
        h = h.astype(bf16)
        g = (gh * slope).astype(bf16)
        hid[rs, :] = h
        gp[rs, :] = g
        gb = gb + rows_sum(g.astype(f32))
        acc[rs, :] += dot(h, down_c)
        gn2[rs, :] += dot(g, up_c, NT)
    gupb_ref[...] = gb
    slot = lax.rem(j, 2)
    put(stage_down, slot, dot(hid[...], cot_ref[...], TN), 2 * (fc // (2 * steps * r)) if split else 0)
    put(stage_up, slot, dot(n2[...], gp[...], TN), split)
    for c in moves(j):
        c.start()

    @pl.when(j == steps - 1)
    def _():
        sums = [jnp.zeros((1, width), f32)] * 4
        for i in range(tiles):
            rs = pl.ds(i * TILE, TILE)
            out_ref[rs, :] = acc[rs, :].astype(bf16)
            xhat, rstd = ln_parts(mid[rs, :])
            dn = gn2[rs, :]
            cot = cot_ref[rs, :].astype(f32)
            gm = cot + ln_back(xhat, rstd, dn, vec_ref[2:3, :])
            mid[rs, :] = gm
            ga = gm.astype(bf16)
            hid[rs, :] = ga
            ga_ref[rs, :] = dot(ga, wo[...], NT).astype(bf16)
            sums = [s + rows_sum(v) for s, v in zip(sums, (dn * xhat, dn, cot, ga.astype(f32)))]
        gvec_ref[...] = jnp.concatenate(sums + [jnp.zeros((4, width), f32)], axis=0)
        mid_copy = pltpu.make_async_copy(mid, gm_hbm, gm_sem)
        mid_copy.start()
        grad_out = dot(att_ref[...], hid[...], TN)
        for c in moves(j - 1) + moves(j):
            c.wait()
        put(stage_up, 0, grad_out, split)
        last = out_copies()
        for c in last:
            c.start()
        for c in last:
            c.wait()
        mid_copy.wait()


def ffn_both(idx, x, t, att, cot, vecs, upb, pieces, ff, split):
    rows, width = x.shape
    n = len(pieces)
    fc = width
    steps = ff // fc
    sd = jax.ShapeDtypeStruct
    V = pltpu.VMEM
    if split:
        half = split // 2
        r = width // split
        grads = [sd((half, (2 * steps + 1) * r, width), bf16)] * 2
        stages = [V((2, 2, half, r, width), bf16), V((2, 2, fc // (2 * steps * r), steps * r, width), bf16)]
    else:
        grads = [sd((steps + 1, width, width), bf16), sd((ff, width), bf16)]
        stages = [V((2, width, width), bf16)] * 2
    return pl.pallas_call(
        functools.partial(ffn_kernel, n, split, steps),
        grid_spec=pltpu.PrefetchScalarGridSpec(
            num_scalar_prefetch=1,
            grid=(steps,),
            in_specs=[whole_spec((rows, width)), whole_spec((rows, 1)), whole_spec((rows, width)), whole_spec((rows, width)),
                      whole_spec(vecs.shape), pl.BlockSpec((1, fc), lambda j, *_: (0, j))] + [any_spec()] * n,
            out_specs=[whole_spec((rows, width)), whole_spec((rows, width)), whole_spec((8, width)),
                       pl.BlockSpec((1, fc), lambda j, *_: (0, j)), any_spec(), any_spec(), any_spec()],
            scratch_shapes=[V((width, width), bf16), V((width, ff), bf16), V((ff, width), bf16),
                            V((rows, width), f32), V((rows, width), bf16),
                            V((rows, width), f32), V((rows, width), f32),
                            V((rows, fc), bf16), V((rows, fc), bf16), *stages,
                            pltpu.SemaphoreType.DMA((6 * n,)), pltpu.SemaphoreType.DMA((2, 4)), pltpu.SemaphoreType.DMA],
        ),
        out_shape=[sd((rows, width), bf16), sd((rows, width), bf16), sd((8, width), f32), sd((1, ff), f32),
                   sd((rows, width), f32), *grads],
        compiler_params=params(),
        cost_estimate=cost(60),
        name="ffn_both",
    )(idx, x, t, att, cot, vecs, upb, *pieces)


def gqkv_kernel(split, idx_ref, normed_ref, gp_ref, *rest):
    outs, nt = rest[:-1], rest[-1]

    @pl.when(pl.program_id(0) == 0)
    def _():
        nt[...] = normed_ref[...].T

    grad = dot(nt[...], gp_ref[...])
    if split:
        keep, send = split_cores(grad, lax.rem(idx_ref[0], 2), split)
        outs[0][...] = keep.astype(bf16)
        outs[1][...] = send.astype(bf16)
    else:
        outs[0][0] = grad.astype(bf16)


def qkv_weight_grad(idx, normed, gp, split):
    rows, width = normed.shape
    sd = jax.ShapeDtypeStruct
    if split:
        half, r = split // 2, width // split
        out_specs = [pl.BlockSpec((half, r, width), lambda j, *_: (0, j, 0))] * 2
        out_shape = [sd((half, 3 * r, width), bf16)] * 2
    else:
        out_specs = [pl.BlockSpec((1, width, width), lambda j, *_: (j, 0, 0))]
        out_shape = [sd((3, width, width), bf16)]
    return pl.pallas_call(
        functools.partial(gqkv_kernel, split),
        grid_spec=pltpu.PrefetchScalarGridSpec(
            num_scalar_prefetch=1,
            grid=(3,),
            in_specs=[whole_spec((rows, width)), pl.BlockSpec((rows, width), lambda j, *_: (0, j))],
            out_specs=out_specs,
            scratch_shapes=[pltpu.VMEM((width, rows), bf16)],
        ),
        out_shape=out_shape,
        compiler_params=params(),
        cost_estimate=cost(8),
        name="qkv_weight_grad",
    )(idx, normed, gp)


def first_kernel(n, idx_ref, x_ref, t_ref, gm_ref, gp_ref, vec_ref, *rest):
    pieces, (gi_ref, gvec_ref, w_scr, sem) = rest[:n], rest[n:]
    i = pl.program_id(0)
    width = x_ref.shape[1]

    @pl.when(i == 0)
    def _():
        for c in qkv_copies(idx_ref, pieces, w_scr, sem):
            c.start()
        gvec_ref[...] = jnp.zeros_like(gvec_ref)
        for c in qkv_copies(idx_ref, pieces, w_scr, sem):
            c.wait()

    t = t_ref[...]
    dn = dot(gp_ref[...], w_scr[...], NT)
    start = x_ref[...].astype(f32) + t * vec_ref[0:1, :]
    xhat, rstd = ln_parts(start)
    gs = gm_ref[...] + ln_back(xhat, rstd, dn, vec_ref[1:2, :])
    gi_ref[...] = gs.astype(bf16)
    parts = [t * gs, dn * xhat, dn, gp_ref[:, :width].astype(f32), gp_ref[:, 2 * width :].astype(f32)]
    gvec_ref[...] += jnp.concatenate([rows_sum(v) for v in parts] + [jnp.zeros((3, width), f32)], axis=0)


def first_backward(idx, x, t, gm, gp, vecs, pieces):
    rows, width = x.shape
    n = len(pieces)
    sd = jax.ShapeDtypeStruct
    return pl.pallas_call(
        functools.partial(first_kernel, n),
        grid_spec=pltpu.PrefetchScalarGridSpec(
            num_scalar_prefetch=1,
            grid=(rows // TILE,),
            in_specs=[row_spec(width), row_spec(1), row_spec(width), row_spec(3 * width), whole_spec(vecs.shape)] + [any_spec()] * n,
            out_specs=[row_spec(width), whole_spec((8, width))],
            scratch_shapes=[pltpu.VMEM((width, 3 * width), bf16), pltpu.SemaphoreType.DMA((n,))],
        ),
        out_shape=[sd((rows, width), bf16), sd((8, width), f32)],
        compiler_params=params(),
        cost_estimate=cost(11),
        name="first_backward",
    )(idx, x, t, gm, gp, vecs, *pieces)


SHARDS = 8


def swap(value, axis, size, bit_mask):
    return lax.ppermute(value, axis, [(i, i ^ bit_mask) for i in range(size)])


def near(value):
    return swap(value, "fsdp", SHARDS, 1)


def along_x(value):
    return swap(value, "fsdp", SHARDS, 2)


def along_y(value):
    return swap(value, "fsdp", SHARDS, 4)


def with_near(far):
    pieces = []
    for piece in far:
        pieces += [piece, near(piece)]
    return pieces


def in_order(pieces, order):
    stacked = pieces.astype(f32)
    hit = (jnp.arange(stacked.shape[0])[:, None] == order[None, :]).astype(f32)
    return jnp.sum(hit.reshape(hit.shape + (1,) * (stacked.ndim - 1)) * stacked[None], axis=1)


def blocks_of(weight, width):
    r = weight.shape[0]
    return jnp.transpose(weight.reshape(r, -1, width), (1, 0, 2)).reshape(-1, width)


def far_first(kept, came, spot):
    place = spot // 2
    cut = kept.shape[1] // 32 * 16

    def total(mask, rows):
        pick = lambda v: lax.dynamic_index_in_dim(v, place ^ mask, 0, keepdims=False)[rows].astype(f32)
        return (pick(kept) + pick(came)).astype(kept.dtype)

    top, low = slice(None, cut), slice(cut, None)
    stay = (total(0, top), total(2, top), total(0, low), total(1, low))
    go_x = jnp.stack([total(1, top), total(3, top)])
    go_y = jnp.stack([total(2, low), total(3, low)])
    return stay, go_x, go_y


def add_low(a, b):
    return (a.astype(f32) + b.astype(f32)).astype(a.dtype)


def far_second(stay, from_x, from_y):
    own_top, y_top, own_low, x_low = stay
    return (add_low(own_top, from_x[0]), add_low(own_low, from_y[0])), add_low(y_top, from_x[1]), add_low(x_low, from_y[1])


def far_third(own, from_y, from_x):
    return jnp.concatenate([add_low(own[0], from_y), add_low(own[1], from_x)])


def halves(owned, spot):
    parts = owned.reshape(2, owned.shape[0] // 2, owned.shape[1])
    side = spot % 2
    return (
        lax.dynamic_index_in_dim(parts, side, 0, keepdims=False),
        lax.dynamic_index_in_dim(parts, 1 - side, 0, keepdims=False),
    )


def rows_first(kept, sent, size):
    return add_low(kept, swap(sent, "dp", size, 1))


def rows_middle(half, size):
    step = 2
    while step < size:
        half = add_low(half, swap(half, "dp", size, step))
        step *= 2
    return half


def rows_last(half, size, spot):
    other = swap(half, "dp", size, 1)
    even = spot % 2 == 0
    return jnp.concatenate([jnp.where(even, half, other), jnp.where(even, other, half)]).astype(f32)


def sum_owned(packed, spot, size):
    if size != SHARDS:
        return lax.psum_scatter(packed, "fsdp", scatter_dimension=0)
    total = lax.dynamic_index_in_dim(packed, spot, 0, keepdims=False)
    for m in range(1, size):
        total = total + swap(lax.dynamic_index_in_dim(packed, spot ^ m, 0, keepdims=False), "fsdp", size, m)
    return total


def sum_planes(value, size):
    terms = [value] + [swap(value, "dp", size, m) for m in range(1, size)]
    while len(terms) > 1:
        terms = [a + b for a, b in zip(terms[::2], terms[1::2])]
    return terms[0]


def on_device(
    sizes,
    inputs,
    time_of_row,
    coords,
    segment_ids,
    cotangent,
    time_weight,
    ln1_gain,
    ln1_bias,
    w_qkv,
    q_bias,
    v_bias,
    w_out,
    out_bias,
    kernel_mean,
    kernel_width,
    kernel_map,
    ln2_gain,
    ln2_bias,
    w_up,
    up_bias,
    w_down,
    down_bias,
):
    n, planes = sizes
    direct = n == SHARDS
    split = n if direct else 0
    barrier = lax.optimization_barrier
    spot = lax.axis_index("fsdp")
    level = lax.axis_index("dp")
    order = (spot ^ jnp.arange(n)).astype(jnp.int32)
    width = inputs.shape[1]
    r = w_qkv.shape[0]
    heads = kernel_map.shape[1]
    own_kernels = kernel_map.shape[0]
    kernels = own_kernels * n
    wide = up_bias.shape[0] // r
    ff = n * wide * r
    scale = (width // heads) ** (-0.5)
    times = time_of_row[:, None]

    kernel_cols = jnp.concatenate([kernel_map, kernel_mean[:, None], kernel_width[:, None]], axis=1)
    vectors = (time_weight, ln1_gain, ln1_bias, q_bias, v_bias, out_bias, ln2_gain, ln2_bias, down_bias)
    vectors = jnp.concatenate([jnp.stack(vectors), up_bias.reshape(wide, r)])
    if direct:
        lanes = 128
        small = jnp.concatenate(
            [jnp.pad(v, ((0, 0), (0, lanes - v.shape[1]))) for v in (kernel_cols, vectors)]
        )
        pair = jnp.stack([small, near(small)])
        pair, w_first, w_second, coords, segment_ids, times = barrier(
            (pair, w_qkv, (w_out, w_up, w_down), coords, segment_ids, times)
        )
        small_far = [swap(pair, "fsdp", n, 2 * m) for m in range(1, n // 2)]
        qkv_far = [w_first] + [swap(w_first, "fsdp", n, 2 * m) for m in range(1, n // 2)]
        second = jnp.concatenate([w_second[0], blocks_of(w_second[1], width), w_second[2]])
        small_all = in_order(jnp.concatenate([pair] + small_far), order)
        kernel_cols, vectors = small_all[:, :own_kernels], small_all[:, own_kernels:, :r]
    else:
        kernel_cols = lax.all_gather(kernel_cols, "fsdp", axis=0).astype(f32)
        vectors = lax.all_gather(vectors, "fsdp", axis=0).astype(f32)
        qkv_p = (lax.all_gather(w_qkv, "fsdp", axis=0, tiled=True),)
        ffn_p = tuple(lax.all_gather(w, "fsdp", axis=0, tiled=True) for w in (w_out, w_up, w_down))
    kernel_cols = kernel_cols.reshape(kernels, -1)

    aux_win, aux_col = aux_of(coords, segment_ids)
    gmat, amat, kernel_columns = kernel_consts(
        kernel_cols[:, heads], kernel_cols[:, heads + 1], kernel_cols[:, :heads].astype(bf16)
    )
    bmat = amat.T
    done = attn_bias(0, aux_win, aux_col, gmat, bmat, ())
    if direct:
        done, second, qkv_far = barrier((done, second, qkv_far))
        qkv_p = tuple(with_near(qkv_far))
        from_x, from_y = along_x(second), along_y(second)
    bias, feats = attn_bias(1, aux_win, aux_col, gmat, bmat, done)
    vecs = jnp.transpose(vectors[:, :9], (1, 0, 2)).reshape(9, width)
    up_bias_all = vectors[:, 9:].reshape(1, ff)

    def rows_of(*picked):
        return jnp.concatenate([vecs[p : p + 1] for p in picked] + [jnp.zeros((8 - len(picked), width), f32)])

    first_rows, ffn_rows, back_rows = rows_of(0, 1, 2, 3, 4), rows_of(0, 5, 6, 7, 8), rows_of(0, 1)
    if direct:
        bias, qkv_p, ready = barrier((bias, qkv_p, (first_rows, ffn_rows, back_rows, up_bias_all, amat, kernel_columns)))
        first_rows, ffn_rows, back_rows, up_bias_all, amat, kernel_columns = ready
    normed, queries, keys, values = qkv_forward(order, inputs, times, first_rows, qkv_p, scale)
    if direct:
        cut = (1 + wide) * r
        queries, from_x, from_y = barrier((queries, from_x, from_y))
        top_d, low_d = along_y(from_x[:cut]), along_x(from_y[cut:])
        ffn_p = with_near((second, from_x, from_y))
    attended, probs = attn_fwd(1, queries, keys, values, bias, attn_fwd(0, queries, keys, values, bias, ()))
    if direct:
        attended, top_d, low_d, ffn_p = barrier((attended, top_d, low_d, ffn_p))
        ffn_p = tuple(ffn_p + with_near((top_d, low_d)))

    output, grad_attended, ffn_vecs, grad_up_bias, grad_middle, ffn_keep, ffn_send = ffn_both(
        order, inputs, times, attended, cotangent, ffn_rows, up_bias_all, ffn_p, ff, split
    )
    up_rows = wide * r

    def backward(part, before):
        return attn_bwd(part, queries, grad_attended, keys, values, probs, scale, before)

    def feat(part, before):
        return attn_feat(part, grad_scores, feats, aux_win, aux_col, amat, kernel_columns, before)

    def scattered(array, blocks):
        owned = lax.psum_scatter(array.reshape(blocks, n, -1, width), "fsdp", scatter_dimension=1)
        return owned.reshape(-1, width)

    if direct:
        ffn_came = near(ffn_send)
        done = backward(0, ())
        done, a = barrier((done, far_first(ffn_keep, ffn_came, spot)))
        a = (a[0], along_x(a[1]), along_y(a[2]))
        grad_projected, grad_scores = backward(3, backward(2, backward(1, done)))
        qkv_keep, qkv_send = qkv_weight_grad(order, normed, grad_projected, split)
        qkv_keep, qkv_send, a = barrier((qkv_keep, qkv_send, far_second(*a)))
        a = (a[0], along_y(a[1]), along_x(a[2]))
        c = far_first(qkv_keep, near(qkv_send), spot)
    else:
        grad_projected, grad_scores = backward(3, backward(2, backward(1, backward(0, ()))))
        a = jnp.concatenate([scattered(ffn_keep[:wide], wide), scattered(ffn_send, 1), scattered(ffn_keep[wide:], 1)])
        c = scattered(qkv_weight_grad(order, normed, grad_projected, split)[0], 3)
    grad_inputs, first_vecs = first_backward(
        order, inputs, times, grad_middle, grad_projected, back_rows, qkv_p
    )
    if direct:
        grad_scores, first_vecs, a, c = barrier((grad_scores, first_vecs, far_third(*a), c))
        c = (c[0], along_x(c[1]), along_y(c[2]))
    a = lax.psum(a, "dp")

    sums = feat(0, ())
    if direct:
        sums, c = barrier((sums, far_second(*c)))
        c = (c[0], along_y(c[1]), along_x(c[2]))
    sums = feat(1, sums)
    if direct:
        c = far_third(*c)
    sums, c = barrier((sums, halves(c, level)))
    c = rows_first(*c, planes)
    sums = feat(2, sums)
    sums, c = barrier((sums, c))
    c = rows_middle(c, planes)
    kernel_part = feat(3, sums)[2].reshape(n, own_kernels, -1)
    kernel_part, c = barrier((kernel_part, c))

    grad_rows = [first_vecs[:5], ffn_vecs[3:4], ffn_vecs[:3]]
    vector_rows = jnp.transpose(jnp.concatenate(grad_rows).reshape(9, n, r), (1, 0, 2))
    vector_rows = jnp.concatenate([vector_rows, grad_up_bias.reshape(n, wide, r)], axis=1)
    vector_rows = jnp.pad(vector_rows, ((0, 0), (0, 0), (0, kernel_part.shape[2] - r)))
    small, a = barrier((sum_owned(jnp.concatenate([kernel_part, vector_rows], axis=1), spot, n), a))
    small = sum_planes(small, planes)
    gaussians, vectors = small[:own_kernels], small[own_kernels:, :r]
    grad_qkv = rows_last(c, planes, level)
    grad_up, grad_down, grad_out = a[:up_rows], a[up_rows : 2 * up_rows], a[2 * up_rows :]

    def columns(array):
        return jnp.transpose(array.reshape(-1, r, width), (1, 0, 2)).reshape(r, -1)

    return (
        output,
        grad_inputs,
        vectors[0],
        vectors[1],
        vectors[2],
        columns(grad_qkv),
        vectors[3],
        vectors[4],
        grad_out.astype(f32),
        vectors[5],
        gaussians[:, heads],
        gaussians[:, heads + 1],
        gaussians[:, :heads],
        vectors[6],
        vectors[7],
        columns(grad_up).astype(f32),
        vectors[9:].reshape(up_rows),
        grad_down.astype(f32),
        vectors[8],
    )


def solution(mesh):
    rows, split, whole = P(("fsdp", "dp"), None), P("fsdp"), P("fsdp", None)
    placed = (
        rows,
        P(("fsdp", "dp")),
        P(None, ("fsdp", "dp")),
        P(("fsdp", "dp")),
        rows,
        split,
        split,
        split,
        whole,
        split,
        split,
        whole,
        split,
        split,
        split,
        whole,
        split,
        split,
        whole,
        split,
        whole,
        split,
    )
    out_placed = (
        rows,
        rows,
        split,
        split,
        split,
        whole,
        split,
        split,
        whole,
        split,
        split,
        split,
        whole,
        split,
        split,
        whole,
        split,
        whole,
        split,
    )
    return jax.shard_map(
        functools.partial(on_device, (mesh.shape["fsdp"], mesh.shape["dp"])),
        mesh=mesh,
        in_specs=placed,
        out_specs=out_placed,
        check_vma=False,
    )
```

time: 424 us -> 351 us (0.83)
  Pallas kernels: 288 us -> 207 us
  between operations: 1.68 us -> 15 us
  starting transfers between devices: 47.6 us -> 39 us
  other arithmetic: 21.6 us -> 27.3 us
  waiting for transfers between devices: 35.6 us -> 30.7 us
    pallas_call x4, Pallas kernels: 61.4 us -> 32.7 us  [attn_bwd(): pl.pallas_call(functools.partial(skip_refs, functools.partial(bwd_kernel,...]
    pallas_call x4 -> x2, Pallas kernels: 44.6 us -> 22.2 us  [attn_fwd(): pl.pallas_call(functools.partial(skip_refs, fwd_kernel, n_in, len(before)...]
    pallas_call x1, Pallas kernels: 71 us -> 55.1 us  [ffn_both(): pl.pallas_call(functools.partial(ffn_kernel, n, split, steps), grid_spec=...]
    pallas_call x5 -> x6, Pallas kernels: 80.6 us -> 66.2 us  [the longest x4 40.1 us: attn_feat(): pl.pallas_call(functools.partial(feat_kernel, len(before), last), grid=(p...]
    ppermute x53 -> x43, starting transfers between devices: 47.6 us -> 38.9 us  [swap(): return lax.ppermute(value, axis, [(i, i ^ bit_mask) for i in range(size)])]
    ppermute x53 -> x43, waiting for transfers between devices: 35.6 us -> 30.6 us  [swap(): return lax.ppermute(value, axis, [(i, i ^ bit_mask) for i in range(size)])]
  transfers between devices with their start and end apart: 53 -> 44, of which waited for: 13 -> 13; matrix products, arithmetic and copies ran while one was open for 6% -> 10% of each run, Pallas kernels for 47% -> 44%
where the time goes in v3:
time: 351 us; the launch traced here: 347 us
  Pallas kernels  207 us (59%)
  starting transfers between devices  39 us (11%)
  waiting for transfers between devices  30.7 us (9%)
  local copies, waits for them, and re-layouts  28.2 us (8%)
  other arithmetic  27.3 us (8%)
  between operations  15 us (4%)
    pallas_call x1, Pallas kernels, ffn_both(): pl.pallas_call(functools.partial(ffn_kernel, n, split, steps), grid_spec=...  55.1 us
    pallas_call x4, Pallas kernels, attn_feat(): pl.pallas_call(functools.partial(feat_kernel, len(before), last), grid=(p...  40.1 us
    ppermute x43, starting transfers between devices, swap(): return lax.ppermute(value, axis, [(i, i ^ bit_mask) for i in range(size)])  38.9 us
    pallas_call x4, Pallas kernels, attn_bwd(): pl.pallas_call(functools.partial(skip_refs, functools.partial(bwd_kernel,...  32.7 us
    ppermute x43, waiting for transfers between devices, swap(): return lax.ppermute(value, axis, [(i, i ^ bit_mask) for i in range(size)])  30.6 us
    pallas_call x2, Pallas kernels, attn_bias(): pl.pallas_call(functools.partial(skip_refs, bias_kernel, n_in, len(before...  26.1 us
    pallas_call x2, Pallas kernels, attn_fwd(): pl.pallas_call(functools.partial(skip_refs, fwd_kernel, n_in, len(before)...  22.2 us
    pallas_call x1, Pallas kernels, first_backward(): pl.pallas_call(functools.partial(first_kernel, n), grid_spec=pltpu.Prefet...  11.6 us
  transfers between devices with their start and end apart: 44, of which 13 were waited for; matrix products, arithmetic and copies ran while one was open for 10% of the time, Pallas kernels for 44%

profile of v3, /device:TPU:0, one launch (start us, length us, event | category | flops | bytes accessed | tf_op | source)
XLA Modules:
  0.0 347.0 jit_solution(4280858870798695890)
XLA Ops:
  10.3 1.5 concatenate.57
  13.2 2.9 collective-permute-start.1
  16.1 1.5 collective-permute-start.2
  17.7 1.9 collective-permute-start.4
  19.6 1.5 collective-permute-start.5
  23.8 1.1 copy.258
  25.7 1.3 copy.216
  27.0 1.1 copy.238.t_ref
  29.7 0.8 copy.236.refs_2_
  30.8 0.9 copy.259
  31.7 13.1 %attn_bias.2 = (f32[32,128,1024]{2,1,0:T(8,128)}, bf16[32,1024,512]{2,1,0:T(8,128)(2,1)}) custom-call(f32[32,8,128]{2,1,0:T(8,128)} %copy-done.1, f32[1024,4]{1,0:T(8,128)} %bitcast.285, bf16[1024,128]{1,0:T(8,128)(2,1)} %copy.236.refs_2_, bf16[256,1024]{1,0:T(8,128)(2,1)} %bitcast.291), custom_call_target="tpu_custom_call" | custom-call | flops 13841999872 | tf_op jit(solution)/shard_map/attn_bias/pallas_call | solution.py:283
  49.2 1.9 collective-permute-start.11
  51.2 1.5 collective-permute-start.12
  53.3 13.0 %attn_bias.3 = (f32[32,128,1024]{2,1,0:T(8,128)}, bf16[32,1024,512]{2,1,0:T(8,128)(2,1)}) custom-call(f32[32,8,128]{2,1,0:T(8,128)} %copy-done.1, f32[1024,4]{1,0:T(8,128)} %bitcast.286, bf16[1024,128]{1,0:T(8,128)(2,1)} %copy.236.refs_2_, bf16[256,1024]{1,0:T(8,128)(2,1)} %bitcast.292, ...), custom_call_target="tpu_custom_call", output_to_operand_aliasing={{0}: (4, {}), {1}: (5, {})} | custom-call | flops 13841999872 | tf_op jit(solution)/shard_map/attn_bias/pallas_call | solution.py:283
  67.5 10.2 %qkv_forward.1 = (bf16[1024,768]{1,0:T(8,128)(2,1)}, bf16[1024,768]{1,0:T(8,128)(2,1)}, bf16[1024,768]{1,0:T(8,128)(2,1)}, bf16[1024,768]{1,0:T(8,128)(2,1)}) custom-call(s32[8]{0:T(128)} %copy-done.9, bf16[1024,768]{1,0:T(8,128)(2,1)} %x_ref.5, f32[1024,1]{1,0:T(8,128)} %copy.238.t_ref, f32[8,768]{1,0:T(8,128)} %concatenate.63.vec_ref, ...), custom_call_target="tpu_custom_call" | custom-call | flops 11534999552 | tf_op jit(solution)/shard_map/qkv_forward/pallas_call | solution.py:508
  77.7 3.4 collective-permute-done.11.rest_2_
  81.1 1.5 collective-permute-done.12.rest_4_
  82.5 1.2 slice.443
  84.3 1.1 slice.444
  85.4 1.6 collective-permute-start.13
  87.5 11.1 %attn_fwd.2 = (bf16[1024,768]{1,0:T(8,128)(2,1)}, bf16[32,128,1024]{2,1,0:T(8,128)(2,1)}) custom-call(bf16[1024,768]{1,0:T(8,128)(2,1)} %get-tuple-element.167.refs_0_, bf16[1024,768]{1,0:T(8,128)(2,1)} %get-tuple-element.168.refs_1_.refs_2_, bf16[1024,768]{1,0:T(8,128)(2,1)} %get-tuple-element.169.refs_2_.refs_3_, f32[32,128,1024]{2,1,0:T(8,128)} %get-tuple-element.170.refs_3_), custom_call_target="tpu_custom_call" | custom-call | flops 9228000256 | tf_op jit(solution)/shard_map/attn_fwd/pallas_call | solution.py:306
  98.6 11.1 %attn_fwd.3 = (bf16[1024,768]{1,0:T(8,128)(2,1)}, bf16[32,128,1024]{2,1,0:T(8,128)(2,1)}) custom-call(bf16[1024,768]{1,0:T(8,128)(2,1)} %get-tuple-element.167.refs_0_, bf16[1024,768]{1,0:T(8,128)(2,1)} %get-tuple-element.168.refs_1_.refs_2_, bf16[1024,768]{1,0:T(8,128)(2,1)} %get-tuple-element.169.refs_2_.refs_3_, ...), custom_call_target="tpu_custom_call", output_to_operand_aliasing={{0}: (4, {}), {1}: (5, {})} | custom-call | flops 9228000256 | tf_op jit(solution)/shard_map/attn_fwd/pallas_call | solution.py:306
  110.3 2.8 collective-permute-done.19.rest_9_
  113.9 0.9 copy-done.11
  114.8 55.1 %ffn_both.1 = (bf16[1024,768]{1,0:T(8,128)(2,1)}, bf16[1024,768]{1,0:T(8,128)(2,1)}, f32[8,768]{1,0:T(8,128)}, f32[1,3072]{1,0:T(1,128)}, f32[1024,768]{1,0:T(8,...) custom-call(s32[8]{0:T(128)} %copy-done.9, bf16[1024,768]{1,0:T(8,128)(2,1)} %x_ref.5, ...), custom_call_target="tpu_custom_call" | custom-call | flops 69209997312 | tf_op jit(solution)/shard_map/ffn_both/pallas_call | solution.py:690
  170.1 1.0 copy.243.amat_ref
  173.1 1.4 reduce.43
  174.6 8.2 %attn_bwd.4 = (bf16[1024,2304]{1,0:T(8,128)(2,1)}, bf16[32,512,256]{2,1,0:T(8,128)(2,1)}) custom-call(bf16[1024,768]{1,0:T(8,128)(2,1)} %get-tuple-element.167.refs_0_, bf16[1024,768]{1,0:T(8,128)(2,1)} %get-tuple-element.189.refs_1_, bf16[1024,768]{1,0:T(8,128)(2,1)} %get-tuple-element.168.refs_1_.refs_2_, ...), custom_call_target="tpu_custom_call" | custom-call | flops 6920999936 | tf_op jit(solution)/shard_map/attn_bwd/pallas_call | solution.py:331
  182.8 5.2 %add_convert_fusion.3 = (bf16[1,432,768]{2,1,0:T(8,128)(2,1)S(1)}, bf16[1,432,768]{2,1,0:T(8,128)(2,1)S(1)}, bf16[432,768]{1,0:T(8,128)(2,1)S(1)}, bf16[432,768]...) fusion(bf16[4,864,768]{2,1,0:T(8,128)(2,1)} %collective-permute, ...), kind=kLoop, calls=%fused_computation.15 | loop fusion | flops 10616832 | bytes 15925268 | tf_op jit(solution)/shard_map/convert_element_type | solution.py:841
  188.0 1.3 pad_maximum_fusion.1
  189.6 1.7 collective-permute-start.21
  191.3 8.1 %attn_bwd.5 = (bf16[1024,2304]{1,0:T(8,128)(2,1)}, bf16[32,512,256]{2,1,0:T(8,128)(2,1)}) custom-call(bf16[1024,768]{1,0:T(8,128)(2,1)} %get-tuple-element.167.refs_0_, bf16[1024,768]{1,0:T(8,128)(2,1)} %get-tuple-element.189.refs_1_, bf16[1024,768]{1,0:T(8,128)(2,1)} %get-tuple-element.168.refs_1_.refs_2_, ...), custom_call_target="tpu_custom_call", output_to_operand_aliasing={{0}: (5, {}), {1}: (6, {})} | custom-call | flops 6920999936 | tf_op jit(solution)/shard_map/attn_bwd/pallas_call | solution.py:331
  199.5 8.1 %attn_bwd.6 = (bf16[1024,2304]{1,0:T(8,128)(2,1)}, bf16[32,512,256]{2,1,0:T(8,128)(2,1)}) custom-call(bf16[1024,768]{1,0:T(8,128)(2,1)} %get-tuple-element.167.refs_0_, bf16[1024,768]{1,0:T(8,128)(2,1)} %get-tuple-element.189.refs_1_, bf16[1024,768]{1,0:T(8,128)(2,1)} %get-tuple-element.168.refs_1_.refs_2_, ...), custom_call_target="tpu_custom_call", output_to_operand_aliasing={{0}: (5, {}), {1}: (6, {})} | custom-call | flops 6920999936 | tf_op jit(solution)/shard_map/attn_bwd/pallas_call | solution.py:331
  207.6 8.2 %attn_bwd.7 = (bf16[1024,2304]{1,0:T(8,128)(2,1)}, bf16[32,512,256]{2,1,0:T(8,128)(2,1)}) custom-call(bf16[1024,768]{1,0:T(8,128)(2,1)} %get-tuple-element.167.refs_0_, bf16[1024,768]{1,0:T(8,128)(2,1)} %get-tuple-element.189.refs_1_, bf16[1024,768]{1,0:T(8,128)(2,1)} %get-tuple-element.168.refs_1_.refs_2_, ...), custom_call_target="tpu_custom_call", output_to_operand_aliasing={{0}: (5, {}), {1}: (6, {})} | custom-call | flops 6920999936 | tf_op jit(solution)/shard_map/attn_bwd/pallas_call | solution.py:331
  215.8 9.0 %qkv_weight_grad.1 = (bf16[4,288,768]{2,1,0:T(8,128)(2,1)}, bf16[4,288,768]{2,1,0:T(8,128)(2,1)}) custom-call(s32[8]{0:T(128)} %copy-done.9, bf16[1024,768]{1,0:T(8,128)(2,1)} %get-tuple-element.206.normed_ref, bf16[1024,2304]{1,0:T(8,128)(2,1)} %get-tuple-element.201.gp_ref), custom_call_target="tpu_custom_call" | custom-call | flops 9228000256 | tf_op jit(solution)/shard_map/qkv_weight_grad/pallas_call | solution.py:739
  224.8 1.6 fusion
  226.4 2.5 fusion.1
  228.9 1.5 collective-permute-start.23
  231.0 11.6 %first_backward.1 = (bf16[1024,768]{1,0:T(8,128)(2,1)}, f32[8,768]{1,0:T(8,128)}) custom-call(s32[8]{0:T(128)} %copy-done.9, bf16[1024,768]{1,0:T(8,128)(2,1)} %x_ref.5, f32[1024,1]{1,0:T(8,128)} %copy.238.t_ref, f32[1024,768]{1,0:T(8,128)} %get-tuple-element.188.gm_ref, bf16[1024,2304]{1,0:T(8,128)(2,1)} %get-tuple-element.201.gp_ref, ...), custom_call_target="tpu_custom_call" | custom-call | flops 12688499712 | tf_op jit(solution)/shard_map/first_backward/pallas_call | solution.py:782
  242.6 3.8 %collective-permute-done.23 = bf16[432,768]{1,0:T(8,128)(2,1)S(1)} collective-permute-done((bf16[432,768]{1,0:T(8,128)(2,1)}, bf16[432,768]{1,0:T(8,128)(2,1)S(1)}, u32[]{:S(2)}, u32[]{:S(2)}) %collective-permute-start.23) | collective-permute-done | bytes 663584 | tf_op jit(solution)/shard_map/ppermute | solution.py:802
  246.6 0.9 collective-permute-done.24
  247.7 1.1 pad_maximum_fusion.3
  249.6 2.0 add_convert_fusion.15
  253.0 9.7 %attn_feat.4 = (f32[1024,256]{1,0:T(8,128)}, f32[2,128,128]{2,1,0:T(8,128)}) custom-call(bf16[32,512,256]{2,1,0:T(8,128)(2,1)} %get-tuple-element.221.ds_ref, bf16[32,1024,512]{2,1,0:T(8,128)(2,1)} %get-tuple-element.222.f_ref, f32[32,8,128]{2,1,0:T(8,128)} %copy-done.1, f32[1024,4]{1,0:T(8,128)} %bitcast.287, bf16[1024,256]{1,0:T(8,128)(2,1)} %copy.243.amat_ref, ...), custom_call_target="tpu_custom_call" | custom-call | flops 9228000256 | tf_op jit(solution)/shard_map/attn_feat/pallas_call | solution.py:354
  264.1 1.1 collective-permute-start.28
  265.8 9.9 %attn_feat.5 = (f32[1024,256]{1,0:T(8,128)}, f32[2,128,128]{2,1,0:T(8,128)}) custom-call(bf16[32,512,256]{2,1,0:T(8,128)(2,1)} %get-tuple-element.221.ds_ref, bf16[32,1024,512]{2,1,0:T(8,128)(2,1)} %get-tuple-element.222.f_ref, f32[32,8,128]{2,1,0:T(8,128)} %copy-done.1, f32[1024,4]{1,0:T(8,128)} %bitcast.288, bf16[1024,256]{1,0:T(8,128)(2,1)} %copy.243.amat_ref, ...), custom_call_target="tpu_custom_call" | custom-call | flops 9228000256 | tf_op jit(solution)/shard_map/attn_feat/pallas_call | solution.py:354
  276.0 1.7 collective-permute-start.30
  277.6 9.9 %attn_feat.6 = (f32[1024,256]{1,0:T(8,128)}, f32[2,128,128]{2,1,0:T(8,128)}) custom-call(bf16[32,512,256]{2,1,0:T(8,128)(2,1)} %get-tuple-element.221.ds_ref, bf16[32,1024,512]{2,1,0:T(8,128)(2,1)} %get-tuple-element.222.f_ref, f32[32,8,128]{2,1,0:T(8,128)} %copy-done.1, f32[1024,4]{1,0:T(8,128)} %bitcast.289, bf16[1024,256]{1,0:T(8,128)(2,1)} %copy.243.amat_ref, ...), custom_call_target="tpu_custom_call" | custom-call | flops 9228000256 | tf_op jit(solution)/shard_map/attn_feat/pallas_call | solution.py:354
  288.0 2.3 collective-permute-start.31
  290.3 10.6 %attn_feat.7 = (f32[1024,256]{1,0:T(8,128)}, f32[2,128,128]{2,1,0:T(8,128)}, f32[128,128]{1,0:T(8,128)}) custom-call(bf16[32,512,256]{2,1,0:T(8,128)(2,1)} %get-tuple-element.221.ds_ref, bf16[32,1024,512]{2,1,0:T(8,128)(2,1)} %get-tuple-element.222.f_ref, f32[32,8,128]{2,1,0:T(8,128)} %copy-done.1, f32[1024,4]{1,0:T(8,128)} %bitcast.290, ...), custom_call_target="tpu_custom_call" | custom-call | flops 9228000256 | tf_op jit(solution)/shard_map/attn_feat/pallas_call | solution.py:354
  301.0 5.4 %collective-permute-done.31 = bf16[144,768]{1,0:T(8,128)(2,1)S(1)} collective-permute-done((bf16[144,768]{1,0:T(8,128)(2,1)S(1)}, bf16[144,768]{1,0:T(8,128)(2,1)S(1)}, u32[]{:S(2)}, u32[]{:S(2)}) %collective-permute-start.31) | collective-permute-done | bytes 221216 | tf_op jit(solution)/shard_map/ppermute | solution.py:802
  306.5 0.8 fusion.33
  307.4 1.5 collective-permute-start.33
  309.2 1.6 collective-permute-start.35
  311.6 2.5 collective-permute-start.37
  315.0 1.2 collective-permute-done.37
  316.3 1.9 collective-permute-done.38
  318.9 7.8 %collective-permute-done.42 = bf16[144,768]{1,0:T(8,128)(2,1)S(1)} collective-permute-done((bf16[144,768]{1,0:T(8,128)(2,1)S(1)}, bf16[144,768]{1,0:T(8,128)(2,1)S(1)}, u32[]{:S(2)}, u32[]{:S(2)}) %collective-permute-start.42) | collective-permute-done | bytes 221216 | tf_op jit(solution)/shard_map/ppermute | solution.py:802
  326.8 1.0 copy.248
  327.7 2.4 collective-permute-start.40
  330.2 2.0 collective-permute-start.41
  332.1 2.4 slice_convert_fusion
  334.6 1.6 slice_convert_fusion.1
  336.2 1.1 copy.249
  (223 shorter events, 32.4 us)
Async XLA Ops:
  7.2 17.8 %copy-start.5 = (bf16[96,768]{1,0:T(8,128)(2,1)S(1)}, bf16[96,768]{1,0:T(8,128)(2,1)}, u32[]{:S(2)}) copy-start(bf16[96,768]{1,0:T(8,128)(2,1)} %param.33) | copy-start | bytes 442372
  7.2 17.8 %copy-start.4 = (bf16[384,768]{1,0:T(8,128)(2,1)S(1)}, bf16[384,768]{1,0:T(8,128)(2,1)}, u32[]{:S(2)}) copy-start(bf16[384,768]{1,0:T(8,128)(2,1)} %param.42) | copy-start | bytes 1769476
  7.2 320.5 %all-reduce.5.cloned.1.call-start = ((), (), s32[]{:S(2)}) async-start(), calls=%async_computation | async-start | bytes 2654208 | tf_op jit(solution)/shard_map/psum | solution.py:1039
  11.8 1.3 collective-permute-start
  12.3 12.8 %copy-start.9 = (s32[8]{0:T(128)}, s32[8]{0:T(128)S(1)}, u32[]{:S(2)}) copy-start(s32[8]{0:T(128)S(1)} %iota_xor_fusion.idx_ref) | copy-start | bytes 100
  13.2 14.8 %collective-permute-start.1 = (bf16[2,29,128]{2,0,1:T(2,128)(2,1)S(1)}, bf16[2,29,128]{2,0,1:T(2,128)(2,1)S(1)}, u32[]{:S(2)}, u32[]{:S(2)}) collective-permute-start(bf16[2,29,128]{2,0,1:T(2,128)(2,1)S(1)} %pad_maximum_fusion.10), channel_id=1, source_target_pairs={{0,8},{4,12},{8,0},{12,4},{16,24},{20,28},{24,16},{28,20},{1,9},{5... | collective-permute-start | bytes 44552 | tf_op jit(solution)/shard_map/ppermute | solution.py:802
  16.1 11.9 %collective-permute-start.2 = (bf16[2,29,128]{2,0,1:T(2,128)(2,1)S(1)}, bf16[2,29,128]{2,0,1:T(2,128)(2,1)S(1)}, u32[]{:S(2)}, u32[]{:S(2)}) collective-permute-start(bf16[2,29,128]{2,0,1:T(2,128)(2,1)S(1)} %pad_maximum_fusion.10), channel_id=1, source_target_pairs={{0,16},{4,20},{8,24},{12,28},{16,0},{20,4},{24,8},{28,12},{1,17},{... | collective-permute-start | bytes 44552 | tf_op jit(solution)/shard_map/ppermute | solution.py:802
  17.6 10.4 %collective-permute-start.3 = (bf16[2,29,128]{2,0,1:T(2,128)(2,1)S(1)}, bf16[2,29,128]{2,0,1:T(2,128)(2,1)S(1)}, u32[]{:S(2)}, u32[]{:S(2)}) collective-permute-start(bf16[2,29,128]{2,0,1:T(2,128)(2,1)S(1)} %pad_maximum_fusion.10), channel_id=1, source_target_pairs={{0,24},{4,28},{8,16},{12,20},{16,8},{20,12},{24,0},{28,4},{1,25},{... | collective-permute-start | bytes 44552 | tf_op jit(solution)/shard_map/ppermute | solution.py:802
  17.7 30.1 %collective-permute-start.4 = (bf16[96,2304]{1,0:T(8,128)(2,1)}, bf16[96,2304]{1,0:T(8,128)(2,1)S(1)}, u32[]{:S(2)}, u32[]{:S(2)}) collective-permute-start(bf16[96,2304]{1,0:T(8,128)(2,1)} %rest_0_.1), channel_id=1, source_target_pairs={{0,8},{4,12},{8,0},{12,4},{16,24},{20,28},{24,16},{28,20},{1,9},{5... | collective-permute-start | bytes 1327112 | tf_op jit(solution)/shard_map/ppermute | solution.py:802
  19.6 28.1 %collective-permute-start.5 = (bf16[96,2304]{1,0:T(8,128)(2,1)}, bf16[96,2304]{1,0:T(8,128)(2,1)}, u32[]{:S(2)}, u32[]{:S(2)}) collective-permute-start(bf16[96,2304]{1,0:T(8,128)(2,1)} %rest_0_.1), channel_id=1, source_target_pairs={{0,16},{4,20},{8,24},{12,28},{16,0},{20,4},{24,8},{28,12},{1,17},{... | collective-permute-start | bytes 1327112 | tf_op jit(solution)/shard_map/ppermute | solution.py:802
  23.8 1.3 copy-start.1
  25.0 0.7 copy-start.6
  25.0 2.0 copy-start.8
  25.0 3.0 copy-start.13
  25.7 40.6 %copy-start.3 = (bf16[864,768]{1,0:T(8,128)(2,1)}, bf16[864,768]{1,0:T(8,128)(2,1)S(1)}, u32[]{:S(2)}) copy-start(bf16[864,768]{1,0:T(8,128)(2,1)S(1)} %pad_maximum_fusion.rest_0_) | copy-start | bytes 3981316
  28.0 19.7 %collective-permute-start.6 = (bf16[96,2304]{1,0:T(8,128)(2,1)S(1)}, bf16[96,2304]{1,0:T(8,128)(2,1)}, u32[]{:S(2)}, u32[]{:S(2)}) collective-permute-start(bf16[96,2304]{1,0:T(8,128)(2,1)S(1)} %copy-done.13), channel_id=1, source_target_pairs={{0,24},{4,28},{8,16},{12,20},{16,8},{20,12},{24,0},{28,4},{1,25},{... | collective-permute-start | bytes 1327112 | tf_op jit(solution)/shard_map/ppermute | solution.py:802
  47.7 18.6 %copy-start.14 = (bf16[96,2304]{1,0:T(8,128)(2,1)}, bf16[96,2304]{1,0:T(8,128)(2,1)S(1)}, u32[]{:S(2)}) copy-start(bf16[96,2304]{1,0:T(8,128)(2,1)S(1)} %collective-permute-done.4.rest_2_) | copy-start | bytes 1327108
  47.7 5.4 %collective-permute-start.10 = (bf16[96,2304]{1,0:T(8,128)(2,1)}, bf16[96,2304]{1,0:T(8,128)(2,1)S(1)}, u32[]{:S(2)}, u32[]{:S(2)}) collective-permute-start(bf16[96,2304]{1,0:T(8,128)(2,1)} %collective-permute-done.6.rest_6_), channel_id=1, source_target_pairs={{0,4},{4,0},{8,12},{12,8},{16,20},{20,16},{24,28},{28,24},{1,5},{5... | collective-permute-start | bytes 1327112 | tf_op jit(solution)/shard_map/ppermute | solution.py:802
  49.2 31.8 %collective-permute-start.11 = (bf16[864,768]{1,0:T(8,128)(2,1)S(1)}, bf16[864,768]{1,0:T(8,128)(2,1)}, u32[]{:S(2)}, u32[]{:S(2)}) collective-permute-start(bf16[864,768]{1,0:T(8,128)(2,1)S(1)} %pad_maximum_fusion.rest_0_), channel_id=1, source_target_pairs={{0,8},{4,12},{8,0},{12,4},{16,24},{20,28},{24,16},{28,20},{1,9},{5... | collective-permute-start | bytes 3981320 | tf_op jit(solution)/shard_map/ppermute | solution.py:802
  51.2 31.4 %collective-permute-start.12 = (bf16[864,768]{1,0:T(8,128)(2,1)S(1)}, bf16[864,768]{1,0:T(8,128)(2,1)}, u32[]{:S(2)}, u32[]{:S(2)}) collective-permute-start(bf16[864,768]{1,0:T(8,128)(2,1)S(1)} %pad_maximum_fusion.rest_0_), channel_id=1, source_target_pairs={{0,16},{4,20},{8,24},{12,28},{16,0},{20,4},{24,8},{28,12},{1,17},{... | collective-permute-start | bytes 3981320 | tf_op jit(solution)/shard_map/ppermute | solution.py:802
  52.7 13.6 %collective-permute-start.7 = (bf16[96,2304]{1,0:T(8,128)(2,1)S(1)}, bf16[96,2304]{1,0:T(8,128)(2,1)S(1)}, u32[]{:S(2)}, u32[]{:S(2)}) collective-permute-start(bf16[96,2304]{1,0:T(8,128)(2,1)S(1)} %copy-done.13), channel_id=1, source_target_pairs={{0,4},{4,0},{8,12},{12,8},{16,20},{20,16},{24,28},{28,24},{1,5},{5... | collective-permute-start | bytes 1327112 | tf_op jit(solution)/shard_map/ppermute | solution.py:802
  52.7 14.0 %collective-permute-start.8 = (bf16[96,2304]{1,0:T(8,128)(2,1)S(1)}, bf16[96,2304]{1,0:T(8,128)(2,1)S(1)}, u32[]{:S(2)}, u32[]{:S(2)}) collective-permute-start(bf16[96,2304]{1,0:T(8,128)(2,1)S(1)} %collective-permute-done.4.rest_2_), channel_id=1, source_target_pairs={{0,4},{4,0},{8,12},{12,8},{16,20},{20,16},{24,28},{28,24},{1,5},{5... | collective-permute-start | bytes 1327112 | tf_op jit(solution)/shard_map/ppermute | solution.py:802
  53.2 13.1 %copy-start.15 = (bf16[96,2304]{1,0:T(8,128)(2,1)}, bf16[96,2304]{1,0:T(8,128)(2,1)S(1)}, u32[]{:S(2)}) copy-start(bf16[96,2304]{1,0:T(8,128)(2,1)S(1)} %collective-permute-done.10.rest_7_) | copy-start | bytes 1327108
  53.2 13.5 %collective-permute-start.9 = (bf16[96,2304]{1,0:T(8,128)(2,1)}, bf16[96,2304]{1,0:T(8,128)(2,1)}, u32[]{:S(2)}, u32[]{:S(2)}) collective-permute-start(bf16[96,2304]{1,0:T(8,128)(2,1)} %collective-permute-done.5.rest_4_), channel_id=1, source_target_pairs={{0,4},{4,0},{8,12},{12,8},{16,20},{20,16},{24,28},{28,24},{1,5},{5... | collective-permute-start | bytes 1327112 | tf_op jit(solution)/shard_map/ppermute | solution.py:802
  66.3 0.8 copy-start.16
  66.3 43.4 %collective-permute-start.15 = (bf16[864,768]{1,0:T(8,128)(2,1)S(1)}, bf16[864,768]{1,0:T(8,128)(2,1)}, u32[]{:S(2)}, u32[]{:S(2)}) collective-permute-start(bf16[864,768]{1,0:T(8,128)(2,1)S(1)} %pad_maximum_fusion.rest_0_), channel_id=1, source_target_pairs={{0,4},{4,0},{8,12},{12,8},{16,20},{20,16},{24,28},{28,24},{1,5},{5... | collective-permute-start | bytes 3981320 | tf_op jit(solution)/shard_map/ppermute | solution.py:802
  66.7 0.8 copy-start.17
  83.7 26.1 %collective-permute-start.16 = (bf16[864,768]{1,0:T(8,128)(2,1)}, bf16[864,768]{1,0:T(8,128)(2,1)}, u32[]{:S(2)}, u32[]{:S(2)}) collective-permute-start(bf16[864,768]{1,0:T(8,128)(2,1)} %collective-permute-done.11.rest_2_), channel_id=1, source_target_pairs={{0,4},{4,0},{8,12},{12,8},{16,20},{20,16},{24,28},{28,24},{1,5},{5... | collective-permute-start | bytes 3981320 | tf_op jit(solution)/shard_map/ppermute | solution.py:802
  83.8 26.0 %collective-permute-start.17 = (bf16[864,768]{1,0:T(8,128)(2,1)}, bf16[864,768]{1,0:T(8,128)(2,1)}, u32[]{:S(2)}, u32[]{:S(2)}) collective-permute-start(bf16[864,768]{1,0:T(8,128)(2,1)} %collective-permute-done.12.rest_4_), channel_id=1, source_target_pairs={{0,4},{4,0},{8,12},{12,8},{16,20},{20,16},{24,28},{28,24},{1,5},{5... | collective-permute-start | bytes 3981320 | tf_op jit(solution)/shard_map/ppermute | solution.py:802
  85.4 24.3 %collective-permute-start.13 = (bf16[480,768]{1,0:T(8,128)(2,1)S(1)}, bf16[480,768]{1,0:T(8,128)(2,1)S(1)}, u32[]{:S(2)}, u32[]{:S(2)}) collective-permute-start(bf16[480,768]{1,0:T(8,128)(2,1)S(1)} %slice.443), channel_id=1, source_target_pairs={{0,16},{4,20},{8,24},{12,28},{16,0},{20,4},{24,8},{28,12},{1,17},{... | collective-permute-start | bytes 2211848 | tf_op jit(solution)/shard_map/ppermute | solution.py:802
  86.9 22.8 %collective-permute-start.14 = (bf16[384,768]{1,0:T(8,128)(2,1)S(1)}, bf16[384,768]{1,0:T(8,128)(2,1)}, u32[]{:S(2)}, u32[]{:S(2)}) collective-permute-start(bf16[384,768]{1,0:T(8,128)(2,1)S(1)} %slice.444), channel_id=1, source_target_pairs={{0,8},{4,12},{8,0},{12,4},{16,24},{20,28},{24,16},{28,20},{1,9},{5... | collective-permute-start | bytes 1769480 | tf_op jit(solution)/shard_map/ppermute | solution.py:802
  109.7 3.4 copy-start.10
  109.8 60.3 %copy-start = (bf16[32,8,8,128]{3,1,2,0:T(8,128)(2,1)S(1)}, bf16[32,8,8,128]{3,1,2,0:T(8,128)(2,1)}, u32[]{:S(2)}) copy-start(bf16[32,8,8,128]{3,1,2,0:T(8,128)(2,1)} %copy.259) | copy-start | bytes 1572868
  109.8 3.3 collective-permute-start.18
  109.8 3.3 collective-permute-start.19
  113.1 0.8 copy-start.12
  113.9 0.9 copy-start.11
  169.9 12.9 %collective-permute-start.20 = (bf16[4,864,768]{2,1,0:T(8,128)(2,1)}, bf16[4,864,768]{2,1,0:T(8,128)(2,1)}, u32[]{:S(2)}, u32[]{:S(2)}) collective-permute-start(bf16[4,864,768]{2,1,0:T(8,128)(2,1)} %get-tuple-element.194), channel_id=1, source_target_pairs={{0,4},{4,0},{8,12},{12,8},{16,20},{20,16},{24,28},{28,24},{1,5},{5... | collective-permute-start | bytes 15925256 | tf_op jit(solution)/shard_map/ppermute | solution.py:802
  189.3 35.5 %collective-permute-start.22 = (bf16[2,432,768]{2,1,0:T(8,128)(2,1)S(1)}, bf16[2,432,768]{2,1,0:T(8,128)(2,1)}, u32[]{:S(2)}, u32[]{:S(2)}) collective-permute-start(bf16[2,432,768]{2,1,0:T(8,128)(2,1)S(1)} %get-tuple-element.212), channel_id=1, source_target_pairs={{0,16},{4,20},{8,24},{12,28},{16,0},{20,4},{24,8},{28,12},{1,17},{... | collective-permute-start | bytes 3981320 | tf_op jit(solution)/shard_map/ppermute | solution.py:802
  189.6 36.8 %collective-permute-start.21 = (bf16[2,432,768]{2,1,0:T(8,128)(2,1)}, bf16[2,432,768]{2,1,0:T(8,128)(2,1)}, u32[]{:S(2)}, u32[]{:S(2)}) collective-permute-start(bf16[2,432,768]{2,1,0:T(8,128)(2,1)} %get-tuple-element.210), channel_id=1, source_target_pairs={{0,8},{4,12},{8,0},{12,4},{16,24},{20,28},{24,16},{28,20},{1,9},{5... | collective-permute-start | bytes 3981320 | tf_op jit(solution)/shard_map/ppermute | solution.py:802
  228.9 19.9 %collective-permute-start.25 = (bf16[4,288,768]{2,1,0:T(8,128)(2,1)}, bf16[4,288,768]{2,1,0:T(8,128)(2,1)}, u32[]{:S(2)}, u32[]{:S(2)}) collective-permute-start(bf16[4,288,768]{2,1,0:T(8,128)(2,1)} %get-tuple-element.220), channel_id=1, source_target_pairs={{0,4},{4,0},{8,12},{12,8},{16,20},{20,16},{24,28},{28,24},{1,5},{5... | collective-permute-start | bytes 5308424 | tf_op jit(solution)/shard_map/ppermute | solution.py:802
  228.9 17.5 %collective-permute-start.23 = (bf16[432,768]{1,0:T(8,128)(2,1)}, bf16[432,768]{1,0:T(8,128)(2,1)S(1)}, u32[]{:S(2)}, u32[]{:S(2)}) collective-permute-start(bf16[432,768]{1,0:T(8,128)(2,1)} %get-tuple-element.216), channel_id=1, source_target_pairs={{0,16},{4,20},{8,24},{12,28},{16,0},{20,4},{24,8},{28,12},{1,17},{... | collective-permute-start | bytes 1990664 | tf_op jit(solution)/shard_map/ppermute | solution.py:802
  230.4 17.0 %collective-permute-start.24 = (bf16[432,768]{1,0:T(8,128)(2,1)S(1)}, bf16[432,768]{1,0:T(8,128)(2,1)S(1)}, u32[]{:S(2)}, u32[]{:S(2)}) collective-permute-start(bf16[432,768]{1,0:T(8,128)(2,1)S(1)} %get-tuple-element.218), channel_id=1, source_target_pairs={{0,8},{4,12},{8,0},{12,4},{16,24},{20,28},{24,16},{28,20},{1,9},{5... | collective-permute-start | bytes 1990664 | tf_op jit(solution)/shard_map/ppermute | solution.py:802
  247.7 2.0 copy-start.2
  251.7 11.5 %collective-permute-start.27 = (bf16[2,144,768]{2,1,0:T(8,128)(2,1)S(1)}, bf16[2,144,768]{2,1,0:T(8,128)(2,1)S(1)}, u32[]{:S(2)}, u32[]{:S(2)}) collective-permute-start(bf16[2,144,768]{2,1,0:T(8,128)(2,1)S(1)} %pad_maximum_fusion.5), channel_id=1, source_target_pairs={{0,16},{4,20},{8,24},{12,28},{16,0},{20,4},{24,8},{28,12},{1,17},{... | collective-permute-start | bytes 1327112 | tf_op jit(solution)/shard_map/ppermute | solution.py:802
  252.4 11.5 %collective-permute-start.26 = (bf16[2,144,768]{2,1,0:T(8,128)(2,1)S(1)}, bf16[2,144,768]{2,1,0:T(8,128)(2,1)S(1)}, u32[]{:S(2)}, u32[]{:S(2)}) collective-permute-start(bf16[2,144,768]{2,1,0:T(8,128)(2,1)S(1)} %pad_maximum_fusion.4), channel_id=1, source_target_pairs={{0,8},{4,12},{8,0},{12,4},{16,24},{20,28},{24,16},{28,20},{1,9},{5... | collective-permute-start | bytes 1327112 | tf_op jit(solution)/shard_map/ppermute | solution.py:802
  253.0 9.7 %copy-start.7 = (f32[8,768]{1,0:T(8,128)S(1)}, f32[8,768]{1,0:T(8,128)}, u32[]{:S(2)}) copy-start(f32[8,768]{1,0:T(8,128)} %get-tuple-element.252) | copy-start | bytes 73732
  264.1 11.7 %collective-permute-start.28 = (bf16[144,768]{1,0:T(8,128)(2,1)S(1)}, bf16[144,768]{1,0:T(8,128)(2,1)S(1)}, u32[]{:S(2)}, u32[]{:S(2)}) collective-permute-start(bf16[144,768]{1,0:T(8,128)(2,1)S(1)} %get-tuple-element.238), channel_id=1, source_target_pairs={{0,16},{4,20},{8,24},{12,28},{16,0},{20,4},{24,8},{28,12},{1,17},{... | collective-permute-start | bytes 663560 | tf_op jit(solution)/shard_map/ppermute | solution.py:802
  265.2 10.6 %collective-permute-start.29 = (bf16[144,768]{1,0:T(8,128)(2,1)S(1)}, bf16[144,768]{1,0:T(8,128)(2,1)S(1)}, u32[]{:S(2)}, u32[]{:S(2)}) collective-permute-start(bf16[144,768]{1,0:T(8,128)(2,1)S(1)} %get-tuple-element.240), channel_id=1, source_target_pairs={{0,8},{4,12},{8,0},{12,4},{16,24},{20,28},{24,16},{28,20},{1,9},{5... | collective-permute-start | bytes 663560 | tf_op jit(solution)/shard_map/ppermute | solution.py:802
  276.0 12.0 %collective-permute-start.30 = (bf16[144,768]{1,0:T(8,128)(2,1)S(1)}, bf16[144,768]{1,0:T(8,128)(2,1)S(1)}, u32[]{:S(2)}, u32[]{:S(2)}) collective-permute-start(bf16[144,768]{1,0:T(8,128)(2,1)S(1)} %get-tuple-element.246), channel_id=1, source_target_pairs={{0,1},{1,0},{2,3},{3,2},{4,5},{5,4},{6,7},{7,6},{8,9},{9,8},{10,11... | collective-permute-start | bytes 663560 | tf_op jit(solution)/shard_map/ppermute | solution.py:802
  288.0 18.4 %collective-permute-start.31 = (bf16[144,768]{1,0:T(8,128)(2,1)S(1)}, bf16[144,768]{1,0:T(8,128)(2,1)S(1)}, u32[]{:S(2)}, u32[]{:S(2)}) collective-permute-start(bf16[144,768]{1,0:T(8,128)(2,1)S(1)} %add_convert_fusion.11), channel_id=1, source_target_pairs={{0,2},{1,3},{2,0},{3,1},{4,6},{5,7},{6,4},{7,5},{8,10},{9,11},{10,... | collective-permute-start | bytes 663560 | tf_op jit(solution)/shard_map/ppermute | solution.py:802
  307.3 4.3 %collective-permute-start.32 = (f32[29,128]{1,0:T(8,128)S(1)}, f32[29,128]{1,0:T(8,128)S(1)}, u32[]{:S(2)}, u32[]{:S(2)}) collective-permute-start(f32[29,128]{1,0:T(8,128)S(1)} %get-tuple-element.304), channel_id=1, source_target_pairs={{0,4},{4,0},{8,12},{12,8},{16,20},{20,16},{24,28},{28,24},{1,5},{5... | collective-permute-start | bytes 44552 | tf_op jit(solution)/shard_map/ppermute | solution.py:802
  307.4 6.7 %collective-permute-start.33 = (f32[29,128]{1,0:T(8,128)S(1)}, f32[29,128]{1,0:T(8,128)S(1)}, u32[]{:S(2)}, u32[]{:S(2)}) collective-permute-start(f32[29,128]{1,0:T(8,128)S(1)} %get-tuple-element.305), channel_id=1, source_target_pairs={{0,8},{4,12},{8,0},{12,4},{16,24},{20,28},{24,16},{28,20},{1,9},{5... | collective-permute-start | bytes 44552 | tf_op jit(solution)/shard_map/ppermute | solution.py:802
  308.9 5.4 %collective-permute-start.34 = (f32[29,128]{1,0:T(8,128)S(1)}, f32[29,128]{1,0:T(8,128)S(1)}, u32[]{:S(2)}, u32[]{:S(2)}) collective-permute-start(f32[29,128]{1,0:T(8,128)S(1)} %get-tuple-element.306), channel_id=1, source_target_pairs={{0,12},{4,8},{8,4},{12,0},{16,28},{20,24},{24,20},{28,16},{1,13},{... | collective-permute-start | bytes 44552 | tf_op jit(solution)/shard_map/ppermute | solution.py:802
  309.2 5.8 %collective-permute-start.35 = (f32[29,128]{1,0:T(8,128)S(1)}, f32[29,128]{1,0:T(8,128)S(1)}, u32[]{:S(2)}, u32[]{:S(2)}) collective-permute-start(f32[29,128]{1,0:T(8,128)S(1)} %get-tuple-element.307), channel_id=1, source_target_pairs={{0,16},{4,20},{8,24},{12,28},{16,0},{20,4},{24,8},{28,12},{1,17},{... | collective-permute-start | bytes 44552 | tf_op jit(solution)/shard_map/ppermute | solution.py:802
  310.8 4.2 %collective-permute-start.36 = (f32[29,128]{1,0:T(8,128)S(1)}, f32[29,128]{1,0:T(8,128)S(1)}, u32[]{:S(2)}, u32[]{:S(2)}) collective-permute-start(f32[29,128]{1,0:T(8,128)S(1)} %get-tuple-element.308), channel_id=1, source_target_pairs={{0,20},{4,16},{8,28},{12,24},{16,4},{20,0},{24,12},{28,8},{1,21},{... | collective-permute-start | bytes 44552 | tf_op jit(solution)/shard_map/ppermute | solution.py:802
  311.6 4.6 %collective-permute-start.37 = (f32[29,128]{1,0:T(8,128)S(1)}, f32[29,128]{1,0:T(8,128)S(1)}, u32[]{:S(2)}, u32[]{:S(2)}) collective-permute-start(f32[29,128]{1,0:T(8,128)S(1)} %get-tuple-element.309), channel_id=1, source_target_pairs={{0,24},{4,28},{8,16},{12,20},{16,8},{20,12},{24,0},{28,4},{1,25},{... | collective-permute-start | bytes 44552 | tf_op jit(solution)/shard_map/ppermute | solution.py:802
  314.1 4.1 %collective-permute-start.38 = (f32[29,128]{1,0:T(8,128)S(1)}, f32[29,128]{1,0:T(8,128)S(1)}, u32[]{:S(2)}, u32[]{:S(2)}) collective-permute-start(f32[29,128]{1,0:T(8,128)S(1)} %fusion.22), channel_id=1, source_target_pairs={{0,28},{4,24},{8,20},{12,16},{16,12},{20,8},{24,4},{28,0},{1,29},{... | collective-permute-start | bytes 44552 | tf_op jit(solution)/shard_map/ppermute | solution.py:802
  314.3 12.3 %collective-permute-start.42 = (bf16[144,768]{1,0:T(8,128)(2,1)S(1)}, bf16[144,768]{1,0:T(8,128)(2,1)S(1)}, u32[]{:S(2)}, u32[]{:S(2)}) collective-permute-start(bf16[144,768]{1,0:T(8,128)(2,1)S(1)} %add_convert_fusion.10), channel_id=1, source_target_pairs={{0,1},{1,0},{2,3},{3,2},{4,5},{5,4},{6,7},{7,6},{8,9},{9,8},{10,11... | collective-permute-start | bytes 663560 | tf_op jit(solution)/shard_map/ppermute | solution.py:802
  327.7 9.6 %collective-permute-start.39 = (f32[29,128]{1,0:T(8,128)S(1)}, f32[29,128]{1,0:T(8,128)S(1)}, u32[]{:S(2)}, u32[]{:S(2)}) collective-permute-start(f32[29,128]{1,0:T(8,128)S(1)} %fusion.31), channel_id=1, source_target_pairs={{0,1},{1,0},{2,3},{3,2},{4,5},{5,4},{6,7},{7,6},{8,9},{9,8},{10,11... | collective-permute-start | bytes 44552 | tf_op jit(solution)/shard_map/ppermute | solution.py:802
  327.7 9.6 %collective-permute-start.40 = (f32[29,128]{1,0:T(8,128)S(1)}, f32[29,128]{1,0:T(8,128)S(1)}, u32[]{:S(2)}, u32[]{:S(2)}) collective-permute-start(f32[29,128]{1,0:T(8,128)S(1)} %fusion.31), channel_id=1, source_target_pairs={{0,2},{1,3},{2,0},{3,1},{4,6},{5,7},{6,4},{7,5},{8,10},{9,11},{10,... | collective-permute-start | bytes 44552 | tf_op jit(solution)/shard_map/ppermute | solution.py:802
  330.2 7.2 %collective-permute-start.41 = (f32[29,128]{1,0:T(8,128)S(1)}, f32[29,128]{1,0:T(8,128)S(1)}, u32[]{:S(2)}, u32[]{:S(2)}) collective-permute-start(f32[29,128]{1,0:T(8,128)S(1)} %fusion.31), channel_id=1, source_target_pairs={{0,3},{1,2},{2,1},{3,0},{4,7},{5,6},{6,5},{7,4},{8,11},{9,10},{10,... | collective-permute-start | bytes 44552 | tf_op jit(solution)/shard_map/ppermute | solution.py:802
Sparse Core Ops, SparseCore 0:
  253.1 70.6 all-reduce.4

commit v4 on v3

--- a/solution.py
+++ b/solution.py
@@ -92,7 +92,7 @@
     return jnp.concatenate(slots, axis=0).astype(bf16)
 
 
-def bias_kernel(aw_ref, ac_ref, gmat_ref, bmat_ref, b_ref, f_ref, t_scr):
+def bias_kernel(aw_ref, ac_ref, gmat_ref, amat_ref, b_ref, f_ref, t_scr):
     @pl.loop(0, STEP // PAIR)
     def _(s):
         chunks = [s * PAIR + u for u in range(PAIR)]
@@ -101,7 +101,7 @@
         dist = [distance_rows(a, w) for a, w in zip(ac, aw)]
         e = [dot(gmat_ref[...], d) for d in dist]
         f = [jnp.exp2(v).astype(bf16) for v in e]
-        bias = [dot(bmat_ref[...], v) for v in f]
+        bias = [dot(amat_ref[...], v, TN) for v in f]
         for u, t in enumerate(chunks):
             f_ref[t] = f[u]
             joined = ac[u][:, 3:4] == aw[u][3:4, :]
@@ -192,11 +192,11 @@
 
 
 def feat_kernel(n_before, last, ds_ref, f_ref, aw_ref, ac_ref, amat_ref, kcol_ref, *rest):
-    before, (m0_ref, s_ref, *out_ref, rho_scr, gf_scr) = rest[:n_before], rest[n_before:]
+    before, (m_ref, s_ref, *out_ref, rho_scr, gf_scr, m0_ref) = rest[:n_before], rest[n_before:]
 
     @pl.when(pl.program_id(0) == 0)
     def _():
-        m0_ref[...] = before[0][...] if before else jnp.zeros_like(m0_ref)
+        m0_ref[...] = jnp.zeros_like(m0_ref)
         s_ref[...] = before[1][...] if before else jnp.zeros_like(s_ref)
 
     for u in range(FEAT_STEP):
@@ -222,23 +222,26 @@
                 s_ref[0, ks, :] = s1
                 s_ref[1, ks, :] = s2
 
-    if last:
-
-        @pl.when(pl.program_id(0) == pl.num_programs(0) - 1)
-        def _():
-            out_ref[0][...] = kernel_grads(m0_ref, s_ref, kcol_ref[...])
-
-
-def kernel_grads(m0_ref, s_ref, kcol):
+    @pl.when(pl.program_id(0) == pl.num_programs(0) - 1)
+    def _():
+        n = kcol_ref.shape[0]
+        lanes = lax.broadcasted_iota(jnp.int32, (n, 256), 1)
+        m = jnp.zeros((n, 256), f32)
+        for r in range(8):
+            m = jnp.where(lanes % 8 == r, m0_ref[n * r : n * r + n, :], m)
+        if before:
+            m = m + before[0][...]
+        m_ref[...] = m
+        if last:
+            out_ref[0][...] = kernel_grads(m, s_ref, kcol_ref[...])
+
+
+def kernel_grads(m, s_ref, kcol):
     n = kcol.shape[0]
-    lanes = lax.broadcasted_iota(jnp.int32, (n, 256), 1)
-    m = jnp.zeros((n, 256), f32)
-    for r in range(8):
-        m = jnp.where(lanes % 8 == r, m0_ref[n * r : n * r + n, :], m)
     heads = lax.broadcasted_iota(jnp.int32, (256, 128), 0) // 8 == lax.broadcasted_iota(jnp.int32, (256, 128), 1)
     heads = heads.astype(f32).astype(bf16)
     g_map = sum(dot(v.astype(bf16), heads) for v in parts3(m))
-    lanes = lanes[:, :128]
+    lanes = lax.broadcasted_iota(jnp.int32, (n, 128), 1)
     s0 = jnp.sum(jnp.where(lanes < 32, g_map * kcol, 0.0), axis=-1, keepdims=True)
     s1 = jnp.sum(s_ref[0], axis=-1, keepdims=True)
     s2 = jnp.sum(s_ref[1], axis=-1, keepdims=True)
@@ -262,7 +265,7 @@
 
 
 BIAS_PARTS = 2
-FWD_PARTS = 2
+FWD_PARTS = 1
 BWD_PARTS = 4
 FEAT_PARTS = 4
 
@@ -275,7 +278,7 @@
     return pl.BlockSpec(shape, lambda i: (part,) + (0,) * (len(shape) - 1))
 
 
-def attn_bias(part, aw, ac, gmat, bmat, before):
+def attn_bias(part, aw, ac, gmat, amat, before):
     c = aw.shape[0]
     per = c // BIAS_PARTS // STEP
     base = part * per
@@ -284,16 +287,16 @@
         functools.partial(skip_refs, bias_kernel, n_in, len(before)),
         grid=(per,),
         in_specs=[
-            shifted((STEP, 8, WIN), base), shifted((STEP * CH, 4), base), full_spec(gmat.shape), full_spec(bmat.shape),
+            shifted((STEP, 8, WIN), base), shifted((STEP * CH, 4), base), full_spec(gmat.shape), full_spec(amat.shape),
         ] + [pl.BlockSpec(memory_space=pl.ANY)] * len(before),
         out_specs=[shifted((STEP, WIN, 1024), base), shifted((STEP, 1024, 4 * WIN), base)],
         out_shape=[jax.ShapeDtypeStruct((c, WIN, 1024), f32), jax.ShapeDtypeStruct((c, 1024, 4 * WIN), bf16)],
         scratch_shapes=[pltpu.VMEM((PAIR, 1024, WIN), f32)],
         input_output_aliases={n_in + t: t for t in range(len(before))},
         compiler_params=params(),
-        cost_estimate=cost(24 // BIAS_PARTS),
+        cost_estimate=cost(4 // BIAS_PARTS),
         name="attn_bias",
-    )(aw, ac, gmat, bmat, *before)
+    )(aw, ac, gmat, amat, *before)
 
 
 def attn_fwd(part, q, k, v, bias, before):
@@ -340,7 +343,7 @@
         scratch_shapes=[pltpu.VMEM((rows // BWD_PARTS, width), f32)] * 2,
         input_output_aliases={n_in + t: t for t in range(len(before))},
         compiler_params=params(),
-        cost_estimate=cost(24 // BWD_PARTS),
+        cost_estimate=cost(2),
         name="attn_bwd",
     )(q, do, k, v, p, *before)
 
@@ -350,7 +353,7 @@
     base = part * per
     last = part == FEAT_PARTS - 1
     n = kcol.shape[0]
-    shapes = [(1024, 256), (2, n, WIN)] + [(n, 128)] * last
+    shapes = [(n, 256), (2, n, WIN)] + [(n, 128)] * last
     return pl.pallas_call(
         functools.partial(feat_kernel, len(before), last),
         grid=(per,),
@@ -361,9 +364,11 @@
         ] + [full_spec(b.shape) for b in before],
         out_specs=[full_spec(s) for s in shapes],
         out_shape=[jax.ShapeDtypeStruct(s, f32) for s in shapes],
-        scratch_shapes=[pltpu.VMEM((FEAT_STEP, 8, 4 * WIN), f32), pltpu.VMEM((FEAT_STEP, 1024, 4 * WIN), f32)],
+        scratch_shapes=[
+            pltpu.VMEM((FEAT_STEP, 8, 4 * WIN), f32), pltpu.VMEM((FEAT_STEP, 1024, 4 * WIN), f32), pltpu.VMEM((1024, 256), f32),
+        ],
         compiler_params=params(),
-        cost_estimate=cost(32 // FEAT_PARTS),
+        cost_estimate=cost(1),
         name="attn_feat",
     )(ds, feats, aw, ac, amat, kcol, *before)
 
@@ -402,6 +407,7 @@
 
 
 TILE = 256
+BLOCK = 512
 epsilon = 1e-05
 
 
@@ -478,6 +484,10 @@
     return pl.BlockSpec(shape, lambda i, *_: (0,) * len(shape))
 
 
+def sub_tiles():
+    return [pl.ds(i * TILE, TILE) for i in range(BLOCK // TILE)]
+
+
 def qkv_kernel(n, scale, idx_ref, x_ref, t_ref, vec_ref, *rest):
     pieces, (normed_ref, q_ref, k_ref, v_ref, w_scr, sem) = rest[:n], rest[n:]
     width = x_ref.shape[1]
@@ -487,15 +497,16 @@
         for c in qkv_copies(idx_ref, pieces, w_scr, sem):
             c.start()
 
-    start = x_ref[...].astype(f32) + t_ref[...] * vec_ref[0:1, :]
-    normed = (ln_parts(start)[0] * vec_ref[1:2, :] + vec_ref[2:3, :]).astype(bf16)
-    normed_ref[...] = normed
+    for rs in sub_tiles():
+        start = x_ref[rs, :].astype(f32) + t_ref[rs, :] * vec_ref[0:1, :]
+        normed_ref[rs, :] = (ln_parts(start)[0] * vec_ref[1:2, :] + vec_ref[2:3, :]).astype(bf16)
 
     @pl.when(pl.program_id(0) == 0)
     def _():
         for c in qkv_copies(idx_ref, pieces, w_scr, sem):
             c.wait()
 
+    normed = normed_ref[...]
     q_ref[...] = ((dot(normed, w_scr[:, :width]) + vec_ref[3:4, :]) * scale).astype(bf16)
     k_ref[...] = dot(normed, w_scr[:, width : 2 * width]).astype(bf16)
     v_ref[...] = (dot(normed, w_scr[:, 2 * width :]) + vec_ref[4:5, :]).astype(bf16)
@@ -509,9 +520,9 @@
         functools.partial(qkv_kernel, n, scale),
         grid_spec=pltpu.PrefetchScalarGridSpec(
             num_scalar_prefetch=1,
-            grid=(rows // TILE,),
-            in_specs=[row_spec(width), row_spec(1), whole_spec(vecs.shape)] + [any_spec()] * n,
-            out_specs=[row_spec(width)] * 4,
+            grid=(rows // BLOCK,),
+            in_specs=[row_spec(width, BLOCK), row_spec(1, BLOCK), whole_spec(vecs.shape)] + [any_spec()] * n,
+            out_specs=[row_spec(width, BLOCK)] * 4,
             scratch_shapes=[pltpu.VMEM((width, 3 * width), bf16), pltpu.SemaphoreType.DMA((n,))],
         ),
         out_shape=[out] * 4,
@@ -540,7 +551,7 @@
 
 def ffn_kernel(n, split, steps, idx_ref, x_ref, t_ref, att_ref, cot_ref, vec_ref, upb_ref, *rest):
     pieces = rest[:n]
-    (out_ref, ga_ref, gvec_ref, gupb_ref, gm_hbm, keep_hbm, send_hbm,
+    (out_ref, ga_ref, gvec_ref, gm_hbm, keep_hbm, send_hbm,
      wo, up, down, mid, n2, acc, gn2, hid, gp, stage_up, stage_down, sem, out_sem, gm_sem) = rest[n:]
     j = pl.program_id(0)
     rows, width = x_ref.shape
@@ -635,7 +646,7 @@
         gb = gb + rows_sum(g.astype(f32))
         acc[rs, :] += dot(h, down_c)
         gn2[rs, :] += dot(g, up_c, NT)
-    gupb_ref[...] = gb
+    gvec_ref[pl.ds(4 + j, 1), :] = gb
     slot = lax.rem(j, 2)
     put(stage_down, slot, dot(hid[...], cot_ref[...], TN), 2 * (fc // (2 * steps * r)) if split else 0)
     put(stage_up, slot, dot(n2[...], gp[...], TN), split)
@@ -657,7 +668,7 @@
             hid[rs, :] = ga
             ga_ref[rs, :] = dot(ga, wo[...], NT).astype(bf16)
             sums = [s + rows_sum(v) for s, v in zip(sums, (dn * xhat, dn, cot, ga.astype(f32)))]
-        gvec_ref[...] = jnp.concatenate(sums + [jnp.zeros((4, width), f32)], axis=0)
+        gvec_ref[0:4, :] = jnp.concatenate(sums, axis=0)
         mid_copy = pltpu.make_async_copy(mid, gm_hbm, gm_sem)
         mid_copy.start()
         grad_out = dot(att_ref[...], hid[...], TN)
@@ -694,15 +705,15 @@
             grid=(steps,),
             in_specs=[whole_spec((rows, width)), whole_spec((rows, 1)), whole_spec((rows, width)), whole_spec((rows, width)),
                       whole_spec(vecs.shape), pl.BlockSpec((1, fc), lambda j, *_: (0, j))] + [any_spec()] * n,
-            out_specs=[whole_spec((rows, width)), whole_spec((rows, width)), whole_spec((8, width)),
-                       pl.BlockSpec((1, fc), lambda j, *_: (0, j)), any_spec(), any_spec(), any_spec()],
+            out_specs=[whole_spec((rows, width)), whole_spec((rows, width)), whole_spec((4 + steps, width)),
+                       any_spec(), any_spec(), any_spec()],
             scratch_shapes=[V((width, width), bf16), V((width, ff), bf16), V((ff, width), bf16),
                             V((rows, width), f32), V((rows, width), bf16),
                             V((rows, width), f32), V((rows, width), f32),
                             V((rows, fc), bf16), V((rows, fc), bf16), *stages,
                             pltpu.SemaphoreType.DMA((6 * n,)), pltpu.SemaphoreType.DMA((2, 4)), pltpu.SemaphoreType.DMA],
         ),
-        out_shape=[sd((rows, width), bf16), sd((rows, width), bf16), sd((8, width), f32), sd((1, ff), f32),
+        out_shape=[sd((rows, width), bf16), sd((rows, width), bf16), sd((4 + steps, width), f32),
                    sd((rows, width), f32), *grads],
         compiler_params=params(),
         cost_estimate=cost(60),
@@ -747,7 +758,7 @@
         ),
         out_shape=out_shape,
         compiler_params=params(),
-        cost_estimate=cost(8),
+        cost_estimate=cost(2),
         name="qkv_weight_grad",
     )(idx, normed, gp)
 
@@ -759,20 +770,25 @@
 
     @pl.when(i == 0)
     def _():
-        for c in qkv_copies(idx_ref, pieces, w_scr, sem):
+        copies = qkv_copies(idx_ref, pieces, w_scr, sem)
+        for c in copies:
             c.start()
         gvec_ref[...] = jnp.zeros_like(gvec_ref)
-        for c in qkv_copies(idx_ref, pieces, w_scr, sem):
+        for c in copies:
             c.wait()
 
-    t = t_ref[...]
-    dn = dot(gp_ref[...], w_scr[...], NT)
-    start = x_ref[...].astype(f32) + t * vec_ref[0:1, :]
-    xhat, rstd = ln_parts(start)
-    gs = gm_ref[...] + ln_back(xhat, rstd, dn, vec_ref[1:2, :])
-    gi_ref[...] = gs.astype(bf16)
-    parts = [t * gs, dn * xhat, dn, gp_ref[:, :width].astype(f32), gp_ref[:, 2 * width :].astype(f32)]
-    gvec_ref[...] += jnp.concatenate([rows_sum(v) for v in parts] + [jnp.zeros((3, width), f32)], axis=0)
+    sums = None
+    dns = [dot(gp_ref[rs, :], w_scr[...], NT) for rs in sub_tiles()]
+    for rs, dn in zip(sub_tiles(), dns):
+        t = t_ref[rs, :]
+        start = x_ref[rs, :].astype(f32) + t * vec_ref[0:1, :]
+        xhat, rstd = ln_parts(start)
+        gs = gm_ref[rs, :] + ln_back(xhat, rstd, dn, vec_ref[1:2, :])
+        gi_ref[rs, :] = gs.astype(bf16)
+        parts = [t * gs, dn * xhat, dn, gp_ref[rs, :width].astype(f32), gp_ref[rs, 2 * width :].astype(f32)]
+        parts = [rows_sum(v) for v in parts]
+        sums = parts if sums is None else [a + b for a, b in zip(sums, parts)]
+    gvec_ref[...] += jnp.concatenate(sums + [jnp.zeros((3, width), f32)], axis=0)
 
 
 def first_backward(idx, x, t, gm, gp, vecs, pieces):
@@ -783,14 +799,14 @@
         functools.partial(first_kernel, n),
         grid_spec=pltpu.PrefetchScalarGridSpec(
             num_scalar_prefetch=1,
-            grid=(rows // TILE,),
-            in_specs=[row_spec(width), row_spec(1), row_spec(width), row_spec(3 * width), whole_spec(vecs.shape)] + [any_spec()] * n,
-            out_specs=[row_spec(width), whole_spec((8, width))],
+            grid=(rows // BLOCK,),
+            in_specs=[row_spec(width, BLOCK), row_spec(1, BLOCK), row_spec(width, BLOCK), row_spec(3 * width, BLOCK), whole_spec(vecs.shape)] + [any_spec()] * n,
+            out_specs=[row_spec(width, BLOCK), whole_spec((8, width))],
             scratch_shapes=[pltpu.VMEM((width, 3 * width), bf16), pltpu.SemaphoreType.DMA((n,))],
         ),
         out_shape=[sd((rows, width), bf16), sd((8, width), f32)],
         compiler_params=params(),
-        cost_estimate=cost(11),
+        cost_estimate=cost(3),
         name="first_backward",
     )(idx, x, t, gm, gp, vecs, *pieces)
 
@@ -832,32 +848,37 @@
     return jnp.transpose(weight.reshape(r, -1, width), (1, 0, 2)).reshape(-1, width)
 
 
-def far_first(kept, came, spot):
-    place = spot // 2
-    cut = kept.shape[1] // 32 * 16
-
-    def total(mask, rows):
-        pick = lambda v: lax.dynamic_index_in_dim(v, place ^ mask, 0, keepdims=False)[rows].astype(f32)
-        return (pick(kept) + pick(came)).astype(kept.dtype)
-
-    top, low = slice(None, cut), slice(cut, None)
-    stay = (total(0, top), total(2, top), total(0, low), total(1, low))
-    go_x = jnp.stack([total(1, top), total(3, top)])
-    go_y = jnp.stack([total(2, low), total(3, low)])
-    return stay, go_x, go_y
-
-
-def add_low(a, b):
-    return (a.astype(f32) + b.astype(f32)).astype(a.dtype)
-
-
-def far_second(stay, from_x, from_y):
-    own_top, y_top, own_low, x_low = stay
-    return (add_low(own_top, from_x[0]), add_low(own_low, from_y[0])), add_low(y_top, from_x[1]), add_low(x_low, from_y[1])
+def add_low(*terms):
+    total = terms[0].astype(f32)
+    for term in terms[1:]:
+        total = total + term.astype(f32)
+    return total.astype(terms[0].dtype)
+
+
+def place_rows(arrays, spot, mask, rows):
+    return [lax.dynamic_index_in_dim(v, (spot // 2) ^ mask, 0, keepdims=False)[rows] for v in arrays]
+
+
+def cut_of(arrays):
+    cut = arrays[0].shape[1] // 32 * 16
+    return slice(None, cut), slice(cut, None)
+
+
+def far_first(arrays, spot):
+    top, low = cut_of(arrays)
+    total = lambda mask, rows: add_low(*place_rows(arrays, spot, mask, rows))
+    return jnp.stack([total(1, top), total(3, top)]), jnp.stack([total(2, low), total(3, low)])
+
+
+def far_second(arrays, from_x, from_y, spot):
+    top, low = cut_of(arrays)
+    total = lambda mask, rows, more: add_low(*place_rows(arrays, spot, mask, rows), more)
+    own = total(0, top, from_x[0]), total(0, low, from_y[0])
+    return own, total(2, top, from_x[1]), total(1, low, from_y[1])
 
 
 def far_third(own, from_y, from_x):
-    return jnp.concatenate([add_low(own[0], from_y), add_low(own[1], from_x)])
+    return add_low(own[0], from_y), add_low(own[1], from_x)
 
 
 def halves(owned, spot):
@@ -945,13 +966,13 @@
     scale = (width // heads) ** (-0.5)
     times = time_of_row[:, None]
 
-    kernel_cols = jnp.concatenate([kernel_map, kernel_mean[:, None], kernel_width[:, None]], axis=1)
     vectors = (time_weight, ln1_gain, ln1_bias, q_bias, v_bias, out_bias, ln2_gain, ln2_bias, down_bias)
-    vectors = jnp.concatenate([jnp.stack(vectors), up_bias.reshape(wide, r)])
     if direct:
         lanes = 128
-        small = jnp.concatenate(
-            [jnp.pad(v, ((0, 0), (0, lanes - v.shape[1]))) for v in (kernel_cols, vectors)]
+        pieces = [v[None] for v in vectors] + [up_bias.reshape(-1, lanes), kernel_mean[None], kernel_width[None], kernel_map]
+        small = sum(
+            jnp.pad(v, ((at, 32 - at - v.shape[0]), (0, lanes - v.shape[1])))
+            for at, v in zip((*range(9), 9, 12, 13, 16), pieces)
         )
         pair = jnp.stack([small, near(small)])
         pair, w_first, w_second, coords, segment_ids, times = barrier(
@@ -961,27 +982,26 @@
         qkv_far = [w_first] + [swap(w_first, "fsdp", n, 2 * m) for m in range(1, n // 2)]
         second = jnp.concatenate([w_second[0], blocks_of(w_second[1], width), w_second[2]])
         small_all = in_order(jnp.concatenate([pair] + small_far), order)
-        kernel_cols, vectors = small_all[:, :own_kernels], small_all[:, own_kernels:, :r]
+        vectors, up_bias_all = small_all[:, :9, :r], small_all[:, 9:12].reshape(1, ff)
+        mean_all, width_all = (small_all[:, at, :own_kernels].reshape(kernels) for at in (12, 13))
+        map_all = small_all[:, 16 : 16 + own_kernels, :heads].reshape(kernels, heads)
     else:
-        kernel_cols = lax.all_gather(kernel_cols, "fsdp", axis=0).astype(f32)
-        vectors = lax.all_gather(vectors, "fsdp", axis=0).astype(f32)
+        gathered = lambda v: lax.all_gather(v, "fsdp", axis=0, tiled=True).astype(f32)
+        vectors = lax.all_gather(jnp.stack(vectors), "fsdp", axis=0).astype(f32)
+        up_bias_all, map_all = gathered(up_bias)[None], gathered(kernel_map)
+        mean_all, width_all = gathered(kernel_mean), gathered(kernel_width)
         qkv_p = (lax.all_gather(w_qkv, "fsdp", axis=0, tiled=True),)
         ffn_p = tuple(lax.all_gather(w, "fsdp", axis=0, tiled=True) for w in (w_out, w_up, w_down))
-    kernel_cols = kernel_cols.reshape(kernels, -1)
 
     aux_win, aux_col = aux_of(coords, segment_ids)
-    gmat, amat, kernel_columns = kernel_consts(
-        kernel_cols[:, heads], kernel_cols[:, heads + 1], kernel_cols[:, :heads].astype(bf16)
-    )
-    bmat = amat.T
-    done = attn_bias(0, aux_win, aux_col, gmat, bmat, ())
+    gmat, amat, kernel_columns = kernel_consts(mean_all, width_all, map_all.astype(bf16))
+    done = attn_bias(0, aux_win, aux_col, gmat, amat, ())
     if direct:
         done, second, qkv_far = barrier((done, second, qkv_far))
         qkv_p = tuple(with_near(qkv_far))
         from_x, from_y = along_x(second), along_y(second)
-    bias, feats = attn_bias(1, aux_win, aux_col, gmat, bmat, done)
-    vecs = jnp.transpose(vectors[:, :9], (1, 0, 2)).reshape(9, width)
-    up_bias_all = vectors[:, 9:].reshape(1, ff)
+    bias, feats = attn_bias(1, aux_win, aux_col, gmat, amat, done)
+    vecs = jnp.transpose(vectors, (1, 0, 2)).reshape(9, width)
 
     def rows_of(*picked):
         return jnp.concatenate([vecs[p : p + 1] for p in picked] + [jnp.zeros((8 - len(picked), width), f32)])
@@ -996,12 +1016,12 @@
         queries, from_x, from_y = barrier((queries, from_x, from_y))
         top_d, low_d = along_y(from_x[:cut]), along_x(from_y[cut:])
         ffn_p = with_near((second, from_x, from_y))
-    attended, probs = attn_fwd(1, queries, keys, values, bias, attn_fwd(0, queries, keys, values, bias, ()))
+    attended, probs = attn_fwd(0, queries, keys, values, bias, ())
     if direct:
         attended, top_d, low_d, ffn_p = barrier((attended, top_d, low_d, ffn_p))
         ffn_p = tuple(ffn_p + with_near((top_d, low_d)))
 
-    output, grad_attended, ffn_vecs, grad_up_bias, grad_middle, ffn_keep, ffn_send = ffn_both(
+    output, grad_attended, ffn_vecs, grad_middle, ffn_keep, ffn_send = ffn_both(
         order, inputs, times, attended, cotangent, ffn_rows, up_bias_all, ffn_p, ff, split
     )
     up_rows = wide * r
@@ -1017,51 +1037,64 @@
         return owned.reshape(-1, width)
 
     if direct:
-        ffn_came = near(ffn_send)
+        a = (ffn_keep, near(ffn_send))
         done = backward(0, ())
-        done, a = barrier((done, far_first(ffn_keep, ffn_came, spot)))
-        a = (a[0], along_x(a[1]), along_y(a[2]))
+        done, go_x, go_y = barrier((done, *far_first(a, spot)))
+        from_x, from_y = along_x(go_x), along_y(go_y)
         grad_projected, grad_scores = backward(3, backward(2, backward(1, done)))
         qkv_keep, qkv_send = qkv_weight_grad(order, normed, grad_projected, split)
-        qkv_keep, qkv_send, a = barrier((qkv_keep, qkv_send, far_second(*a)))
-        a = (a[0], along_y(a[1]), along_x(a[2]))
-        c = far_first(qkv_keep, near(qkv_send), spot)
+        qkv_keep, qkv_send, (own, go_y, go_x) = barrier((qkv_keep, qkv_send, far_second(a, from_x, from_y, spot)))
+        from_y, from_x = along_y(go_y), along_x(go_x)
+        c = (qkv_keep, near(qkv_send))
+        c_go = far_first(c, spot)
     else:
         grad_projected, grad_scores = backward(3, backward(2, backward(1, backward(0, ()))))
-        a = jnp.concatenate([scattered(ffn_keep[:wide], wide), scattered(ffn_send, 1), scattered(ffn_keep[wide:], 1)])
-        c = scattered(qkv_weight_grad(order, normed, grad_projected, split)[0], 3)
+        a = scattered(ffn_keep[:wide], wide)
+        b = jnp.concatenate([scattered(ffn_send, 1), scattered(ffn_keep[wide:], 1)])
+        qkv_owned = scattered(qkv_weight_grad(order, normed, grad_projected, split)[0], 3)
     grad_inputs, first_vecs = first_backward(
         order, inputs, times, grad_middle, grad_projected, back_rows, qkv_p
     )
     if direct:
-        grad_scores, first_vecs, a, c = barrier((grad_scores, first_vecs, far_third(*a), c))
-        c = (c[0], along_x(c[1]), along_y(c[2]))
-    a = lax.psum(a, "dp")
-
+        top, low = far_third(own, from_y, from_x)
+        a, b = top[:up_rows], jnp.concatenate([top[up_rows:], low])
+        a, b = halves(a, level), halves(b, level)
+        grad_scores, first_vecs, a, b, c_go = barrier((grad_scores, first_vecs, a, b, c_go))
+        c_from = along_x(c_go[0]), along_y(c_go[1])
+    else:
+        a, b = halves(a, level), halves(b, level)
+    a, b = rows_first(*a, planes), rows_first(*b, planes)
     sums = feat(0, ())
     if direct:
-        sums, c = barrier((sums, far_second(*c)))
-        c = (c[0], along_y(c[1]), along_x(c[2]))
+        sums, a, (own, go_y, go_x) = barrier((sums, a, far_second(c, *c_from, spot)))
+        from_y, from_x = along_y(go_y), along_x(go_x)
+    a = rows_middle(a, planes)
     sums = feat(1, sums)
     if direct:
-        c = far_third(*c)
-    sums, c = barrier((sums, halves(c, level)))
+        qkv_owned = jnp.concatenate(far_third(own, from_y, from_x))
+    sums, a, b, c = barrier((sums, a, b, halves(qkv_owned, level)))
     c = rows_first(*c, planes)
+    b = rows_middle(b, planes)
     sums = feat(2, sums)
     sums, c = barrier((sums, c))
     c = rows_middle(c, planes)
-    kernel_part = feat(3, sums)[2].reshape(n, own_kernels, -1)
-    kernel_part, c = barrier((kernel_part, c))
-
-    grad_rows = [first_vecs[:5], ffn_vecs[3:4], ffn_vecs[:3]]
-    vector_rows = jnp.transpose(jnp.concatenate(grad_rows).reshape(9, n, r), (1, 0, 2))
-    vector_rows = jnp.concatenate([vector_rows, grad_up_bias.reshape(n, wide, r)], axis=1)
-    vector_rows = jnp.pad(vector_rows, ((0, 0), (0, 0), (0, kernel_part.shape[2] - r)))
-    small, a = barrier((sum_owned(jnp.concatenate([kernel_part, vector_rows], axis=1), spot, n), a))
+    grad_up = rows_last(a, planes, level)
+    kernel_part, b, c = barrier((feat(3, sums)[2], b, c))
+    kernel_part = kernel_part.reshape(n, own_kernels, -1)
+    grad_low, grad_qkv = rows_last(b, planes, level), rows_last(c, planes, level)
+
+    lanes = kernel_part.shape[2]
+    grad_rows = jnp.concatenate([first_vecs[:5], ffn_vecs[3:4], ffn_vecs[:3]]).reshape(9, n, r)
+    grad_rows = jnp.pad(jnp.transpose(grad_rows, (1, 0, 2)), ((0, 0), (0, 0), (0, lanes - r)))
+    up_bias_rows = ffn_vecs[4:].reshape(n, -1)
+    up_bias_rows = jnp.pad(up_bias_rows, ((0, 0), (0, -up_bias_rows.shape[1] % lanes))).reshape(n, -1, lanes)
+    vector_rows = jnp.concatenate([grad_rows, up_bias_rows], axis=1)
+    small = sum_owned(jnp.concatenate([kernel_part, vector_rows], axis=1), spot, n)
+    small, grad_up, grad_low, grad_qkv = barrier((small, grad_up, grad_low, grad_qkv))
     small = sum_planes(small, planes)
-    gaussians, vectors = small[:own_kernels], small[own_kernels:, :r]
-    grad_qkv = rows_last(c, planes, level)
-    grad_up, grad_down, grad_out = a[:up_rows], a[up_rows : 2 * up_rows], a[2 * up_rows :]
+    gaussians, vectors = small[:own_kernels], small[own_kernels : own_kernels + 9, :r]
+    grad_up_bias = small[own_kernels + 9 :].reshape(-1)[:up_rows]
+    grad_down, grad_out = grad_low[:up_rows], grad_low[up_rows:]
 
     def columns(array):
         return jnp.transpose(array.reshape(-1, r, width), (1, 0, 2)).reshape(r, -1)
@@ -1083,7 +1116,7 @@
         vectors[6],
         vectors[7],
         columns(grad_up).astype(f32),
-        vectors[9:].reshape(up_rows),
+        grad_up_bias,
         grad_down.astype(f32),
         vectors[8],
     )

time: 351 us -> 332 us (0.946)
  between operations: 15 us -> 1.75 us
  starting transfers between devices: 39 us -> 47.5 us
  other arithmetic: 27.3 us -> 20.4 us
  Pallas kernels: 207 us -> 202 us
  local copies, waits for them, and re-layouts: 28.2 us -> 24.5 us
    ppermute x43 -> x49, starting transfers between devices: 38.9 us -> 47.5 us  [swap(): return lax.ppermute(value, axis, [(i, i ^ bit_mask) for i in range(size)])]
    pallas_call x2 -> x1, Pallas kernels: 22.2 us -> 19.8 us  [attn_fwd(): pl.pallas_call(functools.partial(skip_refs, fwd_kernel, n_in, len(before)...]
    ppermute x43 -> x49, waiting for transfers between devices: 30.6 us -> 32.3 us  [swap(): return lax.ppermute(value, axis, [(i, i ^ bit_mask) for i in range(size)])]
    convert_element_type x14 -> x17, other arithmetic: 16.1 us -> 14.6 us  [the longest x14 14.4 us: add_low(): return total.astype(terms[0].dtype)]
  transfers between devices with their start and end apart: 44 -> 49, of which waited for: 13 -> 13; matrix products, arithmetic and copies ran while one was open for 10% -> 8% of each run, Pallas kernels for 44% -> 45%
where the time goes in v4:
time: 332 us; the launch traced here: 329 us
  Pallas kernels  202 us (61%)
  starting transfers between devices  47.5 us (14%)
  waiting for transfers between devices  32.3 us (10%)
  local copies, waits for them, and re-layouts  24.5 us (7%)
  other arithmetic  20.4 us (6%)
    pallas_call x1, Pallas kernels, ffn_both(): pl.pallas_call(functools.partial(ffn_kernel, n, split, steps), grid_spec=...  55.1 us
    ppermute x49, starting transfers between devices, swap(): return lax.ppermute(value, axis, [(i, i ^ bit_mask) for i in range(size)])  47.5 us
    pallas_call x4, Pallas kernels, attn_feat(): pl.pallas_call(functools.partial(feat_kernel, len(before), last), grid=(p...  37.9 us
    pallas_call x4, Pallas kernels, attn_bwd(): pl.pallas_call(functools.partial(skip_refs, functools.partial(bwd_kernel,...  32.7 us
    ppermute x49, waiting for transfers between devices, swap(): return lax.ppermute(value, axis, [(i, i ^ bit_mask) for i in range(size)])  32.3 us
    pallas_call x2, Pallas kernels, attn_bias(): pl.pallas_call(functools.partial(skip_refs, bias_kernel, n_in, len(before...  26.1 us
    pallas_call x1, Pallas kernels, attn_fwd(): pl.pallas_call(functools.partial(skip_refs, fwd_kernel, n_in, len(before)...  19.8 us
    convert_element_type x14, other arithmetic, add_low(): return total.astype(terms[0].dtype)  14.4 us
  transfers between devices with their start and end apart: 49, of which 13 were waited for; matrix products, arithmetic and copies ran while one was open for 8% of the time, Pallas kernels for 45%

profile of v4, /device:TPU:0, one launch (start us, length us, event | category | flops | bytes accessed | tf_op | source)
XLA Modules:
  0.0 328.5 jit_solution(894713666866300175)
XLA Ops:
  0.7 0.9 pad_add_fusion
  2.9 2.8 collective-permute-start.1
  5.8 1.5 collective-permute-start.2
  7.3 2.0 collective-permute-start.4
  9.2 1.5 collective-permute-start.5
  13.4 1.1 copy.144
  15.3 1.2 copy.116
  16.6 1.0 copy.126.t_ref
  19.5 1.0 copy.122.refs_3_
  20.5 13.1 %attn_bias.2 = (f32[32,128,1024]{2,1,0:T(8,128)}, bf16[32,1024,512]{2,1,0:T(8,128)(2,1)}) custom-call(f32[32,8,128]{2,1,0:T(8,128)} %copy-done.2, f32[1024,4]{1,0:T(8,128)} %bitcast.251, bf16[1024,128]{1,0:T(8,128)(2,1)} %copy.121.refs_2_, bf16[1024,256]{1,0:T(8,128)(2,1)} %copy.122.refs_3_), custom_call_target="tpu_custom_call" | custom-call | flops 2307000064 | tf_op jit(solution)/shard_map/attn_bias/pallas_call | solution.py:286
  36.1 1.9 collective-permute-start.11
  38.0 1.5 collective-permute-start.12
  42.7 13.0 %attn_bias.3 = (f32[32,128,1024]{2,1,0:T(8,128)}, bf16[32,1024,512]{2,1,0:T(8,128)(2,1)}) custom-call(f32[32,8,128]{2,1,0:T(8,128)} %copy-done.2, f32[1024,4]{1,0:T(8,128)} %bitcast.252, bf16[1024,128]{1,0:T(8,128)(2,1)} %copy.121.refs_2_, bf16[1024,256]{1,0:T(8,128)(2,1)} %copy.122.refs_3_, ...), custom_call_target="tpu_custom_call", output_to_operand_aliasing={{0}: (4, {}), {1}: (5, {})} | custom-call | flops 2307000064 | tf_op jit(solution)/shard_map/attn_bias/pallas_call | solution.py:286
  55.8 9.7 %qkv_forward.1 = (bf16[1024,768]{1,0:T(8,128)(2,1)}, bf16[1024,768]{1,0:T(8,128)(2,1)}, bf16[1024,768]{1,0:T(8,128)(2,1)}, bf16[1024,768]{1,0:T(8,128)(2,1)}) custom-call(s32[8]{0:T(128)} %copy-done.16, bf16[1024,768]{1,0:T(8,128)(2,1)} %x_ref.5, f32[1024,1]{1,0:T(8,128)} %copy.126.t_ref, f32[8,768]{1,0:T(8,128)} %concatenate.53.vec_ref, ...), custom_call_target="tpu_custom_call" | custom-call | flops 11534999552 | tf_op jit(solution)/shard_map/qkv_forward/pallas_call | solution.py:519
  65.5 1.9 collective-permute-done.11.rest_2_
  67.4 1.5 collective-permute-done.12.rest_4_
  68.9 1.2 slice.437
  70.6 1.1 slice.438
  71.7 1.6 collective-permute-start.13
  73.9 19.8 %attn_fwd.1 = (bf16[1024,768]{1,0:T(8,128)(2,1)}, bf16[32,128,1024]{2,1,0:T(8,128)(2,1)}) custom-call(bf16[1024,768]{1,0:T(8,128)(2,1)} %get-tuple-element.165.refs_0_, bf16[1024,768]{1,0:T(8,128)(2,1)} %get-tuple-element.166.refs_1_.refs_2_, bf16[1024,768]{1,0:T(8,128)(2,1)} %get-tuple-element.167.refs_2_.refs_3_, f32[32,128,1024]{2,1,0:T(8,128)} %get-tuple-element.168.refs_3_), custom_call_target="tpu_custom_call" | custom-call | flops 18456000512 | tf_op jit(solution)/shard_map/attn_fwd/pallas_call | solution.py:309
  94.3 2.8 collective-permute-done.19.rest_9_
  97.8 0.9 copy-done.18
  98.7 55.1 %ffn_both.1 = (bf16[1024,768]{1,0:T(8,128)(2,1)}, bf16[1024,768]{1,0:T(8,128)(2,1)}, f32[8,768]{1,0:T(8,128)}, f32[1024,768]{1,0:T(8,128)}, bf16[4,864,768]{2,1,0:T(8,128)(2,1)}, /*index=5*/bf16[4,864,768]{2,1,0:T(8,128)(2,1)}) custom-call(s32[8]{0:T(128)} %copy-done.16, bf16[1024,768]{1,0:T(8,128)(2,1)} %x_ref.5, f32[1024,1]{1,0:T(8,128)} %copy.126.t_ref, ...), custom_call_target="tpu_custom_call" | custom-call | flops 69209997312 | tf_op jit(solution)/shard_map/ffn_both/pallas_call | solution.py:701
  154.0 8.2 %attn_bwd.4 = (bf16[1024,2304]{1,0:T(8,128)(2,1)}, bf16[32,512,256]{2,1,0:T(8,128)(2,1)}) custom-call(bf16[1024,768]{1,0:T(8,128)(2,1)} %get-tuple-element.165.refs_0_, bf16[1024,768]{1,0:T(8,128)(2,1)} %get-tuple-element.185.refs_1_, bf16[1024,768]{1,0:T(8,128)(2,1)} %get-tuple-element.166.refs_1_.refs_2_, ...), custom_call_target="tpu_custom_call" | custom-call | flops 2307000064 | tf_op jit(solution)/shard_map/attn_bwd/pallas_call | solution.py:334
  163.0 3.1 add_convert_fusion.7
  166.4 1.6 collective-permute-start.21
  168.4 8.1 %attn_bwd.5 = (bf16[1024,2304]{1,0:T(8,128)(2,1)}, bf16[32,512,256]{2,1,0:T(8,128)(2,1)}) custom-call(bf16[1024,768]{1,0:T(8,128)(2,1)} %get-tuple-element.165.refs_0_, bf16[1024,768]{1,0:T(8,128)(2,1)} %get-tuple-element.185.refs_1_, bf16[1024,768]{1,0:T(8,128)(2,1)} %get-tuple-element.166.refs_1_.refs_2_, ...), custom_call_target="tpu_custom_call", output_to_operand_aliasing={{0}: (5, {}), {1}: (6, {})} | custom-call | flops 2307000064 | tf_op jit(solution)/shard_map/attn_bwd/pallas_call | solution.py:334
  176.6 8.2 %attn_bwd.6 = (bf16[1024,2304]{1,0:T(8,128)(2,1)}, bf16[32,512,256]{2,1,0:T(8,128)(2,1)}) custom-call(bf16[1024,768]{1,0:T(8,128)(2,1)} %get-tuple-element.165.refs_0_, bf16[1024,768]{1,0:T(8,128)(2,1)} %get-tuple-element.185.refs_1_, bf16[1024,768]{1,0:T(8,128)(2,1)} %get-tuple-element.166.refs_1_.refs_2_, ...), custom_call_target="tpu_custom_call", output_to_operand_aliasing={{0}: (5, {}), {1}: (6, {})} | custom-call | flops 2307000064 | tf_op jit(solution)/shard_map/attn_bwd/pallas_call | solution.py:334
  184.7 8.2 %attn_bwd.7 = (bf16[1024,2304]{1,0:T(8,128)(2,1)}, bf16[32,512,256]{2,1,0:T(8,128)(2,1)}) custom-call(bf16[1024,768]{1,0:T(8,128)(2,1)} %get-tuple-element.165.refs_0_, bf16[1024,768]{1,0:T(8,128)(2,1)} %get-tuple-element.185.refs_1_, bf16[1024,768]{1,0:T(8,128)(2,1)} %get-tuple-element.166.refs_1_.refs_2_, ...), custom_call_target="tpu_custom_call", output_to_operand_aliasing={{0}: (5, {}), {1}: (6, {})} | custom-call | flops 2307000064 | tf_op jit(solution)/shard_map/attn_bwd/pallas_call | solution.py:334
  192.9 8.9 %qkv_weight_grad.1 = (bf16[4,288,768]{2,1,0:T(8,128)(2,1)}, bf16[4,288,768]{2,1,0:T(8,128)(2,1)}) custom-call(s32[8]{0:T(128)} %copy-done.16, bf16[1024,768]{1,0:T(8,128)(2,1)} %get-tuple-element.202.normed_ref, bf16[1024,2304]{1,0:T(8,128)(2,1)} %get-tuple-element.197.gp_ref), custom_call_target="tpu_custom_call" | custom-call | flops 2307000064 | tf_op jit(solution)/shard_map/qkv_weight_grad/pallas_call | solution.py:750
  201.9 5.1 %fusion.3 = (bf16[432,768]{1,0:T(8,128)(2,1)}, bf16[432,768]{1,0:T(8,128)(2,1)S(1)}, bf16[432,768]{1,0:T(8,128)(2,1)S(1)}, bf16[432,768]{1,0:T(8,128)(2,1)S(1)}) fusion(bf16[2,432,768]{2,1,0:T(8,128)(2,1)} %collective-permute-done.22, bf16[4,864,768]{2,1,0:T(8,128)(2,1)} %collective-permute-done.20, s32[]{:T(128)S(6)} %select_n.175, s32[]{:T(128)S(6)} %add.411, ...), kind=kLoop, calls=%fused_computation.22 | loop fusion | flops 7962624 | bytes 10616848 | tf_op jit(solution)/shard_map/convert_element_type | solution.py:855
  206.9 1.7 collective-permute-start.23
  209.0 11.8 %first_backward.1 = (bf16[1024,768]{1,0:T(8,128)(2,1)}, f32[8,768]{1,0:T(8,128)}) custom-call(s32[8]{0:T(128)} %copy-done.16, bf16[1024,768]{1,0:T(8,128)(2,1)} %x_ref.5, f32[1024,1]{1,0:T(8,128)} %copy.126.t_ref, f32[1024,768]{1,0:T(8,128)} %get-tuple-element.184.gm_ref, bf16[1024,2304]{1,0:T(8,128)(2,1)} %get-tuple-element.197.gp_ref, ...), custom_call_target="tpu_custom_call" | custom-call | flops 3460499968 | tf_op jit(solution)/shard_map/first_backward/pallas_call | solution.py:798
  220.8 3.4 %collective-permute-done.23 = bf16[432,768]{1,0:T(8,128)(2,1)S(1)} collective-permute-done((bf16[432,768]{1,0:T(8,128)(2,1)S(1)}, bf16[432,768]{1,0:T(8,128)(2,1)S(1)}, u32[]{:S(2)}, u32[]{:S(2)}) %collective-permute-start.23) | collective-permute-done | bytes 663584 | tf_op jit(solution)/shard_map/ppermute | solution.py:818
  227.6 1.5 add_convert_fusion.23
  230.0 1.6 collective-permute-start.26
  232.0 1.1 collective-permute-start.28
  233.0 1.0 copy.131.amat_ref
  234.6 9.3 %attn_feat.4 = (f32[128,256]{1,0:T(8,128)}, f32[2,128,128]{2,1,0:T(8,128)}) custom-call(bf16[32,512,256]{2,1,0:T(8,128)(2,1)} %get-tuple-element.213.ds_ref, bf16[32,1024,512]{2,1,0:T(8,128)(2,1)} %get-tuple-element.214.f_ref, f32[32,8,128]{2,1,0:T(8,128)} %copy-done.2, f32[1024,4]{1,0:T(8,128)} %bitcast.253, bf16[1024,256]{1,0:T(8,128)(2,1)} %copy.131.amat_ref, ...), custom_call_target="tpu_custom_call" | custom-call | flops 1153500032 | tf_op jit(solution)/shard_map/attn_feat/pallas_call | solution.py:357
  243.9 1.0 add_convert_fusion.13
  244.9 1.9 fusion.9
  246.8 1.0 collective-permute-start.31
  247.9 1.1 add_convert_fusion.11
  248.9 1.7 collective-permute-start.32
  250.6 2.6 collective-permute-start.29
  253.2 9.4 %attn_feat.5 = (f32[128,256]{1,0:T(8,128)}, f32[2,128,128]{2,1,0:T(8,128)}) custom-call(bf16[32,512,256]{2,1,0:T(8,128)(2,1)} %get-tuple-element.213.ds_ref, bf16[32,1024,512]{2,1,0:T(8,128)(2,1)} %get-tuple-element.214.f_ref, f32[32,8,128]{2,1,0:T(8,128)} %copy-done.2, f32[1024,4]{1,0:T(8,128)} %bitcast.254, bf16[1024,256]{1,0:T(8,128)(2,1)} %copy.131.amat_ref, ...), custom_call_target="tpu_custom_call" | custom-call | flops 1153500032 | tf_op jit(solution)/shard_map/attn_feat/pallas_call | solution.py:357
  262.8 1.7 collective-permute-done.29
  265.4 3.4 %collective-permute-start.34 = (bf16[240,768]{1,0:T(8,128)(2,1)S(1)}, bf16[240,768]{1,0:T(8,128)(2,1)S(1)}, u32[]{:S(2)}, u32[]{:S(2)}) collective-permute-start(bf16[240,768]{1,0:T(8,128)(2,1)S(1)} %add_convert_fusion.11), channel_id=1, source_target_pairs={{0,2},{1,3},{2,0},{3,1},{4,6},{5,7},{6,4},{7,5},{8,10},{9,11},{10,... | collective-permute-start | bytes 1105928 | tf_op jit(solution)/shard_map/ppermute | solution.py:818
  268.9 9.6 %attn_feat.6 = (f32[128,256]{1,0:T(8,128)}, f32[2,128,128]{2,1,0:T(8,128)}) custom-call(bf16[32,512,256]{2,1,0:T(8,128)(2,1)} %get-tuple-element.213.ds_ref, bf16[32,1024,512]{2,1,0:T(8,128)(2,1)} %get-tuple-element.214.f_ref, f32[32,8,128]{2,1,0:T(8,128)} %copy-done.2, f32[1024,4]{1,0:T(8,128)} %bitcast.255, bf16[1024,256]{1,0:T(8,128)(2,1)} %copy.131.amat_ref, ...), custom_call_target="tpu_custom_call" | custom-call | flops 1153500032 | tf_op jit(solution)/shard_map/attn_feat/pallas_call | solution.py:357
  278.5 0.9 collective-permute-start.35
  279.5 9.7 %attn_feat.7 = (f32[128,256]{1,0:T(8,128)}, f32[2,128,128]{2,1,0:T(8,128)}, f32[128,128]{1,0:T(8,128)}) custom-call(bf16[32,512,256]{2,1,0:T(8,128)(2,1)} %get-tuple-element.213.ds_ref, bf16[32,1024,512]{2,1,0:T(8,128)(2,1)} %get-tuple-element.214.f_ref, f32[32,8,128]{2,1,0:T(8,128)} %copy-done.2, f32[1024,4]{1,0:T(8,128)} %bitcast.256, ...), custom_call_target="tpu_custom_call" | custom-call | flops 1153500032 | tf_op jit(solution)/shard_map/attn_feat/pallas_call | solution.py:357
  289.3 5.5 %collective-permute-done.35 = bf16[144,768]{1,0:T(8,128)(2,1)S(1)} collective-permute-done((bf16[144,768]{1,0:T(8,128)(2,1)S(1)}, bf16[144,768]{1,0:T(8,128)(2,1)S(1)}, u32[]{:S(2)}, u32[]{:S(2)}) %collective-permute-start.35) | collective-permute-done | bytes 221216 | tf_op jit(solution)/shard_map/ppermute | solution.py:818
  295.5 1.5 collective-permute-start.38
  296.9 1.4 collective-permute-start.39
  298.6 1.2 collective-permute-start.41
  299.9 1.5 collective-permute-start.42
  301.5 2.0 collective-permute-start.44
  304.0 5.8 %collective-permute-done.45 = bf16[144,768]{1,0:T(8,128)(2,1)S(1)} collective-permute-done((bf16[144,768]{1,0:T(8,128)(2,1)S(1)}, bf16[144,768]{1,0:T(8,128)(2,1)S(1)}, u32[]{:S(2)}, u32[]{:S(2)}) %collective-permute-start.45) | collective-permute-done | bytes 221216 | tf_op jit(solution)/shard_map/ppermute | solution.py:818
  309.9 7.2 %collective-permute-done.44 = bf16[240,768]{1,0:T(8,128)(2,1)S(1)} collective-permute-done((bf16[240,768]{1,0:T(8,128)(2,1)S(1)}, bf16[240,768]{1,0:T(8,128)(2,1)S(1)}, u32[]{:S(2)}, u32[]{:S(2)}) %collective-permute-start.44) | collective-permute-done | bytes 368672 | tf_op jit(solution)/shard_map/ppermute | solution.py:818
  317.6 2.7 collective-permute-start.47
  320.3 1.4 collective-permute-start.48
  321.7 1.1 slice.498
  323.5 1.1 copy.137
  324.7 1.0 copy.136
  (230 shorter events, 28.7 us)
Async XLA Ops:
  0.7 13.9 %copy-start.10 = (bf16[96,768]{1,0:T(8,128)(2,1)S(1)}, bf16[96,768]{1,0:T(8,128)(2,1)}, u32[]{:S(2)}) copy-start(bf16[96,768]{1,0:T(8,128)(2,1)} %param.33) | copy-start | bytes 442372
  0.7 13.9 %copy-start.5 = (bf16[384,768]{1,0:T(8,128)(2,1)S(1)}, bf16[384,768]{1,0:T(8,128)(2,1)}, u32[]{:S(2)}) copy-start(bf16[384,768]{1,0:T(8,128)(2,1)} %param.42) | copy-start | bytes 1769476
  1.6 1.3 collective-permute-start
  2.1 12.6 %copy-start.16 = (s32[8]{0:T(128)}, s32[8]{0:T(128)S(1)}, u32[]{:S(2)}) copy-start(s32[8]{0:T(128)S(1)} %iota_xor_fusion.idx_ref) | copy-start | bytes 100
  2.9 14.7 %collective-permute-start.1 = (bf16[2,32,128]{2,1,0:T(8,128)(2,1)S(1)}, bf16[2,32,128]{2,1,0:T(8,128)(2,1)S(1)}, u32[]{:S(2)}, u32[]{:S(2)}) collective-permute-start(bf16[2,32,128]{2,1,0:T(8,128)(2,1)S(1)} %pad_maximum_fusion.8), channel_id=1, source_target_pairs={{0,8},{4,12},{8,0},{12,4},{16,24},{20,28},{24,16},{28,20},{1,9},{5... | collective-permute-start | bytes 49160 | tf_op jit(solution)/shard_map/ppermute | solution.py:818
  5.8 11.9 %collective-permute-start.2 = (bf16[2,32,128]{2,1,0:T(8,128)(2,1)S(1)}, bf16[2,32,128]{2,1,0:T(8,128)(2,1)S(1)}, u32[]{:S(2)}, u32[]{:S(2)}) collective-permute-start(bf16[2,32,128]{2,1,0:T(8,128)(2,1)S(1)} %pad_maximum_fusion.8), channel_id=1, source_target_pairs={{0,16},{4,20},{8,24},{12,28},{16,0},{20,4},{24,8},{28,12},{1,17},{... | collective-permute-start | bytes 49160 | tf_op jit(solution)/shard_map/ppermute | solution.py:818
  7.3 10.4 %collective-permute-start.3 = (bf16[2,32,128]{2,1,0:T(8,128)(2,1)S(1)}, bf16[2,32,128]{2,1,0:T(8,128)(2,1)S(1)}, u32[]{:S(2)}, u32[]{:S(2)}) collective-permute-start(bf16[2,32,128]{2,1,0:T(8,128)(2,1)S(1)} %pad_maximum_fusion.8), channel_id=1, source_target_pairs={{0,24},{4,28},{8,16},{12,20},{16,8},{20,12},{24,0},{28,4},{1,25},{... | collective-permute-start | bytes 49160 | tf_op jit(solution)/shard_map/ppermute | solution.py:818
  7.3 26.4 %collective-permute-start.4 = (bf16[96,2304]{1,0:T(8,128)(2,1)}, bf16[96,2304]{1,0:T(8,128)(2,1)S(1)}, u32[]{:S(2)}, u32[]{:S(2)}) collective-permute-start(bf16[96,2304]{1,0:T(8,128)(2,1)} %rest_0_.1), channel_id=1, source_target_pairs={{0,8},{4,12},{8,0},{12,4},{16,24},{20,28},{24,16},{28,20},{1,9},{5... | collective-permute-start | bytes 1327112 | tf_op jit(solution)/shard_map/ppermute | solution.py:818
  9.2 24.5 %collective-permute-start.5 = (bf16[96,2304]{1,0:T(8,128)(2,1)}, bf16[96,2304]{1,0:T(8,128)(2,1)}, u32[]{:S(2)}, u32[]{:S(2)}) collective-permute-start(bf16[96,2304]{1,0:T(8,128)(2,1)} %rest_0_.1), channel_id=1, source_target_pairs={{0,16},{4,20},{8,24},{12,28},{16,0},{20,4},{24,8},{28,12},{1,17},{... | collective-permute-start | bytes 1327112 | tf_op jit(solution)/shard_map/ppermute | solution.py:818
  14.6 1.9 copy-start.15
  14.6 3.0 copy-start.6
  15.3 40.3 %copy-start.4 = (bf16[864,768]{1,0:T(8,128)(2,1)}, bf16[864,768]{1,0:T(8,128)(2,1)S(1)}, u32[]{:S(2)}) copy-start(bf16[864,768]{1,0:T(8,128)(2,1)S(1)} %pad_maximum_fusion.rest_0_) | copy-start | bytes 3981316
  17.6 16.1 %collective-permute-start.6 = (bf16[96,2304]{1,0:T(8,128)(2,1)S(1)}, bf16[96,2304]{1,0:T(8,128)(2,1)S(1)}, u32[]{:S(2)}, u32[]{:S(2)}) collective-permute-start(bf16[96,2304]{1,0:T(8,128)(2,1)S(1)} %copy-done.6), channel_id=1, source_target_pairs={{0,24},{4,28},{8,16},{12,20},{16,8},{20,12},{24,0},{28,4},{1,25},{... | collective-permute-start | bytes 1327112 | tf_op jit(solution)/shard_map/ppermute | solution.py:818
  19.5 14.2 %copy-start = (bf16[32,8,8,128]{3,1,2,0:T(8,128)(2,1)}, bf16[32,8,8,128]{3,1,2,0:T(8,128)(2,1)S(1)}, u32[]{:S(2)}) copy-start(bf16[32,8,8,128]{3,1,2,0:T(8,128)(2,1)S(1)} %copy.145) | copy-start | bytes 1572868
  33.7 21.9 %copy-start.7 = (bf16[96,2304]{1,0:T(8,128)(2,1)}, bf16[96,2304]{1,0:T(8,128)(2,1)S(1)}, u32[]{:S(2)}) copy-start(bf16[96,2304]{1,0:T(8,128)(2,1)S(1)} %collective-permute-done.4.rest_2_) | copy-start | bytes 1327108
  33.7 21.9 %copy-start.8 = (bf16[96,2304]{1,0:T(8,128)(2,1)}, bf16[96,2304]{1,0:T(8,128)(2,1)S(1)}, u32[]{:S(2)}) copy-start(bf16[96,2304]{1,0:T(8,128)(2,1)S(1)} %collective-permute-done.6.rest_6_) | copy-start | bytes 1327108
  33.7 4.3 %collective-permute-start.10 = (bf16[96,2304]{1,0:T(8,128)(2,1)S(1)}, bf16[96,2304]{1,0:T(8,128)(2,1)S(1)}, u32[]{:S(2)}, u32[]{:S(2)}) collective-permute-start(bf16[96,2304]{1,0:T(8,128)(2,1)S(1)} %collective-permute-done.6.rest_6_), channel_id=1, source_target_pairs={{0,4},{4,0},{8,12},{12,8},{16,20},{20,16},{24,28},{28,24},{1,5},{5... | collective-permute-start | bytes 1327112 | tf_op jit(solution)/shard_map/ppermute | solution.py:818
  35.0 20.7 %collective-permute-start.7 = (bf16[96,2304]{1,0:T(8,128)(2,1)S(1)}, bf16[96,2304]{1,0:T(8,128)(2,1)}, u32[]{:S(2)}, u32[]{:S(2)}) collective-permute-start(bf16[96,2304]{1,0:T(8,128)(2,1)S(1)} %copy-done.6), channel_id=1, source_target_pairs={{0,4},{4,0},{8,12},{12,8},{16,20},{20,16},{24,28},{28,24},{1,5},{5... | collective-permute-start | bytes 1327112 | tf_op jit(solution)/shard_map/ppermute | solution.py:818
  35.5 20.3 %collective-permute-start.8 = (bf16[96,2304]{1,0:T(8,128)(2,1)S(1)}, bf16[96,2304]{1,0:T(8,128)(2,1)}, u32[]{:S(2)}, u32[]{:S(2)}) collective-permute-start(bf16[96,2304]{1,0:T(8,128)(2,1)S(1)} %collective-permute-done.4.rest_2_), channel_id=1, source_target_pairs={{0,4},{4,0},{8,12},{12,8},{16,20},{20,16},{24,28},{28,24},{1,5},{5... | collective-permute-start | bytes 1327112 | tf_op jit(solution)/shard_map/ppermute | solution.py:818
  35.5 20.3 %collective-permute-start.9 = (bf16[96,2304]{1,0:T(8,128)(2,1)}, bf16[96,2304]{1,0:T(8,128)(2,1)}, u32[]{:S(2)}, u32[]{:S(2)}) collective-permute-start(bf16[96,2304]{1,0:T(8,128)(2,1)} %collective-permute-done.5.rest_4_), channel_id=1, source_target_pairs={{0,4},{4,0},{8,12},{12,8},{16,20},{20,16},{24,28},{28,24},{1,5},{5... | collective-permute-start | bytes 1327112 | tf_op jit(solution)/shard_map/ppermute | solution.py:818
  36.1 31.4 %collective-permute-start.11 = (bf16[864,768]{1,0:T(8,128)(2,1)S(1)}, bf16[864,768]{1,0:T(8,128)(2,1)}, u32[]{:S(2)}, u32[]{:S(2)}) collective-permute-start(bf16[864,768]{1,0:T(8,128)(2,1)S(1)} %pad_maximum_fusion.rest_0_), channel_id=1, source_target_pairs={{0,8},{4,12},{8,0},{12,4},{16,24},{20,28},{24,16},{28,20},{1,9},{5... | collective-permute-start | bytes 3981320 | tf_op jit(solution)/shard_map/ppermute | solution.py:818
  38.0 17.7 %copy-start.9 = (bf16[96,2304]{1,0:T(8,128)(2,1)}, bf16[96,2304]{1,0:T(8,128)(2,1)S(1)}, u32[]{:S(2)}) copy-start(bf16[96,2304]{1,0:T(8,128)(2,1)S(1)} %collective-permute-done.10.rest_7_) | copy-start | bytes 1327108
  38.0 30.9 %collective-permute-start.12 = (bf16[864,768]{1,0:T(8,128)(2,1)S(1)}, bf16[864,768]{1,0:T(8,128)(2,1)}, u32[]{:S(2)}, u32[]{:S(2)}) collective-permute-start(bf16[864,768]{1,0:T(8,128)(2,1)S(1)} %pad_maximum_fusion.rest_0_), channel_id=1, source_target_pairs={{0,16},{4,20},{8,24},{12,28},{16,0},{20,4},{24,8},{28,12},{1,17},{... | collective-permute-start | bytes 3981320 | tf_op jit(solution)/shard_map/ppermute | solution.py:818
  55.7 37.9 %collective-permute-start.15 = (bf16[864,768]{1,0:T(8,128)(2,1)S(1)}, bf16[864,768]{1,0:T(8,128)(2,1)}, u32[]{:S(2)}, u32[]{:S(2)}) collective-permute-start(bf16[864,768]{1,0:T(8,128)(2,1)S(1)} %pad_maximum_fusion.rest_0_), channel_id=1, source_target_pairs={{0,4},{4,0},{8,12},{12,8},{16,20},{20,16},{24,28},{28,24},{1,5},{5... | collective-permute-start | bytes 3981320 | tf_op jit(solution)/shard_map/ppermute | solution.py:818
  70.1 23.6 %collective-permute-start.16 = (bf16[864,768]{1,0:T(8,128)(2,1)}, bf16[864,768]{1,0:T(8,128)(2,1)}, u32[]{:S(2)}, u32[]{:S(2)}) collective-permute-start(bf16[864,768]{1,0:T(8,128)(2,1)} %collective-permute-done.11.rest_2_), channel_id=1, source_target_pairs={{0,4},{4,0},{8,12},{12,8},{16,20},{20,16},{24,28},{28,24},{1,5},{5... | collective-permute-start | bytes 3981320 | tf_op jit(solution)/shard_map/ppermute | solution.py:818
  70.1 23.5 %collective-permute-start.17 = (bf16[864,768]{1,0:T(8,128)(2,1)}, bf16[864,768]{1,0:T(8,128)(2,1)}, u32[]{:S(2)}, u32[]{:S(2)}) collective-permute-start(bf16[864,768]{1,0:T(8,128)(2,1)} %collective-permute-done.12.rest_4_), channel_id=1, source_target_pairs={{0,4},{4,0},{8,12},{12,8},{16,20},{20,16},{24,28},{28,24},{1,5},{5... | collective-permute-start | bytes 3981320 | tf_op jit(solution)/shard_map/ppermute | solution.py:818
  71.7 21.9 %collective-permute-start.13 = (bf16[480,768]{1,0:T(8,128)(2,1)S(1)}, bf16[480,768]{1,0:T(8,128)(2,1)S(1)}, u32[]{:S(2)}, u32[]{:S(2)}) collective-permute-start(bf16[480,768]{1,0:T(8,128)(2,1)S(1)} %slice.437), channel_id=1, source_target_pairs={{0,16},{4,20},{8,24},{12,28},{16,0},{20,4},{24,8},{28,12},{1,17},{... | collective-permute-start | bytes 2211848 | tf_op jit(solution)/shard_map/ppermute | solution.py:818
  73.3 20.3 %collective-permute-start.14 = (bf16[384,768]{1,0:T(8,128)(2,1)S(1)}, bf16[384,768]{1,0:T(8,128)(2,1)}, u32[]{:S(2)}, u32[]{:S(2)}) collective-permute-start(bf16[384,768]{1,0:T(8,128)(2,1)S(1)} %slice.438), channel_id=1, source_target_pairs={{0,8},{4,12},{8,0},{12,4},{16,24},{20,28},{24,16},{28,20},{1,9},{5... | collective-permute-start | bytes 1769480 | tf_op jit(solution)/shard_map/ppermute | solution.py:818
  93.7 3.4 %copy-start.17 = (bf16[480,768]{1,0:T(8,128)(2,1)}, bf16[480,768]{1,0:T(8,128)(2,1)S(1)}, u32[]{:S(2)}) copy-start(bf16[480,768]{1,0:T(8,128)(2,1)S(1)} %collective-permute-done.13.rest_6_) | copy-start | bytes 2211844
  93.7 3.3 %collective-permute-start.18 = (bf16[480,768]{1,0:T(8,128)(2,1)S(1)}, bf16[480,768]{1,0:T(8,128)(2,1)S(1)}, u32[]{:S(2)}, u32[]{:S(2)}) collective-permute-start(bf16[480,768]{1,0:T(8,128)(2,1)S(1)} %collective-permute-done.13.rest_6_), channel_id=1, source_target_pairs={{0,4},{4,0},{8,12},{12,8},{16,20},{20,16},{24,28},{28,24},{1,5},{5... | collective-permute-start | bytes 2211848 | tf_op jit(solution)/shard_map/ppermute | solution.py:818
  93.8 3.3 collective-permute-start.19
  153.8 9.2 %collective-permute-start.20 = (bf16[4,864,768]{2,1,0:T(8,128)(2,1)}, bf16[4,864,768]{2,1,0:T(8,128)(2,1)}, u32[]{:S(2)}, u32[]{:S(2)}) collective-permute-start(bf16[4,864,768]{2,1,0:T(8,128)(2,1)} %get-tuple-element.190), channel_id=1, source_target_pairs={{0,4},{4,0},{8,12},{12,8},{16,20},{20,16},{24,28},{28,24},{1,5},{5... | collective-permute-start | bytes 15925256 | tf_op jit(solution)/shard_map/ppermute | solution.py:818
  166.4 35.5 %collective-permute-start.21 = (bf16[2,432,768]{2,1,0:T(8,128)(2,1)S(1)}, bf16[2,432,768]{2,1,0:T(8,128)(2,1)}, u32[]{:S(2)}, u32[]{:S(2)}) collective-permute-start(bf16[2,432,768]{2,1,0:T(8,128)(2,1)S(1)} %pad_maximum_fusion.1), channel_id=1, source_target_pairs={{0,8},{4,12},{8,0},{12,4},{16,24},{20,28},{24,16},{28,20},{1,9},{5... | collective-permute-start | bytes 3981320 | tf_op jit(solution)/shard_map/ppermute | solution.py:818
  167.9 33.9 %collective-permute-start.22 = (bf16[2,432,768]{2,1,0:T(8,128)(2,1)S(1)}, bf16[2,432,768]{2,1,0:T(8,128)(2,1)}, u32[]{:S(2)}, u32[]{:S(2)}) collective-permute-start(bf16[2,432,768]{2,1,0:T(8,128)(2,1)S(1)} %pad_maximum_fusion.2), channel_id=1, source_target_pairs={{0,16},{4,20},{8,24},{12,28},{16,0},{20,4},{24,8},{28,12},{1,17},{... | collective-permute-start | bytes 3981320 | tf_op jit(solution)/shard_map/ppermute | solution.py:818
  206.9 20.0 %collective-permute-start.25 = (bf16[4,288,768]{2,1,0:T(8,128)(2,1)}, bf16[4,288,768]{2,1,0:T(8,128)(2,1)}, u32[]{:S(2)}, u32[]{:S(2)}) collective-permute-start(bf16[4,288,768]{2,1,0:T(8,128)(2,1)} %get-tuple-element.212), channel_id=1, source_target_pairs={{0,4},{4,0},{8,12},{12,8},{16,20},{20,16},{24,28},{28,24},{1,5},{5... | collective-permute-start | bytes 5308424 | tf_op jit(solution)/shard_map/ppermute | solution.py:818
  206.9 17.3 %collective-permute-start.23 = (bf16[432,768]{1,0:T(8,128)(2,1)S(1)}, bf16[432,768]{1,0:T(8,128)(2,1)S(1)}, u32[]{:S(2)}, u32[]{:S(2)}) collective-permute-start(bf16[432,768]{1,0:T(8,128)(2,1)S(1)} %get-tuple-element.208), channel_id=1, source_target_pairs={{0,16},{4,20},{8,24},{12,28},{16,0},{20,4},{24,8},{28,12},{1,17},{... | collective-permute-start | bytes 1990664 | tf_op jit(solution)/shard_map/ppermute | solution.py:818
  208.6 17.3 %collective-permute-start.24 = (bf16[432,768]{1,0:T(8,128)(2,1)}, bf16[432,768]{1,0:T(8,128)(2,1)S(1)}, u32[]{:S(2)}, u32[]{:S(2)}) collective-permute-start(bf16[432,768]{1,0:T(8,128)(2,1)} %get-tuple-element.210), channel_id=1, source_target_pairs={{0,8},{4,12},{8,0},{12,4},{16,24},{20,28},{24,16},{28,20},{1,9},{5... | collective-permute-start | bytes 1990664 | tf_op jit(solution)/shard_map/ppermute | solution.py:818
  229.1 3.9 %copy-start.1 = (bf16[32,8,8,128]{3,1,2,0:T(8,128)(2,1)S(1)}, bf16[32,8,8,128]{3,1,2,0:T(8,128)(2,1)}, u32[]{:S(2)}) copy-start(bf16[32,8,8,128]{3,1,2,0:T(8,128)(2,1)} %copy-done) | copy-start | bytes 1572868
  229.1 4.9 %copy-start.13 = (f32[8,768]{1,0:T(8,128)S(1)}, f32[8,768]{1,0:T(8,128)}, u32[]{:S(2)}) copy-start(f32[8,768]{1,0:T(8,128)} %get-tuple-element.247) | copy-start | bytes 73732
  230.0 13.9 %collective-permute-start.26 = (bf16[192,768]{1,0:T(8,128)(2,1)}, bf16[192,768]{1,0:T(8,128)(2,1)}, u32[]{:S(2)}, u32[]{:S(2)}) collective-permute-start(bf16[192,768]{1,0:T(8,128)(2,1)} %get-tuple-element.220), channel_id=1, source_target_pairs={{0,1},{1,0},{2,3},{3,2},{4,5},{5,4},{6,7},{7,6},{8,9},{9,8},{10,11... | collective-permute-start | bytes 884744 | tf_op jit(solution)/shard_map/ppermute | solution.py:818
  231.5 13.4 %collective-permute-start.27 = (bf16[2,144,768]{2,1,0:T(8,128)(2,1)}, bf16[2,144,768]{2,1,0:T(8,128)(2,1)}, u32[]{:S(2)}, u32[]{:S(2)}) collective-permute-start(bf16[2,144,768]{2,1,0:T(8,128)(2,1)} %pad_maximum_fusion.4), channel_id=1, source_target_pairs={{0,8},{4,12},{8,0},{12,4},{16,24},{20,28},{24,16},{28,20},{1,9},{5... | collective-permute-start | bytes 1327112 | tf_op jit(solution)/shard_map/ppermute | solution.py:818
  232.0 13.0 %collective-permute-start.28 = (bf16[2,144,768]{2,1,0:T(8,128)(2,1)S(1)}, bf16[2,144,768]{2,1,0:T(8,128)(2,1)}, u32[]{:S(2)}, u32[]{:S(2)}) collective-permute-start(bf16[2,144,768]{2,1,0:T(8,128)(2,1)S(1)} %pad_maximum_fusion.5), channel_id=1, source_target_pairs={{0,16},{4,20},{8,24},{12,28},{16,0},{20,4},{24,8},{28,12},{1,17},{... | collective-permute-start | bytes 1327112 | tf_op jit(solution)/shard_map/ppermute | solution.py:818
  234.1 13.8 %collective-permute-start.30 = (bf16[240,768]{1,0:T(8,128)(2,1)}, bf16[240,768]{1,0:T(8,128)(2,1)}, u32[]{:S(2)}, u32[]{:S(2)}) collective-permute-start(bf16[240,768]{1,0:T(8,128)(2,1)} %get-tuple-element.229), channel_id=1, source_target_pairs={{0,1},{1,0},{2,3},{3,2},{4,5},{5,4},{6,7},{7,6},{8,9},{9,8},{10,11... | collective-permute-start | bytes 1105928 | tf_op jit(solution)/shard_map/ppermute | solution.py:818
  246.8 15.7 %collective-permute-start.31 = (bf16[144,768]{1,0:T(8,128)(2,1)S(1)}, bf16[144,768]{1,0:T(8,128)(2,1)S(1)}, u32[]{:S(2)}, u32[]{:S(2)}) collective-permute-start(bf16[144,768]{1,0:T(8,128)(2,1)S(1)} %get-tuple-element.231), channel_id=1, source_target_pairs={{0,16},{4,20},{8,24},{12,28},{16,0},{20,4},{24,8},{28,12},{1,17},{... | collective-permute-start | bytes 663560 | tf_op jit(solution)/shard_map/ppermute | solution.py:818
  248.9 13.7 %collective-permute-start.32 = (bf16[144,768]{1,0:T(8,128)(2,1)S(1)}, bf16[144,768]{1,0:T(8,128)(2,1)S(1)}, u32[]{:S(2)}, u32[]{:S(2)}) collective-permute-start(bf16[144,768]{1,0:T(8,128)(2,1)S(1)} %get-tuple-element.233), channel_id=1, source_target_pairs={{0,8},{4,12},{8,0},{12,4},{16,24},{20,28},{24,16},{28,20},{1,9},{5... | collective-permute-start | bytes 663560 | tf_op jit(solution)/shard_map/ppermute | solution.py:818
  250.6 13.9 %collective-permute-start.29 = (bf16[192,768]{1,0:T(8,128)(2,1)S(1)}, bf16[192,768]{1,0:T(8,128)(2,1)S(1)}, u32[]{:S(2)}, u32[]{:S(2)}) collective-permute-start(bf16[192,768]{1,0:T(8,128)(2,1)S(1)} %add_convert_fusion.13), channel_id=1, source_target_pairs={{0,2},{1,3},{2,0},{3,1},{4,6},{5,7},{6,4},{7,5},{8,10},{9,11},{10,... | collective-permute-start | bytes 884744 | tf_op jit(solution)/shard_map/ppermute | solution.py:818
  262.7 2.6 copy-start.14
  264.5 13.9 %collective-permute-start.33 = (bf16[144,768]{1,0:T(8,128)(2,1)S(1)}, bf16[144,768]{1,0:T(8,128)(2,1)S(1)}, u32[]{:S(2)}, u32[]{:S(2)}) collective-permute-start(bf16[144,768]{1,0:T(8,128)(2,1)S(1)} %get-tuple-element.239), channel_id=1, source_target_pairs={{0,1},{1,0},{2,3},{3,2},{4,5},{5,4},{6,7},{7,6},{8,9},{9,8},{10,11... | collective-permute-start | bytes 663560 | tf_op jit(solution)/shard_map/ppermute | solution.py:818
  265.4 23.8 %collective-permute-start.34 = (bf16[240,768]{1,0:T(8,128)(2,1)S(1)}, bf16[240,768]{1,0:T(8,128)(2,1)S(1)}, u32[]{:S(2)}, u32[]{:S(2)}) collective-permute-start(bf16[240,768]{1,0:T(8,128)(2,1)S(1)} %add_convert_fusion.11), channel_id=1, source_target_pairs={{0,2},{1,3},{2,0},{3,1},{4,6},{5,7},{6,4},{7,5},{8,10},{9,11},{10,... | collective-permute-start | bytes 1105928 | tf_op jit(solution)/shard_map/ppermute | solution.py:818
  268.9 26.6 %collective-permute-start.43 = (bf16[192,768]{1,0:T(8,128)(2,1)S(1)}, bf16[192,768]{1,0:T(8,128)(2,1)S(1)}, u32[]{:S(2)}, u32[]{:S(2)}) collective-permute-start(bf16[192,768]{1,0:T(8,128)(2,1)S(1)} %add_convert_fusion.12), channel_id=1, source_target_pairs={{0,1},{1,0},{2,3},{3,2},{4,5},{5,4},{6,7},{7,6},{8,9},{9,8},{10,11... | collective-permute-start | bytes 884744 | tf_op jit(solution)/shard_map/ppermute | solution.py:818
  278.5 16.2 %collective-permute-start.35 = (bf16[144,768]{1,0:T(8,128)(2,1)S(1)}, bf16[144,768]{1,0:T(8,128)(2,1)S(1)}, u32[]{:S(2)}, u32[]{:S(2)}) collective-permute-start(bf16[144,768]{1,0:T(8,128)(2,1)S(1)} %add_convert_fusion.15), channel_id=1, source_target_pairs={{0,2},{1,3},{2,0},{3,1},{4,6},{5,7},{6,4},{7,5},{8,10},{9,11},{10,... | collective-permute-start | bytes 663560 | tf_op jit(solution)/shard_map/ppermute | solution.py:818
  289.2 5.6 %copy-start.11 = (f32[128,128]{1,0:T(8,128)S(1)}, f32[128,128]{1,0:T(8,128)}, u32[]{:S(2)}) copy-start(f32[128,128]{1,0:T(8,128)} %get-tuple-element.245) | copy-start | bytes 196612
  294.9 3.8 %collective-permute-start.36 = (f32[28,128]{1,0:T(8,128)S(1)}, f32[28,128]{1,0:T(8,128)S(1)}, u32[]{:S(2)}, u32[]{:S(2)}) collective-permute-start(f32[28,128]{1,0:T(8,128)S(1)} %get-tuple-element.303), channel_id=1, source_target_pairs={{0,4},{4,0},{8,12},{12,8},{16,20},{20,16},{24,28},{28,24},{1,5},{5... | collective-permute-start | bytes 43016 | tf_op jit(solution)/shard_map/ppermute | solution.py:818
  295.0 4.9 %collective-permute-start.37 = (f32[28,128]{1,0:T(8,128)S(1)}, f32[28,128]{1,0:T(8,128)S(1)}, u32[]{:S(2)}, u32[]{:S(2)}) collective-permute-start(f32[28,128]{1,0:T(8,128)S(1)} %get-tuple-element.309), channel_id=1, source_target_pairs={{0,8},{4,12},{8,0},{12,4},{16,24},{20,28},{24,16},{28,20},{1,9},{5... | collective-permute-start | bytes 43016 | tf_op jit(solution)/shard_map/ppermute | solution.py:818
  295.5 5.9 %collective-permute-start.38 = (f32[28,128]{1,0:T(8,128)S(1)}, f32[28,128]{1,0:T(8,128)S(1)}, u32[]{:S(2)}, u32[]{:S(2)}) collective-permute-start(f32[28,128]{1,0:T(8,128)S(1)} %get-tuple-element.308), channel_id=1, source_target_pairs={{0,12},{4,8},{8,4},{12,0},{16,28},{20,24},{24,20},{28,16},{1,13},{... | collective-permute-start | bytes 43016 | tf_op jit(solution)/shard_map/ppermute | solution.py:818
  296.9 4.6 %collective-permute-start.39 = (f32[28,128]{1,0:T(8,128)S(1)}, f32[28,128]{1,0:T(8,128)S(1)}, u32[]{:S(2)}, u32[]{:S(2)}) collective-permute-start(f32[28,128]{1,0:T(8,128)S(1)} %get-tuple-element.307), channel_id=1, source_target_pairs={{0,16},{4,20},{8,24},{12,28},{16,0},{20,4},{24,8},{28,12},{1,17},{... | collective-permute-start | bytes 43016 | tf_op jit(solution)/shard_map/ppermute | solution.py:818
  298.3 5.2 %collective-permute-start.40 = (f32[28,128]{1,0:T(8,128)S(1)}, f32[28,128]{1,0:T(8,128)S(1)}, u32[]{:S(2)}, u32[]{:S(2)}) collective-permute-start(f32[28,128]{1,0:T(8,128)S(1)} %get-tuple-element.306), channel_id=1, source_target_pairs={{0,20},{4,16},{8,28},{12,24},{16,4},{20,0},{24,12},{28,8},{1,21},{... | collective-permute-start | bytes 43016 | tf_op jit(solution)/shard_map/ppermute | solution.py:818
  298.6 4.9 %collective-permute-start.41 = (f32[28,128]{1,0:T(8,128)S(1)}, f32[28,128]{1,0:T(8,128)S(1)}, u32[]{:S(2)}, u32[]{:S(2)}) collective-permute-start(f32[28,128]{1,0:T(8,128)S(1)} %get-tuple-element.305), channel_id=1, source_target_pairs={{0,24},{4,28},{8,16},{12,20},{16,8},{20,12},{24,0},{28,4},{1,25},{... | collective-permute-start | bytes 43016 | tf_op jit(solution)/shard_map/ppermute | solution.py:818
  299.9 4.1 %collective-permute-start.42 = (f32[28,128]{1,0:T(8,128)S(1)}, f32[28,128]{1,0:T(8,128)S(1)}, u32[]{:S(2)}, u32[]{:S(2)}) collective-permute-start(f32[28,128]{1,0:T(8,128)S(1)} %get-tuple-element.304), channel_id=1, source_target_pairs={{0,28},{4,24},{8,20},{12,16},{16,12},{20,8},{24,4},{28,0},{1,29},{... | collective-permute-start | bytes 43016 | tf_op jit(solution)/shard_map/ppermute | solution.py:818
  301.4 8.3 %collective-permute-start.45 = (bf16[144,768]{1,0:T(8,128)(2,1)S(1)}, bf16[144,768]{1,0:T(8,128)(2,1)S(1)}, u32[]{:S(2)}, u32[]{:S(2)}) collective-permute-start(bf16[144,768]{1,0:T(8,128)(2,1)S(1)} %add_convert_fusion.14), channel_id=1, source_target_pairs={{0,1},{1,0},{2,3},{3,2},{4,5},{5,4},{6,7},{7,6},{8,9},{9,8},{10,11... | collective-permute-start | bytes 663560 | tf_op jit(solution)/shard_map/ppermute | solution.py:818
  301.5 15.6 %collective-permute-start.44 = (bf16[240,768]{1,0:T(8,128)(2,1)S(1)}, bf16[240,768]{1,0:T(8,128)(2,1)S(1)}, u32[]{:S(2)}, u32[]{:S(2)}) collective-permute-start(bf16[240,768]{1,0:T(8,128)(2,1)S(1)} %add_convert_fusion.10), channel_id=1, source_target_pairs={{0,1},{1,0},{2,3},{3,2},{4,5},{5,4},{6,7},{7,6},{8,9},{9,8},{10,11... | collective-permute-start | bytes 1105928 | tf_op jit(solution)/shard_map/ppermute | solution.py:818
  317.2 8.4 %collective-permute-start.46 = (f32[28,128]{1,0:T(8,128)S(1)}, f32[28,128]{1,0:T(8,128)S(1)}, u32[]{:S(2)}, u32[]{:S(2)}) collective-permute-start(f32[28,128]{1,0:T(8,128)S(1)} %fusion.17), channel_id=1, source_target_pairs={{0,1},{1,0},{2,3},{3,2},{4,5},{5,4},{6,7},{7,6},{8,9},{9,8},{10,11... | collective-permute-start | bytes 43016 | tf_op jit(solution)/shard_map/ppermute | solution.py:818
  317.6 8.0 %collective-permute-start.47 = (f32[28,128]{1,0:T(8,128)S(1)}, f32[28,128]{1,0:T(8,128)S(1)}, u32[]{:S(2)}, u32[]{:S(2)}) collective-permute-start(f32[28,128]{1,0:T(8,128)S(1)} %fusion.17), channel_id=1, source_target_pairs={{0,2},{1,3},{2,0},{3,1},{4,6},{5,7},{6,4},{7,5},{8,10},{9,11},{10,... | collective-permute-start | bytes 43016 | tf_op jit(solution)/shard_map/ppermute | solution.py:818
  320.3 5.5 %collective-permute-start.48 = (f32[28,128]{1,0:T(8,128)S(1)}, f32[28,128]{1,0:T(8,128)S(1)}, u32[]{:S(2)}, u32[]{:S(2)}) collective-permute-start(f32[28,128]{1,0:T(8,128)S(1)} %fusion.17), channel_id=1, source_target_pairs={{0,3},{1,2},{2,1},{3,0},{4,7},{5,6},{6,5},{7,4},{8,11},{9,10},{10,... | collective-permute-start | bytes 43016 | tf_op jit(solution)/shard_map/ppermute | solution.py:818
  (5 other events, 5.3 us)

commit v5 on v4

--- a/solution.py
+++ b/solution.py
@@ -533,13 +533,12 @@
 
 
 def gelu_parts(x):
-    a = jnp.abs(x)
-    t = 1.0 / (1.0 + (0.3275911 * math.sqrt(0.5)) * a)
-    e = jnp.exp(-0.5 * x * x)
-    poly = t * (0.254829592 + t * (-0.284496736 + t * (1.421413741 + t * (-1.453152027 + t * 1.061405429))))
-    tail = 0.5 * poly * e
+    t = 1.0 / (1.0 + (0.3275911 * math.sqrt(0.5)) * jnp.abs(x))
+    e = jnp.exp2((-0.5 * math.log2(math.e)) * (x * x))
+    poly = t * (0.127414796 + t * (-0.142248368 + t * (0.7107068705 + t * (-0.7265760135 + t * 0.5307027145))))
+    tail = poly * e
     cdf = jnp.where(x >= 0, 1.0 - tail, tail)
-    return x * cdf, cdf + x * e * (1.0 / math.sqrt(2.0 * math.pi))
+    return x * cdf, cdf + (x * (1.0 / math.sqrt(2.0 * math.pi))) * e
 
 
 def split_cores(value, core, owners):
@@ -873,12 +872,13 @@
 def far_second(arrays, from_x, from_y, spot):
     top, low = cut_of(arrays)
     total = lambda mask, rows, more: add_low(*place_rows(arrays, spot, mask, rows), more)
-    own = total(0, top, from_x[0]), total(0, low, from_y[0])
-    return own, total(2, top, from_x[1]), total(1, low, from_y[1])
-
-
-def far_third(own, from_y, from_x):
-    return add_low(own[0], from_y), add_low(own[1], from_x)
+    return total(2, top, from_x[1]), total(1, low, from_y[1])
+
+
+def far_third(arrays, from_x, from_y, last_y, last_x, spot):
+    top, low = cut_of(arrays)
+    total = lambda rows, *more: add_low(*place_rows(arrays, spot, 0, rows), *more)
+    return total(top, from_x[0], last_y), total(low, from_y[0], last_x)
 
 
 def halves(owned, spot):
@@ -908,12 +908,13 @@
     return jnp.concatenate([jnp.where(even, half, other), jnp.where(even, other, half)]).astype(f32)
 
 
-def sum_owned(packed, spot, size):
+def sum_owned(packed, tied, spot, size):
     if size != SHARDS:
         return lax.psum_scatter(packed, "fsdp", scatter_dimension=0)
     total = lax.dynamic_index_in_dim(packed, spot, 0, keepdims=False)
     for m in range(1, size):
-        total = total + swap(lax.dynamic_index_in_dim(packed, spot ^ m, 0, keepdims=False), "fsdp", size, m)
+        source = packed if m <= size // 2 else tied
+        total = total + swap(lax.dynamic_index_in_dim(source, spot ^ m, 0, keepdims=False), "fsdp", size, m)
     return total
 
 
@@ -1043,8 +1044,9 @@
         from_x, from_y = along_x(go_x), along_y(go_y)
         grad_projected, grad_scores = backward(3, backward(2, backward(1, done)))
         qkv_keep, qkv_send = qkv_weight_grad(order, normed, grad_projected, split)
-        qkv_keep, qkv_send, (own, go_y, go_x) = barrier((qkv_keep, qkv_send, far_second(a, from_x, from_y, spot)))
-        from_y, from_x = along_y(go_y), along_x(go_x)
+        a_from = from_x, from_y
+        qkv_keep, qkv_send, (go_y, go_x) = barrier((qkv_keep, qkv_send, far_second(a, *a_from, spot)))
+        a_last = along_y(go_y), along_x(go_x)
         c = (qkv_keep, near(qkv_send))
         c_go = far_first(c, spot)
     else:
@@ -1056,7 +1058,7 @@
         order, inputs, times, grad_middle, grad_projected, back_rows, qkv_p
     )
     if direct:
-        top, low = far_third(own, from_y, from_x)
+        top, low = far_third(a, *a_from, *a_last, spot)
         a, b = top[:up_rows], jnp.concatenate([top[up_rows:], low])
         a, b = halves(a, level), halves(b, level)
         grad_scores, first_vecs, a, b, c_go = barrier((grad_scores, first_vecs, a, b, c_go))
@@ -1066,12 +1068,12 @@
     a, b = rows_first(*a, planes), rows_first(*b, planes)
     sums = feat(0, ())
     if direct:
-        sums, a, (own, go_y, go_x) = barrier((sums, a, far_second(c, *c_from, spot)))
-        from_y, from_x = along_y(go_y), along_x(go_x)
+        sums, a, (go_y, go_x) = barrier((sums, a, far_second(c, *c_from, spot)))
+        c_last = along_y(go_y), along_x(go_x)
     a = rows_middle(a, planes)
     sums = feat(1, sums)
     if direct:
-        qkv_owned = jnp.concatenate(far_third(own, from_y, from_x))
+        qkv_owned = jnp.concatenate(far_third(c, *c_from, *c_last, spot))
     sums, a, b, c = barrier((sums, a, b, halves(qkv_owned, level)))
     c = rows_first(*c, planes)
     b = rows_middle(b, planes)
@@ -1079,9 +1081,7 @@
     sums, c = barrier((sums, c))
     c = rows_middle(c, planes)
     grad_up = rows_last(a, planes, level)
-    kernel_part, b, c = barrier((feat(3, sums)[2], b, c))
-    kernel_part = kernel_part.reshape(n, own_kernels, -1)
-    grad_low, grad_qkv = rows_last(b, planes, level), rows_last(c, planes, level)
+    kernel_part = feat(3, sums)[2].reshape(n, own_kernels, -1)
 
     lanes = kernel_part.shape[2]
     grad_rows = jnp.concatenate([first_vecs[:5], ffn_vecs[3:4], ffn_vecs[:3]]).reshape(9, n, r)
@@ -1089,7 +1089,10 @@
     up_bias_rows = ffn_vecs[4:].reshape(n, -1)
     up_bias_rows = jnp.pad(up_bias_rows, ((0, 0), (0, -up_bias_rows.shape[1] % lanes))).reshape(n, -1, lanes)
     vector_rows = jnp.concatenate([grad_rows, up_bias_rows], axis=1)
-    small = sum_owned(jnp.concatenate([kernel_part, vector_rows], axis=1), spot, n)
+    packed = jnp.concatenate([kernel_part, vector_rows], axis=1)
+    tied, b, c = barrier((packed, b, c))
+    grad_low, grad_qkv = rows_last(b, planes, level), rows_last(c, planes, level)
+    small = sum_owned(packed, tied, spot, n)
     small, grad_up, grad_low, grad_qkv = barrier((small, grad_up, grad_low, grad_qkv))
     small = sum_planes(small, planes)
     gaussians, vectors = small[:own_kernels], small[own_kernels : own_kernels + 9, :r]

time: 332 us -> 328 us (0.988)
  waiting for transfers between devices: 32.3 us -> 27.9 us
    ppermute x49, waiting for transfers between devices: 32.3 us -> 27.9 us  [swap(): return lax.ppermute(value, axis, [(i, i ^ bit_mask) for i in range(size)])]
    convert_element_type x14 -> x12, other arithmetic: 14.4 us -> 15 us  [add_low(): return total.astype(terms[0].dtype)]
  transfers between devices with their start and end apart: 49 -> 49, of which waited for: 13 -> 12; matrix products, arithmetic and copies ran while one was open for 8% -> 10% of each run, Pallas kernels for 45% -> 45%
where the time goes in v5:
time: 328 us; the launch traced here: 325 us
  Pallas kernels  202 us (62%)
  starting transfers between devices  46.9 us (14%)
  waiting for transfers between devices  27.9 us (9%)
  local copies, waits for them, and re-layouts  24.5 us (7%)
  other arithmetic  21.9 us (7%)
    pallas_call x1, Pallas kernels, ffn_both(): pl.pallas_call(functools.partial(ffn_kernel, n, split, steps), grid_spec=...  54.5 us
    ppermute x49, starting transfers between devices, swap(): return lax.ppermute(value, axis, [(i, i ^ bit_mask) for i in range(size)])  46.9 us
    pallas_call x4, Pallas kernels, attn_feat(): pl.pallas_call(functools.partial(feat_kernel, len(before), last), grid=(p...  38 us
    pallas_call x4, Pallas kernels, attn_bwd(): pl.pallas_call(functools.partial(skip_refs, functools.partial(bwd_kernel,...  32.7 us
    ppermute x49, waiting for transfers between devices, swap(): return lax.ppermute(value, axis, [(i, i ^ bit_mask) for i in range(size)])  27.9 us
    pallas_call x2, Pallas kernels, attn_bias(): pl.pallas_call(functools.partial(skip_refs, bias_kernel, n_in, len(before...  26.1 us
    pallas_call x1, Pallas kernels, attn_fwd(): pl.pallas_call(functools.partial(skip_refs, fwd_kernel, n_in, len(before)...  19.8 us
    convert_element_type x12, other arithmetic, add_low(): return total.astype(terms[0].dtype)  15 us
  transfers between devices with their start and end apart: 49, of which 12 were waited for; matrix products, arithmetic and copies ran while one was open for 10% of the time, Pallas kernels for 45%

profile of v5, /device:TPU:0, one launch (start us, length us, event | category | flops | bytes accessed | tf_op | source)
XLA Modules:
  0.0 324.6 jit_solution(10030997831379251577)
XLA Ops:
  0.7 0.9 pad_add_fusion
  2.9 2.8 collective-permute-start.1
  5.8 1.5 collective-permute-start.2
  7.3 2.0 collective-permute-start.4
  9.2 1.5 collective-permute-start.5
  13.4 1.1 copy.144
  15.3 1.2 copy.116
  16.6 1.0 copy.126.t_ref
  19.5 1.0 copy.122.refs_3_
  20.5 13.1 %attn_bias.2 = (f32[32,128,1024]{2,1,0:T(8,128)}, bf16[32,1024,512]{2,1,0:T(8,128)(2,1)}) custom-call(f32[32,8,128]{2,1,0:T(8,128)} %copy-done.2, f32[1024,4]{1,0:T(8,128)} %bitcast.259, bf16[1024,128]{1,0:T(8,128)(2,1)} %copy.121.refs_2_, bf16[1024,256]{1,0:T(8,128)(2,1)} %copy.122.refs_3_), custom_call_target="tpu_custom_call" | custom-call | flops 2307000064 | tf_op jit(solution)/shard_map/attn_bias/pallas_call | solution.py:286
  36.0 1.9 collective-permute-start.11
  38.0 1.5 collective-permute-start.12
  42.7 12.9 %attn_bias.3 = (f32[32,128,1024]{2,1,0:T(8,128)}, bf16[32,1024,512]{2,1,0:T(8,128)(2,1)}) custom-call(f32[32,8,128]{2,1,0:T(8,128)} %copy-done.2, f32[1024,4]{1,0:T(8,128)} %bitcast.260, bf16[1024,128]{1,0:T(8,128)(2,1)} %copy.121.refs_2_, bf16[1024,256]{1,0:T(8,128)(2,1)} %copy.122.refs_3_, ...), custom_call_target="tpu_custom_call", output_to_operand_aliasing={{0}: (4, {}), {1}: (5, {})} | custom-call | flops 2307000064 | tf_op jit(solution)/shard_map/attn_bias/pallas_call | solution.py:286
  55.7 9.7 %qkv_forward.1 = (bf16[1024,768]{1,0:T(8,128)(2,1)}, bf16[1024,768]{1,0:T(8,128)(2,1)}, bf16[1024,768]{1,0:T(8,128)(2,1)}, bf16[1024,768]{1,0:T(8,128)(2,1)}) custom-call(s32[8]{0:T(128)} %copy-done.15, bf16[1024,768]{1,0:T(8,128)(2,1)} %x_ref.5, f32[1024,1]{1,0:T(8,128)} %copy.126.t_ref, f32[8,768]{1,0:T(8,128)} %concatenate.53.vec_ref, ...), custom_call_target="tpu_custom_call" | custom-call | flops 11534999552 | tf_op jit(solution)/shard_map/qkv_forward/pallas_call | solution.py:519
  65.5 1.9 collective-permute-done.11.rest_2_
  67.4 1.5 collective-permute-done.12.rest_4_
  68.9 1.2 slice.437
  70.6 1.1 slice.438
  71.7 1.6 collective-permute-start.13
  73.8 19.8 %attn_fwd.1 = (bf16[1024,768]{1,0:T(8,128)(2,1)}, bf16[32,128,1024]{2,1,0:T(8,128)(2,1)}) custom-call(bf16[1024,768]{1,0:T(8,128)(2,1)} %get-tuple-element.161.refs_0_, bf16[1024,768]{1,0:T(8,128)(2,1)} %get-tuple-element.162.refs_1_.refs_2_, bf16[1024,768]{1,0:T(8,128)(2,1)} %get-tuple-element.163.refs_2_.refs_3_, f32[32,128,1024]{2,1,0:T(8,128)} %get-tuple-element.164.refs_3_), custom_call_target="tpu_custom_call" | custom-call | flops 18456000512 | tf_op jit(solution)/shard_map/attn_fwd/pallas_call | solution.py:309
  94.3 2.8 collective-permute-done.19.rest_9_
  97.9 0.9 copy-done.17
  98.8 54.5 %ffn_both.1 = (bf16[1024,768]{1,0:T(8,128)(2,1)}, bf16[1024,768]{1,0:T(8,128)(2,1)}, f32[8,768]{1,0:T(8,128)}, f32[1024,768]{1,0:T(8,128)}, bf16[4,864,768]{2,1,0:T(8,128)(2,1)}, /*index=5*/bf16[4,864,768]{2,1,0:T(8,128)(2,1)}) custom-call(s32[8]{0:T(128)} %copy-done.15, bf16[1024,768]{1,0:T(8,128)(2,1)} %x_ref.5, f32[1024,1]{1,0:T(8,128)} %copy.126.t_ref, ...), custom_call_target="tpu_custom_call" | custom-call | flops 69209997312 | tf_op jit(solution)/shard_map/ffn_both/pallas_call | solution.py:700
  153.5 8.2 %attn_bwd.4 = (bf16[1024,2304]{1,0:T(8,128)(2,1)}, bf16[32,512,256]{2,1,0:T(8,128)(2,1)}) custom-call(bf16[1024,768]{1,0:T(8,128)(2,1)} %get-tuple-element.161.refs_0_, bf16[1024,768]{1,0:T(8,128)(2,1)} %get-tuple-element.181.refs_1_, bf16[1024,768]{1,0:T(8,128)(2,1)} %get-tuple-element.162.refs_1_.refs_2_, ...), custom_call_target="tpu_custom_call" | custom-call | flops 2307000064 | tf_op jit(solution)/shard_map/attn_bwd/pallas_call | solution.py:334
  162.5 3.1 add_convert_fusion.3
  165.8 1.6 collective-permute-start.21
  167.9 8.2 %attn_bwd.5 = (bf16[1024,2304]{1,0:T(8,128)(2,1)}, bf16[32,512,256]{2,1,0:T(8,128)(2,1)}) custom-call(bf16[1024,768]{1,0:T(8,128)(2,1)} %get-tuple-element.161.refs_0_, bf16[1024,768]{1,0:T(8,128)(2,1)} %get-tuple-element.181.refs_1_, bf16[1024,768]{1,0:T(8,128)(2,1)} %get-tuple-element.162.refs_1_.refs_2_, ...), custom_call_target="tpu_custom_call", output_to_operand_aliasing={{0}: (5, {}), {1}: (6, {})} | custom-call | flops 2307000064 | tf_op jit(solution)/shard_map/attn_bwd/pallas_call | solution.py:334
  176.0 8.2 %attn_bwd.6 = (bf16[1024,2304]{1,0:T(8,128)(2,1)}, bf16[32,512,256]{2,1,0:T(8,128)(2,1)}) custom-call(bf16[1024,768]{1,0:T(8,128)(2,1)} %get-tuple-element.161.refs_0_, bf16[1024,768]{1,0:T(8,128)(2,1)} %get-tuple-element.181.refs_1_, bf16[1024,768]{1,0:T(8,128)(2,1)} %get-tuple-element.162.refs_1_.refs_2_, ...), custom_call_target="tpu_custom_call", output_to_operand_aliasing={{0}: (5, {}), {1}: (6, {})} | custom-call | flops 2307000064 | tf_op jit(solution)/shard_map/attn_bwd/pallas_call | solution.py:334
  184.2 8.2 %attn_bwd.7 = (bf16[1024,2304]{1,0:T(8,128)(2,1)}, bf16[32,512,256]{2,1,0:T(8,128)(2,1)}) custom-call(bf16[1024,768]{1,0:T(8,128)(2,1)} %get-tuple-element.161.refs_0_, bf16[1024,768]{1,0:T(8,128)(2,1)} %get-tuple-element.181.refs_1_, bf16[1024,768]{1,0:T(8,128)(2,1)} %get-tuple-element.162.refs_1_.refs_2_, ...), custom_call_target="tpu_custom_call", output_to_operand_aliasing={{0}: (5, {}), {1}: (6, {})} | custom-call | flops 2307000064 | tf_op jit(solution)/shard_map/attn_bwd/pallas_call | solution.py:334
  192.4 8.9 %qkv_weight_grad.1 = (bf16[4,288,768]{2,1,0:T(8,128)(2,1)}, bf16[4,288,768]{2,1,0:T(8,128)(2,1)}) custom-call(s32[8]{0:T(128)} %copy-done.15, bf16[1024,768]{1,0:T(8,128)(2,1)} %get-tuple-element.199.normed_ref, bf16[1024,2304]{1,0:T(8,128)(2,1)} %get-tuple-element.193.gp_ref), custom_call_target="tpu_custom_call" | custom-call | flops 2307000064 | tf_op jit(solution)/shard_map/qkv_weight_grad/pallas_call | solution.py:749
  201.3 2.4 fusion.3
  203.8 1.6 collective-permute-start.23
  205.9 11.8 %first_backward.1 = (bf16[1024,768]{1,0:T(8,128)(2,1)}, f32[8,768]{1,0:T(8,128)}) custom-call(s32[8]{0:T(128)} %copy-done.15, bf16[1024,768]{1,0:T(8,128)(2,1)} %x_ref.5, f32[1024,1]{1,0:T(8,128)} %copy.126.t_ref, f32[1024,768]{1,0:T(8,128)} %get-tuple-element.180.gm_ref, bf16[1024,2304]{1,0:T(8,128)(2,1)} %get-tuple-element.193.gp_ref, ...), custom_call_target="tpu_custom_call" | custom-call | flops 3460499968 | tf_op jit(solution)/shard_map/first_backward/pallas_call | solution.py:797
  217.8 3.4 %collective-permute-done.23 = bf16[432,768]{1,0:T(8,128)(2,1)S(1)} collective-permute-done((bf16[432,768]{1,0:T(8,128)(2,1)S(1)}, bf16[432,768]{1,0:T(8,128)(2,1)S(1)}, u32[]{:S(2)}, u32[]{:S(2)}) %collective-permute-start.23) | collective-permute-done | bytes 663584 | tf_op jit(solution)/shard_map/ppermute | solution.py:817
  221.1 1.4 collective-permute-done.24
  222.5 2.7 fusion
  227.6 1.5 add_convert_fusion.15
  230.0 1.5 collective-permute-start.26
  232.6 1.0 copy.131.amat_ref
  234.0 9.3 %attn_feat.4 = (f32[128,256]{1,0:T(8,128)}, f32[2,128,128]{2,1,0:T(8,128)}) custom-call(bf16[32,512,256]{2,1,0:T(8,128)(2,1)} %get-tuple-element.207.ds_ref, bf16[32,1024,512]{2,1,0:T(8,128)(2,1)} %get-tuple-element.208.f_ref, f32[32,8,128]{2,1,0:T(8,128)} %copy-done.2, f32[1024,4]{1,0:T(8,128)} %bitcast.261, bf16[1024,256]{1,0:T(8,128)(2,1)} %copy.131.amat_ref, ...), custom_call_target="tpu_custom_call" | custom-call | flops 1153500032 | tf_op jit(solution)/shard_map/attn_feat/pallas_call | solution.py:357
  243.3 1.0 add_convert_fusion.9
  244.4 1.5 fusion.9
  245.8 1.7 collective-permute-start.31
  247.6 1.5 collective-permute-start.32
  249.1 1.1 add_convert_fusion.7
  250.1 2.6 collective-permute-start.29
  252.8 9.3 %attn_feat.5 = (f32[128,256]{1,0:T(8,128)}, f32[2,128,128]{2,1,0:T(8,128)}) custom-call(bf16[32,512,256]{2,1,0:T(8,128)(2,1)} %get-tuple-element.207.ds_ref, bf16[32,1024,512]{2,1,0:T(8,128)(2,1)} %get-tuple-element.208.f_ref, f32[32,8,128]{2,1,0:T(8,128)} %copy-done.2, f32[1024,4]{1,0:T(8,128)} %bitcast.262, bf16[1024,256]{1,0:T(8,128)(2,1)} %copy.131.amat_ref, ...), custom_call_target="tpu_custom_call" | custom-call | flops 1153500032 | tf_op jit(solution)/shard_map/attn_feat/pallas_call | solution.py:357
  262.1 1.5 fusion.6
  264.1 1.4 collective-permute-start.33
  265.6 2.7 collective-permute-start.38
  268.4 9.6 %attn_feat.6 = (f32[128,256]{1,0:T(8,128)}, f32[2,128,128]{2,1,0:T(8,128)}) custom-call(bf16[32,512,256]{2,1,0:T(8,128)(2,1)} %get-tuple-element.207.ds_ref, bf16[32,1024,512]{2,1,0:T(8,128)(2,1)} %get-tuple-element.208.f_ref, f32[32,8,128]{2,1,0:T(8,128)} %copy-done.2, f32[1024,4]{1,0:T(8,128)} %bitcast.263, bf16[1024,256]{1,0:T(8,128)(2,1)} %copy.131.amat_ref, ...), custom_call_target="tpu_custom_call" | custom-call | flops 1153500032 | tf_op jit(solution)/shard_map/attn_feat/pallas_call | solution.py:357
  278.0 1.0 collective-permute-start.39
  279.0 9.7 %attn_feat.7 = (f32[128,256]{1,0:T(8,128)}, f32[2,128,128]{2,1,0:T(8,128)}, f32[128,128]{1,0:T(8,128)}) custom-call(bf16[32,512,256]{2,1,0:T(8,128)(2,1)} %get-tuple-element.207.ds_ref, bf16[32,1024,512]{2,1,0:T(8,128)(2,1)} %get-tuple-element.208.f_ref, f32[32,8,128]{2,1,0:T(8,128)} %copy-done.2, f32[1024,4]{1,0:T(8,128)} %bitcast.264, ...), custom_call_target="tpu_custom_call" | custom-call | flops 1153500032 | tf_op jit(solution)/shard_map/attn_feat/pallas_call | solution.py:357
  290.3 1.3 collective-permute-start.36
  292.4 1.8 collective-permute-done.39
  295.1 2.3 collective-permute-start.42
  297.9 1.7 collective-permute-start.44
  299.6 6.2 %collective-permute-done.45 = bf16[144,768]{1,0:T(8,128)(2,1)S(1)} collective-permute-done((bf16[144,768]{1,0:T(8,128)(2,1)S(1)}, bf16[144,768]{1,0:T(8,128)(2,1)S(1)}, u32[]{:S(2)}, u32[]{:S(2)}) %collective-permute-start.45) | collective-permute-done | bytes 221216 | tf_op jit(solution)/shard_map/ppermute | solution.py:817
  306.0 6.9 %collective-permute-done.44 = bf16[240,768]{1,0:T(8,128)(2,1)S(1)} collective-permute-done((bf16[240,768]{1,0:T(8,128)(2,1)S(1)}, bf16[240,768]{1,0:T(8,128)(2,1)S(1)}, u32[]{:S(2)}, u32[]{:S(2)}) %collective-permute-start.44) | collective-permute-done | bytes 368672 | tf_op jit(solution)/shard_map/ppermute | solution.py:817
  313.7 2.7 collective-permute-start.47
  316.3 1.2 collective-permute-start.48
  317.5 1.1 slice.498
  319.3 1.1 copy.137
  320.4 1.0 copy.136
  (227 shorter events, 30.4 us)
Async XLA Ops:
  0.7 13.9 %copy-start.10 = (bf16[96,768]{1,0:T(8,128)(2,1)S(1)}, bf16[96,768]{1,0:T(8,128)(2,1)}, u32[]{:S(2)}) copy-start(bf16[96,768]{1,0:T(8,128)(2,1)} %param.33) | copy-start | bytes 442372
  0.7 13.9 %copy-start.5 = (bf16[384,768]{1,0:T(8,128)(2,1)S(1)}, bf16[384,768]{1,0:T(8,128)(2,1)}, u32[]{:S(2)}) copy-start(bf16[384,768]{1,0:T(8,128)(2,1)} %param.42) | copy-start | bytes 1769476
  1.6 1.3 collective-permute-start
  2.1 12.6 %copy-start.15 = (s32[8]{0:T(128)}, s32[8]{0:T(128)S(1)}, u32[]{:S(2)}) copy-start(s32[8]{0:T(128)S(1)} %iota_xor_fusion.idx_ref) | copy-start | bytes 100
  2.9 14.7 %collective-permute-start.1 = (bf16[2,32,128]{2,1,0:T(8,128)(2,1)S(1)}, bf16[2,32,128]{2,1,0:T(8,128)(2,1)S(1)}, u32[]{:S(2)}, u32[]{:S(2)}) collective-permute-start(bf16[2,32,128]{2,1,0:T(8,128)(2,1)S(1)} %pad_maximum_fusion.8), channel_id=1, source_target_pairs={{0,8},{4,12},{8,0},{12,4},{16,24},{20,28},{24,16},{28,20},{1,9},{5... | collective-permute-start | bytes 49160 | tf_op jit(solution)/shard_map/ppermute | solution.py:817
  5.8 11.9 %collective-permute-start.2 = (bf16[2,32,128]{2,1,0:T(8,128)(2,1)S(1)}, bf16[2,32,128]{2,1,0:T(8,128)(2,1)S(1)}, u32[]{:S(2)}, u32[]{:S(2)}) collective-permute-start(bf16[2,32,128]{2,1,0:T(8,128)(2,1)S(1)} %pad_maximum_fusion.8), channel_id=1, source_target_pairs={{0,16},{4,20},{8,24},{12,28},{16,0},{20,4},{24,8},{28,12},{1,17},{... | collective-permute-start | bytes 49160 | tf_op jit(solution)/shard_map/ppermute | solution.py:817
  7.3 10.4 %collective-permute-start.3 = (bf16[2,32,128]{2,1,0:T(8,128)(2,1)S(1)}, bf16[2,32,128]{2,1,0:T(8,128)(2,1)S(1)}, u32[]{:S(2)}, u32[]{:S(2)}) collective-permute-start(bf16[2,32,128]{2,1,0:T(8,128)(2,1)S(1)} %pad_maximum_fusion.8), channel_id=1, source_target_pairs={{0,24},{4,28},{8,16},{12,20},{16,8},{20,12},{24,0},{28,4},{1,25},{... | collective-permute-start | bytes 49160 | tf_op jit(solution)/shard_map/ppermute | solution.py:817
  7.3 26.4 %collective-permute-start.4 = (bf16[96,2304]{1,0:T(8,128)(2,1)}, bf16[96,2304]{1,0:T(8,128)(2,1)S(1)}, u32[]{:S(2)}, u32[]{:S(2)}) collective-permute-start(bf16[96,2304]{1,0:T(8,128)(2,1)} %rest_0_.1), channel_id=1, source_target_pairs={{0,8},{4,12},{8,0},{12,4},{16,24},{20,28},{24,16},{28,20},{1,9},{5... | collective-permute-start | bytes 1327112 | tf_op jit(solution)/shard_map/ppermute | solution.py:817
  9.2 24.4 %collective-permute-start.5 = (bf16[96,2304]{1,0:T(8,128)(2,1)}, bf16[96,2304]{1,0:T(8,128)(2,1)}, u32[]{:S(2)}, u32[]{:S(2)}) collective-permute-start(bf16[96,2304]{1,0:T(8,128)(2,1)} %rest_0_.1), channel_id=1, source_target_pairs={{0,16},{4,20},{8,24},{12,28},{16,0},{20,4},{24,8},{28,12},{1,17},{... | collective-permute-start | bytes 1327112 | tf_op jit(solution)/shard_map/ppermute | solution.py:817
  14.6 2.0 copy-start.14
  14.6 3.0 copy-start.6
  15.3 40.3 %copy-start.4 = (bf16[864,768]{1,0:T(8,128)(2,1)}, bf16[864,768]{1,0:T(8,128)(2,1)S(1)}, u32[]{:S(2)}) copy-start(bf16[864,768]{1,0:T(8,128)(2,1)S(1)} %pad_maximum_fusion.rest_0_) | copy-start | bytes 3981316
  17.6 16.1 %collective-permute-start.6 = (bf16[96,2304]{1,0:T(8,128)(2,1)S(1)}, bf16[96,2304]{1,0:T(8,128)(2,1)S(1)}, u32[]{:S(2)}, u32[]{:S(2)}) collective-permute-start(bf16[96,2304]{1,0:T(8,128)(2,1)S(1)} %copy-done.6), channel_id=1, source_target_pairs={{0,24},{4,28},{8,16},{12,20},{16,8},{20,12},{24,0},{28,4},{1,25},{... | collective-permute-start | bytes 1327112 | tf_op jit(solution)/shard_map/ppermute | solution.py:817
  19.5 14.1 %copy-start = (bf16[32,8,8,128]{3,1,2,0:T(8,128)(2,1)}, bf16[32,8,8,128]{3,1,2,0:T(8,128)(2,1)S(1)}, u32[]{:S(2)}) copy-start(bf16[32,8,8,128]{3,1,2,0:T(8,128)(2,1)S(1)} %copy.145) | copy-start | bytes 1572868
  33.7 21.9 %copy-start.7 = (bf16[96,2304]{1,0:T(8,128)(2,1)}, bf16[96,2304]{1,0:T(8,128)(2,1)S(1)}, u32[]{:S(2)}) copy-start(bf16[96,2304]{1,0:T(8,128)(2,1)S(1)} %collective-permute-done.4.rest_2_) | copy-start | bytes 1327108
  33.7 21.9 %copy-start.8 = (bf16[96,2304]{1,0:T(8,128)(2,1)}, bf16[96,2304]{1,0:T(8,128)(2,1)S(1)}, u32[]{:S(2)}) copy-start(bf16[96,2304]{1,0:T(8,128)(2,1)S(1)} %collective-permute-done.6.rest_6_) | copy-start | bytes 1327108
  33.7 4.3 %collective-permute-start.10 = (bf16[96,2304]{1,0:T(8,128)(2,1)S(1)}, bf16[96,2304]{1,0:T(8,128)(2,1)S(1)}, u32[]{:S(2)}, u32[]{:S(2)}) collective-permute-start(bf16[96,2304]{1,0:T(8,128)(2,1)S(1)} %collective-permute-done.6.rest_6_), channel_id=1, source_target_pairs={{0,4},{4,0},{8,12},{12,8},{16,20},{20,16},{24,28},{28,24},{1,5},{5... | collective-permute-start | bytes 1327112 | tf_op jit(solution)/shard_map/ppermute | solution.py:817
  35.0 20.7 %collective-permute-start.7 = (bf16[96,2304]{1,0:T(8,128)(2,1)S(1)}, bf16[96,2304]{1,0:T(8,128)(2,1)}, u32[]{:S(2)}, u32[]{:S(2)}) collective-permute-start(bf16[96,2304]{1,0:T(8,128)(2,1)S(1)} %copy-done.6), channel_id=1, source_target_pairs={{0,4},{4,0},{8,12},{12,8},{16,20},{20,16},{24,28},{28,24},{1,5},{5... | collective-permute-start | bytes 1327112 | tf_op jit(solution)/shard_map/ppermute | solution.py:817
  35.5 20.3 %collective-permute-start.8 = (bf16[96,2304]{1,0:T(8,128)(2,1)S(1)}, bf16[96,2304]{1,0:T(8,128)(2,1)}, u32[]{:S(2)}, u32[]{:S(2)}) collective-permute-start(bf16[96,2304]{1,0:T(8,128)(2,1)S(1)} %collective-permute-done.4.rest_2_), channel_id=1, source_target_pairs={{0,4},{4,0},{8,12},{12,8},{16,20},{20,16},{24,28},{28,24},{1,5},{5... | collective-permute-start | bytes 1327112 | tf_op jit(solution)/shard_map/ppermute | solution.py:817
  35.5 20.3 %collective-permute-start.9 = (bf16[96,2304]{1,0:T(8,128)(2,1)}, bf16[96,2304]{1,0:T(8,128)(2,1)}, u32[]{:S(2)}, u32[]{:S(2)}) collective-permute-start(bf16[96,2304]{1,0:T(8,128)(2,1)} %collective-permute-done.5.rest_4_), channel_id=1, source_target_pairs={{0,4},{4,0},{8,12},{12,8},{16,20},{20,16},{24,28},{28,24},{1,5},{5... | collective-permute-start | bytes 1327112 | tf_op jit(solution)/shard_map/ppermute | solution.py:817
  36.0 31.4 %collective-permute-start.11 = (bf16[864,768]{1,0:T(8,128)(2,1)S(1)}, bf16[864,768]{1,0:T(8,128)(2,1)}, u32[]{:S(2)}, u32[]{:S(2)}) collective-permute-start(bf16[864,768]{1,0:T(8,128)(2,1)S(1)} %pad_maximum_fusion.rest_0_), channel_id=1, source_target_pairs={{0,8},{4,12},{8,0},{12,4},{16,24},{20,28},{24,16},{28,20},{1,9},{5... | collective-permute-start | bytes 3981320 | tf_op jit(solution)/shard_map/ppermute | solution.py:817
  38.0 17.6 %copy-start.9 = (bf16[96,2304]{1,0:T(8,128)(2,1)}, bf16[96,2304]{1,0:T(8,128)(2,1)S(1)}, u32[]{:S(2)}) copy-start(bf16[96,2304]{1,0:T(8,128)(2,1)S(1)} %collective-permute-done.10.rest_7_) | copy-start | bytes 1327108
  38.0 30.9 %collective-permute-start.12 = (bf16[864,768]{1,0:T(8,128)(2,1)S(1)}, bf16[864,768]{1,0:T(8,128)(2,1)}, u32[]{:S(2)}, u32[]{:S(2)}) collective-permute-start(bf16[864,768]{1,0:T(8,128)(2,1)S(1)} %pad_maximum_fusion.rest_0_), channel_id=1, source_target_pairs={{0,16},{4,20},{8,24},{12,28},{16,0},{20,4},{24,8},{28,12},{1,17},{... | collective-permute-start | bytes 3981320 | tf_op jit(solution)/shard_map/ppermute | solution.py:817
  55.6 38.0 %collective-permute-start.15 = (bf16[864,768]{1,0:T(8,128)(2,1)S(1)}, bf16[864,768]{1,0:T(8,128)(2,1)}, u32[]{:S(2)}, u32[]{:S(2)}) collective-permute-start(bf16[864,768]{1,0:T(8,128)(2,1)S(1)} %pad_maximum_fusion.rest_0_), channel_id=1, source_target_pairs={{0,4},{4,0},{8,12},{12,8},{16,20},{20,16},{24,28},{28,24},{1,5},{5... | collective-permute-start | bytes 3981320 | tf_op jit(solution)/shard_map/ppermute | solution.py:817
  70.0 23.7 %collective-permute-start.16 = (bf16[864,768]{1,0:T(8,128)(2,1)}, bf16[864,768]{1,0:T(8,128)(2,1)}, u32[]{:S(2)}, u32[]{:S(2)}) collective-permute-start(bf16[864,768]{1,0:T(8,128)(2,1)} %collective-permute-done.11.rest_2_), channel_id=1, source_target_pairs={{0,4},{4,0},{8,12},{12,8},{16,20},{20,16},{24,28},{28,24},{1,5},{5... | collective-permute-start | bytes 3981320 | tf_op jit(solution)/shard_map/ppermute | solution.py:817
  70.1 23.6 %collective-permute-start.17 = (bf16[864,768]{1,0:T(8,128)(2,1)}, bf16[864,768]{1,0:T(8,128)(2,1)}, u32[]{:S(2)}, u32[]{:S(2)}) collective-permute-start(bf16[864,768]{1,0:T(8,128)(2,1)} %collective-permute-done.12.rest_4_), channel_id=1, source_target_pairs={{0,4},{4,0},{8,12},{12,8},{16,20},{20,16},{24,28},{28,24},{1,5},{5... | collective-permute-start | bytes 3981320 | tf_op jit(solution)/shard_map/ppermute | solution.py:817
  71.7 22.0 %collective-permute-start.13 = (bf16[480,768]{1,0:T(8,128)(2,1)S(1)}, bf16[480,768]{1,0:T(8,128)(2,1)S(1)}, u32[]{:S(2)}, u32[]{:S(2)}) collective-permute-start(bf16[480,768]{1,0:T(8,128)(2,1)S(1)} %slice.437), channel_id=1, source_target_pairs={{0,16},{4,20},{8,24},{12,28},{16,0},{20,4},{24,8},{28,12},{1,17},{... | collective-permute-start | bytes 2211848 | tf_op jit(solution)/shard_map/ppermute | solution.py:817
  73.3 20.4 %collective-permute-start.14 = (bf16[384,768]{1,0:T(8,128)(2,1)S(1)}, bf16[384,768]{1,0:T(8,128)(2,1)}, u32[]{:S(2)}, u32[]{:S(2)}) collective-permute-start(bf16[384,768]{1,0:T(8,128)(2,1)S(1)} %slice.438), channel_id=1, source_target_pairs={{0,8},{4,12},{8,0},{12,4},{16,24},{20,28},{24,16},{28,20},{1,9},{5... | collective-permute-start | bytes 1769480 | tf_op jit(solution)/shard_map/ppermute | solution.py:817
  93.7 3.4 %copy-start.16 = (bf16[480,768]{1,0:T(8,128)(2,1)}, bf16[480,768]{1,0:T(8,128)(2,1)S(1)}, u32[]{:S(2)}) copy-start(bf16[480,768]{1,0:T(8,128)(2,1)S(1)} %collective-permute-done.13.rest_6_) | copy-start | bytes 2211844
  93.7 3.3 %collective-permute-start.18 = (bf16[480,768]{1,0:T(8,128)(2,1)S(1)}, bf16[480,768]{1,0:T(8,128)(2,1)S(1)}, u32[]{:S(2)}, u32[]{:S(2)}) collective-permute-start(bf16[480,768]{1,0:T(8,128)(2,1)S(1)} %collective-permute-done.13.rest_6_), channel_id=1, source_target_pairs={{0,4},{4,0},{8,12},{12,8},{16,20},{20,16},{24,28},{28,24},{1,5},{5... | collective-permute-start | bytes 2211848 | tf_op jit(solution)/shard_map/ppermute | solution.py:817
  93.8 3.3 %collective-permute-start.19 = (bf16[384,768]{1,0:T(8,128)(2,1)}, bf16[384,768]{1,0:T(8,128)(2,1)S(1)}, u32[]{:S(2)}, u32[]{:S(2)}) collective-permute-start(bf16[384,768]{1,0:T(8,128)(2,1)} %collective-permute-done.14.rest_8_), channel_id=1, source_target_pairs={{0,4},{4,0},{8,12},{12,8},{16,20},{20,16},{24,28},{28,24},{1,5},{5... | collective-permute-start | bytes 1769480 | tf_op jit(solution)/shard_map/ppermute | solution.py:817
  153.3 9.2 %collective-permute-start.20 = (bf16[4,864,768]{2,1,0:T(8,128)(2,1)}, bf16[4,864,768]{2,1,0:T(8,128)(2,1)}, u32[]{:S(2)}, u32[]{:S(2)}) collective-permute-start(bf16[4,864,768]{2,1,0:T(8,128)(2,1)} %get-tuple-element.186), channel_id=1, source_target_pairs={{0,4},{4,0},{8,12},{12,8},{16,20},{20,16},{24,28},{28,24},{1,5},{5... | collective-permute-start | bytes 15925256 | tf_op jit(solution)/shard_map/ppermute | solution.py:817
  165.8 35.5 %collective-permute-start.21 = (bf16[2,432,768]{2,1,0:T(8,128)(2,1)S(1)}, bf16[2,432,768]{2,1,0:T(8,128)(2,1)S(1)}, u32[]{:S(2)}, u32[]{:S(2)}) collective-permute-start(bf16[2,432,768]{2,1,0:T(8,128)(2,1)S(1)} %pad_maximum_fusion.1), channel_id=1, source_target_pairs={{0,8},{4,12},{8,0},{12,4},{16,24},{20,28},{24,16},{28,20},{1,9},{5... | collective-permute-start | bytes 3981320 | tf_op jit(solution)/shard_map/ppermute | solution.py:817
  167.4 33.9 %collective-permute-start.22 = (bf16[2,432,768]{2,1,0:T(8,128)(2,1)S(1)}, bf16[2,432,768]{2,1,0:T(8,128)(2,1)}, u32[]{:S(2)}, u32[]{:S(2)}) collective-permute-start(bf16[2,432,768]{2,1,0:T(8,128)(2,1)S(1)} %pad_maximum_fusion.2), channel_id=1, source_target_pairs={{0,16},{4,20},{8,24},{12,28},{16,0},{20,4},{24,8},{28,12},{1,17},{... | collective-permute-start | bytes 3981320 | tf_op jit(solution)/shard_map/ppermute | solution.py:817
  203.7 23.2 %collective-permute-start.25 = (bf16[4,288,768]{2,1,0:T(8,128)(2,1)}, bf16[4,288,768]{2,1,0:T(8,128)(2,1)}, u32[]{:S(2)}, u32[]{:S(2)}) collective-permute-start(bf16[4,288,768]{2,1,0:T(8,128)(2,1)} %get-tuple-element.206), channel_id=1, source_target_pairs={{0,4},{4,0},{8,12},{12,8},{16,20},{20,16},{24,28},{28,24},{1,5},{5... | collective-permute-start | bytes 5308424 | tf_op jit(solution)/shard_map/ppermute | solution.py:817
  203.8 17.3 %collective-permute-start.23 = (bf16[432,768]{1,0:T(8,128)(2,1)S(1)}, bf16[432,768]{1,0:T(8,128)(2,1)S(1)}, u32[]{:S(2)}, u32[]{:S(2)}) collective-permute-start(bf16[432,768]{1,0:T(8,128)(2,1)S(1)} %get-tuple-element.203), channel_id=1, source_target_pairs={{0,16},{4,20},{8,24},{12,28},{16,0},{20,4},{24,8},{28,12},{1,17},{... | collective-permute-start | bytes 1990664 | tf_op jit(solution)/shard_map/ppermute | solution.py:817
  205.4 17.1 %collective-permute-start.24 = (bf16[432,768]{1,0:T(8,128)(2,1)S(1)}, bf16[432,768]{1,0:T(8,128)(2,1)}, u32[]{:S(2)}, u32[]{:S(2)}) collective-permute-start(bf16[432,768]{1,0:T(8,128)(2,1)S(1)} %get-tuple-element.204), channel_id=1, source_target_pairs={{0,8},{4,12},{8,0},{12,4},{16,24},{20,28},{24,16},{28,20},{1,9},{5... | collective-permute-start | bytes 1990664 | tf_op jit(solution)/shard_map/ppermute | solution.py:817
  226.0 1.6 copy-start.3
  229.1 3.5 %copy-start.1 = (bf16[32,8,8,128]{3,1,2,0:T(8,128)(2,1)S(1)}, bf16[32,8,8,128]{3,1,2,0:T(8,128)(2,1)}, u32[]{:S(2)}) copy-start(bf16[32,8,8,128]{3,1,2,0:T(8,128)(2,1)} %copy-done) | copy-start | bytes 1572868
  229.1 4.5 %copy-start.12 = (f32[8,768]{1,0:T(8,128)S(1)}, f32[8,768]{1,0:T(8,128)}, u32[]{:S(2)}) copy-start(f32[8,768]{1,0:T(8,128)} %get-tuple-element.236) | copy-start | bytes 73732
  230.0 13.3 %collective-permute-start.26 = (bf16[192,768]{1,0:T(8,128)(2,1)}, bf16[192,768]{1,0:T(8,128)(2,1)}, u32[]{:S(2)}, u32[]{:S(2)}) collective-permute-start(bf16[192,768]{1,0:T(8,128)(2,1)} %get-tuple-element.214), channel_id=1, source_target_pairs={{0,1},{1,0},{2,3},{3,2},{4,5},{5,4},{6,7},{7,6},{8,9},{9,8},{10,11... | collective-permute-start | bytes 884744 | tf_op jit(solution)/shard_map/ppermute | solution.py:817
  231.5 12.8 %collective-permute-start.27 = (bf16[2,144,768]{2,1,0:T(8,128)(2,1)}, bf16[2,144,768]{2,1,0:T(8,128)(2,1)}, u32[]{:S(2)}, u32[]{:S(2)}) collective-permute-start(bf16[2,144,768]{2,1,0:T(8,128)(2,1)} %pad_maximum_fusion.4), channel_id=1, source_target_pairs={{0,8},{4,12},{8,0},{12,4},{16,24},{20,28},{24,16},{28,20},{1,9},{5... | collective-permute-start | bytes 1327112 | tf_op jit(solution)/shard_map/ppermute | solution.py:817
  232.1 12.3 %collective-permute-start.28 = (bf16[2,144,768]{2,1,0:T(8,128)(2,1)S(1)}, bf16[2,144,768]{2,1,0:T(8,128)(2,1)}, u32[]{:S(2)}, u32[]{:S(2)}) collective-permute-start(bf16[2,144,768]{2,1,0:T(8,128)(2,1)S(1)} %pad_maximum_fusion.5), channel_id=1, source_target_pairs={{0,16},{4,20},{8,24},{12,28},{16,0},{20,4},{24,8},{28,12},{1,17},{... | collective-permute-start | bytes 1327112 | tf_op jit(solution)/shard_map/ppermute | solution.py:817
  233.7 15.4 %collective-permute-start.30 = (bf16[240,768]{1,0:T(8,128)(2,1)}, bf16[240,768]{1,0:T(8,128)(2,1)}, u32[]{:S(2)}, u32[]{:S(2)}) collective-permute-start(bf16[240,768]{1,0:T(8,128)(2,1)} %get-tuple-element.223), channel_id=1, source_target_pairs={{0,1},{1,0},{2,3},{3,2},{4,5},{5,4},{6,7},{7,6},{8,9},{9,8},{10,11... | collective-permute-start | bytes 1105928 | tf_op jit(solution)/shard_map/ppermute | solution.py:817
  245.8 16.3 %collective-permute-start.31 = (bf16[144,768]{1,0:T(8,128)(2,1)S(1)}, bf16[144,768]{1,0:T(8,128)(2,1)S(1)}, u32[]{:S(2)}, u32[]{:S(2)}) collective-permute-start(bf16[144,768]{1,0:T(8,128)(2,1)S(1)} %get-tuple-element.224), channel_id=1, source_target_pairs={{0,16},{4,20},{8,24},{12,28},{16,0},{20,4},{24,8},{28,12},{1,17},{... | collective-permute-start | bytes 663560 | tf_op jit(solution)/shard_map/ppermute | solution.py:817
  247.6 14.6 %collective-permute-start.32 = (bf16[144,768]{1,0:T(8,128)(2,1)S(1)}, bf16[144,768]{1,0:T(8,128)(2,1)S(1)}, u32[]{:S(2)}, u32[]{:S(2)}) collective-permute-start(bf16[144,768]{1,0:T(8,128)(2,1)S(1)} %get-tuple-element.225), channel_id=1, source_target_pairs={{0,8},{4,12},{8,0},{12,4},{16,24},{20,28},{24,16},{28,20},{1,9},{5... | collective-permute-start | bytes 663560 | tf_op jit(solution)/shard_map/ppermute | solution.py:817
  250.1 13.8 %collective-permute-start.29 = (bf16[192,768]{1,0:T(8,128)(2,1)S(1)}, bf16[192,768]{1,0:T(8,128)(2,1)S(1)}, u32[]{:S(2)}, u32[]{:S(2)}) collective-permute-start(bf16[192,768]{1,0:T(8,128)(2,1)S(1)} %add_convert_fusion.9), channel_id=1, source_target_pairs={{0,2},{1,3},{2,0},{3,1},{4,6},{5,7},{6,4},{7,5},{8,10},{9,11},{10,... | collective-permute-start | bytes 884744 | tf_op jit(solution)/shard_map/ppermute | solution.py:817
  263.7 1.9 copy-start.13
  264.1 13.9 %collective-permute-start.33 = (bf16[144,768]{1,0:T(8,128)(2,1)S(1)}, bf16[144,768]{1,0:T(8,128)(2,1)S(1)}, u32[]{:S(2)}, u32[]{:S(2)}) collective-permute-start(bf16[144,768]{1,0:T(8,128)(2,1)S(1)} %get-tuple-element.231), channel_id=1, source_target_pairs={{0,1},{1,0},{2,3},{3,2},{4,5},{5,4},{6,7},{7,6},{8,9},{9,8},{10,11... | collective-permute-start | bytes 663560 | tf_op jit(solution)/shard_map/ppermute | solution.py:817
  265.6 26.0 %collective-permute-start.38 = (bf16[240,768]{1,0:T(8,128)(2,1)S(1)}, bf16[240,768]{1,0:T(8,128)(2,1)S(1)}, u32[]{:S(2)}, u32[]{:S(2)}) collective-permute-start(bf16[240,768]{1,0:T(8,128)(2,1)S(1)} %add_convert_fusion.7), channel_id=1, source_target_pairs={{0,2},{1,3},{2,0},{3,1},{4,6},{5,7},{6,4},{7,5},{8,10},{9,11},{10,... | collective-permute-start | bytes 1105928 | tf_op jit(solution)/shard_map/ppermute | solution.py:817
  268.3 22.0 %collective-permute-start.43 = (bf16[192,768]{1,0:T(8,128)(2,1)S(1)}, bf16[192,768]{1,0:T(8,128)(2,1)S(1)}, u32[]{:S(2)}, u32[]{:S(2)}) collective-permute-start(bf16[192,768]{1,0:T(8,128)(2,1)S(1)} %add_convert_fusion.8), channel_id=1, source_target_pairs={{0,1},{1,0},{2,3},{3,2},{4,5},{5,4},{6,7},{7,6},{8,9},{9,8},{10,11... | collective-permute-start | bytes 884744 | tf_op jit(solution)/shard_map/ppermute | solution.py:817
  278.0 16.2 %collective-permute-start.39 = (bf16[144,768]{1,0:T(8,128)(2,1)S(1)}, bf16[144,768]{1,0:T(8,128)(2,1)S(1)}, u32[]{:S(2)}, u32[]{:S(2)}) collective-permute-start(bf16[144,768]{1,0:T(8,128)(2,1)S(1)} %add_convert_fusion.11), channel_id=1, source_target_pairs={{0,2},{1,3},{2,0},{3,1},{4,6},{5,7},{6,4},{7,5},{8,10},{9,11},{10,... | collective-permute-start | bytes 663560 | tf_op jit(solution)/shard_map/ppermute | solution.py:817
  289.6 4.7 %collective-permute-start.34 = (f32[28,128]{1,0:T(8,128)S(1)}, f32[28,128]{1,0:T(8,128)S(1)}, u32[]{:S(2)}, u32[]{:S(2)}) collective-permute-start(f32[28,128]{1,0:T(8,128)S(1)} %get-tuple-element.291), channel_id=1, source_target_pairs={{0,4},{4,0},{8,12},{12,8},{16,20},{20,16},{24,28},{28,24},{1,5},{5... | collective-permute-start | bytes 43016 | tf_op jit(solution)/shard_map/ppermute | solution.py:817
  289.7 5.4 %collective-permute-start.35 = (f32[28,128]{1,0:T(8,128)S(1)}, f32[28,128]{1,0:T(8,128)S(1)}, u32[]{:S(2)}, u32[]{:S(2)}) collective-permute-start(f32[28,128]{1,0:T(8,128)S(1)} %get-tuple-element.294), channel_id=1, source_target_pairs={{0,8},{4,12},{8,0},{12,4},{16,24},{20,28},{24,16},{28,20},{1,9},{5... | collective-permute-start | bytes 43016 | tf_op jit(solution)/shard_map/ppermute | solution.py:817
  290.3 7.2 %collective-permute-start.36 = (f32[28,128]{1,0:T(8,128)S(1)}, f32[28,128]{1,0:T(8,128)S(1)}, u32[]{:S(2)}, u32[]{:S(2)}) collective-permute-start(f32[28,128]{1,0:T(8,128)S(1)} %get-tuple-element.293), channel_id=1, source_target_pairs={{0,12},{4,8},{8,4},{12,0},{16,28},{20,24},{24,20},{28,16},{1,13},{... | collective-permute-start | bytes 43016 | tf_op jit(solution)/shard_map/ppermute | solution.py:817
  291.6 6.2 %collective-permute-start.37 = (f32[28,128]{1,0:T(8,128)S(1)}, f32[28,128]{1,0:T(8,128)S(1)}, u32[]{:S(2)}, u32[]{:S(2)}) collective-permute-start(f32[28,128]{1,0:T(8,128)S(1)} %get-tuple-element.292), channel_id=1, source_target_pairs={{0,16},{4,20},{8,24},{12,28},{16,0},{20,4},{24,8},{28,12},{1,17},{... | collective-permute-start | bytes 43016 | tf_op jit(solution)/shard_map/ppermute | solution.py:817
  294.3 5.3 %collective-permute-start.40 = (f32[28,128]{1,0:T(8,128)S(1)}, f32[28,128]{1,0:T(8,128)S(1)}, u32[]{:S(2)}, u32[]{:S(2)}) collective-permute-start(f32[28,128]{1,0:T(8,128)S(1)} %get-tuple-element.295), channel_id=1, source_target_pairs={{0,20},{4,16},{8,28},{12,24},{16,4},{20,0},{24,12},{28,8},{1,21},{... | collective-permute-start | bytes 43016 | tf_op jit(solution)/shard_map/ppermute | solution.py:817
  294.4 5.2 %collective-permute-start.41 = (f32[28,128]{1,0:T(8,128)S(1)}, f32[28,128]{1,0:T(8,128)S(1)}, u32[]{:S(2)}, u32[]{:S(2)}) collective-permute-start(f32[28,128]{1,0:T(8,128)S(1)} %get-tuple-element.297), channel_id=1, source_target_pairs={{0,24},{4,28},{8,16},{12,20},{16,8},{20,12},{24,0},{28,4},{1,25},{... | collective-permute-start | bytes 43016 | tf_op jit(solution)/shard_map/ppermute | solution.py:817
  295.1 4.5 %collective-permute-start.42 = (f32[28,128]{1,0:T(8,128)S(1)}, f32[28,128]{1,0:T(8,128)S(1)}, u32[]{:S(2)}, u32[]{:S(2)}) collective-permute-start(f32[28,128]{1,0:T(8,128)S(1)} %get-tuple-element.296), channel_id=1, source_target_pairs={{0,28},{4,24},{8,20},{12,16},{16,12},{20,8},{24,4},{28,0},{1,29},{... | collective-permute-start | bytes 43016 | tf_op jit(solution)/shard_map/ppermute | solution.py:817
  297.5 8.4 %collective-permute-start.45 = (bf16[144,768]{1,0:T(8,128)(2,1)S(1)}, bf16[144,768]{1,0:T(8,128)(2,1)S(1)}, u32[]{:S(2)}, u32[]{:S(2)}) collective-permute-start(bf16[144,768]{1,0:T(8,128)(2,1)S(1)} %add_convert_fusion.10), channel_id=1, source_target_pairs={{0,1},{1,0},{2,3},{3,2},{4,5},{5,4},{6,7},{7,6},{8,9},{9,8},{10,11... | collective-permute-start | bytes 663560 | tf_op jit(solution)/shard_map/ppermute | solution.py:817
  297.9 15.0 %collective-permute-start.44 = (bf16[240,768]{1,0:T(8,128)(2,1)S(1)}, bf16[240,768]{1,0:T(8,128)(2,1)S(1)}, u32[]{:S(2)}, u32[]{:S(2)}) collective-permute-start(bf16[240,768]{1,0:T(8,128)(2,1)S(1)} %add_convert_fusion.6), channel_id=1, source_target_pairs={{0,1},{1,0},{2,3},{3,2},{4,5},{5,4},{6,7},{7,6},{8,9},{9,8},{10,11... | collective-permute-start | bytes 1105928 | tf_op jit(solution)/shard_map/ppermute | solution.py:817
  313.0 8.4 %collective-permute-start.46 = (f32[28,128]{1,0:T(8,128)S(1)}, f32[28,128]{1,0:T(8,128)S(1)}, u32[]{:S(2)}, u32[]{:S(2)}) collective-permute-start(f32[28,128]{1,0:T(8,128)S(1)} %fusion.17), channel_id=1, source_target_pairs={{0,1},{1,0},{2,3},{3,2},{4,5},{5,4},{6,7},{7,6},{8,9},{9,8},{10,11... | collective-permute-start | bytes 43016 | tf_op jit(solution)/shard_map/ppermute | solution.py:817
  313.7 7.7 %collective-permute-start.47 = (f32[28,128]{1,0:T(8,128)S(1)}, f32[28,128]{1,0:T(8,128)S(1)}, u32[]{:S(2)}, u32[]{:S(2)}) collective-permute-start(f32[28,128]{1,0:T(8,128)S(1)} %fusion.17), channel_id=1, source_target_pairs={{0,2},{1,3},{2,0},{3,1},{4,6},{5,7},{6,4},{7,5},{8,10},{9,11},{10,... | collective-permute-start | bytes 43016 | tf_op jit(solution)/shard_map/ppermute | solution.py:817
  316.3 5.5 %collective-permute-start.48 = (f32[28,128]{1,0:T(8,128)S(1)}, f32[28,128]{1,0:T(8,128)S(1)}, u32[]{:S(2)}, u32[]{:S(2)}) collective-permute-start(f32[28,128]{1,0:T(8,128)S(1)} %fusion.17), channel_id=1, source_target_pairs={{0,3},{1,2},{2,1},{3,0},{4,7},{5,6},{6,5},{7,4},{8,11},{9,10},{10,... | collective-permute-start | bytes 43016 | tf_op jit(solution)/shard_map/ppermute | solution.py:817
  (4 other events, 3.7 us)

commit v6 on v5

--- a/solution.py
+++ b/solution.py
@@ -1048,7 +1048,6 @@
         qkv_keep, qkv_send, (go_y, go_x) = barrier((qkv_keep, qkv_send, far_second(a, *a_from, spot)))
         a_last = along_y(go_y), along_x(go_x)
         c = (qkv_keep, near(qkv_send))
-        c_go = far_first(c, spot)
     else:
         grad_projected, grad_scores = backward(3, backward(2, backward(1, backward(0, ()))))
         a = scattered(ffn_keep[:wide], wide)
@@ -1061,7 +1060,9 @@
         top, low = far_third(a, *a_from, *a_last, spot)
         a, b = top[:up_rows], jnp.concatenate([top[up_rows:], low])
         a, b = halves(a, level), halves(b, level)
-        grad_scores, first_vecs, a, b, c_go = barrier((grad_scores, first_vecs, a, b, c_go))
+        a, b, c = barrier((a, b, c))
+        c_go = far_first(c, spot)
+        grad_scores, first_vecs, c_go = barrier((grad_scores, first_vecs, c_go))
         c_from = along_x(c_go[0]), along_y(c_go[1])
     else:
         a, b = halves(a, level), halves(b, level)

time: 328 us -> 327 us (level)
  transfers between devices with their start and end apart: 49 -> 49, of which waited for: 12 -> 12; matrix products, arithmetic and copies ran while one was open for 10% -> 11% of each run, Pallas kernels for 45% -> 45%
where the time goes in v6:
time: 327 us; the launch traced here: 324 us
  Pallas kernels  202 us (62%)
  starting transfers between devices  47.2 us (14%)
  waiting for transfers between devices  27.9 us (9%)
  local copies, waits for them, and re-layouts  23.8 us (7%)
  other arithmetic  21.9 us (7%)
    pallas_call x1, Pallas kernels, ffn_both(): pl.pallas_call(functools.partial(ffn_kernel, n, split, steps), grid_spec=...  54.5 us
    ppermute x49, starting transfers between devices, swap(): return lax.ppermute(value, axis, [(i, i ^ bit_mask) for i in range(size)])  47.2 us
    pallas_call x4, Pallas kernels, attn_feat(): pl.pallas_call(functools.partial(feat_kernel, len(before), last), grid=(p...  38 us
    pallas_call x4, Pallas kernels, attn_bwd(): pl.pallas_call(functools.partial(skip_refs, functools.partial(bwd_kernel,...  32.7 us
    ppermute x49, waiting for transfers between devices, swap(): return lax.ppermute(value, axis, [(i, i ^ bit_mask) for i in range(size)])  27.9 us
    pallas_call x2, Pallas kernels, attn_bias(): pl.pallas_call(functools.partial(skip_refs, bias_kernel, n_in, len(before...  26.1 us
    pallas_call x1, Pallas kernels, attn_fwd(): pl.pallas_call(functools.partial(skip_refs, fwd_kernel, n_in, len(before)...  19.8 us
    convert_element_type x12, other arithmetic, add_low(): return total.astype(terms[0].dtype)  15 us
  transfers between devices with their start and end apart: 49, of which 12 were waited for; matrix products, arithmetic and copies ran while one was open for 11% of the time, Pallas kernels for 45%

profile of v6, /device:TPU:0, one launch (start us, length us, event | category | flops | bytes accessed | tf_op | source)
XLA Modules:
  0.0 324.0 jit_solution(2164611415128561172)
XLA Ops:
  0.7 0.9 pad_add_fusion
  2.9 2.8 collective-permute-start.1
  5.8 1.5 collective-permute-start.2
  7.3 2.0 collective-permute-start.4
  9.2 1.5 collective-permute-start.5
  13.4 1.1 copy.144
  15.3 1.2 copy.116
  16.6 1.0 copy.126.t_ref
  19.5 1.0 copy.122.refs_3_
  20.5 13.1 %attn_bias.2 = (f32[32,128,1024]{2,1,0:T(8,128)}, bf16[32,1024,512]{2,1,0:T(8,128)(2,1)}) custom-call(f32[32,8,128]{2,1,0:T(8,128)} %copy-done.2, f32[1024,4]{1,0:T(8,128)} %bitcast.259, bf16[1024,128]{1,0:T(8,128)(2,1)} %copy.121.refs_2_, bf16[1024,256]{1,0:T(8,128)(2,1)} %copy.122.refs_3_), custom_call_target="tpu_custom_call" | custom-call | flops 2307000064 | tf_op jit(solution)/shard_map/attn_bias/pallas_call | solution.py:286
  36.0 1.9 collective-permute-start.11
  38.0 1.5 collective-permute-start.12
  42.7 12.9 %attn_bias.3 = (f32[32,128,1024]{2,1,0:T(8,128)}, bf16[32,1024,512]{2,1,0:T(8,128)(2,1)}) custom-call(f32[32,8,128]{2,1,0:T(8,128)} %copy-done.2, f32[1024,4]{1,0:T(8,128)} %bitcast.260, bf16[1024,128]{1,0:T(8,128)(2,1)} %copy.121.refs_2_, bf16[1024,256]{1,0:T(8,128)(2,1)} %copy.122.refs_3_, ...), custom_call_target="tpu_custom_call", output_to_operand_aliasing={{0}: (4, {}), {1}: (5, {})} | custom-call | flops 2307000064 | tf_op jit(solution)/shard_map/attn_bias/pallas_call | solution.py:286
  55.7 9.7 %qkv_forward.1 = (bf16[1024,768]{1,0:T(8,128)(2,1)}, bf16[1024,768]{1,0:T(8,128)(2,1)}, bf16[1024,768]{1,0:T(8,128)(2,1)}, bf16[1024,768]{1,0:T(8,128)(2,1)}) custom-call(s32[8]{0:T(128)} %copy-done.15, bf16[1024,768]{1,0:T(8,128)(2,1)} %x_ref.5, f32[1024,1]{1,0:T(8,128)} %copy.126.t_ref, f32[8,768]{1,0:T(8,128)} %concatenate.53.vec_ref, ...), custom_call_target="tpu_custom_call" | custom-call | flops 11534999552 | tf_op jit(solution)/shard_map/qkv_forward/pallas_call | solution.py:519
  65.5 1.9 collective-permute-done.11.rest_2_
  67.4 1.5 collective-permute-done.12.rest_4_
  68.9 1.2 slice.437
  70.6 1.1 slice.438
  71.7 1.6 collective-permute-start.13
  73.8 19.8 %attn_fwd.1 = (bf16[1024,768]{1,0:T(8,128)(2,1)}, bf16[32,128,1024]{2,1,0:T(8,128)(2,1)}) custom-call(bf16[1024,768]{1,0:T(8,128)(2,1)} %get-tuple-element.163.refs_0_, bf16[1024,768]{1,0:T(8,128)(2,1)} %get-tuple-element.164.refs_1_.refs_2_, bf16[1024,768]{1,0:T(8,128)(2,1)} %get-tuple-element.165.refs_2_.refs_3_, f32[32,128,1024]{2,1,0:T(8,128)} %get-tuple-element.166.refs_3_), custom_call_target="tpu_custom_call" | custom-call | flops 18456000512 | tf_op jit(solution)/shard_map/attn_fwd/pallas_call | solution.py:309
  94.3 2.8 collective-permute-done.19.rest_9_
  97.9 0.9 copy-done.17
  98.8 54.5 %ffn_both.1 = (bf16[1024,768]{1,0:T(8,128)(2,1)}, bf16[1024,768]{1,0:T(8,128)(2,1)}, f32[8,768]{1,0:T(8,128)}, f32[1024,768]{1,0:T(8,128)}, bf16[4,864,768]{2,1,0:T(8,128)(2,1)}, /*index=5*/bf16[4,864,768]{2,1,0:T(8,128)(2,1)}) custom-call(s32[8]{0:T(128)} %copy-done.15, bf16[1024,768]{1,0:T(8,128)(2,1)} %x_ref.5, f32[1024,1]{1,0:T(8,128)} %copy.126.t_ref, ...), custom_call_target="tpu_custom_call" | custom-call | flops 69209997312 | tf_op jit(solution)/shard_map/ffn_both/pallas_call | solution.py:700
  153.5 8.2 %attn_bwd.4 = (bf16[1024,2304]{1,0:T(8,128)(2,1)}, bf16[32,512,256]{2,1,0:T(8,128)(2,1)}) custom-call(bf16[1024,768]{1,0:T(8,128)(2,1)} %get-tuple-element.163.refs_0_, bf16[1024,768]{1,0:T(8,128)(2,1)} %get-tuple-element.183.refs_1_, bf16[1024,768]{1,0:T(8,128)(2,1)} %get-tuple-element.164.refs_1_.refs_2_, ...), custom_call_target="tpu_custom_call" | custom-call | flops 2307000064 | tf_op jit(solution)/shard_map/attn_bwd/pallas_call | solution.py:334
  162.5 3.1 add_convert_fusion.3
  165.8 1.6 collective-permute-start.21
  167.9 8.2 %attn_bwd.5 = (bf16[1024,2304]{1,0:T(8,128)(2,1)}, bf16[32,512,256]{2,1,0:T(8,128)(2,1)}) custom-call(bf16[1024,768]{1,0:T(8,128)(2,1)} %get-tuple-element.163.refs_0_, bf16[1024,768]{1,0:T(8,128)(2,1)} %get-tuple-element.183.refs_1_, bf16[1024,768]{1,0:T(8,128)(2,1)} %get-tuple-element.164.refs_1_.refs_2_, ...), custom_call_target="tpu_custom_call", output_to_operand_aliasing={{0}: (5, {}), {1}: (6, {})} | custom-call | flops 2307000064 | tf_op jit(solution)/shard_map/attn_bwd/pallas_call | solution.py:334
  176.0 8.2 %attn_bwd.6 = (bf16[1024,2304]{1,0:T(8,128)(2,1)}, bf16[32,512,256]{2,1,0:T(8,128)(2,1)}) custom-call(bf16[1024,768]{1,0:T(8,128)(2,1)} %get-tuple-element.163.refs_0_, bf16[1024,768]{1,0:T(8,128)(2,1)} %get-tuple-element.183.refs_1_, bf16[1024,768]{1,0:T(8,128)(2,1)} %get-tuple-element.164.refs_1_.refs_2_, ...), custom_call_target="tpu_custom_call", output_to_operand_aliasing={{0}: (5, {}), {1}: (6, {})} | custom-call | flops 2307000064 | tf_op jit(solution)/shard_map/attn_bwd/pallas_call | solution.py:334
  184.2 8.2 %attn_bwd.7 = (bf16[1024,2304]{1,0:T(8,128)(2,1)}, bf16[32,512,256]{2,1,0:T(8,128)(2,1)}) custom-call(bf16[1024,768]{1,0:T(8,128)(2,1)} %get-tuple-element.163.refs_0_, bf16[1024,768]{1,0:T(8,128)(2,1)} %get-tuple-element.183.refs_1_, bf16[1024,768]{1,0:T(8,128)(2,1)} %get-tuple-element.164.refs_1_.refs_2_, ...), custom_call_target="tpu_custom_call", output_to_operand_aliasing={{0}: (5, {}), {1}: (6, {})} | custom-call | flops 2307000064 | tf_op jit(solution)/shard_map/attn_bwd/pallas_call | solution.py:334
  192.4 8.9 %qkv_weight_grad.1 = (bf16[4,288,768]{2,1,0:T(8,128)(2,1)}, bf16[4,288,768]{2,1,0:T(8,128)(2,1)}) custom-call(s32[8]{0:T(128)} %copy-done.15, bf16[1024,768]{1,0:T(8,128)(2,1)} %get-tuple-element.201.normed_ref, bf16[1024,2304]{1,0:T(8,128)(2,1)} %get-tuple-element.195.gp_ref), custom_call_target="tpu_custom_call" | custom-call | flops 2307000064 | tf_op jit(solution)/shard_map/qkv_weight_grad/pallas_call | solution.py:749
  201.3 2.4 fusion.3
  203.8 1.6 collective-permute-start.23
  205.9 11.8 %first_backward.1 = (bf16[1024,768]{1,0:T(8,128)(2,1)}, f32[8,768]{1,0:T(8,128)}) custom-call(s32[8]{0:T(128)} %copy-done.15, bf16[1024,768]{1,0:T(8,128)(2,1)} %x_ref.5, f32[1024,1]{1,0:T(8,128)} %copy.126.t_ref, f32[1024,768]{1,0:T(8,128)} %get-tuple-element.182.gm_ref, bf16[1024,2304]{1,0:T(8,128)(2,1)} %get-tuple-element.195.gp_ref, ...), custom_call_target="tpu_custom_call" | custom-call | flops 3460499968 | tf_op jit(solution)/shard_map/first_backward/pallas_call | solution.py:797
  217.8 3.4 %collective-permute-done.23 = bf16[432,768]{1,0:T(8,128)(2,1)S(1)} collective-permute-done((bf16[432,768]{1,0:T(8,128)(2,1)S(1)}, bf16[432,768]{1,0:T(8,128)(2,1)S(1)}, u32[]{:S(2)}, u32[]{:S(2)}) %collective-permute-start.23) | collective-permute-done | bytes 663584 | tf_op jit(solution)/shard_map/ppermute | solution.py:817
  221.1 1.4 collective-permute-done.24
  222.5 2.7 fusion
  226.9 1.5 collective-permute-start.26
  228.4 1.5 add_convert_fusion.15
  231.9 1.0 copy.131.amat_ref
  233.7 9.3 %attn_feat.4 = (f32[128,256]{1,0:T(8,128)}, f32[2,128,128]{2,1,0:T(8,128)}) custom-call(bf16[32,512,256]{2,1,0:T(8,128)(2,1)} %get-tuple-element.211.ds_ref, bf16[32,1024,512]{2,1,0:T(8,128)(2,1)} %get-tuple-element.212.f_ref, f32[32,8,128]{2,1,0:T(8,128)} %copy-done.2, f32[1024,4]{1,0:T(8,128)} %bitcast.261, bf16[1024,256]{1,0:T(8,128)(2,1)} %copy.131.amat_ref, ...), custom_call_target="tpu_custom_call" | custom-call | flops 1153500032 | tf_op jit(solution)/shard_map/attn_feat/pallas_call | solution.py:357
  243.0 1.0 add_convert_fusion.9
  244.1 1.5 fusion.9
  245.5 1.6 collective-permute-start.31
  247.1 1.5 collective-permute-start.32
  248.6 1.1 add_convert_fusion.7
  249.7 2.7 collective-permute-start.29
  252.3 9.3 %attn_feat.5 = (f32[128,256]{1,0:T(8,128)}, f32[2,128,128]{2,1,0:T(8,128)}) custom-call(bf16[32,512,256]{2,1,0:T(8,128)(2,1)} %get-tuple-element.211.ds_ref, bf16[32,1024,512]{2,1,0:T(8,128)(2,1)} %get-tuple-element.212.f_ref, f32[32,8,128]{2,1,0:T(8,128)} %copy-done.2, f32[1024,4]{1,0:T(8,128)} %bitcast.262, bf16[1024,256]{1,0:T(8,128)(2,1)} %copy.131.amat_ref, ...), custom_call_target="tpu_custom_call" | custom-call | flops 1153500032 | tf_op jit(solution)/shard_map/attn_feat/pallas_call | solution.py:357
  261.7 1.5 fusion.6
  263.9 0.9 collective-permute-start.33
  264.9 2.9 collective-permute-start.38
  267.8 9.6 %attn_feat.6 = (f32[128,256]{1,0:T(8,128)}, f32[2,128,128]{2,1,0:T(8,128)}) custom-call(bf16[32,512,256]{2,1,0:T(8,128)(2,1)} %get-tuple-element.211.ds_ref, bf16[32,1024,512]{2,1,0:T(8,128)(2,1)} %get-tuple-element.212.f_ref, f32[32,8,128]{2,1,0:T(8,128)} %copy-done.2, f32[1024,4]{1,0:T(8,128)} %bitcast.263, bf16[1024,256]{1,0:T(8,128)(2,1)} %copy.131.amat_ref, ...), custom_call_target="tpu_custom_call" | custom-call | flops 1153500032 | tf_op jit(solution)/shard_map/attn_feat/pallas_call | solution.py:357
  277.4 1.4 collective-permute-start.39
  278.8 9.7 %attn_feat.7 = (f32[128,256]{1,0:T(8,128)}, f32[2,128,128]{2,1,0:T(8,128)}, f32[128,128]{1,0:T(8,128)}) custom-call(bf16[32,512,256]{2,1,0:T(8,128)(2,1)} %get-tuple-element.211.ds_ref, bf16[32,1024,512]{2,1,0:T(8,128)(2,1)} %get-tuple-element.212.f_ref, f32[32,8,128]{2,1,0:T(8,128)} %copy-done.2, f32[1024,4]{1,0:T(8,128)} %bitcast.264, ...), custom_call_target="tpu_custom_call" | custom-call | flops 1153500032 | tf_op jit(solution)/shard_map/attn_feat/pallas_call | solution.py:357
  290.1 1.2 collective-permute-start.36
  292.2 1.0 collective-permute-done.39
  294.1 2.2 collective-permute-start.42
  297.1 1.4 collective-permute-start.44
  298.5 6.2 %collective-permute-done.45 = bf16[144,768]{1,0:T(8,128)(2,1)S(1)} collective-permute-done((bf16[144,768]{1,0:T(8,128)(2,1)S(1)}, bf16[144,768]{1,0:T(8,128)(2,1)S(1)}, u32[]{:S(2)}, u32[]{:S(2)}) %collective-permute-start.45) | collective-permute-done | bytes 221216 | tf_op jit(solution)/shard_map/ppermute | solution.py:817
  304.8 7.1 %collective-permute-done.44 = bf16[240,768]{1,0:T(8,128)(2,1)S(1)} collective-permute-done((bf16[240,768]{1,0:T(8,128)(2,1)S(1)}, bf16[240,768]{1,0:T(8,128)(2,1)S(1)}, u32[]{:S(2)}, u32[]{:S(2)}) %collective-permute-start.44) | collective-permute-done | bytes 368672 | tf_op jit(solution)/shard_map/ppermute | solution.py:817
  312.0 0.9 collective-permute-start.46
  312.9 2.8 collective-permute-start.47
  316.5 1.1 slice.498
  318.3 1.1 copy.137
  319.5 1.0 copy.136
  (227 shorter events, 31.3 us)
Async XLA Ops:
  0.7 13.9 %copy-start.10 = (bf16[96,768]{1,0:T(8,128)(2,1)S(1)}, bf16[96,768]{1,0:T(8,128)(2,1)}, u32[]{:S(2)}) copy-start(bf16[96,768]{1,0:T(8,128)(2,1)} %param.33) | copy-start | bytes 442372
  0.7 13.9 %copy-start.5 = (bf16[384,768]{1,0:T(8,128)(2,1)S(1)}, bf16[384,768]{1,0:T(8,128)(2,1)}, u32[]{:S(2)}) copy-start(bf16[384,768]{1,0:T(8,128)(2,1)} %param.42) | copy-start | bytes 1769476
  1.6 1.3 collective-permute-start
  2.1 12.6 %copy-start.15 = (s32[8]{0:T(128)}, s32[8]{0:T(128)S(1)}, u32[]{:S(2)}) copy-start(s32[8]{0:T(128)S(1)} %iota_xor_fusion.idx_ref) | copy-start | bytes 100
  2.9 14.7 %collective-permute-start.1 = (bf16[2,32,128]{2,1,0:T(8,128)(2,1)S(1)}, bf16[2,32,128]{2,1,0:T(8,128)(2,1)S(1)}, u32[]{:S(2)}, u32[]{:S(2)}) collective-permute-start(bf16[2,32,128]{2,1,0:T(8,128)(2,1)S(1)} %pad_maximum_fusion.8), channel_id=1, source_target_pairs={{0,8},{4,12},{8,0},{12,4},{16,24},{20,28},{24,16},{28,20},{1,9},{5... | collective-permute-start | bytes 49160 | tf_op jit(solution)/shard_map/ppermute | solution.py:817
  5.8 11.9 %collective-permute-start.2 = (bf16[2,32,128]{2,1,0:T(8,128)(2,1)S(1)}, bf16[2,32,128]{2,1,0:T(8,128)(2,1)S(1)}, u32[]{:S(2)}, u32[]{:S(2)}) collective-permute-start(bf16[2,32,128]{2,1,0:T(8,128)(2,1)S(1)} %pad_maximum_fusion.8), channel_id=1, source_target_pairs={{0,16},{4,20},{8,24},{12,28},{16,0},{20,4},{24,8},{28,12},{1,17},{... | collective-permute-start | bytes 49160 | tf_op jit(solution)/shard_map/ppermute | solution.py:817
  7.3 10.4 %collective-permute-start.3 = (bf16[2,32,128]{2,1,0:T(8,128)(2,1)S(1)}, bf16[2,32,128]{2,1,0:T(8,128)(2,1)S(1)}, u32[]{:S(2)}, u32[]{:S(2)}) collective-permute-start(bf16[2,32,128]{2,1,0:T(8,128)(2,1)S(1)} %pad_maximum_fusion.8), channel_id=1, source_target_pairs={{0,24},{4,28},{8,16},{12,20},{16,8},{20,12},{24,0},{28,4},{1,25},{... | collective-permute-start | bytes 49160 | tf_op jit(solution)/shard_map/ppermute | solution.py:817
  7.3 26.4 %collective-permute-start.4 = (bf16[96,2304]{1,0:T(8,128)(2,1)}, bf16[96,2304]{1,0:T(8,128)(2,1)S(1)}, u32[]{:S(2)}, u32[]{:S(2)}) collective-permute-start(bf16[96,2304]{1,0:T(8,128)(2,1)} %rest_0_.1), channel_id=1, source_target_pairs={{0,8},{4,12},{8,0},{12,4},{16,24},{20,28},{24,16},{28,20},{1,9},{5... | collective-permute-start | bytes 1327112 | tf_op jit(solution)/shard_map/ppermute | solution.py:817
  9.2 24.4 %collective-permute-start.5 = (bf16[96,2304]{1,0:T(8,128)(2,1)}, bf16[96,2304]{1,0:T(8,128)(2,1)}, u32[]{:S(2)}, u32[]{:S(2)}) collective-permute-start(bf16[96,2304]{1,0:T(8,128)(2,1)} %rest_0_.1), channel_id=1, source_target_pairs={{0,16},{4,20},{8,24},{12,28},{16,0},{20,4},{24,8},{28,12},{1,17},{... | collective-permute-start | bytes 1327112 | tf_op jit(solution)/shard_map/ppermute | solution.py:817
  14.6 2.0 copy-start.14
  14.6 3.0 copy-start.6
  15.3 40.3 %copy-start.4 = (bf16[864,768]{1,0:T(8,128)(2,1)}, bf16[864,768]{1,0:T(8,128)(2,1)S(1)}, u32[]{:S(2)}) copy-start(bf16[864,768]{1,0:T(8,128)(2,1)S(1)} %pad_maximum_fusion.rest_0_) | copy-start | bytes 3981316
  17.6 16.1 %collective-permute-start.6 = (bf16[96,2304]{1,0:T(8,128)(2,1)S(1)}, bf16[96,2304]{1,0:T(8,128)(2,1)S(1)}, u32[]{:S(2)}, u32[]{:S(2)}) collective-permute-start(bf16[96,2304]{1,0:T(8,128)(2,1)S(1)} %copy-done.6), channel_id=1, source_target_pairs={{0,24},{4,28},{8,16},{12,20},{16,8},{20,12},{24,0},{28,4},{1,25},{... | collective-permute-start | bytes 1327112 | tf_op jit(solution)/shard_map/ppermute | solution.py:817
  19.5 14.1 %copy-start = (bf16[32,8,8,128]{3,1,2,0:T(8,128)(2,1)}, bf16[32,8,8,128]{3,1,2,0:T(8,128)(2,1)S(1)}, u32[]{:S(2)}) copy-start(bf16[32,8,8,128]{3,1,2,0:T(8,128)(2,1)S(1)} %copy.145) | copy-start | bytes 1572868
  33.7 21.9 %copy-start.7 = (bf16[96,2304]{1,0:T(8,128)(2,1)}, bf16[96,2304]{1,0:T(8,128)(2,1)S(1)}, u32[]{:S(2)}) copy-start(bf16[96,2304]{1,0:T(8,128)(2,1)S(1)} %collective-permute-done.4.rest_2_) | copy-start | bytes 1327108
  33.7 21.9 %copy-start.8 = (bf16[96,2304]{1,0:T(8,128)(2,1)}, bf16[96,2304]{1,0:T(8,128)(2,1)S(1)}, u32[]{:S(2)}) copy-start(bf16[96,2304]{1,0:T(8,128)(2,1)S(1)} %collective-permute-done.6.rest_6_) | copy-start | bytes 1327108
  33.7 4.3 %collective-permute-start.10 = (bf16[96,2304]{1,0:T(8,128)(2,1)S(1)}, bf16[96,2304]{1,0:T(8,128)(2,1)S(1)}, u32[]{:S(2)}, u32[]{:S(2)}) collective-permute-start(bf16[96,2304]{1,0:T(8,128)(2,1)S(1)} %collective-permute-done.6.rest_6_), channel_id=1, source_target_pairs={{0,4},{4,0},{8,12},{12,8},{16,20},{20,16},{24,28},{28,24},{1,5},{5... | collective-permute-start | bytes 1327112 | tf_op jit(solution)/shard_map/ppermute | solution.py:817
  35.0 20.7 %collective-permute-start.7 = (bf16[96,2304]{1,0:T(8,128)(2,1)S(1)}, bf16[96,2304]{1,0:T(8,128)(2,1)}, u32[]{:S(2)}, u32[]{:S(2)}) collective-permute-start(bf16[96,2304]{1,0:T(8,128)(2,1)S(1)} %copy-done.6), channel_id=1, source_target_pairs={{0,4},{4,0},{8,12},{12,8},{16,20},{20,16},{24,28},{28,24},{1,5},{5... | collective-permute-start | bytes 1327112 | tf_op jit(solution)/shard_map/ppermute | solution.py:817
  35.5 20.3 %collective-permute-start.8 = (bf16[96,2304]{1,0:T(8,128)(2,1)S(1)}, bf16[96,2304]{1,0:T(8,128)(2,1)}, u32[]{:S(2)}, u32[]{:S(2)}) collective-permute-start(bf16[96,2304]{1,0:T(8,128)(2,1)S(1)} %collective-permute-done.4.rest_2_), channel_id=1, source_target_pairs={{0,4},{4,0},{8,12},{12,8},{16,20},{20,16},{24,28},{28,24},{1,5},{5... | collective-permute-start | bytes 1327112 | tf_op jit(solution)/shard_map/ppermute | solution.py:817
  35.5 20.3 %collective-permute-start.9 = (bf16[96,2304]{1,0:T(8,128)(2,1)}, bf16[96,2304]{1,0:T(8,128)(2,1)}, u32[]{:S(2)}, u32[]{:S(2)}) collective-permute-start(bf16[96,2304]{1,0:T(8,128)(2,1)} %collective-permute-done.5.rest_4_), channel_id=1, source_target_pairs={{0,4},{4,0},{8,12},{12,8},{16,20},{20,16},{24,28},{28,24},{1,5},{5... | collective-permute-start | bytes 1327112 | tf_op jit(solution)/shard_map/ppermute | solution.py:817
  36.0 31.4 %collective-permute-start.11 = (bf16[864,768]{1,0:T(8,128)(2,1)S(1)}, bf16[864,768]{1,0:T(8,128)(2,1)}, u32[]{:S(2)}, u32[]{:S(2)}) collective-permute-start(bf16[864,768]{1,0:T(8,128)(2,1)S(1)} %pad_maximum_fusion.rest_0_), channel_id=1, source_target_pairs={{0,8},{4,12},{8,0},{12,4},{16,24},{20,28},{24,16},{28,20},{1,9},{5... | collective-permute-start | bytes 3981320 | tf_op jit(solution)/shard_map/ppermute | solution.py:817
  38.0 17.6 %copy-start.9 = (bf16[96,2304]{1,0:T(8,128)(2,1)}, bf16[96,2304]{1,0:T(8,128)(2,1)S(1)}, u32[]{:S(2)}) copy-start(bf16[96,2304]{1,0:T(8,128)(2,1)S(1)} %collective-permute-done.10.rest_7_) | copy-start | bytes 1327108
  38.0 30.9 %collective-permute-start.12 = (bf16[864,768]{1,0:T(8,128)(2,1)S(1)}, bf16[864,768]{1,0:T(8,128)(2,1)}, u32[]{:S(2)}, u32[]{:S(2)}) collective-permute-start(bf16[864,768]{1,0:T(8,128)(2,1)S(1)} %pad_maximum_fusion.rest_0_), channel_id=1, source_target_pairs={{0,16},{4,20},{8,24},{12,28},{16,0},{20,4},{24,8},{28,12},{1,17},{... | collective-permute-start | bytes 3981320 | tf_op jit(solution)/shard_map/ppermute | solution.py:817
  55.6 38.0 %collective-permute-start.15 = (bf16[864,768]{1,0:T(8,128)(2,1)S(1)}, bf16[864,768]{1,0:T(8,128)(2,1)}, u32[]{:S(2)}, u32[]{:S(2)}) collective-permute-start(bf16[864,768]{1,0:T(8,128)(2,1)S(1)} %pad_maximum_fusion.rest_0_), channel_id=1, source_target_pairs={{0,4},{4,0},{8,12},{12,8},{16,20},{20,16},{24,28},{28,24},{1,5},{5... | collective-permute-start | bytes 3981320 | tf_op jit(solution)/shard_map/ppermute | solution.py:817
  70.0 23.7 %collective-permute-start.16 = (bf16[864,768]{1,0:T(8,128)(2,1)}, bf16[864,768]{1,0:T(8,128)(2,1)}, u32[]{:S(2)}, u32[]{:S(2)}) collective-permute-start(bf16[864,768]{1,0:T(8,128)(2,1)} %collective-permute-done.11.rest_2_), channel_id=1, source_target_pairs={{0,4},{4,0},{8,12},{12,8},{16,20},{20,16},{24,28},{28,24},{1,5},{5... | collective-permute-start | bytes 3981320 | tf_op jit(solution)/shard_map/ppermute | solution.py:817
  70.1 23.6 %collective-permute-start.17 = (bf16[864,768]{1,0:T(8,128)(2,1)}, bf16[864,768]{1,0:T(8,128)(2,1)}, u32[]{:S(2)}, u32[]{:S(2)}) collective-permute-start(bf16[864,768]{1,0:T(8,128)(2,1)} %collective-permute-done.12.rest_4_), channel_id=1, source_target_pairs={{0,4},{4,0},{8,12},{12,8},{16,20},{20,16},{24,28},{28,24},{1,5},{5... | collective-permute-start | bytes 3981320 | tf_op jit(solution)/shard_map/ppermute | solution.py:817
  71.7 22.0 %collective-permute-start.13 = (bf16[480,768]{1,0:T(8,128)(2,1)S(1)}, bf16[480,768]{1,0:T(8,128)(2,1)S(1)}, u32[]{:S(2)}, u32[]{:S(2)}) collective-permute-start(bf16[480,768]{1,0:T(8,128)(2,1)S(1)} %slice.437), channel_id=1, source_target_pairs={{0,16},{4,20},{8,24},{12,28},{16,0},{20,4},{24,8},{28,12},{1,17},{... | collective-permute-start | bytes 2211848 | tf_op jit(solution)/shard_map/ppermute | solution.py:817
  73.3 20.4 %collective-permute-start.14 = (bf16[384,768]{1,0:T(8,128)(2,1)S(1)}, bf16[384,768]{1,0:T(8,128)(2,1)}, u32[]{:S(2)}, u32[]{:S(2)}) collective-permute-start(bf16[384,768]{1,0:T(8,128)(2,1)S(1)} %slice.438), channel_id=1, source_target_pairs={{0,8},{4,12},{8,0},{12,4},{16,24},{20,28},{24,16},{28,20},{1,9},{5... | collective-permute-start | bytes 1769480 | tf_op jit(solution)/shard_map/ppermute | solution.py:817
  93.7 3.4 %copy-start.16 = (bf16[480,768]{1,0:T(8,128)(2,1)}, bf16[480,768]{1,0:T(8,128)(2,1)S(1)}, u32[]{:S(2)}) copy-start(bf16[480,768]{1,0:T(8,128)(2,1)S(1)} %collective-permute-done.13.rest_6_) | copy-start | bytes 2211844
  93.7 3.3 %collective-permute-start.18 = (bf16[480,768]{1,0:T(8,128)(2,1)S(1)}, bf16[480,768]{1,0:T(8,128)(2,1)S(1)}, u32[]{:S(2)}, u32[]{:S(2)}) collective-permute-start(bf16[480,768]{1,0:T(8,128)(2,1)S(1)} %collective-permute-done.13.rest_6_), channel_id=1, source_target_pairs={{0,4},{4,0},{8,12},{12,8},{16,20},{20,16},{24,28},{28,24},{1,5},{5... | collective-permute-start | bytes 2211848 | tf_op jit(solution)/shard_map/ppermute | solution.py:817
  93.8 3.3 %collective-permute-start.19 = (bf16[384,768]{1,0:T(8,128)(2,1)}, bf16[384,768]{1,0:T(8,128)(2,1)S(1)}, u32[]{:S(2)}, u32[]{:S(2)}) collective-permute-start(bf16[384,768]{1,0:T(8,128)(2,1)} %collective-permute-done.14.rest_8_), channel_id=1, source_target_pairs={{0,4},{4,0},{8,12},{12,8},{16,20},{20,16},{24,28},{28,24},{1,5},{5... | collective-permute-start | bytes 1769480 | tf_op jit(solution)/shard_map/ppermute | solution.py:817
  153.3 9.2 %collective-permute-start.20 = (bf16[4,864,768]{2,1,0:T(8,128)(2,1)}, bf16[4,864,768]{2,1,0:T(8,128)(2,1)}, u32[]{:S(2)}, u32[]{:S(2)}) collective-permute-start(bf16[4,864,768]{2,1,0:T(8,128)(2,1)} %get-tuple-element.188), channel_id=1, source_target_pairs={{0,4},{4,0},{8,12},{12,8},{16,20},{20,16},{24,28},{28,24},{1,5},{5... | collective-permute-start | bytes 15925256 | tf_op jit(solution)/shard_map/ppermute | solution.py:817
  165.8 35.5 %collective-permute-start.21 = (bf16[2,432,768]{2,1,0:T(8,128)(2,1)S(1)}, bf16[2,432,768]{2,1,0:T(8,128)(2,1)S(1)}, u32[]{:S(2)}, u32[]{:S(2)}) collective-permute-start(bf16[2,432,768]{2,1,0:T(8,128)(2,1)S(1)} %pad_maximum_fusion.1), channel_id=1, source_target_pairs={{0,8},{4,12},{8,0},{12,4},{16,24},{20,28},{24,16},{28,20},{1,9},{5... | collective-permute-start | bytes 3981320 | tf_op jit(solution)/shard_map/ppermute | solution.py:817
  167.4 33.9 %collective-permute-start.22 = (bf16[2,432,768]{2,1,0:T(8,128)(2,1)S(1)}, bf16[2,432,768]{2,1,0:T(8,128)(2,1)}, u32[]{:S(2)}, u32[]{:S(2)}) collective-permute-start(bf16[2,432,768]{2,1,0:T(8,128)(2,1)S(1)} %pad_maximum_fusion.2), channel_id=1, source_target_pairs={{0,16},{4,20},{8,24},{12,28},{16,0},{20,4},{24,8},{28,12},{1,17},{... | collective-permute-start | bytes 3981320 | tf_op jit(solution)/shard_map/ppermute | solution.py:817
  203.7 23.2 %collective-permute-start.25 = (bf16[4,288,768]{2,1,0:T(8,128)(2,1)}, bf16[4,288,768]{2,1,0:T(8,128)(2,1)}, u32[]{:S(2)}, u32[]{:S(2)}) collective-permute-start(bf16[4,288,768]{2,1,0:T(8,128)(2,1)} %get-tuple-element.208), channel_id=1, source_target_pairs={{0,4},{4,0},{8,12},{12,8},{16,20},{20,16},{24,28},{28,24},{1,5},{5... | collective-permute-start | bytes 5308424 | tf_op jit(solution)/shard_map/ppermute | solution.py:817
  203.8 17.3 %collective-permute-start.23 = (bf16[432,768]{1,0:T(8,128)(2,1)S(1)}, bf16[432,768]{1,0:T(8,128)(2,1)S(1)}, u32[]{:S(2)}, u32[]{:S(2)}) collective-permute-start(bf16[432,768]{1,0:T(8,128)(2,1)S(1)} %get-tuple-element.205), channel_id=1, source_target_pairs={{0,16},{4,20},{8,24},{12,28},{16,0},{20,4},{24,8},{28,12},{1,17},{... | collective-permute-start | bytes 1990664 | tf_op jit(solution)/shard_map/ppermute | solution.py:817
  205.4 17.1 %collective-permute-start.24 = (bf16[432,768]{1,0:T(8,128)(2,1)S(1)}, bf16[432,768]{1,0:T(8,128)(2,1)}, u32[]{:S(2)}, u32[]{:S(2)}) collective-permute-start(bf16[432,768]{1,0:T(8,128)(2,1)S(1)} %get-tuple-element.206), channel_id=1, source_target_pairs={{0,8},{4,12},{8,0},{12,4},{16,24},{20,28},{24,16},{28,20},{1,9},{5... | collective-permute-start | bytes 1990664 | tf_op jit(solution)/shard_map/ppermute | solution.py:817
  226.0 2.4 copy-start.3
  226.9 16.1 %collective-permute-start.26 = (bf16[192,768]{1,0:T(8,128)(2,1)}, bf16[192,768]{1,0:T(8,128)(2,1)}, u32[]{:S(2)}, u32[]{:S(2)}) collective-permute-start(bf16[192,768]{1,0:T(8,128)(2,1)} %get-tuple-element.218), channel_id=1, source_target_pairs={{0,1},{1,0},{2,3},{3,2},{4,5},{5,4},{6,7},{7,6},{8,9},{9,8},{10,11... | collective-permute-start | bytes 884744 | tf_op jit(solution)/shard_map/ppermute | solution.py:817
  229.9 1.9 copy-start.1
  229.9 2.9 copy-start.12
  230.8 13.3 %collective-permute-start.27 = (bf16[2,144,768]{2,1,0:T(8,128)(2,1)}, bf16[2,144,768]{2,1,0:T(8,128)(2,1)}, u32[]{:S(2)}, u32[]{:S(2)}) collective-permute-start(bf16[2,144,768]{2,1,0:T(8,128)(2,1)} %pad_maximum_fusion.4), channel_id=1, source_target_pairs={{0,8},{4,12},{8,0},{12,4},{16,24},{20,28},{24,16},{28,20},{1,9},{5... | collective-permute-start | bytes 1327112 | tf_op jit(solution)/shard_map/ppermute | solution.py:817
  231.3 12.7 %collective-permute-start.28 = (bf16[2,144,768]{2,1,0:T(8,128)(2,1)S(1)}, bf16[2,144,768]{2,1,0:T(8,128)(2,1)}, u32[]{:S(2)}, u32[]{:S(2)}) collective-permute-start(bf16[2,144,768]{2,1,0:T(8,128)(2,1)S(1)} %pad_maximum_fusion.5), channel_id=1, source_target_pairs={{0,16},{4,20},{8,24},{12,28},{16,0},{20,4},{24,8},{28,12},{1,17},{... | collective-permute-start | bytes 1327112 | tf_op jit(solution)/shard_map/ppermute | solution.py:817
  232.9 15.7 %collective-permute-start.30 = (bf16[240,768]{1,0:T(8,128)(2,1)}, bf16[240,768]{1,0:T(8,128)(2,1)}, u32[]{:S(2)}, u32[]{:S(2)}) collective-permute-start(bf16[240,768]{1,0:T(8,128)(2,1)} %get-tuple-element.227), channel_id=1, source_target_pairs={{0,1},{1,0},{2,3},{3,2},{4,5},{5,4},{6,7},{7,6},{8,9},{9,8},{10,11... | collective-permute-start | bytes 1105928 | tf_op jit(solution)/shard_map/ppermute | solution.py:817
  245.5 16.2 %collective-permute-start.31 = (bf16[144,768]{1,0:T(8,128)(2,1)S(1)}, bf16[144,768]{1,0:T(8,128)(2,1)S(1)}, u32[]{:S(2)}, u32[]{:S(2)}) collective-permute-start(bf16[144,768]{1,0:T(8,128)(2,1)S(1)} %get-tuple-element.228), channel_id=1, source_target_pairs={{0,16},{4,20},{8,24},{12,28},{16,0},{20,4},{24,8},{28,12},{1,17},{... | collective-permute-start | bytes 663560 | tf_op jit(solution)/shard_map/ppermute | solution.py:817
  247.1 14.6 %collective-permute-start.32 = (bf16[144,768]{1,0:T(8,128)(2,1)S(1)}, bf16[144,768]{1,0:T(8,128)(2,1)S(1)}, u32[]{:S(2)}, u32[]{:S(2)}) collective-permute-start(bf16[144,768]{1,0:T(8,128)(2,1)S(1)} %get-tuple-element.229), channel_id=1, source_target_pairs={{0,8},{4,12},{8,0},{12,4},{16,24},{20,28},{24,16},{28,20},{1,9},{5... | collective-permute-start | bytes 663560 | tf_op jit(solution)/shard_map/ppermute | solution.py:817
  249.7 14.1 %collective-permute-start.29 = (bf16[192,768]{1,0:T(8,128)(2,1)S(1)}, bf16[192,768]{1,0:T(8,128)(2,1)S(1)}, u32[]{:S(2)}, u32[]{:S(2)}) collective-permute-start(bf16[192,768]{1,0:T(8,128)(2,1)S(1)} %add_convert_fusion.9), channel_id=1, source_target_pairs={{0,2},{1,3},{2,0},{3,1},{4,6},{5,7},{6,4},{7,5},{8,10},{9,11},{10,... | collective-permute-start | bytes 884744 | tf_op jit(solution)/shard_map/ppermute | solution.py:817
  263.2 1.5 copy-start.13
  263.9 13.5 %collective-permute-start.33 = (bf16[144,768]{1,0:T(8,128)(2,1)S(1)}, bf16[144,768]{1,0:T(8,128)(2,1)S(1)}, u32[]{:S(2)}, u32[]{:S(2)}) collective-permute-start(bf16[144,768]{1,0:T(8,128)(2,1)S(1)} %get-tuple-element.235), channel_id=1, source_target_pairs={{0,1},{1,0},{2,3},{3,2},{4,5},{5,4},{6,7},{7,6},{8,9},{9,8},{10,11... | collective-permute-start | bytes 663560 | tf_op jit(solution)/shard_map/ppermute | solution.py:817
  264.9 26.5 %collective-permute-start.38 = (bf16[240,768]{1,0:T(8,128)(2,1)S(1)}, bf16[240,768]{1,0:T(8,128)(2,1)S(1)}, u32[]{:S(2)}, u32[]{:S(2)}) collective-permute-start(bf16[240,768]{1,0:T(8,128)(2,1)S(1)} %add_convert_fusion.7), channel_id=1, source_target_pairs={{0,2},{1,3},{2,0},{3,1},{4,6},{5,7},{6,4},{7,5},{8,10},{9,11},{10,... | collective-permute-start | bytes 1105928 | tf_op jit(solution)/shard_map/ppermute | solution.py:817
  267.7 22.4 %collective-permute-start.43 = (bf16[192,768]{1,0:T(8,128)(2,1)S(1)}, bf16[192,768]{1,0:T(8,128)(2,1)S(1)}, u32[]{:S(2)}, u32[]{:S(2)}) collective-permute-start(bf16[192,768]{1,0:T(8,128)(2,1)S(1)} %add_convert_fusion.8), channel_id=1, source_target_pairs={{0,1},{1,0},{2,3},{3,2},{4,5},{5,4},{6,7},{7,6},{8,9},{9,8},{10,11... | collective-permute-start | bytes 884744 | tf_op jit(solution)/shard_map/ppermute | solution.py:817
  277.4 15.7 %collective-permute-start.39 = (bf16[144,768]{1,0:T(8,128)(2,1)S(1)}, bf16[144,768]{1,0:T(8,128)(2,1)S(1)}, u32[]{:S(2)}, u32[]{:S(2)}) collective-permute-start(bf16[144,768]{1,0:T(8,128)(2,1)S(1)} %add_convert_fusion.11), channel_id=1, source_target_pairs={{0,2},{1,3},{2,0},{3,1},{4,6},{5,7},{6,4},{7,5},{8,10},{9,11},{10,... | collective-permute-start | bytes 663560 | tf_op jit(solution)/shard_map/ppermute | solution.py:817
  289.4 4.0 %collective-permute-start.34 = (f32[28,128]{1,0:T(8,128)S(1)}, f32[28,128]{1,0:T(8,128)S(1)}, u32[]{:S(2)}, u32[]{:S(2)}) collective-permute-start(f32[28,128]{1,0:T(8,128)S(1)} %get-tuple-element.295), channel_id=1, source_target_pairs={{0,4},{4,0},{8,12},{12,8},{16,20},{20,16},{24,28},{28,24},{1,5},{5... | collective-permute-start | bytes 43016 | tf_op jit(solution)/shard_map/ppermute | solution.py:817
  289.5 4.6 %collective-permute-start.35 = (f32[28,128]{1,0:T(8,128)S(1)}, f32[28,128]{1,0:T(8,128)S(1)}, u32[]{:S(2)}, u32[]{:S(2)}) collective-permute-start(f32[28,128]{1,0:T(8,128)S(1)} %get-tuple-element.298), channel_id=1, source_target_pairs={{0,8},{4,12},{8,0},{12,4},{16,24},{20,28},{24,16},{28,20},{1,9},{5... | collective-permute-start | bytes 43016 | tf_op jit(solution)/shard_map/ppermute | solution.py:817
  290.1 6.2 %collective-permute-start.36 = (f32[28,128]{1,0:T(8,128)S(1)}, f32[28,128]{1,0:T(8,128)S(1)}, u32[]{:S(2)}, u32[]{:S(2)}) collective-permute-start(f32[28,128]{1,0:T(8,128)S(1)} %get-tuple-element.297), channel_id=1, source_target_pairs={{0,12},{4,8},{8,4},{12,0},{16,28},{20,24},{24,20},{28,16},{1,13},{... | collective-permute-start | bytes 43016 | tf_op jit(solution)/shard_map/ppermute | solution.py:817
  291.4 5.7 %collective-permute-start.37 = (f32[28,128]{1,0:T(8,128)S(1)}, f32[28,128]{1,0:T(8,128)S(1)}, u32[]{:S(2)}, u32[]{:S(2)}) collective-permute-start(f32[28,128]{1,0:T(8,128)S(1)} %get-tuple-element.296), channel_id=1, source_target_pairs={{0,16},{4,20},{8,24},{12,28},{16,0},{20,4},{24,8},{28,12},{1,17},{... | collective-permute-start | bytes 43016 | tf_op jit(solution)/shard_map/ppermute | solution.py:817
  293.2 5.2 %collective-permute-start.40 = (f32[28,128]{1,0:T(8,128)S(1)}, f32[28,128]{1,0:T(8,128)S(1)}, u32[]{:S(2)}, u32[]{:S(2)}) collective-permute-start(f32[28,128]{1,0:T(8,128)S(1)} %get-tuple-element.299), channel_id=1, source_target_pairs={{0,20},{4,16},{8,28},{12,24},{16,4},{20,0},{24,12},{28,8},{1,21},{... | collective-permute-start | bytes 43016 | tf_op jit(solution)/shard_map/ppermute | solution.py:817
  293.4 5.0 %collective-permute-start.41 = (f32[28,128]{1,0:T(8,128)S(1)}, f32[28,128]{1,0:T(8,128)S(1)}, u32[]{:S(2)}, u32[]{:S(2)}) collective-permute-start(f32[28,128]{1,0:T(8,128)S(1)} %get-tuple-element.301), channel_id=1, source_target_pairs={{0,24},{4,28},{8,16},{12,20},{16,8},{20,12},{24,0},{28,4},{1,25},{... | collective-permute-start | bytes 43016 | tf_op jit(solution)/shard_map/ppermute | solution.py:817
  294.1 4.4 %collective-permute-start.42 = (f32[28,128]{1,0:T(8,128)S(1)}, f32[28,128]{1,0:T(8,128)S(1)}, u32[]{:S(2)}, u32[]{:S(2)}) collective-permute-start(f32[28,128]{1,0:T(8,128)S(1)} %get-tuple-element.300), channel_id=1, source_target_pairs={{0,28},{4,24},{8,20},{12,16},{16,12},{20,8},{24,4},{28,0},{1,29},{... | collective-permute-start | bytes 43016 | tf_op jit(solution)/shard_map/ppermute | solution.py:817
  296.4 8.3 %collective-permute-start.45 = (bf16[144,768]{1,0:T(8,128)(2,1)S(1)}, bf16[144,768]{1,0:T(8,128)(2,1)S(1)}, u32[]{:S(2)}, u32[]{:S(2)}) collective-permute-start(bf16[144,768]{1,0:T(8,128)(2,1)S(1)} %add_convert_fusion.10), channel_id=1, source_target_pairs={{0,1},{1,0},{2,3},{3,2},{4,5},{5,4},{6,7},{7,6},{8,9},{9,8},{10,11... | collective-permute-start | bytes 663560 | tf_op jit(solution)/shard_map/ppermute | solution.py:817
  297.1 14.8 %collective-permute-start.44 = (bf16[240,768]{1,0:T(8,128)(2,1)S(1)}, bf16[240,768]{1,0:T(8,128)(2,1)S(1)}, u32[]{:S(2)}, u32[]{:S(2)}) collective-permute-start(bf16[240,768]{1,0:T(8,128)(2,1)S(1)} %add_convert_fusion.6), channel_id=1, source_target_pairs={{0,1},{1,0},{2,3},{3,2},{4,5},{5,4},{6,7},{7,6},{8,9},{9,8},{10,11... | collective-permute-start | bytes 1105928 | tf_op jit(solution)/shard_map/ppermute | solution.py:817
  312.0 8.4 %collective-permute-start.46 = (f32[28,128]{1,0:T(8,128)S(1)}, f32[28,128]{1,0:T(8,128)S(1)}, u32[]{:S(2)}, u32[]{:S(2)}) collective-permute-start(f32[28,128]{1,0:T(8,128)S(1)} %fusion.17), channel_id=1, source_target_pairs={{0,1},{1,0},{2,3},{3,2},{4,5},{5,4},{6,7},{7,6},{8,9},{9,8},{10,11... | collective-permute-start | bytes 43016 | tf_op jit(solution)/shard_map/ppermute | solution.py:817
  312.9 7.5 %collective-permute-start.47 = (f32[28,128]{1,0:T(8,128)S(1)}, f32[28,128]{1,0:T(8,128)S(1)}, u32[]{:S(2)}, u32[]{:S(2)}) collective-permute-start(f32[28,128]{1,0:T(8,128)S(1)} %fusion.17), channel_id=1, source_target_pairs={{0,2},{1,3},{2,0},{3,1},{4,6},{5,7},{6,4},{7,5},{8,10},{9,11},{10,... | collective-permute-start | bytes 43016 | tf_op jit(solution)/shard_map/ppermute | solution.py:817
  315.7 5.5 %collective-permute-start.48 = (f32[28,128]{1,0:T(8,128)S(1)}, f32[28,128]{1,0:T(8,128)S(1)}, u32[]{:S(2)}, u32[]{:S(2)}) collective-permute-start(f32[28,128]{1,0:T(8,128)S(1)} %fusion.17), channel_id=1, source_target_pairs={{0,3},{1,2},{2,1},{3,0},{4,7},{5,6},{6,5},{7,4},{8,11},{9,10},{10,... | collective-permute-start | bytes 43016 | tf_op jit(solution)/shard_map/ppermute | solution.py:817
  (4 other events, 3.7 us)
